TPU v7x, 128 devices: a whole 4x4x4 slice. The times are simulated.
128 devices in a mesh: section: 2 (over x_hi), dp: 16 (over x_lo, z, core), shard: 4 (over y).
Axes of the slice: x: 4 (x_hi: 2, x_lo: 2; x = x_hi * 2 + x_lo), y: 4, z: 4, core: 2. Of those that a mesh axis runs over, the one named last changes fastest.
Arguments:
- tokens: bfloat16 [128, 128, 1536], P(('dp', 'shard')), may hold values from -6 to 6
- cotangent: bfloat16 [128, 128, 1536], P(('dp', 'shard')), may hold values from -6 to 6
- lengths: int32 [128], P(('dp', 'shard')), may hold values from 1 to 128, 12288 in all
- norm_gain: bfloat16 [2, 1536], P('section', 'shard'), may hold values from 0.5 to 1.5
- in_weight: bfloat16 [2, 1536, 6448], P('section', 'shard'), may hold values from -0.15625 to 0.15625
- conv_weight: bfloat16 [2, 4, 3328], P('section', None, 'shard'), may hold values from -3 to 3
- conv_bias: bfloat16 [2, 3328], P('section', 'shard'), may hold values from -3 to 3
- dt_bias: bfloat16 [2, 48], P('section'), may hold values from -6 to -2
- a_log: bfloat16 [2, 48], P('section'), may hold values from 0 to 2
- d_skip: bfloat16 [2, 48], P('section'), may hold values from 0.5 to 1.5
- gate_gain: bfloat16 [2, 3072], P('section', 'shard'), may hold values from 0.5 to 1.5
- out_weight: bfloat16 [2, 3072, 1536], P('section', 'shard'), may hold values from -0.109375 to 0.109375
Outputs:
- ends: float32 [2, 128, 128, 1536], P('section', ('dp', 'shard'))
- grad_norm_gain: float32 [2, 1536], P('section', 'shard')
- grad_in_weight: float32 [2, 1536, 6448], P('section', 'shard')
- grad_conv_weight: float32 [2, 4, 3328], P('section', None, 'shard')
- grad_conv_bias: float32 [2, 3328], P('section', 'shard')
- grad_dt_bias: float32 [2, 48], P('section')
- grad_a_log: float32 [2, 48], P('section')
- grad_d_skip: float32 [2, 48], P('section')
- grad_gate_gain: float32 [2, 3072], P('section', 'shard')
- grad_out_weight: float32 [2, 3072, 1536], P('section', 'shard')
Inputs may be any that keep to these rules, and one draw needn't show every extreme that they name: `lengths`: some sequence has all 128 positions live.
All inputs are finite; a program needn't handle non-finite values. No bound on the sum of `lengths` on one device may be relied on, other than what follows from the above.
Results may differ from a plain program's by a relative error of at most 0.015.
Values may be sent and summed in bfloat16 or wider, within the bound.
No kernel may reach another device: no remote copies, remote signals or barrier semaphores. Data moves between devices by JAX's collectives and lax.ppermute only.
A program may use at most 704 MiB of HBM per device.

v0:
```python
import jax
import jax.numpy as jnp
from jax import lax
from jax.sharding import PartitionSpec as P

SPAN = 256


def from_partner(value, axis, stride):
    return lax.ppermute(value, axis, [(i, i ^ 1 << stride) for i in range(lax.axis_size(axis))])


def scan_heads(values, inbound, outbound, step_size, rate):
    length = values.shape[0]
    heads = values.shape[1]
    head_dim = values.shape[2]
    state = inbound.shape[1]
    block_len = min(SPAN, length)
    blocks = length // block_len
    highest = lax.Precision.HIGHEST
    running = jnp.cumsum((step_size * rate[None, :]).reshape(blocks, block_len, heads), axis=1)
    scaled = (values * step_size[:, :, None]).reshape(blocks, block_len, heads, head_dim)
    keys_in = inbound.reshape(blocks, block_len, state)
    queries = outbound.reshape(blocks, block_len, state)
    scores = jnp.einsum("cqn,csn->cqs", queries, keys_in, precision=highest)
    causal = jnp.arange(block_len)[:, None] >= jnp.arange(block_len)[None, :]
    gaps = running[:, :, None, :] - running[:, None, :, :]
    decays = jnp.exp(jnp.where(causal[None, :, :, None], gaps, -1e30))
    inner = jnp.einsum("cqs,cqsh,cshp->cqhp", scores, decays, scaled, precision=highest)
    tails = jnp.exp(running[:, -1:, :] - running)
    states = jnp.einsum("csn,csh,cshp->chpn", keys_in, tails, scaled, precision=highest)
    block_decay = jnp.exp(running[:, -1, :])

    def carry_state(carried, item):
        return (carried * item[0][:, None, None] + item[1], carried)

    _, before = lax.scan(
        carry_state, jnp.zeros((heads, head_dim, state), jnp.float32), (block_decay, states)
    )
    outer = jnp.einsum("cqn,cqh,chpn->cqhp", queries, jnp.exp(running), before, precision=highest)
    return (inner + outer).reshape(length, heads, head_dim)


def input_norm(inputs, norm_gain):
    return inputs * lax.rsqrt(jnp.mean(inputs * inputs, axis=-1, keepdims=True) + 1e-05) * norm_gain


def layer_middle(projected, conv_weight, conv_bias, dt_bias, a_log, d_skip, gate_gain):
    length = projected.shape[0]
    tap_count = conv_weight.shape[0]
    inner_width = gate_gain.shape[0]
    heads = dt_bias.shape[0]
    head_dim = inner_width // heads
    state = (projected.shape[1] - 2 * inner_width - heads) // 2
    gate_in = projected[:, :inner_width]
    conv_in = projected[:, inner_width : 2 * inner_width + 2 * state]
    step_raw = projected[:, 2 * inner_width + 2 * state :]
    padded = jnp.pad(conv_in, ((tap_count - 1, 0), (0, 0)))
    convolved = conv_bias[None, :] + jnp.zeros_like(conv_in)
    for offset in range(tap_count):
        convolved = convolved + padded[offset : offset + length] * conv_weight[offset][None, :]
    mixed = jax.nn.silu(convolved)
    values = mixed[:, :inner_width].reshape(length, heads, head_dim)
    inbound = mixed[:, inner_width : inner_width + state]
    outbound = mixed[:, inner_width + state :]
    step_size = jax.nn.softplus(step_raw + dt_bias[None, :])
    rate = -jnp.exp(a_log)
    scanned = (
        scan_heads(values, inbound, outbound, step_size, rate) + d_skip[None, :, None] * values
    )
    gated = scanned.reshape(length, inner_width) * jax.nn.silu(gate_in)
    return gated * lax.rsqrt(jnp.mean(gated * gated, axis=-1, keepdims=True) + 1e-05) * gate_gain


def regroup(array, axis_dim, outer_count, inner_count):
    shape_now = array.shape
    parted = (
        shape_now[:axis_dim]
        + (outer_count, inner_count, shape_now[axis_dim] // (outer_count * inner_count))
        + shape_now[axis_dim + 1 :]
    )
    return jnp.swapaxes(array.reshape(parted), axis_dim, axis_dim + 1).reshape(shape_now)


def shards(
    tokens,
    cotangent,
    lengths,
    norm_gain,
    in_weight,
    conv_weight,
    conv_bias,
    dt_bias,
    a_log,
    d_skip,
    gate_gain,
    out_weight,
):
    gathered = (
        lax.all_gather(norm_gain, "shard", axis=1, tiled=True),
        lax.all_gather(in_weight, "shard", axis=1, tiled=True),
        lax.all_gather(conv_weight, "shard", axis=2, tiled=True),
        lax.all_gather(conv_bias, "shard", axis=1, tiled=True),
        lax.all_gather(gate_gain, "shard", axis=1, tiled=True),
        lax.all_gather(out_weight, "shard", axis=1, tiled=True),
    )
    in_low = gathered[1][0]
    out_low = gathered[5][0]
    params = (
        gathered[0][0],
        gathered[1][0],
        gathered[2][0],
        gathered[3][0],
        dt_bias[0],
        a_log[0],
        d_skip[0],
        gathered[4][0],
        gathered[5][0],
    )
    params = tuple((array.astype(jnp.float32) for array in params))
    batch_count = tokens.shape[0]
    seq_len = tokens.shape[1]
    model_width = tokens.shape[2]
    keep_ids = (0, 1, 2, 3, 4, 5, 6, 7, 8)
    row_masks = (jnp.arange(seq_len, dtype=jnp.int32)[None, :] < lengths[:, None]).astype(
        jnp.float32
    )
    section_index = lax.axis_index("section")
    zero_row = jnp.zeros((seq_len, model_width), jnp.float32)
    zero_sent = jnp.zeros((seq_len, model_width), jnp.bfloat16)
    zero_grads = tuple((jnp.zeros_like(params[index]) for index in keep_ids))
    totals = zero_grads
    first_rows = [zero_row] * batch_count
    second_rows = [zero_row] * batch_count
    incoming = zero_sent

    def layer_forward(inputs, row_mask):
        normed = input_norm(inputs, params[0])
        projected = jnp.dot(normed.astype(jnp.bfloat16), in_low, preferred_element_type=jnp.float32)
        normed_out = layer_middle(
            projected, params[2], params[3], params[4], params[5], params[6], params[7]
        )
        branch = jnp.dot(
            normed_out.astype(jnp.bfloat16), out_low, preferred_element_type=jnp.float32
        )
        return inputs + row_mask[:, None] * branch

    def backward_pass(item_index, inputs, grad_out):
        row_mask = row_masks[item_index]
        normed, pull_norm = jax.vjp(input_norm, inputs, params[0])
        normed_low = normed.astype(jnp.bfloat16)
        projected = jnp.dot(normed_low, in_low, preferred_element_type=jnp.float32)
        normed_out, pull_middle = jax.vjp(
            layer_middle,
            projected,
            params[2],
            params[3],
            params[4],
            params[5],
            params[6],
            params[7],
        )
        out_in_low = normed_out.astype(jnp.bfloat16)
        branch = jnp.dot(out_in_low, out_low, preferred_element_type=jnp.float32)
        result = inputs + row_mask[:, None] * branch
        branch_grad = (row_mask[:, None] * grad_out).astype(jnp.bfloat16)
        normed_out_grad = lax.dot_general(
            branch_grad, out_low, (((1,), (1,)), ((), ())), preferred_element_type=jnp.float32
        )
        middle_grads = pull_middle(normed_out_grad)
        proj_grad = middle_grads[0].astype(jnp.bfloat16)
        normed_grad = lax.dot_general(
            proj_grad, in_low, (((1,), (1,)), ((), ())), preferred_element_type=jnp.float32
        )
        inputs_grad, gain_grad = pull_norm(normed_grad)
        input_grad = grad_out + inputs_grad
        in_grad = lax.dot_general(
            normed_low, proj_grad, (((0,), (0,)), ((), ())), preferred_element_type=jnp.float32
        )
        out_grad = lax.dot_general(
            out_in_low, branch_grad, (((0,), (0,)), ((), ())), preferred_element_type=jnp.float32
        )
        picked = (
            gain_grad,
            in_grad,
            middle_grads[1],
            middle_grads[2],
            middle_grads[3],
            middle_grads[4],
            middle_grads[5],
            middle_grads[6],
            out_grad,
        )
        extras = (normed_low, proj_grad, out_in_low, branch_grad)
        return (result, picked, input_grad, extras)

    for period in range(batch_count + 2):

        def first_section(arrived):
            outgoing = zero_sent
            if period < batch_count:
                outgoing = layer_forward(
                    tokens[period].astype(jnp.float32), row_masks[period]
                ).astype(jnp.bfloat16)
            if period >= 2:
                item_index = period - 2
                _, picked, input_grad, extras = backward_pass(
                    item_index, tokens[item_index].astype(jnp.float32), arrived.astype(jnp.float32)
                )
                return (outgoing, picked, input_grad)
            return (outgoing, zero_grads, zero_row)

        def second_section(arrived):
            item_index = period - 1
            if 0 <= item_index < batch_count:
                result, picked, input_grad, extras = backward_pass(
                    item_index,
                    arrived.astype(jnp.float32),
                    cotangent[item_index].astype(jnp.float32),
                )
                return (input_grad.astype(jnp.bfloat16), picked, result)
            return (zero_sent, zero_grads, zero_row)

        returned = lax.cond(section_index == 0, first_section, second_section, incoming)
        outgoing, param_grads, kept_row = (returned[0], returned[1], returned[2])
        totals = tuple((left + right for left, right in zip(totals, param_grads)))
        if period >= 2:
            first_rows[period - 2] = kept_row
        if 1 <= period <= batch_count:
            second_rows[period - 1] = kept_row
        if period < batch_count + 1:
            incoming = from_partner(outgoing, "section", 0)
    ends = jnp.where(section_index == 0, jnp.stack(first_rows), jnp.stack(second_rows))[None]
    grads_by = dict(zip(keep_ids, totals))
    head_grads = lax.psum((grads_by[4], grads_by[5], grads_by[6]), ("dp", "shard"))
    large = (grads_by[0], grads_by[1], grads_by[2], grads_by[3], grads_by[7], grads_by[8])
    shard_count = lax.axis_size("shard")
    data_count = lax.axis_size("dp")
    dims_list = (0, 0, 1, 0, 0, 0)
    arranged = tuple(
        (
            regroup(array, axis_dim, shard_count, data_count)
            for array, axis_dim in zip(large, dims_list)
        )
    )
    pieces = (
        lax.psum_scatter(arranged[0], ("dp", "shard"), scatter_dimension=0, tiled=True),
        lax.psum_scatter(arranged[1], ("dp", "shard"), scatter_dimension=0, tiled=True),
        lax.psum_scatter(arranged[2], ("dp", "shard"), scatter_dimension=1, tiled=True),
        lax.psum_scatter(arranged[3], ("dp", "shard"), scatter_dimension=0, tiled=True),
        lax.psum_scatter(arranged[4], ("dp", "shard"), scatter_dimension=0, tiled=True),
        lax.psum_scatter(arranged[5], ("dp", "shard"), scatter_dimension=0, tiled=True),
    )
    owned = (
        lax.all_gather(pieces[0].astype(jnp.bfloat16), "dp", axis=0, tiled=True).astype(
            jnp.float32
        ),
        lax.all_gather(pieces[1].astype(jnp.bfloat16), "dp", axis=0, tiled=True).astype(
            jnp.float32
        ),
        lax.all_gather(pieces[2].astype(jnp.bfloat16), "dp", axis=1, tiled=True).astype(
            jnp.float32
        ),
        lax.all_gather(pieces[3].astype(jnp.bfloat16), "dp", axis=0, tiled=True).astype(
            jnp.float32
        ),
        lax.all_gather(pieces[4].astype(jnp.bfloat16), "dp", axis=0, tiled=True).astype(
            jnp.float32
        ),
        lax.all_gather(pieces[5].astype(jnp.bfloat16), "dp", axis=0, tiled=True).astype(
            jnp.float32
        ),
    )
    return (
        ends,
        owned[0][None],
        owned[1][None],
        owned[2][None],
        owned[3][None],
        head_grads[0][None],
        head_grads[1][None],
        head_grads[2][None],
        owned[4][None],
        owned[5][None],
    )


def solution(mesh):
    return jax.shard_map(
        shards,
        mesh=mesh,
        in_specs=(
            P(("dp", "shard"), None, None),
            P(("dp", "shard"), None, None),
            P(("dp", "shard")),
            P("section", "shard"),
            P("section", "shard", None),
            P("section", None, "shard"),
            P("section", "shard"),
            P("section", None),
            P("section", None),
            P("section", None),
            P("section", "shard"),
            P("section", "shard", None),
        ),
        out_specs=(
            P("section", ("dp", "shard"), None, None),
            P("section", "shard"),
            P("section", "shard", None),
            P("section", None, "shard"),
            P("section", "shard"),
            P("section", None),
            P("section", None),
            P("section", None),
            P("section", "shard"),
            P("section", "shard", None),
        ),
        check_vma=False,
    )
```

profile of v0, /device:TPU:4, one launch (start us, length us, event | category | flops | bytes accessed | tf_op | source)
XLA Modules:
  0.0 1961.2 jit_solution(12343584259527020408)
XLA Ops:
  28.5 11.9 all_gather.40
  41.2 31.1 %all_gather.39 = bf16[1,4,3328]{1,0,2:T(2,128)(2,1)S(1)} all-gather(bf16[1,4,832]{1,0,2:T(2,128)(2,1)S(1)} %copy.515), channel_id=1, replica_groups=mesh['section'=2,'dp'=16,'shard'=4] {'shard'}, dimensions={2}, use_global_device_ids=true | all-gather | bytes 33280 | tf_op jit(solution)/shard_map/all_gather | solution.py:102
  85.8 32.2 %all-gather.8.cloned.1.call-done = bf16[1,3072,1536]{2,1,0:T(8,128)(2,1)} async-done(((bf16[1,768,1536]{2,1,0:T(8,128)(2,1)}), bf16[1,3072,1536]{2,1,0:T(8,128)(2,1)}) %all-gather.8.cloned.1.call-update) | async-done | bytes 9437200 | tf_op jit(solution)/shard_map/all_gather | solution.py:105
  117.9 185.2 %all-gather.6.cloned.1.call-done = bf16[1,1536,6448]{2,1,0:T(8,128)(2,1)} async-done(((bf16[1,384,6448]{2,1,0:T(8,128)(2,1)}), bf16[1,1536,6448]{2,1,0:T(8,128)(2,1)}) %all-gather.6.cloned.1.call-update) | async-done | bytes 19808272 | tf_op jit(solution)/shard_map/all_gather | solution.py:101
  308.4 30.2 %collective-permute-start = (bf16[128,1536]{1,0:T(8,128)(2,1)S(1)}, bf16[128,1536]{1,0:T(8,128)(2,1)S(1)}, u32[]{:S(2)}, u32[]{:S(2)}) collective-permute-start(bf16[128,1536]{1,0:T(8,128)(2,1)S(1)} %get-tuple-element.1257), channel_id=1, source_target_pairs={{0,64},{64,0},{1,65},{65,1},{2,66},{66,2},{3,67},{67,3},{4,68},{68... | collective-permute-start | bytes 1179656 | tf_op jit(solution)/shard_map/ppermute | solution.py:10
  347.7 144.9 %conditional.8 = (f32[1536]{0:T(1024)S(1)}, f32[1536,6448]{0,1:T(8,128)}, f32[4,3328]{1,0:T(4,128)}, f32[3328]{0:T(1024)}, f32[48]{0:T(128)S(1)}, /*index=5*/f32...) conditional(s32[]{:T(128)} %convert_element_type.224, ...), branch_computations={%region_5.28_spmd, %region_27.32_spmd} | conditional | flops 15599221760 | bytes 365691296
  352.1 12.4 fusion.169
  465.7 17.1 fusion.167
  494.0 11.8 collective-permute-done.1
  506.5 160.5 %conditional.9 = (bf16[128,1536]{1,0:T(8,128)(2,1)S(1)}, f32[1536,6448]{0,1:T(8,128)}, f32[3072,1536]{1,0:T(8,128)}, f32[]{:T(128)}, f32[128,3328]{0,1:T(8,128)}...) conditional(s32[]{:T(128)} %convert_element_type.224, ...), branch_computations={%region_31.43_spmd, %region_42.54_spmd} | conditional | flops 15592204288 | bytes 364410432
  523.3 12.4 fusion.268
  613.2 11.7 fusion.253
  635.9 16.9 fusion.267
  678.2 33.4 %conditional.10 = (f32[1536]{0:T(1024)S(1)}, f32[1536,6448]{0,1:T(8,128)}, f32[4,3328]{1,0:T(4,128)S(1)}, f32[3328]{0:T(1024)S(1)}, f32[48]{0:T(128)S(1)}, /*ind...) conditional(s32[]{:T(128)} %convert_element_type.224, ...), branch_computations={%region_53.55_spmd, %region_54.77_spmd} | conditional | flops 14389885952 | bytes 350733440 | solution.py:224
  689.1 13.3 broadcast_in_dim.372
  711.6 18.7 add_add_fusion.9
  737.3 51.2 %add_add_fusion.8 = f32[1536,6448]{0,1:T(8,128)} fusion(f32[1536,6448]{0,1:T(8,128)} %get-tuple-element.687, f32[1536,6448]{0,1:T(8,128)} %get-tuple-element.685, f32[1536,6448]{0,1:T(8,128)} %get-tuple-element.686), kind=kLoop, calls=%fused_computation.755 | loop fusion | flops 19808256 | bytes 158466048 | tf_op jit(solution)/shard_map/add | solution.py:226
  788.5 36.8 %copy.523 = f32[1536,6448]{1,0:T(8,128)} copy(f32[1536,6448]{0,1:T(8,128)} %add_add_fusion.8) | data formatting | bytes 79233024 | tf_op jit(solution)/shard_map/add | solution.py:226
  825.3 28.8 %copy.524 = f32[16,4,24,6448]{3,2,1,0:T(8,128)} copy(f32[16,4,24,6448]{3,2,0,1:T(8,128)} %bitcast.738) | data formatting | bytes 79233024 | tf_op jit(solution)/shard_map/transpose | solution.py:82
  854.2 291.1 %reduce-scatter.7.cloned.1.call-done = f32[48,1536]{1,0:T(8,128)} async-done(((f32[3072,1536]{1,0:T(8,128)}), f32[48,1536]{1,0:T(8,128)}) %reduce-scatter.7.cloned.1.call-update) | async-done | bytes 294928 | tf_op jit(solution)/shard_map/reduce_scatter | solution.py:252
  1147.0 435.2 %reduce-scatter.9.cloned.1.call-done = f32[24,6448]{1,0:T(8,128)} async-done(((f32[1536,6448]{1,0:T(8,128)}), f32[24,6448]{1,0:T(8,128)}) %reduce-scatter.9.cloned.1.call-update) | async-done | bytes 619024
  1603.4 279.3 %all-reduce.75 = (bf16[1536]{0:T(1024)(128)(2,1)S(1)}, bf16[3328]{0:T(1024)(128)(2,1)S(1)}, bf16[3072]{0:T(1024)(128)(2,1)S(1)}, bf16[4,3328]{1,0:T(4,128)(2,1)S...) all-reduce(f32[1536]{0:T(1024)S(1)} %reshape.1611, ...), channel_id=2, replica_groups=mesh['section'=2,'dp'=16,'shard'=4] {'dp','shard'}, use_global_device_ids=true, to_apply=%region_77.79.clone | all-reduce | flops 21392 | bytes 128640
  1883.6 27.6 %all-reduce.76 = (bf16[384]{0:T(512)(128)(2,1)S(1)}, bf16[832]{0:T(1024)(128)(2,1)S(1)}, bf16[768]{0:T(1024)(128)(2,1)S(1)}) all-reduce(bf16[384]{0:T(512)(128)(2,1)S(1)} %dynamic-update-slice.1, bf16[832]{0:T(1024)(128)(2,1)S(1)} %dynamic-update-slice.2, ...), channel_id=1, replica_groups=mesh['section'=2,'dp'=16,'shard'=4] {'dp'}, use_global_device_ids=true, to_apply=%add.67 | all-reduce | flops 1984 | bytes 7936
  1913.0 15.9 all-gather
  (484 shorter events, 336.3 us)
Async XLA Ops:
  7.2 110.7 %all-gather.8.cloned.1.call-start = ((), (), s32[]{:S(2)}) async-start(), calls=%async_computation.3 | async-start | bytes 11796480 | tf_op jit(solution)/shard_map/all_gather | solution.py:105
  7.9 295.2 %all-gather.6.cloned.1.call-start = ((), (), s32[]{:S(2)}) async-start(), calls=%async_computation.2 | async-start | bytes 25067520 | tf_op jit(solution)/shard_map/all_gather | solution.py:101
  15.5 1129.7 %reduce-scatter.7.cloned.1.call-start = ((), (), s32[]{:S(2)}) async-start(), calls=%async_computation.5 | async-start | bytes 19169280 | tf_op jit(solution)/shard_map/reduce_scatter | solution.py:252
  72.3 230.8 %copy-start.12 = (bf16[2,128,1536]{2,1,0:T(8,128)(2,1)S(1)}, bf16[2,128,1536]{2,1,0:T(8,128)(2,1)}, u32[]{:S(2)}) copy-start(bf16[2,128,1536]{2,1,0:T(8,128)(2,1)} %param.21) | copy-start | bytes 2359300
  85.8 262.0 %copy-start.131 = (f32[48]{0:T(128)}, f32[48]{0:T(128)S(1)}, u32[]{:S(2)}) copy-start(f32[48]{0:T(128)S(1)} %get-tuple-element.1169) | copy-start | bytes 580
  308.4 39.4 %collective-permute-start = (bf16[128,1536]{1,0:T(8,128)(2,1)S(1)}, bf16[128,1536]{1,0:T(8,128)(2,1)S(1)}, u32[]{:S(2)}, u32[]{:S(2)}) collective-permute-start(bf16[128,1536]{1,0:T(8,128)(2,1)S(1)} %get-tuple-element.1257), channel_id=1, source_target_pairs={{0,64},{64,0},{1,65},{65,1},{2,66},{66,2},{3,67},{67,3},{4,68},{68... | collective-permute-start | bytes 1179656 | tf_op jit(solution)/shard_map/ppermute | solution.py:10
  350.4 28.6 %copy-start.143 = (pred[128,128]{1,0:T(8,128)(4,1)}, pred[128,128]{1,0:T(8,128)(4,1)S(1)}, u32[]{:S(2)}) copy-start(pred[128,128]{1,0:T(8,128)(4,1)S(1)} %iota_compare_fusion.2) | copy-start | bytes 49156 | tf_op jit(solution)/shard_map/conditional.2
  493.9 11.9 collective-permute-start.1
  510.2 43.3 %copy-start.141 = (pred[128,128]{1,0:T(8,128)(4,1)}, pred[128,128]{1,0:T(8,128)(4,1)S(1)}, u32[]{:S(2)}) copy-start(pred[128,128]{1,0:T(8,128)(4,1)S(1)} %iota_compare_fusion.3) | copy-start | bytes 49156 | tf_op jit(solution)/shard_map/conditional.1
  511.7 30.3 %copy-start.96 = (f32[3328]{0:T(1024)}, f32[3328]{0:T(1024)S(1)}, u32[]{:S(2)}) copy-start(f32[3328]{0:T(1024)S(1)} %get-tuple-element.1009) | copy-start | bytes 39940 | tf_op jit(solution)/shard_map/conditional.1
  511.7 30.3 %copy-start.98 = (f32[3328]{0:T(1024)}, f32[3328]{0:T(1024)S(1)}, u32[]{:S(2)}) copy-start(f32[3328]{0:T(1024)S(1)} %get-tuple-element.1010) | copy-start | bytes 39940 | tf_op jit(solution)/shard_map/conditional.1
  511.7 30.3 %copy-start.100 = (f32[3328]{0:T(1024)}, f32[3328]{0:T(1024)S(1)}, u32[]{:S(2)}) copy-start(f32[3328]{0:T(1024)S(1)} %get-tuple-element.1011) | copy-start | bytes 39940 | tf_op jit(solution)/shard_map/conditional.1
  511.7 30.3 %copy-start.108 = (f32[3328]{0:T(1024)}, f32[3328]{0:T(1024)S(1)}, u32[]{:S(2)}) copy-start(f32[3328]{0:T(1024)S(1)} %get-tuple-element.1012) | copy-start | bytes 39940 | tf_op jit(solution)/shard_map/conditional.1
  537.5 65.0 %copy-start.80 = (f32[128,48]{0,1:T(8,128)}, f32[128,48]{0,1:T(8,128)S(1)}, u32[]{:S(2)}) copy-start(f32[128,48]{0,1:T(8,128)S(1)} %get-tuple-element.1208) | copy-start | bytes 73732 | tf_op jit(solution)/shard_map/conditional.1
  566.9 35.7 %copy-start = (f32[128,3072]{0,1:T(8,128)}, f32[128,3072]{0,1:T(8,128)S(1)}, u32[]{:S(2)}) copy-start(f32[128,3072]{0,1:T(8,128)S(1)} %get-tuple-element.1210) | copy-start | bytes 4718596 | tf_op jit(solution)/shard_map/conditional.1
  667.1 11.1 collective-permute-start.2
  737.2 844.9 %reduce-scatter.9.cloned.1.call-start = ((), (), s32[]{:S(2)}) async-start(), calls=%async_computation.7 | async-start | bytes 40734720
  854.0 735.9 %copy-start.30 = (f32[128,3072]{0,1:T(8,128)S(1)}, f32[128,3072]{0,1:T(8,128)}, u32[]{:S(2)}) copy-start(f32[128,3072]{0,1:T(8,128)} %get-tuple-element.707) | copy-start | bytes 4718596
  854.1 729.9 %copy-start.197 = (u32[128]{0:T(128)S(1)}, u32[128]{0:T(128)}, u32[]{:S(2)}) copy-start(u32[128]{0:T(128)} %constant.525) | copy-start | bytes 1540
  854.1 732.5 %copy-start.196 = (u32[128]{0:T(128)S(1)}, u32[128]{0:T(128)}, u32[]{:S(2)}) copy-start(u32[128]{0:T(128)} %constant.494) | copy-start | bytes 1540
  854.1 735.8 %copy-start.2 = (f32[128,3072]{0,1:T(8,128)S(1)}, f32[128,3072]{0,1:T(8,128)}, u32[]{:S(2)}) copy-start(f32[128,3072]{0,1:T(8,128)} %get-tuple-element.706) | copy-start | bytes 4718596
  854.1 1078.0 %all-gather.12.cloned.1.call-start = ((), (), s32[]{:S(2)}) async-start(), calls=%async_computation.6 | async-start | bytes 2506752 | tf_op jit(solution)/shard_map/all_gather | solution.py:270
  1146.9 789.7 %all-gather.10.cloned.1.call-start = ((), (), s32[]{:S(2)}) async-start(), calls=%async_computation.4 | async-start | bytes 5326848 | tf_op jit(solution)/shard_map/all_gather | solution.py:258
  1601.6 328.1 %copy-start.77 = (f32[1,1,128,1536]{3,2,1,0:T(8,128)S(1)}, f32[1,1,128,1536]{3,2,1,0:T(8,128)}, u32[]{:S(2)}) copy-start(f32[1,1,128,1536]{3,2,1,0:T(8,128)} %get-tuple-element.679) | copy-start | bytes 2359300
  (116 other events, 820.4 us)
Sparse Core Ops, SparseCore 0:
  9.7 108.2 all-gather.7
  120.2 182.9 all-gather.5
  737.4 407.8 reduce-scatter.6
  1147.5 434.5 reduce-scatter.8
  1583.8 35.6 all-gather.11
  1621.2 39.2 all-gather.9
where the time goes:
time: 1970 us; the launch traced here: 1960 us
  waiting for transfers between devices  976 us (50%)
  blocking collectives  387 us (20%)
  matrix products  182 us (9%)
  other arithmetic  169 us (9%)
  local copies, waits for them, and re-layouts  157 us (8%)
  loops' own time  39.7 us (2%)
  starting transfers between devices  30.7 us (2%)
  between operations  19.7 us (1%)
    unnamed x7, waiting for transfers between devices  436 us
    unnamed x3, blocking collectives  318 us
    reduce_scatter x1, waiting for transfers between devices, shards(): lax.psum_scatter(arranged[5], ('dp', 'shard'), scatter_dimension=0, tiled...  291 us
    all_gather x1, waiting for transfers between devices, shards(): lax.all_gather(in_weight, 'shard', axis=1, tiled=True)  185 us
    add x6, other arithmetic, shards(): totals = tuple((left + right for left, right in zip(totals, param_grads)))  70 us
    dot_general x6, matrix products, scan_heads(): jnp.einsum('cqs,cqsh,cshp->cqhp', scores, decays, scaled, precision=highest)  42.2 us
  transfers between devices with their start and end apart: 9, of which 7 were waited for; matrix products, arithmetic and copies ran while one was open for 8% of the time, Pallas kernels for 0%

commit v1 on v0

v1 whole, which is shorter than its diff:
```python
import jax
import jax.numpy as jnp
from jax import lax
from jax.experimental import pallas as pl
from jax.experimental.pallas import tpu as pltpu
from jax.sharding import PartitionSpec as P

F32 = jnp.float32
BF16 = jnp.bfloat16
HI = lax.Precision.HIGHEST
EPS = 1e-05
T = 128
LANES = 128
HEAD = 64
SLOTS = 4
ROWS = SLOTS * T
PAIRS = 6
VMEM_LIMIT = 56 * 1024 * 1024


def sigmoid(v):
    return 0.5 * jnp.tanh(0.5 * v) + 0.5


def softplus(v):
    return jnp.maximum(v, 0.0) + jnp.log1p(jnp.exp(-jnp.abs(v)))


def dot(a, b):
    return jnp.dot(a, b, preferred_element_type=F32)


def dot_nt(a, b, precision=None):
    return lax.dot_general(
        a, b, (((1,), (1,)), ((), ())), preferred_element_type=F32, precision=precision
    )


def dot_tn(a, b, precision=None):
    return lax.dot_general(
        a, b, (((0,), (0,)), ((), ())), preferred_element_type=F32, precision=precision
    )


def iota(axis):
    return lax.broadcasted_iota(jnp.int32, (T, LANES), axis)


def shift_down(v, steps):
    return jnp.where(iota(0) >= steps, pltpu.roll(v, steps, 0), 0.0)


def shift_up(v, steps):
    return jnp.where(iota(0) < T - steps, pltpu.roll(v, T - steps, 0), 0.0)


def conv_taps(cin):
    return [shift_down(cin, 3), shift_down(cin, 2), shift_down(cin, 1), cin]


def conv_sum(taps, par):
    total = par[4:5, :] + taps[0] * par[0:1, :]
    for k in range(1, 4):
        total = total + taps[k] * par[k : k + 1, :]
    return total


def conv_back(dcv, par):
    total = dcv * par[3:4, :]
    for m in range(1, 4):
        total = total + shift_up(dcv, m) * par[3 - m : 4 - m, :]
    return total


def column_sum(v):
    return jnp.sum(v, axis=0, keepdims=True)


def slot(k):
    return slice(k * T, (k + 1) * T)


def tri(lower):
    if lower:
        return (iota(0) >= iota(1)).astype(F32)
    return (iota(0) <= iota(1)).astype(F32)


def step_prep(k, pbc, dtp, run_col, run_row, step_wide):
    step = softplus(pbc[slot(k), 256:384] + dtp[0:1, :])
    run = jnp.dot(tri(True), step * dtp[1:2, :], precision=HI, preferred_element_type=F32)
    run_row[k] = jnp.transpose(run)
    left = iota(1) < HEAD
    for p in range(PAIRS):
        a, b = 2 * p, 2 * p + 1
        run_col[a, slot(k), :] = jnp.broadcast_to(run[:, a : a + 1], (T, LANES))
        run_col[b, slot(k), :] = jnp.broadcast_to(run[:, b : b + 1], (T, LANES))
        step_wide[p, slot(k), :] = jnp.where(
            left,
            jnp.broadcast_to(step[:, a : a + 1], (T, LANES)),
            jnp.broadcast_to(step[:, b : b + 1], (T, LANES)),
        )
    return step


def halves(v):
    left = iota(1) < HEAD
    zero = jnp.zeros_like(v)
    return jnp.concatenate([jnp.where(left, v, zero), jnp.where(left, zero, v)], axis=0)


def forward_kernel(with_grad, *refs):
    xs = refs[:SLOTS]
    refs = refs[SLOTS:]
    if with_grad:
        gs = refs[:SLOTS]
        refs = refs[SLOTS:]
    (gain, wg, wv, wbc, wout, pv, pbcv, dtp) = refs[:8]
    refs = refs[8:]
    outs = refs[:SLOTS]
    (stats, normed, proj, y_out, pbc) = refs[SLOTS : SLOTS + 5]
    (scores, run_col, run_row, step_wide, u_all, square, cross, *more) = refs[SLOTS + 5 :]
    i = pl.program_id(0)

    @pl.when(i == 0)
    def _prep():
        for k in range(SLOTS):
            x = xs[k][...].astype(F32)
            scale = lax.rsqrt(jnp.mean(x * x, axis=1, keepdims=True) + EPS)
            normed[slot(k), :] = (x * scale * gain[...]).astype(BF16)
            if with_grad:
                more[0][slot(k), :] = gs[k][...]
        pbc[...] = dot(
            normed[...], jnp.concatenate([wbc[0], wbc[1], wbc[2]], axis=1)
        )
        for k in range(SLOTS):
            cv = conv_sum(conv_taps(pbc[slot(k), 0:128]), pbcv[:, 0:128])
            inbound = cv * sigmoid(cv)
            cv = conv_sum(conv_taps(pbc[slot(k), 128:256]), pbcv[:, 128:256])
            outbound = cv * sigmoid(cv)
            scores[k] = dot_nt(outbound, inbound, HI) * tri(True)
            step_prep(k, pbc, dtp, run_col, run_row, step_wide)
        square[...] = jnp.zeros_like(square)
        cross[...] = jnp.zeros_like(cross)

    @pl.when(i > 0)
    def _pair():
        p = i - 1
        proj[0] = dot(normed[...], jnp.concatenate([wg[0], wv[0]], axis=1))
        par = pv[...]
        if with_grad:
            q_all = dot_nt(more[0][...], wout[pl.ds(pl.multiple_of(p * T, T), T), :])
        for k in range(SLOTS):
            gate = proj[0, slot(k), 0:128]
            cv = conv_sum(conv_taps(proj[0, slot(k), 128:256]), par)
            values = cv * sigmoid(cv)
            scaled = (values * step_wide[p, slot(k), :]).astype(BF16)
            weights = []
            for h in range(2):
                gap = run_col[2 * p + h, slot(k), :] - run_row[k, pl.ds(2 * p + h, 1), :]
                decay = jnp.exp(jnp.minimum(gap, 0.0))
                weights.append((scores[k] * decay).astype(BF16))
            y = dot(jnp.concatenate(weights, axis=1), halves(scaled))
            y_out[0, slot(k), :] = y
            scanned = y + par[6:7, :] * values
            gated = scanned * (gate * sigmoid(gate))
            square[slot(k), :] += gated * gated
            scaled_out = gated * par[5:6, :]
            u_all[p, slot(k), :] = scaled_out.astype(BF16)
            if with_grad:
                cross[slot(k), :] += q_all[slot(k), :] * scaled_out

    @pl.when(i == PAIRS)
    def _finish():
        u = jnp.concatenate([u_all[p] for p in range(PAIRS)], axis=1)
        width = wout.shape[1]
        for n in range(0, width, 512):
            part = dot(u, wout[:, n : n + 512]).astype(BF16)
            for k in range(SLOTS):
                outs[k][:, n : n + 512] = part[slot(k), :]
        ones = jnp.ones((8, LANES), F32)
        stats[0] = dot_nt(ones, square[...], HI)
        stats[1] = dot_nt(ones, cross[...], HI)


def const_spec(shape):
    zeros = (0,) * len(shape)
    return pl.BlockSpec(shape, lambda i: zeros)


def pair_of(i):
    return jnp.clip(i - 1, 0, PAIRS - 1)


def forward(x_slots, g_slots, w, wout, gain, pv, pbcv, dtp):
    width = x_slots[0].shape[1]
    inner = wout.shape[0]
    with_grad = g_slots is not None
    xg = list(x_slots) + (list(g_slots) if with_grad else [])
    in_specs = [const_spec((T, width)) for _ in xg] + [
        const_spec((1, width)),
        pl.BlockSpec((1, width, LANES), lambda i: (pair_of(i), 0, 0)),
        pl.BlockSpec((1, width, LANES), lambda i: (PAIRS + pair_of(i), 0, 0)),
        pl.BlockSpec((4, width, LANES), lambda i: (3, 0, 0)),
        const_spec((inner, width)),
        pl.BlockSpec((8, LANES), lambda i: (0, pair_of(i))),
        const_spec((8, 256)),
        const_spec((8, LANES)),
    ]
    out_shape = [jax.ShapeDtypeStruct((T, width), BF16) for _ in range(SLOTS)] + [
        jax.ShapeDtypeStruct((2, 8, ROWS), F32),
        jax.ShapeDtypeStruct((ROWS, width), BF16),
        jax.ShapeDtypeStruct((PAIRS, ROWS, 256), F32),
        jax.ShapeDtypeStruct((PAIRS, ROWS, LANES), F32),
        jax.ShapeDtypeStruct((ROWS, 384), F32),
    ]
    out_specs = [const_spec((T, width)) for _ in range(SLOTS)] + [
        const_spec((2, 8, ROWS)),
        const_spec((ROWS, width)),
        pl.BlockSpec((1, ROWS, 256), lambda i: (pair_of(i), 0, 0)),
        pl.BlockSpec((1, ROWS, LANES), lambda i: (pair_of(i), 0, 0)),
        const_spec((ROWS, 384)),
    ]
    scratch = [
        pltpu.VMEM((SLOTS, T, T), F32),
        pltpu.VMEM((2 * PAIRS, ROWS, LANES), F32),
        pltpu.VMEM((SLOTS, T, LANES), F32),
        pltpu.VMEM((PAIRS, ROWS, LANES), F32),
        pltpu.VMEM((PAIRS, ROWS, LANES), BF16),
        pltpu.VMEM((ROWS, LANES), F32),
        pltpu.VMEM((ROWS, LANES), F32),
    ]
    if with_grad:
        scratch.append(pltpu.VMEM((ROWS, width), BF16))
    res = pl.pallas_call(
        lambda *refs: forward_kernel(with_grad, *refs),
        grid=(PAIRS + 1,),
        in_specs=in_specs,
        out_specs=out_specs,
        out_shape=out_shape,
        scratch_shapes=scratch,
        compiler_params=pltpu.CompilerParams(vmem_limit_bytes=VMEM_LIMIT),
        name="layer_forward",
    )(*xg, gain, w, w, w, wout, pv, pbcv, dtp)
    return res[:SLOTS], res[SLOTS], res[SLOTS + 1 :]


def head_columns(p):
    target = 2 * p + (iota(0) >= HEAD).astype(jnp.int32)
    one = (iota(1) == target).astype(BF16)
    return jnp.concatenate([one, one], axis=0)


def head_sum(v, columns):
    high = v.astype(BF16)
    low = (v - high.astype(F32)).astype(BF16)
    return dot(jnp.concatenate([high, low], axis=1), columns)


def backward_kernel(*refs):
    gs = refs[:SLOTS]
    (row_stats, normed_t, proj, y_in, pbc, wg, wv, wbc, wout, pv, pbcv, dtp) = refs[
        SLOTS : SLOTS + 12
    ]
    refs = refs[SLOTS + 12 :]
    outs = refs[:SLOTS]
    (grad_g, grad_v, grad_bc, grad_out, small, small_bc, small_dt) = refs[SLOTS : SLOTS + 7]
    (
        g_all,
        scores_t,
        mixed,
        run_col,
        run_row,
        step_wide,
        step_all,
        scale_row,
        cross_row,
        dscores_t,
        dstep,
        drun,
        total,
        u_all,
        d_all,
        d_bc,
    ) = refs[SLOTS + 7 :]
    i = pl.program_id(0)

    @pl.when(i == 0)
    def _prep():
        for k in range(SLOTS):
            g_all[slot(k), :] = gs[k][...]
            cv = conv_sum(conv_taps(pbc[slot(k), 0:128]), pbcv[:, 0:128])
            inbound = cv * sigmoid(cv)
            cv = conv_sum(conv_taps(pbc[slot(k), 128:256]), pbcv[:, 128:256])
            outbound = cv * sigmoid(cv)
            mixed[0, slot(k), :] = inbound
            mixed[1, slot(k), :] = outbound
            scores_t[k] = dot_nt(inbound, outbound, HI) * tri(False)
            step_all[slot(k), :] = step_prep(k, pbc, dtp, run_col, run_row, step_wide)
            scale_row[slot(k), :] = jnp.transpose(
                jnp.broadcast_to(row_stats[k, 0:1, :], (T, LANES))
            )
            cross_row[slot(k), :] = jnp.transpose(
                jnp.broadcast_to(row_stats[k, 1:2, :], (T, LANES))
            )
        dscores_t[...] = jnp.zeros_like(dscores_t)
        dstep[...] = jnp.zeros_like(dstep)
        drun[...] = jnp.zeros_like(drun)
        total[...] = jnp.zeros_like(total)

    @pl.when(i > 0)
    def _pair():
        p = i - 1
        par = pv[...]
        columns = head_columns(p)
        q_all = dot_nt(g_all[...], wout[...])
        sums = [jnp.zeros((1, LANES), F32) for _ in range(8)]
        for k in range(SLOTS):
            gate = proj[0, slot(k), 0:128]
            taps = conv_taps(proj[0, slot(k), 128:256])
            cv = conv_sum(taps, par)
            sig_c = sigmoid(cv)
            values = cv * sig_c
            sig_g = sigmoid(gate)
            silu_g = gate * sig_g
            y = y_in[0, slot(k), :]
            scanned = y + par[6:7, :] * values
            gated = scanned * silu_g
            grad_no = q_all[slot(k), :]
            scale = scale_row[slot(k), :]
            dgated = scale * (grad_no * par[5:6, :]) - cross_row[slot(k), :] * gated
            norm = gated * scale
            sums[5] += column_sum(grad_no * norm)
            u_all[slot(k), :] = (norm * par[5:6, :]).astype(BF16)
            dscan = dgated * silu_g
            dgate = dgated * scanned * (sig_g * (1.0 + gate * (1.0 - sig_g)))
            sums[6] += column_sum(dscan * values)
            wide = step_wide[p, slot(k), :]
            dy = dscan.astype(BF16)
            scaled = (values * wide).astype(BF16)
            dweights = dot_nt(halves(scaled), dy)
            weights = []
            dscore = dscores_t[k]
            for h in range(2):
                gap = run_row[k, pl.ds(2 * p + h, 1), :] - run_col[2 * p + h, slot(k), :]
                decay = jnp.exp(jnp.minimum(gap, 0.0))
                weights.append((scores_t[k] * decay).astype(BF16))
                dscore = dscore + dweights[slot(h), :] * decay
            dscores_t[k] = dscore
            dscaled = dot(jnp.concatenate(weights, axis=1), halves(dy))
            dstep[slot(k), :] += head_sum(dscaled * values, columns)
            drun[slot(k), :] += head_sum(
                dy.astype(F32) * y - scaled.astype(F32) * dscaled, columns
            )
            dvalues = dscaled * wide + par[6:7, :] * dscan
            dcv = dvalues * (sig_c * (1.0 + cv * (1.0 - sig_c)))
            for t in range(4):
                sums[t] += column_sum(dcv * taps[t])
            sums[4] += column_sum(dcv)
            d_all[slot(k), 0:128] = dgate.astype(BF16)
            d_all[slot(k), 128:256] = conv_back(dcv, par).astype(BF16)
        small[0] = jnp.concatenate(sums, axis=0)
        both = dot(normed_t[...], d_all[...])
        grad_g[0] = both[:, 0:128].astype(BF16)
        grad_v[0] = both[:, 128:256].astype(BF16)
        grad_out[...] = dot_tn(u_all[...], g_all[...]).astype(BF16)
        total[...] += dot_nt(d_all[...], jnp.concatenate([wg[0], wv[0]], axis=1))

    @pl.when(i == PAIRS)
    def _finish():
        sums = [[jnp.zeros((1, LANES), F32) for _ in range(8)] for _ in range(2)]
        dt_sums = [jnp.zeros((1, LANES), F32) for _ in range(8)]
        live = iota(1) < 2 * PAIRS
        for k in range(SLOTS):
            dscore = dscores_t[k] * tri(False)
            dmixed = (
                jnp.dot(dscore, mixed[1, slot(k), :], precision=HI, preferred_element_type=F32),
                dot_tn(dscore, mixed[0, slot(k), :], HI),
            )
            for c in range(2):
                lanes = slice(c * LANES, (c + 1) * LANES)
                par = pbcv[:, lanes]
                taps = conv_taps(pbc[slot(k), lanes])
                cv = conv_sum(taps, par)
                sig = sigmoid(cv)
                dcv = dmixed[c] * (sig * (1.0 + cv * (1.0 - sig)))
                for t in range(4):
                    sums[c][t] += column_sum(dcv * taps[t])
                sums[c][4] += column_sum(dcv)
                d_bc[slot(k), lanes] = conv_back(dcv, par).astype(BF16)
            dlog = jnp.dot(
                tri(False), drun[slot(k), :], precision=HI, preferred_element_type=F32
            )
            grad_step = dstep[slot(k), :] + dlog * dtp[1:2, :]
            dt_sums[1] += column_sum(dlog * step_all[slot(k), :])
            draw = grad_step * sigmoid(pbc[slot(k), 256:384] + dtp[0:1, :])
            draw = jnp.where(live, draw, 0.0)
            dt_sums[0] += column_sum(draw)
            d_bc[slot(k), 256:384] = draw.astype(BF16)
        small_bc[0] = jnp.concatenate(sums[0], axis=0)
        small_bc[1] = jnp.concatenate(sums[1], axis=0)
        dt_sums[1] = dt_sums[1] * dtp[1:2, :]
        small_dt[...] = jnp.concatenate(dt_sums, axis=0)
        for b in range(3):
            grad_bc[b] = dot(
                normed_t[...], d_bc[:, b * LANES : (b + 1) * LANES]
            ).astype(BF16)
        grad_bc[3] = jnp.zeros_like(grad_bc[3])
        final = total[...] + dot_nt(
            d_bc[...], jnp.concatenate([wbc[0], wbc[1], wbc[2]], axis=1)
        )
        for k in range(SLOTS):
            outs[k][...] = final[slot(k), :].astype(BF16)


def backward(g_slots, row_stats, normed_t, saved, w, wout, pv, pbcv, dtp):
    proj, y, pbc = saved
    width = g_slots[0].shape[1]
    inner = wout.shape[0]
    in_specs = [const_spec((T, width)) for _ in range(SLOTS)] + [
        const_spec((SLOTS, 8, LANES)),
        const_spec((width, ROWS)),
        pl.BlockSpec((1, ROWS, 256), lambda i: (pair_of(i), 0, 0)),
        pl.BlockSpec((1, ROWS, LANES), lambda i: (pair_of(i), 0, 0)),
        const_spec((ROWS, 384)),
        pl.BlockSpec((1, width, LANES), lambda i: (pair_of(i), 0, 0)),
        pl.BlockSpec((1, width, LANES), lambda i: (PAIRS + pair_of(i), 0, 0)),
        pl.BlockSpec((4, width, LANES), lambda i: (3, 0, 0)),
        pl.BlockSpec((T, width), lambda i: (pair_of(i), 0)),
        pl.BlockSpec((8, LANES), lambda i: (0, pair_of(i))),
        const_spec((8, 256)),
        const_spec((8, LANES)),
    ]
    out_shape = [jax.ShapeDtypeStruct((T, width), BF16) for _ in range(SLOTS)] + [
        jax.ShapeDtypeStruct((PAIRS, width, LANES), BF16),
        jax.ShapeDtypeStruct((PAIRS, width, LANES), BF16),
        jax.ShapeDtypeStruct((4, width, LANES), BF16),
        jax.ShapeDtypeStruct((inner, width), BF16),
        jax.ShapeDtypeStruct((PAIRS, 8, LANES), F32),
        jax.ShapeDtypeStruct((2, 8, LANES), F32),
        jax.ShapeDtypeStruct((8, LANES), F32),
    ]
    out_specs = [const_spec((T, width)) for _ in range(SLOTS)] + [
        pl.BlockSpec((1, width, LANES), lambda i: (pair_of(i), 0, 0)),
        pl.BlockSpec((1, width, LANES), lambda i: (pair_of(i), 0, 0)),
        const_spec((4, width, LANES)),
        pl.BlockSpec((T, width), lambda i: (pair_of(i), 0)),
        pl.BlockSpec((1, 8, LANES), lambda i: (pair_of(i), 0, 0)),
        const_spec((2, 8, LANES)),
        const_spec((8, LANES)),
    ]
    scratch = [
        pltpu.VMEM((ROWS, width), BF16),
        pltpu.VMEM((SLOTS, T, T), F32),
        pltpu.VMEM((2, ROWS, LANES), F32),
        pltpu.VMEM((2 * PAIRS, ROWS, LANES), F32),
        pltpu.VMEM((SLOTS, T, LANES), F32),
        pltpu.VMEM((PAIRS, ROWS, LANES), F32),
        pltpu.VMEM((ROWS, LANES), F32),
        pltpu.VMEM((ROWS, LANES), F32),
        pltpu.VMEM((ROWS, LANES), F32),
        pltpu.VMEM((SLOTS, T, T), F32),
        pltpu.VMEM((ROWS, LANES), F32),
        pltpu.VMEM((ROWS, LANES), F32),
        pltpu.VMEM((ROWS, width), F32),
        pltpu.VMEM((ROWS, LANES), BF16),
        pltpu.VMEM((ROWS, 256), BF16),
        pltpu.VMEM((ROWS, 384), BF16),
    ]
    res = pl.pallas_call(
        backward_kernel,
        grid=(PAIRS + 1,),
        in_specs=in_specs,
        out_specs=out_specs,
        out_shape=out_shape,
        scratch_shapes=scratch,
        compiler_params=pltpu.CompilerParams(vmem_limit_bytes=VMEM_LIMIT),
        name="layer_backward",
    )(*g_slots, row_stats, normed_t, proj, y, pbc, w, w, w, wout, pv, pbcv, dtp)
    return res[:SLOTS], res[SLOTS:]


def ring(n, k):
    return [(i, (i + k) % n) for i in range(n)]


def send_shard(v, k):
    return lax.ppermute(v, "shard", ring(SLOTS, k)) if k else v


def swap_section(v):
    return lax.ppermute(v, "section", [(0, 1), (1, 0)])


def dp_index(x, z, c):
    return x * 8 + z * 2 + c


def dp_pairs(move):
    pairs = []
    for x in range(2):
        for z in range(4):
            for c in range(2):
                pairs.append((dp_index(x, z, c), dp_index(*move(x, z, c))))
    return pairs


def section_pairs(k, layer):
    pairs = []
    for chip in range(4):
        to = (chip + k) % 4
        if to // 2 != layer:
            continue
        for z in range(4):
            for c in range(2):
                pairs.append(
                    (
                        (chip // 2) * 16 + dp_index(chip % 2, z, c),
                        (to // 2) * 16 + dp_index(to % 2, z, c),
                    )
                )
    return pairs


def pick(v, index, axis):
    return lax.dynamic_index_in_dim(v, index, axis, keepdims=False)


def gather_slots(v):
    return [send_shard(v, (-k) % SLOTS) for k in range(SLOTS)]


def scatter_sum(slots):
    parts = [send_shard(slots[k], k) for k in range(SLOTS)]
    return sum(p.astype(F32) for p in parts)


def to_owners(v, layer):
    d = lax.axis_index("dp")
    x, z, c = d // 8, (d // 2) % 4, d % 2
    v = v.reshape((2, 4, 2) + v.shape[1:])
    moved = lax.ppermute(pick(v, 1 - c, 2), "dp", dp_pairs(lambda x, z, c: (x, z, 1 - c)))
    v = (pick(v, c, 2).astype(F32) + moved.astype(F32)).astype(BF16)
    own = pick(v, z, 1).astype(F32)
    for k in range(1, 4):
        moved = lax.ppermute(
            pick(v, (z + k) % 4, 1), "dp", dp_pairs(lambda x, z, c: (x, (z + k) % 4, c))
        )
        own = own + moved.astype(F32)
    v = own.astype(BF16)
    own = pick(v, x, 0).astype(F32)
    for k in range(1, 4):
        moved = lax.ppermute(pick(v, (x + k) % 2, 0), ("section", "dp"), section_pairs(k, layer))
        own = own + moved.astype(F32)
    return own.astype(BF16)


def sum_small(v):
    v = v + lax.ppermute(v, "dp", dp_pairs(lambda x, z, c: (x, z, 1 - c)))
    v = v + sum(
        lax.ppermute(v, "dp", dp_pairs(lambda x, z, c: (x, (z + k) % 4, c))) for k in range(1, 4)
    )
    v = v + lax.ppermute(v, "dp", dp_pairs(lambda x, z, c: (1 - x, z, c)))
    return v + swap_section(v)


def in_order(parts, sign):
    j = lax.axis_index("shard")
    stacked = jnp.stack(parts)
    return jnp.take(stacked, (sign * (jnp.arange(SLOTS) - j)) % SLOTS, axis=0)


def shards(
    tokens,
    cotangent,
    lengths,
    norm_gain,
    in_weight,
    conv_weight,
    conv_bias,
    dt_bias,
    a_log,
    d_skip,
    gate_gain,
    out_weight,
):
    sec = lax.axis_index("section")
    d = lax.axis_index("dp")
    j = lax.axis_index("shard")
    width = tokens.shape[2]
    quarter = norm_gain.shape[1]
    channels = conv_bias.shape[1]
    own_cols = gate_gain.shape[1]
    inner = own_cols * SLOTS
    heads = dt_bias.shape[1]
    own_heads = heads // SLOTS
    out_rows = own_cols // 16

    x_own = pick(tokens, sec, 0)
    cot = pick(cotangent, sec, 0)
    length = pick(lengths, sec, 0)
    mask = (jnp.arange(T, dtype=jnp.int32) < length).astype(F32)[:, None]

    with jax.named_scope("weights"):
        padded = jnp.pad(in_weight[0], ((0, 0), (0, 256)))

        def start_of(to):
            return jnp.where(
                d < 6,
                own_cols * to + LANES * d,
                jnp.where(
                    d < 12,
                    inner + own_cols * to + LANES * (d - 6),
                    jnp.where(
                        d < 14, 2 * inner + LANES * (d - 12), 2 * inner + 256 + own_heads * to
                    ),
                ),
            )

        parts = [
            send_shard(
                lax.dynamic_slice(padded, (0, start_of((j + k) % SLOTS)), (quarter, LANES)), k
            )
            for k in range(SLOTS)
        ]
        w_own = in_order(parts, -1).reshape(width, LANES)
        o_own = lax.dynamic_slice(out_weight[0], (out_rows * d, 0), (out_rows, width))
        w_other, o_other = swap_section(w_own), swap_section(o_own)
        first = sec == 0
        w_low = [jnp.where(first, w_own, w_other), jnp.where(first, w_other, w_own)]
        o_low = [jnp.where(first, o_own, o_other), jnp.where(first, o_other, o_own)]
        w_full = [lax.all_gather(v, "dp", axis=0, tiled=False) for v in w_low]
        o_full = [
            lax.all_gather(v, "dp", axis=0, tiled=False).reshape(own_cols, width) for v in o_low
        ]

    with jax.named_scope("small_weights"):
        sizes = [quarter, 4 * channels, channels, own_cols, heads, heads, heads]
        flat = jnp.concatenate(
            [
                norm_gain[0],
                conv_weight[0].reshape(-1),
                conv_bias[0],
                gate_gain[0],
                dt_bias[0],
                a_log[0],
                d_skip[0],
            ]
        )
        flat = jnp.pad(flat, (0, -flat.shape[0] % LANES)).reshape(-1, LANES)
        own = in_order(gather_slots(flat), 1)
        other = swap_section(own)
        small = [jnp.where(first, own, other), jnp.where(first, other, own)]

        def unpack(v):
            v = v.reshape(SLOTS, -1).astype(F32)
            cut, at = [], 0
            for size in sizes:
                cut.append(v[:, at : at + size])
                at += size
            gain = cut[0].reshape(1, width)
            taps = cut[1].reshape(SLOTS, 4, channels).transpose(1, 0, 2).reshape(4, -1)
            bias = cut[2].reshape(1, -1)
            conv = jnp.concatenate([taps, bias, jnp.zeros((3, taps.shape[1]), F32)], axis=0)
            pbcv = conv[:, inner:]
            pv = lax.dynamic_slice(conv, (0, own_cols * j), (8, own_cols))
            pick_heads = lambda u: lax.dynamic_slice(u[0], (own_heads * j,), (own_heads,))
            wide = jnp.repeat(pick_heads(cut[6]), HEAD)[None]
            pv = jnp.concatenate([pv[:5], pick(cut[3], j, 0)[None], wide, pv[7:]], axis=0)
            dtp = jnp.stack([pick_heads(cut[4]), -jnp.exp(pick_heads(cut[5]))])
            dtp = jnp.pad(dtp, ((0, 6), (0, LANES - own_heads)))
            return gain, pv, pbcv, dtp

        params = [unpack(v) for v in small]

    x_f = x_own.astype(F32)
    x_slots = gather_slots(x_own)
    gain, pv, pbcv, dtp = params[0]
    parts, stats, (normed0, *saved0) = forward(
        x_slots, None, w_full[0], o_full[0], gain, pv, pbcv, dtp
    )
    branch = scatter_sum(parts)
    square = scatter_sum([stats[0, 0:1, slot(k)] for k in range(SLOTS)])[0]
    scale0 = lax.rsqrt(square / inner + EPS)
    branch0 = branch * scale0[:, None]
    middle = (x_f + mask * branch0).astype(BF16)
    normed0_t = jnp.transpose(normed0)

    g1 = (mask * cot.astype(F32)).astype(BF16)
    g1_slots = gather_slots(g1)
    m_slots = gather_slots(middle)
    gain1, pv1, pbcv1, dtp1 = params[1]
    parts, stats, (normed1, *saved1) = forward(
        m_slots, g1_slots, w_full[1], o_full[1], gain1, pv1, pbcv1, dtp1
    )
    normed1_t = jnp.transpose(normed1)
    own = stats[:, 0].reshape(2, SLOTS, T)
    back = [send_shard(own, k) for k in range(SLOTS)]
    summed = sum(jnp.roll(back[k], -k, axis=1) for k in range(SLOTS))
    scale1 = lax.rsqrt(summed[0] / inner + EPS)
    cross1 = scale1 * scale1 * scale1 * summed[1] / inner
    rows1 = jnp.pad(jnp.stack([scale1, cross1], axis=1), ((0, 0), (0, 6), (0, 0)))
    branch = scatter_sum(parts) * scale1[0][:, None]
    result = middle.astype(F32) + mask * branch

    def norm_back(x, gain, grad):
        scale = lax.rsqrt(jnp.mean(x * x, axis=1, keepdims=True) + EPS)
        unit = x * scale
        dn = grad * gain
        dx = scale * (dn - unit * jnp.mean(dn * unit, axis=1, keepdims=True))
        return dx, jnp.sum(grad * unit, axis=0)

    parts, grads1 = backward(
        g1_slots, rows1, normed1_t, saved1, w_full[1], o_full[1], pv1, pbcv1, dtp1
    )
    dx, gain_grad1 = norm_back(middle.astype(F32), gain1, scatter_sum(parts))
    dmiddle = (cot.astype(F32) + dx).astype(BF16)
    g0 = (mask * dmiddle.astype(F32)).astype(BF16)
    cross0 = scale0 * scale0 * jnp.sum(g0.astype(F32) * branch0, axis=1) / inner
    own = jnp.pad(jnp.stack([scale0, cross0]), ((0, 6), (0, 0)))
    rows0 = jnp.stack(gather_slots(own))
    g0_slots = gather_slots(g0)
    parts, grads0 = backward(
        g0_slots, rows0, normed0_t, saved0, w_full[0], o_full[0], pv, pbcv, dtp
    )
    dx, gain_grad0 = norm_back(x_f, gain, scatter_sum(parts))
    dtokens = dmiddle.astype(F32) + dx

    result_moved = lax.ppermute(result.astype(BF16), "section", [(0, 1)]).astype(F32)
    dtokens_moved = lax.ppermute(dtokens.astype(BF16), "section", [(1, 0)]).astype(F32)
    ends = jnp.where(
        first, jnp.stack([dtokens, dtokens_moved]), jnp.stack([result_moved, result])
    )[None]

    owned, small_sums = [], []
    for layer, grads, gain_grad in ((0, grads0, gain_grad0), (1, grads1, gain_grad1)):
        grad_g, grad_v, grad_bc, grad_out, sm, sm_bc, sm_dt = grads
        gw = jnp.concatenate([grad_g, grad_v, grad_bc], axis=0)
        go = grad_out.reshape(16, out_rows, width)
        owned.append((to_owners(gw, layer), to_owners(go, layer)))
        flat = jnp.concatenate(
            [sm.reshape(-1), sm_bc.reshape(-1), sm_dt.reshape(-1), gain_grad]
        ).reshape(-1, LANES)
        small_sums.append(sum_small(flat))
    w_grad = jnp.where(first, owned[0][0], owned[1][0]).reshape(SLOTS, quarter, LANES)
    o_grad = jnp.where(first, owned[0][1], owned[1][1])
    small_sum = jnp.where(first, small_sums[0], small_sums[1])

    parts = [send_shard(pick(w_grad, (j + k) % SLOTS, 0), k) for k in range(SLOTS)]
    w_grad = in_order(parts, -1)
    shared = jnp.sum(w_grad.astype(F32), axis=0, keepdims=True).astype(BF16)
    w_grad = jnp.where((d == 12) | (d == 13), jnp.broadcast_to(shared, w_grad.shape), w_grad)
    w_all = lax.all_gather(w_grad, "dp", axis=0, tiled=False)
    o_all = lax.all_gather(o_grad, "dp", axis=0, tiled=False)
    grad_out_weight = o_all.reshape(own_cols, width).astype(F32)
    by_row = lambda v: v.transpose(2, 1, 0, 3).reshape(quarter, inner).astype(F32)
    grad_in_weight = jnp.concatenate(
        [
            by_row(w_all[0:6]),
            by_row(w_all[6:12]),
            w_all[12:14, 0].transpose(1, 0, 2).reshape(quarter, 256).astype(F32),
            w_all[14, :, :, :own_heads].transpose(1, 0, 2).reshape(quarter, heads).astype(F32),
        ],
        axis=1,
    )

    everyone = in_order(gather_slots(small_sum), 1).reshape(SLOTS, -1)
    n_pair, n_bc = PAIRS * 8 * LANES, 2 * 8 * LANES
    by_pair = everyone[:, :n_pair].reshape(SLOTS, PAIRS, 8, LANES)
    by_pair = by_pair.transpose(2, 0, 1, 3).reshape(8, inner)
    by_bc = jnp.sum(everyone[:, n_pair : n_pair + n_bc], axis=0)
    by_bc = by_bc.reshape(2, 8, LANES).transpose(1, 0, 2).reshape(8, 256)
    at = n_pair + n_bc
    by_dt = everyone[:, at : at + 8 * LANES].reshape(SLOTS, 8, LANES)[:, :, :own_heads]
    by_dt = by_dt.transpose(1, 0, 2).reshape(8, heads)
    gain_total = jnp.sum(everyone[:, at + 8 * LANES :], axis=0)
    conv_total = jnp.concatenate([by_pair[:5], by_bc[:5]], axis=1)
    conv_own = lax.dynamic_slice(conv_total, (0, channels * j), (5, channels))
    grad_skip = jnp.sum(by_pair[6].reshape(heads, HEAD), axis=1)
    return (
        ends,
        lax.dynamic_slice(gain_total, (quarter * j,), (quarter,))[None],
        grad_in_weight[None],
        conv_own[None, :4],
        conv_own[4][None],
        by_dt[0][None],
        by_dt[1][None],
        grad_skip[None],
        lax.dynamic_slice(by_pair[5], (own_cols * j,), (own_cols,))[None],
        grad_out_weight[None],
    )


def solution(mesh):
    return jax.shard_map(
        shards,
        mesh=mesh,
        in_specs=(
            P(("dp", "shard"), None, None),
            P(("dp", "shard"), None, None),
            P(("dp", "shard")),
            P("section", "shard"),
            P("section", "shard", None),
            P("section", None, "shard"),
            P("section", "shard"),
            P("section", None),
            P("section", None),
            P("section", None),
            P("section", "shard"),
            P("section", "shard", None),
        ),
        out_specs=(
            P("section", ("dp", "shard"), None, None),
            P("section", "shard"),
            P("section", "shard", None),
            P("section", None, "shard"),
            P("section", "shard"),
            P("section", None),
            P("section", None),
            P("section", None),
            P("section", "shard"),
            P("section", "shard", None),
        ),
        check_vma=False,
    )
```

time: 1970 us -> 633 us (0.32)
  waiting for transfers between devices: 976 us -> 240 us
  blocking collectives: 387 us -> 0 us
  matrix products: 182 us -> 0 us
  other arithmetic: 169 us -> 56.7 us
  starting transfers between devices: 30.7 us -> 138 us
  Pallas kernels: 0 us -> 104 us
  local copies, waits for them, and re-layouts: 157 us -> 66.9 us
  loops' own time: 39.7 us -> 0 us
    unnamed x7 -> x6, waiting for transfers between devices: 436 us -> 1.27 us
    unnamed x3 -> x0, blocking collectives: 318 us -> none
    reduce_scatter x1 -> x0, waiting for transfers between devices: 291 us -> none  [shards(): lax.psum_scatter(arranged[5], ('dp', 'shard'), scatter_dimension=0, tiled...]
    all_gather x4 -> x6, waiting for transfers between devices: 217 us -> 24.3 us  [the longest x2 24.2 us: shards(): w_full = [lax.all_gather(v, 'dp', axis=0, tiled=False) for v in w_low]]
    ppermute x3 -> x90, waiting for transfers between devices: 31.9 us -> 214 us  [the longest x12 84.6 us: to_owners(): lax.ppermute(pick(v, (z + k) % 4, 1), 'dp', dp_pairs(lambda x, z, c: (x,...]
    dot_general x32 -> x0, matrix products: 182 us -> none  [the longest x6 42.2 us: scan_heads(): jnp.einsum('cqs,cqsh,cshp->cqhp', scores, decays, scaled, precision=highest)]
    ppermute x3 -> x90, starting transfers between devices: 30.4 us -> 138 us  [the longest x45 66 us: send_shard(): return lax.ppermute(v, 'shard', ring(SLOTS, k)) if k else v]
    pallas_call x0 -> x4, Pallas kernels: none -> 104 us  [the longest x2 67.1 us: backward(): pl.pallas_call(backward_kernel, grid=(PAIRS + 1,), in_specs=in_specs, out...]
  transfers between devices with their start and end apart: 9 -> 96, of which waited for: 7 -> 42; matrix products, arithmetic and copies ran while one was open for 8% -> 15% of each run, Pallas kernels for 0% -> 14%
where the time goes in v1:
time: 633 us; the launch traced here: 622 us
  waiting for transfers between devices  240 us (38%)
  starting transfers between devices  138 us (22%)
  Pallas kernels  104 us (16%)
  local copies, waits for them, and re-layouts  66.9 us (11%)
  other arithmetic  56.7 us (9%)
  between operations  16.1 us (3%)
    ppermute x12, waiting for transfers between devices, to_owners(): lax.ppermute(pick(v, (z + k) % 4, 1), 'dp', dp_pairs(lambda x, z, c: (x,...  84.6 us
    ppermute x45, waiting for transfers between devices, send_shard(): return lax.ppermute(v, 'shard', ring(SLOTS, k)) if k else v  74.5 us
    pallas_call x2, Pallas kernels, backward(): pl.pallas_call(backward_kernel, grid=(PAIRS + 1,), in_specs=in_specs, out...  67.1 us
    ppermute x45, starting transfers between devices, send_shard(): return lax.ppermute(v, 'shard', ring(SLOTS, k)) if k else v  66 us
    pallas_call x2, Pallas kernels, forward(): pl.pallas_call(lambda *refs: forward_kernel(with_grad, *refs), grid=(PAIR...  37.3 us
    ppermute x5, waiting for transfers between devices, swap_section(): return lax.ppermute(v, 'section', [(0, 1), (1, 0)])  28.6 us
    ppermute x12, starting transfers between devices, to_owners(): lax.ppermute(pick(v, (x + k) % 2, 0), ('section', 'dp'), section_pairs(k,...  28.3 us
    all_gather x2, waiting for transfers between devices, shards(): w_full = [lax.all_gather(v, 'dp', axis=0, tiled=False) for v in w_low]  24.2 us
  transfers between devices with their start and end apart: 96, of which 42 were waited for; matrix products, arithmetic and copies ran while one was open for 15% of the time, Pallas kernels for 14%

profile of v1, /device:TPU:4, one launch (start us, length us, event | category | flops | bytes accessed | tf_op | source)
XLA Modules:
  0.0 621.7 jit_solution(3084268075582036168)
XLA Ops:
  8.7 6.7 %collective-permute-done.11 = bf16[48,1536]{1,0:T(8,128)(2,1)S(1)} collective-permute-done((bf16[48,1536]{1,0:T(8,128)(2,1)S(1)}, bf16[48,1536]{1,0:T(8,128)(2,1)S(1)}, u32[]{:S(2)}, u32[]{:S(2)}) %collective-permute-start.11) | collective-permute-done | bytes 147488 | tf_op jit(solution)/shard_map/weights/ppermute | solution.py:492
  17.2 7.5 %copy.70 = bf16[1,384,6448]{2,1,0:T(8,128)(2,1)} copy(bf16[1,384,6448]{1,2,0:T(8,128)(2,1)} %param.18) | data formatting | bytes 9904128 | tf_op args[4]
  36.9 16.1 %collective-permute-done.10 = bf16[1536,128]{1,0:T(8,128)(2,1)S(1)} collective-permute-done((bf16[1536,128]{1,0:T(8,128)(2,1)S(1)}, bf16[1536,128]{1,0:T(8,128)(2,1)S(1)}, u32[]{:S(2)}, u32[]{:S(2)}) %collective-permute-start.10) | collective-permute-done | bytes 393248 | tf_op jit(solution)/shard_map/weights/ppermute | solution.py:492
  80.3 20.6 %all-gather.13.cloned.1.call-done = bf16[24576,128]{1,0:T(8,128)(2,1)} async-done(((bf16[1536,128]{1,0:T(8,128)(2,1)}), bf16[24576,128]{1,0:T(8,128)(2,1)}) %all-gather.13.cloned.1.call-update) | async-done | bytes 6291472 | tf_op jit(solution)/shard_map/weights/all_gather | solution.py:632
  101.0 17.8 %layer_forward.2 = (bf16[128,1536]{1,0:T(8,128)(2,1)}, bf16[128,1536]{1,0:T(8,128)(2,1)}, bf16[128,1536]{1,0:T(8,128)(2,1)}, bf16[128,1536]{1,0:T(8,128)(2,1)}, ...) custom-call(bf16[128,1536]{1,0:T(8,128)(2,1)} %copy-done.1, ...), custom_call_target="tpu_custom_call" | custom-call | tf_op jit(solution)/shard_map/layer_forward/pallas_call | solution.py:235
  127.5 10.4 %collective-permute-done.15 = f32[1,128]{1,0:T(1,128)S(1)} collective-permute-done((f32[1,128]{1,0:T(1,128)S(1)}, f32[1,128]{1,0:T(1,128)S(1)}, u32[]{:S(2)}, u32[]{:S(2)}) %collective-permute-start.15) | collective-permute-done | bytes 544 | tf_op jit(solution)/shard_map/ppermute | solution.py:488
  157.5 10.0 %collective-permute-done.18.refs_5_.refs_1_ = bf16[128,1536]{1,0:T(8,128)(2,1)S(1)} collective-permute-done((bf16[128,1536]{1,0:T(8,128)(2,1)S(1)}, bf16[128,1536]{1,0:T(8,128)(2,1)S(1)}, u32[]{:S(2)}, u32[]{:S(2)}) %collective-permute-start.18) | collective-permute-done | bytes 393248 | tf_op jit(solution)/shard_map/ppermute | solution.py:488
  182.5 5.1 collective-permute-done.23.refs_3_
  187.6 19.5 %layer_forward.3 = (bf16[128,1536]{1,0:T(8,128)(2,1)}, bf16[128,1536]{1,0:T(8,128)(2,1)}, bf16[128,1536]{1,0:T(8,128)(2,1)}, bf16[128,1536]{1,0:T(8,128)(2,1)}, ...) custom-call(bf16[128,1536]{1,0:T(8,128)(2,1)} %copy-done.3, ...), custom_call_target="tpu_custom_call" | custom-call | tf_op jit(solution)/shard_map/layer_forward/pallas_call | solution.py:235
  219.7 33.6 %layer_backward.2 = (bf16[128,1536]{1,0:T(8,128)(2,1)}, bf16[128,1536]{1,0:T(8,128)(2,1)}, bf16[128,1536]{1,0:T(8,128)(2,1)}, bf16[128,1536]{1,0:T(8,128)(2,1)},...) custom-call(bf16[128,1536]{1,0:T(8,128)(2,1)} %copy-done.5, ...), custom_call_target="tpu_custom_call" | custom-call | tf_op jit(solution)/shard_map/layer_backward/pallas_call | solution.py:470
  261.5 10.6 %collective-permute-done.27 = bf16[128,1536]{1,0:T(8,128)(2,1)S(1)} collective-permute-done((bf16[128,1536]{1,0:T(8,128)(2,1)}, bf16[128,1536]{1,0:T(8,128)(2,1)S(1)}, u32[]{:S(2)}, u32[]{:S(2)}) %collective-permute-start.27) | collective-permute-done | bytes 393248 | tf_op jit(solution)/shard_map/ppermute | solution.py:488
  289.8 10.1 %collective-permute-done.30.refs_1_ = bf16[128,1536]{1,0:T(8,128)(2,1)S(1)} collective-permute-done((bf16[128,1536]{1,0:T(8,128)(2,1)S(1)}, bf16[128,1536]{1,0:T(8,128)(2,1)S(1)}, u32[]{:S(2)}, u32[]{:S(2)}) %collective-permute-start.30) | collective-permute-done | bytes 393248 | tf_op jit(solution)/shard_map/ppermute | solution.py:488
  304.3 33.6 %layer_backward.3 = (bf16[128,1536]{1,0:T(8,128)(2,1)}, bf16[128,1536]{1,0:T(8,128)(2,1)}, bf16[128,1536]{1,0:T(8,128)(2,1)}, bf16[128,1536]{1,0:T(8,128)(2,1)},...) custom-call(bf16[128,1536]{1,0:T(8,128)(2,1)} %copy-done.11, ...), custom_call_target="tpu_custom_call" | custom-call | tf_op jit(solution)/shard_map/layer_backward/pallas_call | solution.py:470
  360.5 7.2 %collective-permute-done.85 = bf16[2,48,1536]{2,1,0:T(8,128)(2,1)S(1)} collective-permute-done((bf16[2,48,1536]{2,1,0:T(8,128)(2,1)S(1)}, bf16[2,48,1536]{2,1,0:T(8,128)(2,1)S(1)}, u32[]{:S(2)}, u32[]{:S(2)}) %collective-permute-start.85) | collective-permute-done | bytes 294944 | tf_op jit(solution)/shard_map/ppermute | solution.py:546
  388.9 5.2 collective-permute-start.81
  414.7 14.1 %collective-permute-done.67 = bf16[2,1536,128]{2,1,0:T(8,128)(2,1)S(1)} collective-permute-done((bf16[2,1536,128]{2,1,0:T(8,128)(2,1)S(1)}, bf16[2,1536,128]{2,1,0:T(8,128)(2,1)S(1)}, u32[]{:S(2)}, u32[]{:S(2)}) %collective-permute-start.67) | collective-permute-done | bytes 786464 | tf_op jit(solution)/shard_map/ppermute | solution.py:546
  431.6 18.8 %collective-permute-done.68 = bf16[2,1536,128]{2,1,0:T(8,128)(2,1)S(1)} collective-permute-done((bf16[2,1536,128]{2,1,0:T(8,128)(2,1)S(1)}, bf16[2,1536,128]{2,1,0:T(8,128)(2,1)S(1)}, u32[]{:S(2)}, u32[]{:S(2)}) %collective-permute-start.68) | collective-permute-done | bytes 786464 | tf_op jit(solution)/shard_map/ppermute | solution.py:546
  458.3 9.8 %collective-permute-done.60 = bf16[2,1536,128]{2,1,0:T(8,128)(2,1)S(1)} collective-permute-done((bf16[2,1536,128]{2,1,0:T(8,128)(2,1)S(1)}, bf16[2,1536,128]{2,1,0:T(8,128)(2,1)S(1)}, u32[]{:S(2)}, u32[]{:S(2)}) %collective-permute-start.60) | collective-permute-done | bytes 786464 | tf_op jit(solution)/shard_map/ppermute | solution.py:546
  469.3 16.8 %collective-permute-done.61 = bf16[2,1536,128]{2,1,0:T(8,128)(2,1)S(1)} collective-permute-done((bf16[2,1536,128]{2,1,0:T(8,128)(2,1)S(1)}, bf16[2,1536,128]{2,1,0:T(8,128)(2,1)S(1)}, u32[]{:S(2)}, u32[]{:S(2)}) %collective-permute-start.61) | collective-permute-done | bytes 786464 | tf_op jit(solution)/shard_map/ppermute | solution.py:546
  490.2 6.6 %collective-permute-start.64 = (bf16[1536,128]{1,0:T(8,128)(2,1)S(1)}, bf16[1536,128]{1,0:T(8,128)(2,1)}, u32[]{:S(2)}, u32[]{:S(2)}) collective-permute-start(bf16[1536,128]{1,0:T(8,128)(2,1)S(1)} %get-tuple-element.138), channel_id=1, source_target_pairs={{64,0},{68,4},{72,8},{76,12},{80,16},{84,20},{88,24},{92,28},{96,3... | collective-permute-start | bytes 1179656 | tf_op jit(solution)/shard_map/ppermute | solution.py:553
  504.0 8.1 %collective-permute-done.65 = bf16[1536,128]{1,0:T(8,128)(2,1)} collective-permute-done((bf16[1536,128]{1,0:T(8,128)(2,1)S(1)}, bf16[1536,128]{1,0:T(8,128)(2,1)}, u32[]{:S(2)}, u32[]{:S(2)}) %collective-permute-start.65) | collective-permute-done | bytes 393248 | tf_op jit(solution)/shard_map/ppermute | solution.py:553
  532.8 5.0 collective-permute-done.36
  538.7 8.5 %collective-permute-done.37 = bf16[128,1536]{1,0:T(8,128)(2,1)S(1)} collective-permute-done((bf16[128,1536]{1,0:T(8,128)(2,1)}, bf16[128,1536]{1,0:T(8,128)(2,1)S(1)}, u32[]{:S(2)}, u32[]{:S(2)}) %collective-permute-start.37) | collective-permute-done | bytes 393248 | tf_op jit(solution)/shard_map/ppermute | solution.py:488
  608.5 6.1 fusion.2
  (498 shorter events, 297.8 us)
Async XLA Ops:
  7.2 73.1 %all-gather.15.cloned.1.call-start = ((), (), s32[]{:S(2)}) async-start(), calls=%async_computation.1 | async-start | bytes 2506752 | tf_op jit(solution)/shard_map/weights/all_gather | solution.py:634
  17.0 83.9 %all-gather.13.cloned.1.call-start = ((), (), s32[]{:S(2)}) async-start(), calls=%async_computation | async-start | bytes 6684672 | tf_op jit(solution)/shard_map/weights/all_gather | solution.py:632
  53.9 124.3 %all-gather.19.cloned.1.call-start = ((), (), s32[]{:S(2)}) async-start(), calls=%async_computation.3 | async-start | bytes 2506752 | tf_op jit(solution)/shard_map/weights/all_gather | solution.py:634
  54.7 127.2 %all-gather.17.cloned.1.call-start = ((), (), s32[]{:S(2)}) async-start(), calls=%async_computation.2 | async-start | bytes 6684672 | tf_op jit(solution)/shard_map/weights/all_gather | solution.py:632
  55.3 535.4 %all-gather.23.cloned.1.call-start = ((), (), s32[]{:S(2)}) async-start(), calls=%async_computation.5 | async-start | bytes 2506752 | tf_op jit(solution)/shard_map/all_gather | solution.py:754
  151.9 30.0 %collective-permute-start.19 = (bf16[128,1536]{1,0:T(8,128)(2,1)S(1)}, bf16[128,1536]{1,0:T(8,128)(2,1)S(1)}, u32[]{:S(2)}, u32[]{:S(2)}) collective-permute-start(bf16[128,1536]{1,0:T(8,128)(2,1)S(1)} %get-tuple-element.184.refs_4_.refs_0_), channel_id=1, source_target_pairs={{0,2},{1,3},{2,0},{3,1},{4,6},{5,7},{6,4},{7,5},{8,10},{9,11},{10,... | collective-permute-start | bytes 1179656 | tf_op jit(solution)/shard_map/ppermute | solution.py:488
  151.9 30.0 %collective-permute-start.20 = (bf16[128,1536]{1,0:T(8,128)(2,1)S(1)}, bf16[128,1536]{1,0:T(8,128)(2,1)S(1)}, u32[]{:S(2)}, u32[]{:S(2)}) collective-permute-start(bf16[128,1536]{1,0:T(8,128)(2,1)S(1)} %get-tuple-element.184.refs_4_.refs_0_), channel_id=1, source_target_pairs={{0,1},{1,2},{2,3},{3,0},{4,5},{5,6},{6,7},{7,4},{8,9},{9,10},{10,1... | collective-permute-start | bytes 1179656 | tf_op jit(solution)/shard_map/ppermute | solution.py:488
  152.9 29.0 %collective-permute-start.21 = (bf16[128,1536]{1,0:T(8,128)(2,1)S(1)}, bf16[128,1536]{1,0:T(8,128)(2,1)}, u32[]{:S(2)}, u32[]{:S(2)}) collective-permute-start(bf16[128,1536]{1,0:T(8,128)(2,1)S(1)} %get-tuple-element.102.refs_0_), channel_id=1, source_target_pairs={{0,3},{1,0},{2,1},{3,2},{4,7},{5,4},{6,5},{7,6},{8,11},{9,8},{10,9... | collective-permute-start | bytes 1179656 | tf_op jit(solution)/shard_map/ppermute | solution.py:488
  214.4 40.8 %collective-permute-start.40 = (bf16[128,1536]{1,0:T(8,128)(2,1)S(1)}, bf16[128,1536]{1,0:T(8,128)(2,1)S(1)}, u32[]{:S(2)}, u32[]{:S(2)}) collective-permute-start(bf16[128,1536]{1,0:T(8,128)(2,1)S(1)} %copy-done.68), channel_id=1, source_target_pairs={{0,1},{1,2},{2,3},{3,0},{4,5},{5,6},{6,7},{7,4},{8,9},{9,10},{10,1... | collective-permute-start | bytes 1179656 | tf_op jit(solution)/shard_map/ppermute | solution.py:488
  214.4 47.1 %collective-permute-start.41 = (bf16[128,1536]{1,0:T(8,128)(2,1)S(1)}, bf16[128,1536]{1,0:T(8,128)(2,1)S(1)}, u32[]{:S(2)}, u32[]{:S(2)}) collective-permute-start(bf16[128,1536]{1,0:T(8,128)(2,1)S(1)} %copy-done.67), channel_id=1, source_target_pairs={{0,2},{1,3},{2,0},{3,1},{4,6},{5,7},{6,4},{7,5},{8,10},{9,11},{10,... | collective-permute-start | bytes 1179656 | tf_op jit(solution)/shard_map/ppermute | solution.py:488
  216.2 45.3 %collective-permute-start.42 = (bf16[128,1536]{1,0:T(8,128)(2,1)S(1)}, bf16[128,1536]{1,0:T(8,128)(2,1)S(1)}, u32[]{:S(2)}, u32[]{:S(2)}) collective-permute-start(bf16[128,1536]{1,0:T(8,128)(2,1)S(1)} %copy-done.66), channel_id=1, source_target_pairs={{0,3},{1,0},{2,1},{3,2},{4,7},{5,4},{6,5},{7,6},{8,11},{9,8},{10,9... | collective-permute-start | bytes 1179656 | tf_op jit(solution)/shard_map/ppermute | solution.py:488
  288.3 58.3 %collective-permute-start.83 = (bf16[2,4,48,1536]{3,2,0,1:T(8,128)(2,1)}, bf16[2,4,48,1536]{3,2,0,1:T(8,128)(2,1)S(1)}, u32[]{:S(2)}, u32[]{:S(2)}) collective-permute-start(bf16[2,4,48,1536]{3,2,0,1:T(8,128)(2,1)} %bitcast.294), channel_id=1, source_target_pairs={{0,4},{4,0},{8,12},{12,8},{16,20},{20,16},{24,28},{28,24},{32,36},... | collective-permute-start | bytes 3538952 | tf_op jit(solution)/shard_map/ppermute | solution.py:542
  288.3 114.1 %collective-permute-start.66 = (bf16[2,4,1536,128]{3,2,0,1:T(8,128)(2,1)}, bf16[2,4,1536,128]{3,2,0,1:T(8,128)(2,1)}, u32[]{:S(2)}, u32[]{:S(2)}) collective-permute-start(bf16[2,4,1536,128]{3,2,0,1:T(8,128)(2,1)} %bitcast.292), channel_id=1, source_target_pairs={{0,4},{4,0},{8,12},{12,8},{16,20},{20,16},{24,28},{28,24},{32,36},... | collective-permute-start | bytes 9437192 | tf_op jit(solution)/shard_map/ppermute | solution.py:542
  346.6 62.0 %collective-permute-start.59 = (bf16[2,4,1536,128]{3,2,0,1:T(8,128)(2,1)}, bf16[2,4,1536,128]{3,2,0,1:T(8,128)(2,1)}, u32[]{:S(2)}, u32[]{:S(2)}) collective-permute-start(bf16[2,4,1536,128]{3,2,0,1:T(8,128)(2,1)} %bitcast.293), channel_id=1, source_target_pairs={{0,4},{4,0},{8,12},{12,8},{16,20},{20,16},{24,28},{28,24},{32,36},... | collective-permute-start | bytes 9437192 | tf_op jit(solution)/shard_map/ppermute | solution.py:542
  402.3 192.8 %all-gather.21.cloned.1.call-start = ((), (), s32[]{:S(2)}) async-start(), calls=%async_computation.4 | async-start | bytes 6684672 | tf_op jit(solution)/shard_map/all_gather | solution.py:753
  405.4 45.0 %collective-permute-start.68 = (bf16[2,1536,128]{2,1,0:T(8,128)(2,1)S(1)}, bf16[2,1536,128]{2,1,0:T(8,128)(2,1)S(1)}, u32[]{:S(2)}, u32[]{:S(2)}) collective-permute-start(bf16[2,1536,128]{2,1,0:T(8,128)(2,1)S(1)} %get-tuple-element.115), channel_id=1, source_target_pairs={{0,16},{4,20},{8,24},{12,28},{16,0},{20,4},{24,8},{28,12},{32,48},... | collective-permute-start | bytes 2359304 | tf_op jit(solution)/shard_map/ppermute | solution.py:546
  407.1 47.4 %collective-permute-start.69 = (bf16[2,1536,128]{2,1,0:T(8,128)(2,1)S(1)}, bf16[2,1536,128]{2,1,0:T(8,128)(2,1)S(1)}, u32[]{:S(2)}, u32[]{:S(2)}) collective-permute-start(bf16[2,1536,128]{2,1,0:T(8,128)(2,1)S(1)} %get-tuple-element.114), channel_id=1, source_target_pairs={{0,24},{4,28},{8,0},{12,4},{16,8},{20,12},{24,16},{28,20},{32,56},... | collective-permute-start | bytes 2359304 | tf_op jit(solution)/shard_map/ppermute | solution.py:546
  411.6 56.4 %collective-permute-start.60 = (bf16[2,1536,128]{2,1,0:T(8,128)(2,1)S(1)}, bf16[2,1536,128]{2,1,0:T(8,128)(2,1)S(1)}, u32[]{:S(2)}, u32[]{:S(2)}) collective-permute-start(bf16[2,1536,128]{2,1,0:T(8,128)(2,1)S(1)} %get-tuple-element.116), channel_id=1, source_target_pairs={{0,8},{4,12},{8,16},{12,20},{16,24},{20,28},{24,0},{28,4},{32,40},... | collective-permute-start | bytes 2359304 | tf_op jit(solution)/shard_map/ppermute | solution.py:546
  412.5 73.6 %collective-permute-start.61 = (bf16[2,1536,128]{2,1,0:T(8,128)(2,1)S(1)}, bf16[2,1536,128]{2,1,0:T(8,128)(2,1)S(1)}, u32[]{:S(2)}, u32[]{:S(2)}) collective-permute-start(bf16[2,1536,128]{2,1,0:T(8,128)(2,1)S(1)} %get-tuple-element.118), channel_id=1, source_target_pairs={{0,16},{4,20},{8,24},{12,28},{16,0},{20,4},{24,8},{28,12},{32,48},... | collective-permute-start | bytes 2359304 | tf_op jit(solution)/shard_map/ppermute | solution.py:546
  428.8 59.5 %collective-permute-start.62 = (bf16[2,1536,128]{2,1,0:T(8,128)(2,1)S(1)}, bf16[2,1536,128]{2,1,0:T(8,128)(2,1)S(1)}, u32[]{:S(2)}, u32[]{:S(2)}) collective-permute-start(bf16[2,1536,128]{2,1,0:T(8,128)(2,1)S(1)} %get-tuple-element.117), channel_id=1, source_target_pairs={{0,24},{4,28},{8,0},{12,4},{16,8},{20,12},{24,16},{28,20},{32,56},... | collective-permute-start | bytes 2359304 | tf_op jit(solution)/shard_map/ppermute | solution.py:546
  455.0 41.8 %collective-permute-start.70 = (bf16[1536,128]{1,0:T(8,128)(2,1)S(1)}, bf16[1536,128]{1,0:T(8,128)(2,1)S(1)}, u32[]{:S(2)}, u32[]{:S(2)}) collective-permute-start(bf16[1536,128]{1,0:T(8,128)(2,1)S(1)} %get-tuple-element.133), channel_id=1, source_target_pairs={{32,64},{36,68},{40,72},{44,76},{48,80},{52,84},{56,88},{60,92},{6... | collective-permute-start | bytes 1179656 | tf_op jit(solution)/shard_map/ppermute | solution.py:553
  457.0 42.7 %collective-permute-start.71 = (bf16[1536,128]{1,0:T(8,128)(2,1)S(1)}, bf16[1536,128]{1,0:T(8,128)(2,1)}, u32[]{:S(2)}, u32[]{:S(2)}) collective-permute-start(bf16[1536,128]{1,0:T(8,128)(2,1)S(1)} %get-tuple-element.135), channel_id=1, source_target_pairs={{0,64},{4,68},{8,72},{12,76},{16,80},{20,84},{24,88},{28,92},{32,9... | collective-permute-start | bytes 1179656 | tf_op jit(solution)/shard_map/ppermute | solution.py:553
  468.0 31.6 %collective-permute-start.72 = (bf16[1536,128]{1,0:T(8,128)(2,1)S(1)}, bf16[1536,128]{1,0:T(8,128)(2,1)}, u32[]{:S(2)}, u32[]{:S(2)}) collective-permute-start(bf16[1536,128]{1,0:T(8,128)(2,1)S(1)} %get-tuple-element.134), channel_id=1, source_target_pairs={{0,96},{4,100},{8,104},{12,108},{16,112},{20,116},{24,120},{28,124... | collective-permute-start | bytes 1179656 | tf_op jit(solution)/shard_map/ppermute | solution.py:553
  530.5 34.7 %collective-permute-start.43 = (bf16[128,1536]{1,0:T(8,128)(2,1)S(1)}, bf16[128,1536]{1,0:T(8,128)(2,1)S(1)}, u32[]{:S(2)}, u32[]{:S(2)}) collective-permute-start(bf16[128,1536]{1,0:T(8,128)(2,1)S(1)} %copy-done.31), channel_id=1, source_target_pairs={{0,64},{1,65},{2,66},{3,67},{4,68},{5,69},{6,70},{7,71},{8,72},{9,... | collective-permute-start | bytes 1179656 | tf_op jit(solution)/shard_map/ppermute | solution.py:729
  (142 other events, 1959.8 us)
Sparse Core Ops, SparseCore 0:
  17.1 38.4 all-gather.14
  57.9 42.9 all-gather.12
  102.6 35.1 all-gather.18
  139.4 42.4 all-gather.16
  402.5 74.0 all-gather.22
  524.9 45.3 all-gather.20

commit v2 on v1

v2 whole, which is shorter than its diff:
```python
import jax
import jax.numpy as jnp
from jax import lax
from jax.experimental import pallas as pl
from jax.experimental.pallas import tpu as pltpu
from jax.sharding import PartitionSpec as P

F32 = jnp.float32
BF16 = jnp.bfloat16
HI = lax.Precision.HIGHEST
EPS = 1e-05
T = 128
LANES = 128
HEAD = 64
SLOTS = 4
ROWS = SLOTS * T
PAIRS = 6
STEPS = 2
HALF = PAIRS // STEPS
WIDE = HALF * LANES
VMEM_LIMIT = 60 * 1024 * 1024


def sigmoid(v):
    return 0.5 * jnp.tanh(0.5 * v) + 0.5


def softplus(v):
    return jnp.maximum(v, 0.0) + jnp.log1p(jnp.exp(-jnp.abs(v)))


def dot(a, b):
    return jnp.dot(a, b, preferred_element_type=F32)


def dot_nt(a, b, precision=None):
    return lax.dot_general(
        a, b, (((1,), (1,)), ((), ())), preferred_element_type=F32, precision=precision
    )


def dot_tn(a, b, precision=None):
    return lax.dot_general(
        a, b, (((0,), (0,)), ((), ())), preferred_element_type=F32, precision=precision
    )


def iota(axis):
    return lax.broadcasted_iota(jnp.int32, (T, LANES), axis)


def shift_down(v, steps):
    return jnp.where(iota(0) >= steps, pltpu.roll(v, steps, 0), 0.0)


def shift_up(v, steps):
    return jnp.where(iota(0) < T - steps, pltpu.roll(v, T - steps, 0), 0.0)


def conv_taps(cin):
    return [shift_down(cin, 3), shift_down(cin, 2), shift_down(cin, 1), cin]


def conv_sum(taps, par):
    total = par[4:5, :] + taps[0] * par[0:1, :]
    for k in range(1, 4):
        total = total + taps[k] * par[k : k + 1, :]
    return total


def conv_back(dcv, par):
    total = dcv * par[3:4, :]
    for m in range(1, 4):
        total = total + shift_up(dcv, m) * par[3 - m : 4 - m, :]
    return total


def column_sum(v):
    return jnp.sum(v, axis=0, keepdims=True)


def slot(k):
    return slice(k * T, (k + 1) * T)


def tri(lower):
    if lower:
        return (iota(0) >= iota(1)).astype(F32)
    return (iota(0) <= iota(1)).astype(F32)


def step_prep(k, pbc, dtp, run_col, run_row, step_wide):
    step = softplus(pbc[slot(k), 256:384] + dtp[0:1, :])
    run = jnp.dot(tri(True), step * dtp[1:2, :], precision=HI, preferred_element_type=F32)
    run_row[k] = jnp.transpose(run)
    left = iota(1) < HEAD
    for p in range(PAIRS):
        a, b = 2 * p, 2 * p + 1
        run_col[a, slot(k), :] = jnp.broadcast_to(run[:, a : a + 1], (T, LANES))
        run_col[b, slot(k), :] = jnp.broadcast_to(run[:, b : b + 1], (T, LANES))
        step_wide[p, slot(k), :] = jnp.where(
            left,
            jnp.broadcast_to(step[:, a : a + 1], (T, LANES)),
            jnp.broadcast_to(step[:, b : b + 1], (T, LANES)),
        )
    return step


def halves(v):
    left = iota(1) < HEAD
    zero = jnp.zeros_like(v)
    return jnp.concatenate([jnp.where(left, v, zero), jnp.where(left, zero, v)], axis=0)


class Refs:
    pass


def kernel_call(body, name, ins, outs, scratch, cost_us):
    in_names, out_names, scratch_names = list(ins), list(outs), list(scratch)

    def run(*refs):
        rf = Refs()
        for key, ref in zip(in_names + out_names + scratch_names, refs):
            setattr(rf, key, ref)
        body(rf, pl.program_id(0))

    res = pl.pallas_call(
        run,
        grid=(STEPS,),
        in_specs=[pl.BlockSpec(ins[n][1], ins[n][2]) for n in in_names],
        out_specs=[pl.BlockSpec(outs[n][2], outs[n][3]) for n in out_names],
        out_shape=[jax.ShapeDtypeStruct(outs[n][0], outs[n][1]) for n in out_names],
        scratch_shapes=[pltpu.VMEM(*scratch[n]) for n in scratch_names],
        compiler_params=pltpu.CompilerParams(vmem_limit_bytes=VMEM_LIMIT),
        cost_estimate=pl.CostEstimate(
            flops=int(cost_us * 1.1e9), bytes_accessed=1 << 20, transcendentals=0
        ),
        name=name,
    )(*[ins[n][0] for n in in_names])
    return dict(zip(out_names, res))


def whole(v):
    return (v, v.shape, lambda h: (0,) * v.ndim)


def whole_out(shape, dtype):
    return (shape, dtype, shape, lambda h: (0,) * len(shape))


def by_step(v, block):
    return (v, block, lambda h: (h,) + (0,) * (len(block) - 1))


def by_step_out(shape, dtype, block):
    return (shape, dtype, block, lambda h: (h,) + (0,) * (len(block) - 1))


def lanes_by_step(v):
    return (v, (v.shape[0], WIDE), lambda h: (0, h))


def lanes_by_step_out(shape, dtype):
    return (shape, dtype, (shape[0], WIDE), lambda h: (0, h))


def weight_blocks(w):
    half = (8, 3, 16, w.shape[3])
    return {
        "wg": (w, half, lambda h: (h, 0, 0, 0)),
        "wv": (w, half, lambda h: (h, 1, 0, 0)),
        "wbc": (w, (16, 1, 16, w.shape[3]), lambda h: (0, 6, 0, 0)),
    }


def pair_lanes(p):
    return slice(p * LANES, (p + 1) * LANES)


def flat_rows(ref):
    v = ref[...]
    return v.reshape(-1, v.shape[-1])


def mixed_bc(rf, k, c):
    lanes = slice(c * LANES, (c + 1) * LANES)
    cv = conv_sum(conv_taps(rf.pbc[slot(k), lanes]), rf.pbcv[:, lanes])
    return cv * sigmoid(cv)


def forward(x_slots, g_slots, w, dtw, wout, gain, pv, pbcv, dtp):
    width = x_slots[0].shape[1]
    with_grad = g_slots is not None

    def body(rf, h):
        @pl.when(h == 0)
        def _prep():
            for k in range(SLOTS):
                x = getattr(rf, f"x{k}")[...].astype(F32)
                scale = lax.rsqrt(jnp.mean(x * x, axis=1, keepdims=True) + EPS)
                rf.normed[slot(k), :] = (x * scale * rf.gain[...]).astype(BF16)
                if with_grad:
                    rf.g_all[slot(k), :] = getattr(rf, f"g{k}")[...]
            rf.pbc[:, 0:256] = dot_nt(rf.normed[...], flat_rows(rf.wbc))
            rf.pbc[:, 256:384] = dot_nt(rf.normed[...], rf.dtw[...])
            for k in range(SLOTS):
                rf.scores[k] = dot_nt(mixed_bc(rf, k, 1), mixed_bc(rf, k, 0), HI) * tri(True)
                step_prep(k, rf.pbc, rf.dtp, rf.run_col, rf.run_row, rf.step_wide)
            rf.square[...] = jnp.zeros_like(rf.square)
            rf.cross[...] = jnp.zeros_like(rf.cross)

        rf.proj[0, :, 0:WIDE] = dot_nt(rf.normed[...], flat_rows(rf.wg))
        rf.proj[0, :, WIDE : 2 * WIDE] = dot_nt(rf.normed[...], flat_rows(rf.wv))
        if with_grad:
            q_all = dot_nt(rf.g_all[...], rf.wout[pl.ds(pl.multiple_of(h * WIDE, WIDE), WIDE), :])
        for p in range(HALF):
            lanes = pair_lanes(p)
            par = rf.pv[:, lanes]
            pair = HALF * h + p
            for k in range(SLOTS):
                gate = rf.proj[0, slot(k), lanes]
                cv = conv_sum(
                    conv_taps(rf.proj[0, slot(k), WIDE + p * LANES : WIDE + (p + 1) * LANES]), par
                )
                values = cv * sigmoid(cv)
                scaled = (values * rf.step_wide[pair, slot(k), :]).astype(BF16)
                weights = []
                for a in range(2):
                    gap = (
                        rf.run_col[2 * pair + a, slot(k), :]
                        - rf.run_row[k, pl.ds(2 * pair + a, 1), :]
                    )
                    decay = jnp.exp(jnp.minimum(gap, 0.0))
                    weights.append((rf.scores[k] * decay).astype(BF16))
                y = dot(jnp.concatenate(weights, axis=1), halves(scaled))
                rf.y[0, slot(k), lanes] = y
                scanned = y + par[6:7, :] * values
                gated = scanned * (gate * sigmoid(gate))
                rf.square[slot(k), :] += gated * gated
                scaled_out = gated * par[5:6, :]
                rf.u_all[h, slot(k), lanes] = scaled_out.astype(BF16)
                if with_grad:
                    rf.cross[slot(k), :] += q_all[slot(k), lanes] * scaled_out

        @pl.when(h == STEPS - 1)
        def _finish():
            u = jnp.concatenate([rf.u_all[a] for a in range(STEPS)], axis=1)
            for n in range(0, width, 512):
                part = dot(u, rf.wout[:, n : n + 512]).astype(BF16)
                for k in range(SLOTS):
                    getattr(rf, f"out{k}")[:, n : n + 512] = part[slot(k), :]
            ones = jnp.ones((8, LANES), F32)
            rf.stats[0] = dot_nt(ones, rf.square[...], HI)
            rf.stats[1] = dot_nt(ones, rf.cross[...], HI)

    ins = {f"x{k}": whole(v) for k, v in enumerate(x_slots)}
    if with_grad:
        ins.update({f"g{k}": whole(v) for k, v in enumerate(g_slots)})
    ins.update(
        gain=whole(gain),
        **weight_blocks(w),
        dtw=whole(dtw),
        wout=whole(wout),
        pv=lanes_by_step(pv),
        pbcv=whole(pbcv),
        dtp=whole(dtp),
    )
    outs = {f"out{k}": whole_out((T, width), BF16) for k in range(SLOTS)}
    outs.update(
        stats=whole_out((2, 8, ROWS), F32),
        normed=whole_out((ROWS, width), BF16),
        proj=by_step_out((STEPS, ROWS, 2 * WIDE), F32, (1, ROWS, 2 * WIDE)),
        y=by_step_out((STEPS, ROWS, WIDE), F32, (1, ROWS, WIDE)),
        pbc=whole_out((ROWS, 384), F32),
    )
    scratch = dict(
        scores=((SLOTS, T, T), F32),
        run_col=((2 * PAIRS, ROWS, LANES), F32),
        run_row=((SLOTS, T, LANES), F32),
        step_wide=((PAIRS, ROWS, LANES), F32),
        u_all=((STEPS, ROWS, WIDE), BF16),
        square=((ROWS, LANES), F32),
        cross=((ROWS, LANES), F32),
    )
    if with_grad:
        scratch["g_all"] = ((ROWS, width), BF16)
    res = kernel_call(body, "layer_forward", ins, outs, scratch, 18)
    return [res[f"out{k}"] for k in range(SLOTS)], res


def head_columns(pair):
    target = 2 * pair + (iota(0) >= HEAD).astype(jnp.int32)
    one = (iota(1) == target).astype(BF16)
    return jnp.concatenate([one, one], axis=0)


def head_sum(v, columns):
    high = v.astype(BF16)
    low = (v - high.astype(F32)).astype(BF16)
    return dot(jnp.concatenate([high, low], axis=1), columns)


def backward(stages, name, cost_us, saved, layer, have):
    gate, scan, inp, wgate, wscan = (
        s in stages for s in ("gate", "scan", "input", "wgate", "wscan")
    )
    width = saved["normed"].shape[1]
    w, dtw, wout, pv, pbcv, dtp = layer
    elementwise = gate or scan

    def body(rf, h):
        @pl.when(h == 0)
        def _prep():
            for k in range(SLOTS):
                if gate or wgate:
                    rf.g_all[slot(k), :] = getattr(rf, f"g{k}")[...]
                if gate:
                    for row, ref in ((0, rf.scale_row), (1, rf.cross_row)):
                        ref[slot(k), :] = jnp.transpose(
                            jnp.broadcast_to(rf.rows[k, row : row + 1, :], (T, LANES))
                        )
                if scan:
                    inbound, outbound = mixed_bc(rf, k, 0), mixed_bc(rf, k, 1)
                    rf.mixed[0, slot(k), :] = inbound
                    rf.mixed[1, slot(k), :] = outbound
                    rf.scores[k] = dot_nt(inbound, outbound, HI) * tri(False)
                    rf.step_all[slot(k), :] = step_prep(
                        k, rf.pbc, rf.dtp, rf.run_col, rf.run_row, rf.step_wide
                    )
            if scan:
                rf.dscores[...] = jnp.zeros_like(rf.dscores)
                rf.dstep[...] = jnp.zeros_like(rf.dstep)
                rf.drun[...] = jnp.zeros_like(rf.drun)
            if inp:
                rf.total[...] = jnp.zeros_like(rf.total)

        if gate:
            q_all = dot_nt(rf.g_all[...], rf.wout[...])
        for p in range(HALF if elementwise else 0):
            lanes = pair_lanes(p)
            par = rf.pv[:, lanes]
            pair = HALF * h + p
            sums = [jnp.zeros((1, LANES), F32) for _ in range(8)]
            if scan:
                columns = head_columns(pair)
            for k in range(SLOTS):
                taps = conv_taps(rf.proj[0, slot(k), WIDE + p * LANES : WIDE + (p + 1) * LANES])
                cv = conv_sum(taps, par)
                sig_c = sigmoid(cv)
                values = cv * sig_c
                y = rf.y[0, slot(k), lanes]
                if gate:
                    gate_in = rf.proj[0, slot(k), lanes]
                    sig_g = sigmoid(gate_in)
                    silu_g = gate_in * sig_g
                    scanned = y + par[6:7, :] * values
                    gated = scanned * silu_g
                    grad_no = q_all[slot(k), lanes]
                    scale = rf.scale_row[slot(k), :]
                    dgated = scale * (grad_no * par[5:6, :]) - rf.cross_row[slot(k), :] * gated
                    norm = gated * scale
                    sums[5] += column_sum(grad_no * norm)
                    rf.u[slot(k), lanes] = (norm * par[5:6, :]).astype(BF16)
                    dscan = dgated * silu_g
                    dgate = dgated * scanned * (sig_g * (1.0 + gate_in * (1.0 - sig_g)))
                    sums[6] += column_sum(dscan * values)
                    rf.dg[slot(k), lanes] = dgate.astype(BF16)
                    if not scan:
                        rf.dscan[slot(k), lanes] = dscan
                else:
                    dscan = rf.dscan[slot(k), lanes]
                if not scan:
                    continue
                wide = rf.step_wide[pair, slot(k), :]
                dy = dscan.astype(BF16)
                scaled = (values * wide).astype(BF16)
                dweights = dot_nt(halves(scaled), dy)
                weights = []
                dscore = rf.dscores[k]
                for a in range(2):
                    gap = (
                        rf.run_row[k, pl.ds(2 * pair + a, 1), :]
                        - rf.run_col[2 * pair + a, slot(k), :]
                    )
                    decay = jnp.exp(jnp.minimum(gap, 0.0))
                    weights.append((rf.scores[k] * decay).astype(BF16))
                    dscore = dscore + dweights[slot(a), :] * decay
                rf.dscores[k] = dscore
                dscaled = dot(jnp.concatenate(weights, axis=1), halves(dy))
                rf.dstep[slot(k), :] += head_sum(dscaled * values, columns)
                rf.drun[slot(k), :] += head_sum(
                    dy.astype(F32) * y - scaled.astype(F32) * dscaled, columns
                )
                dvalues = dscaled * wide + par[6:7, :] * dscan
                dcv = dvalues * (sig_c * (1.0 + cv * (1.0 - sig_c)))
                for t in range(4):
                    sums[t] += column_sum(dcv * taps[t])
                sums[4] += column_sum(dcv)
                rf.dv[slot(k), lanes] = conv_back(dcv, par).astype(BF16)
            rf.small[p] = jnp.concatenate(sums, axis=0)
        if wgate:
            part = dot_tn(rf.dg[...], rf.normed[...]).astype(BF16)
            rf.ga[:, 0:3] = part.reshape(8, 3, 16, width)
            part = dot_tn(rf.u[...], rf.g_all[...]).astype(BF16)
            rf.ga[:, 3:6] = part.reshape(8, 3, 16, width)
        if wscan:
            part = dot_tn(rf.dv[...], rf.normed[...]).astype(BF16)
            if wgate:
                rf.ga[:, 6:9] = part.reshape(8, 3, 16, width)
                part = dot_tn(rf.dbc_half[...], rf.normed[...]).astype(BF16)
                rf.ga[:, 9] = part.reshape(8, 16, width)
            else:
                rf.gb[pl.ds(8 * h, 8), 0:3] = part.reshape(8, 3, 16, width)
        if inp:
            rf.total[...] += dot(rf.dg[...], flat_rows(rf.wg)) + dot(rf.dv[...], flat_rows(rf.wv))

        @pl.when(h == STEPS - 1)
        def _finish():
            if scan:
                sums = [[jnp.zeros((1, LANES), F32) for _ in range(8)] for _ in range(2)]
                dt_sums = [jnp.zeros((1, LANES), F32) for _ in range(8)]
                live = iota(1) < 2 * PAIRS
                for k in range(SLOTS):
                    dscore = rf.dscores[k] * tri(False)
                    dmixed = (
                        jnp.dot(
                            dscore,
                            rf.mixed[1, slot(k), :],
                            precision=HI,
                            preferred_element_type=F32,
                        ),
                        dot_tn(dscore, rf.mixed[0, slot(k), :], HI),
                    )
                    for c in range(2):
                        lanes = slice(c * LANES, (c + 1) * LANES)
                        par = rf.pbcv[:, lanes]
                        taps = conv_taps(rf.pbc[slot(k), lanes])
                        cv = conv_sum(taps, par)
                        sig = sigmoid(cv)
                        dcv = dmixed[c] * (sig * (1.0 + cv * (1.0 - sig)))
                        for t in range(4):
                            sums[c][t] += column_sum(dcv * taps[t])
                        sums[c][4] += column_sum(dcv)
                        rf.dbc[slot(k), lanes] = conv_back(dcv, par).astype(BF16)
                    dlog = jnp.dot(
                        tri(False), rf.drun[slot(k), :], precision=HI, preferred_element_type=F32
                    )
                    grad_step = rf.dstep[slot(k), :] + dlog * rf.dtp[1:2, :]
                    dt_sums[1] += column_sum(dlog * rf.step_all[slot(k), :])
                    draw = grad_step * sigmoid(rf.pbc[slot(k), 256:384] + rf.dtp[0:1, :])
                    draw = jnp.where(live, draw, 0.0)
                    dt_sums[0] += column_sum(draw)
                    rf.dbc[slot(k), 256:384] = draw.astype(BF16)
                rf.small_bc[0] = jnp.concatenate(sums[0], axis=0)
                rf.small_bc[1] = jnp.concatenate(sums[1], axis=0)
                dt_sums[1] = dt_sums[1] * rf.dtp[1:2, :]
                rf.small_dt[...] = jnp.concatenate(dt_sums, axis=0)
            if wscan and not wgate:
                part = dot_tn(rf.dbc[:, 0:256], rf.normed[...]).astype(BF16)
                rf.gb[:, 3] = part.reshape(16, 16, width)
            if wscan:
                rf.gdt[...] = dot_tn(rf.dbc[:, 256:384], rf.normed[...])[0:16]
            if inp:
                final = (
                    rf.total[...]
                    + dot(rf.dbc[:, 0:256], flat_rows(rf.wbc))
                    + dot(rf.dbc[:, 256:384], rf.dtw[...])
                )
                for k in range(SLOTS):
                    getattr(rf, f"out{k}")[...] = final[slot(k), :].astype(BF16)

    ins, outs, scratch = {}, {}, {}
    heads_cols = STEPS * WIDE
    if gate or wgate:
        ins.update({f"g{k}": whole(v) for k, v in enumerate(have["g"])})
        scratch["g_all"] = ((ROWS, width), BF16)
    if gate:
        ins["rows"] = whole(have["rows"])
        ins["wout"] = (wout, (WIDE, width), lambda h: (h, 0))
        scratch["scale_row"] = ((ROWS, LANES), F32)
        scratch["cross_row"] = ((ROWS, LANES), F32)
        outs["u"] = lanes_by_step_out((ROWS, heads_cols), BF16)
        outs["dg"] = lanes_by_step_out((ROWS, heads_cols), BF16)
        if not scan:
            outs["dscan"] = lanes_by_step_out((ROWS, heads_cols), F32)
    if elementwise:
        ins["proj"] = by_step(saved["proj"], (1, ROWS, 2 * WIDE))
        ins["y"] = by_step(saved["y"], (1, ROWS, WIDE))
        ins["pv"] = lanes_by_step(pv)
        outs["small"] = by_step_out((PAIRS, 8, LANES), F32, (HALF, 8, LANES))
    if scan:
        ins["pbc"] = whole(saved["pbc"])
        ins["pbcv"] = whole(pbcv)
        ins["dtp"] = whole(dtp)
        if not gate:
            ins["dscan"] = lanes_by_step(have["dscan"])
        outs["dv"] = lanes_by_step_out((ROWS, heads_cols), BF16)
        outs["dbc"] = whole_out((ROWS, 384), BF16)
        outs["small_bc"] = whole_out((2, 8, LANES), F32)
        outs["small_dt"] = whole_out((8, LANES), F32)
        scratch.update(
            mixed=((2, ROWS, LANES), F32),
            scores=((SLOTS, T, T), F32),
            run_col=((2 * PAIRS, ROWS, LANES), F32),
            run_row=((SLOTS, T, LANES), F32),
            step_wide=((PAIRS, ROWS, LANES), F32),
            step_all=((ROWS, LANES), F32),
            dscores=((SLOTS, T, T), F32),
            dstep=((ROWS, LANES), F32),
            drun=((ROWS, LANES), F32),
        )
    if inp:
        ins.update(weight_blocks(w))
        ins["dtw"] = whole(dtw)
        scratch["total"] = ((ROWS, width), F32)
        outs.update({f"out{k}": whole_out((T, width), BF16) for k in range(SLOTS)})
    if wgate or wscan:
        ins["normed"] = whole(saved["normed"])
    if not gate and (wgate or inp):
        ins["dg"] = lanes_by_step(have["dg"])
    if wgate and not gate:
        ins["u"] = lanes_by_step(have["u"])
    if not scan and (wscan or inp):
        ins["dv"] = lanes_by_step(have["dv"])
        ins["dbc"] = whole(have["dbc"])
    if wgate and wscan:
        ins["dbc_half"] = (have["dbc"], (ROWS, LANES), lambda h: (0, h))
        outs["ga"] = by_step_out((16, 10, 16, width), BF16, (8, 10, 16, width))
    elif wgate:
        outs["ga"] = by_step_out((16, 6, 16, width), BF16, (8, 6, 16, width))
    elif wscan:
        outs["gb"] = whole_out((16, 4, 16, width), BF16)
    if wscan:
        outs["gdt"] = whole_out((16, width), F32)
    return kernel_call(body, name, ins, outs, scratch, cost_us)


def assemble(parts, dt_rows):
    quarter = parts.shape[2]
    block = 16 * 48
    total = 8 * block + 16 * 16 + dt_rows.shape[0]

    def body(inw, outw, shared, dt, grad_in, grad_out):
        i = pl.program_id(0)

        @pl.when(i < 8)
        def _columns():
            grad_in[...] = inw[...].reshape(block, quarter).astype(F32)

        @pl.when(i < SLOTS)
        def _out():
            grad_out[...] = outw[...].reshape(block, quarter).astype(F32)

        @pl.when(i == 8)
        def _shared():
            grad_in[...] = jnp.zeros_like(grad_in)
            grad_in[0:256, :] = shared[...].reshape(256, quarter).astype(F32)
            grad_in[256 : 256 + dt_rows.shape[0], :] = dt[...]

    last = SLOTS - 1
    return pl.pallas_call(
        body,
        grid=(9,),
        in_specs=[
            pl.BlockSpec(
                (16, 48, quarter),
                lambda i: (0, jnp.where(i < SLOTS, i, jnp.minimum(i + SLOTS, 11)), 0),
            ),
            pl.BlockSpec((16, 48, quarter), lambda i: (0, SLOTS + jnp.minimum(i, last), 0)),
            pl.BlockSpec((16, 16, quarter), lambda i: (0, 36, 0)),
            pl.BlockSpec(dt_rows.shape, lambda i: (0, 0)),
        ],
        out_specs=[
            pl.BlockSpec((block, quarter), lambda i: (i, 0)),
            pl.BlockSpec((block, quarter), lambda i: (0, jnp.minimum(i, last))),
        ],
        out_shape=[
            jax.ShapeDtypeStruct((total, quarter), F32),
            jax.ShapeDtypeStruct((block, SLOTS * quarter), F32),
        ],
        compiler_params=pltpu.CompilerParams(vmem_limit_bytes=VMEM_LIMIT),
        name="assemble",
    )(parts, parts, parts, dt_rows)


def ring(n, k):
    return [(i, (i + k) % n) for i in range(n)]


def send_shard(v, k):
    return lax.ppermute(v, "shard", ring(SLOTS, k)) if k else v


def swap_section(v):
    return lax.ppermute(v, "section", [(0, 1), (1, 0)])


def dp_index(x, z, c):
    return x * 8 + z * 2 + c


def dp_pairs(move):
    pairs = []
    for x in range(2):
        for z in range(4):
            for c in range(2):
                pairs.append((dp_index(x, z, c), dp_index(*move(x, z, c))))
    return pairs


def pick(v, index, axis):
    return lax.dynamic_index_in_dim(v, index, axis, keepdims=False)


def gather_slots(v):
    return [send_shard(v, (-k) % SLOTS) for k in range(SLOTS)]


def scatter_sum(slots):
    parts = [send_shard(slots[k], k) for k in range(SLOTS)]
    return sum(p.astype(F32) for p in parts)


def section_pairs(k, layer):
    pairs = []
    for chip in range(4):
        to = (chip + k) % 4
        if to // 2 != layer:
            continue
        for z in range(4):
            for c in range(2):
                pairs.append(
                    (
                        (chip // 2) * 16 + dp_index(chip % 2, z, c),
                        (to // 2) * 16 + dp_index(to % 2, z, c),
                    )
                )
    return pairs


def sum_cores(v):
    c = lax.axis_index("dp") % 2
    v = v.reshape((2, 4, 2) + v.shape[1:])
    moved = lax.ppermute(pick(v, 1 - c, 2), "dp", dp_pairs(lambda x, z, c: (x, z, 1 - c)))
    return (pick(v, c, 2).astype(F32) + moved.astype(F32)).astype(BF16)


def sum_z(v):
    z = lax.axis_index("dp") // 2 % 4
    own = pick(v, z, 1).astype(F32)
    for k in range(1, 4):
        moved = lax.ppermute(
            pick(v, (z + k) % 4, 1), "dp", dp_pairs(lambda x, z, c: (x, (z + k) % 4, c))
        )
        own = own + moved.astype(F32)
    return own.astype(BF16)


def sum_x(v, layer):
    x = lax.axis_index("dp") // 8
    own = pick(v, x, 0).astype(F32)
    for k in range(1, 4):
        moved = lax.ppermute(pick(v, (x + k) % 2, 0), ("section", "dp"), section_pairs(k, layer))
        own = own + moved.astype(F32)
    return own.astype(BF16)


def sum_small(v):
    v = v + lax.ppermute(v, "dp", dp_pairs(lambda x, z, c: (x, z, 1 - c)))
    v = v + sum(
        lax.ppermute(v, "dp", dp_pairs(lambda x, z, c: (x, (z + k) % 4, c))) for k in range(1, 4)
    )
    return v + lax.ppermute(v, "dp", dp_pairs(lambda x, z, c: (1 - x, z, c)))


def in_order(parts, sign):
    j = lax.axis_index("shard")
    stacked = jnp.stack(parts)
    return jnp.take(stacked, (sign * (jnp.arange(SLOTS) - j)) % SLOTS, axis=0)


def shards(
    tokens,
    cotangent,
    lengths,
    norm_gain,
    in_weight,
    conv_weight,
    conv_bias,
    dt_bias,
    a_log,
    d_skip,
    gate_gain,
    out_weight,
):
    sec = lax.axis_index("section")
    d = lax.axis_index("dp")
    j = lax.axis_index("shard")
    core = d % 2
    first = sec == 0
    width = tokens.shape[2]
    quarter = norm_gain.shape[1]
    channels = conv_bias.shape[1]
    own_cols = gate_gain.shape[1]
    inner = own_cols * SLOTS
    heads = dt_bias.shape[1]
    own_heads = heads // SLOTS
    n_state = 2 * LANES
    piece = own_cols // 16
    piece_bc = n_state // 16

    x_own = pick(tokens, sec, 0)
    cot = pick(cotangent, sec, 0)
    length = pick(lengths, sec, 0)
    mask = (jnp.arange(T, dtype=jnp.int32) < length).astype(F32)[:, None]

    columns = jnp.transpose(in_weight[0])
    with jax.named_scope("weights"):

        def cut(start, rows):
            return lax.dynamic_slice(columns, (start, 0), (rows, quarter))

        def columns_of(to):
            return jnp.concatenate(
                [
                    cut(own_cols * to + piece * d, piece),
                    cut(inner + own_cols * to + piece * d, piece),
                    cut(2 * inner + piece_bc * d, piece_bc),
                ],
                axis=0,
            )

        parts = [send_shard(columns_of((j + k) % SLOTS), k) for k in range(SLOTS)]
        w_own = jnp.transpose(in_order(parts, -1), (1, 0, 2)).reshape(-1, width)
        w_other = swap_section(w_own)
        w0 = jnp.where(first, w_own, w_other)
        w1 = jnp.where(first, w_other, w_own)
        w0, x_own, cot, out_weight, norm_gain = lax.optimization_barrier(
            (w0, x_own, cot, out_weight, norm_gain)
        )
        w0 = lax.all_gather(w0, "dp", axis=0, tiled=False)
        half = own_cols // 2
        o_half = swap_section(lax.dynamic_slice(out_weight[0], (half * core, 0), (half, width)))
        o_rest = lax.ppermute(o_half, "dp", dp_pairs(lambda x, z, c: (x, z, 1 - c)))
        even = core == 0
        o_other = jnp.concatenate(
            [jnp.where(even, o_half, o_rest), jnp.where(even, o_rest, o_half)], axis=0
        )
        o0 = jnp.where(first, out_weight[0], o_other)
        o1 = jnp.where(first, o_other, out_weight[0])

    with jax.named_scope("small_weights"):
        dt_columns = columns[2 * inner + n_state :]
        sizes = [quarter, 4 * channels, channels, own_cols, heads, heads, heads, heads * quarter]
        flat = jnp.concatenate(
            [
                norm_gain[0],
                conv_weight[0].reshape(-1),
                conv_bias[0],
                gate_gain[0],
                dt_bias[0],
                a_log[0],
                d_skip[0],
                dt_columns.reshape(-1),
            ]
        )
        flat = jnp.pad(flat, (0, -flat.shape[0] % LANES)).reshape(-1, LANES)
        own = in_order(gather_slots(flat), 1)
        other = swap_section(own)
        small = [jnp.where(first, own, other), jnp.where(first, other, own)]

        def unpack(v):
            low = v.reshape(SLOTS, -1)
            at = sum(sizes[:-1])
            dtw = low[:, at : at + sizes[-1]].reshape(SLOTS, heads, quarter)
            dtw = lax.dynamic_slice(dtw, (0, own_heads * j, 0), (SLOTS, own_heads, quarter))
            dtw = jnp.transpose(dtw, (1, 0, 2)).reshape(own_heads, width)
            dtw = jnp.pad(dtw, ((0, LANES - own_heads), (0, 0)))
            v = low[:, :at].astype(F32)
            cut, at = [], 0
            for size in sizes[:-1]:
                cut.append(v[:, at : at + size])
                at += size
            gain = cut[0].reshape(1, width)
            taps = cut[1].reshape(SLOTS, 4, channels).transpose(1, 0, 2).reshape(4, -1)
            bias = cut[2].reshape(1, -1)
            conv = jnp.concatenate([taps, bias, jnp.zeros((3, taps.shape[1]), F32)], axis=0)
            pbcv = conv[:, inner:]
            pv = lax.dynamic_slice(conv, (0, own_cols * j), (8, own_cols))
            pick_heads = lambda u: lax.dynamic_slice(u[0], (own_heads * j,), (own_heads,))
            wide = jnp.repeat(pick_heads(cut[6]), HEAD)[None]
            pv = jnp.concatenate([pv[:5], pick(cut[3], j, 0)[None], wide, pv[7:]], axis=0)
            dtp = jnp.stack([pick_heads(cut[4]), -jnp.exp(pick_heads(cut[5]))])
            dtp = jnp.pad(dtp, ((0, 6), (0, LANES - own_heads)))
            return gain, dtw, pv, pbcv, dtp

        gain0, *params0 = unpack(small[0])
        gain1, *params1 = unpack(small[1])

    x_f = x_own.astype(F32)
    g1 = (mask * cot.astype(F32)).astype(BF16)
    x_slots = gather_slots(x_own)
    g1_slots = gather_slots(g1)
    w0, o0, o1, x_slots, g1_slots, gain0, params0, gain1, params1, w1 = lax.optimization_barrier(
        (w0, o0, o1, x_slots, g1_slots, gain0, params0, gain1, params1, w1)
    )
    w1 = lax.all_gather(w1, "dp", axis=0, tiled=False)
    blocks = lambda v: v.reshape(16, 7, 16, width)

    def layer_of(w, o, params):
        dtw, pv, pbcv, dtp = params
        return blocks(w), dtw, o, pv, pbcv, dtp

    def forward_layer(x, g, w, o, gain, params):
        w, dtw, o, pv, pbcv, dtp = layer_of(w, o, params)
        return forward(x, g, w, dtw, o, gain, pv, pbcv, dtp)

    parts, saved0 = forward_layer(x_slots, None, w0, o0, gain0, params0)
    branch = scatter_sum(parts)
    square = scatter_sum([saved0["stats"][0, 0:1, slot(k)] for k in range(SLOTS)])[0]
    scale0 = lax.rsqrt(square / inner + EPS)
    branch0 = branch * scale0[:, None]
    middle = (x_f + mask * branch0).astype(BF16)

    m_slots = gather_slots(middle)
    parts, saved1 = forward_layer(m_slots, g1_slots, w1, o1, gain1, params1)
    own = saved1["stats"][:, 0].reshape(2, SLOTS, T)
    back = [send_shard(own, k) for k in range(SLOTS)]
    summed = sum(jnp.roll(back[k], -k, axis=1) for k in range(SLOTS))
    scale1 = lax.rsqrt(summed[0] / inner + EPS)
    cross1 = scale1 * scale1 * scale1 * summed[1] / inner
    rows1 = jnp.pad(jnp.stack([scale1, cross1], axis=1), ((0, 0), (0, 6), (0, 0)))

    def norm_back(x, gain, grad):
        scale = lax.rsqrt(jnp.mean(x * x, axis=1, keepdims=True) + EPS)
        unit = x * scale
        dn = grad * gain
        dx = scale * (dn - unit * jnp.mean(dn * unit, axis=1, keepdims=True))
        return dx, jnp.sum(grad * unit, axis=0)

    layer1 = layer_of(w1, o1, params1)
    back1 = backward(
        ("gate", "scan", "input"),
        "backward_1",
        28,
        saved1,
        layer1,
        {"g": g1_slots, "rows": rows1},
    )
    dx, gain_grad1 = norm_back(
        middle.astype(F32), gain1, scatter_sum([back1[f"out{k}"] for k in range(SLOTS)])
    )
    grads1 = backward(
        ("wgate", "wscan"), "weight_grads_1", 8, saved1, layer1, {"g": g1_slots, **back1}
    )
    back1.update(grads1)
    branch = scatter_sum(parts) * scale1[0][:, None]
    result = middle.astype(F32) + mask * branch

    by_owner = lambda v: v.reshape(16, -1, width)
    owned1 = lax.psum_scatter(by_owner(back1["ga"]), "dp", scatter_dimension=0, tiled=False)
    owned1 = owned1 + lax.ppermute(owned1, "section", [(0, 1)])

    dmiddle = (cot.astype(F32) + dx).astype(BF16)
    g0 = (mask * dmiddle.astype(F32)).astype(BF16)
    cross0 = scale0 * scale0 * jnp.sum(g0.astype(F32) * branch0, axis=1) / inner
    own = jnp.pad(jnp.stack([scale0, cross0]), ((0, 6), (0, 0)))
    rows0 = jnp.stack(gather_slots(own))
    g0_slots = gather_slots(g0)
    layer0 = layer_of(w0, o0, params0)
    back0 = backward(
        ("gate", "wgate"), "backward_0_gate", 14, saved0, layer0, {"g": g0_slots, "rows": rows0}
    )
    a0 = sum_cores(by_owner(back0["ga"]))
    small_gate = back0["small"]
    back0.update(backward(("scan", "wscan"), "backward_0_scan", 20, saved0, layer0, back0))
    a0 = sum_z(a0)
    b0 = sum_z(sum_cores(by_owner(back0["gb"])))
    small_scan = back0["small"]
    back0.update(backward(("input",), "backward_0_input", 6, saved0, layer0, back0))
    dx, gain_grad0 = norm_back(
        x_f, gain0, scatter_sum([back0[f"out{k}"] for k in range(SLOTS)])
    )
    dtokens = dmiddle.astype(F32) + dx

    result_moved = lax.ppermute(result.astype(BF16), "section", [(0, 1)]).astype(F32)
    dtokens_moved = lax.ppermute(dtokens.astype(BF16), "section", [(1, 0)]).astype(F32)
    ends = jnp.where(
        first, jnp.stack([dtokens, dtokens_moved]), jnp.stack([result_moved, result])
    )[None]

    def to_section(v0, v1):
        kept = jnp.where(first, v0, v1).astype(F32)
        return kept + swap_section(jnp.where(first, v1, v0)).astype(F32)

    def to_rows(v):
        v = v.reshape(-1, SLOTS, quarter)
        return in_order([send_shard(pick(v, (j + k) % SLOTS, 1), k) for k in range(SLOTS)], -1)

    owned0 = jnp.concatenate([sum_x(a0, 0), sum_x(b0, 0)], axis=0)
    owned = jnp.where(first, owned0, owned1)
    by_rows = to_rows(jnp.concatenate([owned[:piece], owned[2 * piece :]], axis=0))
    shared = jnp.sum(by_rows[:, 2 * piece :].astype(F32), axis=0).astype(BF16)
    out_rows = jnp.transpose(owned[piece : 2 * piece].reshape(piece, SLOTS, quarter), (1, 0, 2))
    flat_quarters = lambda v: v.reshape(-1, quarter)
    gathered = lax.all_gather(
        jnp.concatenate(
            [
                flat_quarters(by_rows[:, :piece]),
                flat_quarters(out_rows),
                flat_quarters(by_rows[:, piece : 2 * piece]),
                shared,
            ],
            axis=0,
        ),
        "dp",
        tiled=False,
    )

    def small_of(by_pair, back, gain_grad):
        return jnp.concatenate(
            [
                by_pair.reshape(-1, LANES),
                back["small_bc"].reshape(-1, LANES),
                back["small_dt"],
                gain_grad.reshape(-1, LANES),
                back["gdt"].reshape(-1, LANES),
            ],
            axis=0,
        )

    small0 = small_of(small_gate + small_scan, back0, gain_grad0)
    small1 = small_of(back1["small"], back1, gain_grad1)
    small_sum = sum_small(to_section(small0, small1))
    everyone = in_order(gather_slots(small_sum), 1)
    n_pair, n_bc = PAIRS * 8, 2 * 8
    by_pair = everyone[:, :n_pair].reshape(SLOTS, PAIRS, 8, LANES)
    by_pair = by_pair.transpose(2, 0, 1, 3).reshape(8, inner)
    by_bc = jnp.sum(everyone[:, n_pair : n_pair + n_bc], axis=0)
    by_bc = by_bc.reshape(2, 8, LANES).transpose(1, 0, 2).reshape(8, n_state)
    at = n_pair + n_bc
    by_dt = everyone[:, at : at + 8, :own_heads].transpose(1, 0, 2).reshape(8, heads)
    at += 8
    gain_total = jnp.sum(everyone[:, at : at + width // LANES], axis=0).reshape(-1)
    at += width // LANES
    dt_rows = everyone[:, at:].reshape(SLOTS, 16, SLOTS, quarter)[:, :own_heads]
    dt_rows = pick(dt_rows, j, 2).reshape(heads, quarter)
    conv_total = jnp.concatenate([by_pair[:5], by_bc[:5]], axis=1)
    conv_own = lax.dynamic_slice(conv_total, (0, channels * j), (5, channels))
    grad_skip = jnp.sum(by_pair[6].reshape(heads, HEAD), axis=1)

    grad_in_weight, grad_out_weight = assemble(gathered, dt_rows)
    return (
        ends,
        lax.dynamic_slice(gain_total, (quarter * j,), (quarter,))[None],
        jnp.transpose(grad_in_weight)[None],
        conv_own[None, :4],
        conv_own[4][None],
        by_dt[0][None],
        by_dt[1][None],
        grad_skip[None],
        lax.dynamic_slice(by_pair[5], (own_cols * j,), (own_cols,))[None],
        grad_out_weight[None],
    )


def solution(mesh):
    return jax.shard_map(
        shards,
        mesh=mesh,
        in_specs=(
            P(("dp", "shard"), None, None),
            P(("dp", "shard"), None, None),
            P(("dp", "shard")),
            P("section", "shard"),
            P("section", "shard", None),
            P("section", None, "shard"),
            P("section", "shard"),
            P("section", None),
            P("section", None),
            P("section", None),
            P("section", "shard"),
            P("section", "shard", None),
        ),
        out_specs=(
            P("section", ("dp", "shard"), None, None),
            P("section", "shard"),
            P("section", "shard", None),
            P("section", None, "shard"),
            P("section", "shard"),
            P("section", None),
            P("section", None),
            P("section", None),
            P("section", "shard"),
            P("section", "shard", None),
        ),
        check_vma=False,
    )
```

time: 633 us -> 552 us (0.87)
  the two profiles are of different devices: /device:TPU:4 before, /device:TPU:1 now
where the time goes in v2:
time: 552 us; the launch traced here: 543 us
  waiting for transfers between devices  215 us (39%)
  Pallas kernels  115 us (21%)
  starting transfers between devices  111 us (20%)
  local copies, waits for them, and re-layouts  52.8 us (10%)
  other arithmetic  32.6 us (6%)
  between operations  15.9 us (3%)
    ppermute x45, waiting for transfers between devices, send_shard(): return lax.ppermute(v, 'shard', ring(SLOTS, k)) if k else v  122 us
    pallas_call x7, Pallas kernels, kernel_call(): pl.pallas_call(run, grid=(STEPS,), in_specs=[pl.BlockSpec(ins[n][1], ins[...  106 us
    ppermute x45, starting transfers between devices, send_shard(): return lax.ppermute(v, 'shard', ring(SLOTS, k)) if k else v  53.9 us
    ppermute x4, waiting for transfers between devices, swap_section(): return lax.ppermute(v, 'section', [(0, 1), (1, 0)])  38.8 us
    ppermute x6, waiting for transfers between devices, sum_z(): lax.ppermute(pick(v, (z + k) % 4, 1), 'dp', dp_pairs(lambda x, z, c: (x,...  31.7 us
    ppermute x3, waiting for transfers between devices, sum_small(): lax.ppermute(v, 'dp', dp_pairs(lambda x, z, c: (x, (z + k) % 4, c)))  11.1 us
  transfers between devices with their start and end apart: 76, of which 39 were waited for; matrix products, arithmetic and copies ran while one was open for 14% of the time, Pallas kernels for 10%

profile of v2, /device:TPU:1, one launch (start us, length us, event | category | flops | bytes accessed | tf_op | source)
XLA Modules:
  0.0 542.7 jit_solution(16143688345720117242)
XLA Ops:
  21.3 6.0 %collective-permute-done.3 = bf16[112,1536]{1,0:T(8,128)(2,1)} collective-permute-done((bf16[112,1536]{1,0:T(8,128)(2,1)S(1)}, bf16[112,1536]{1,0:T(8,128)(2,1)}, u32[]{:S(2)}, u32[]{:S(2)}) %collective-permute-start.3) | collective-permute-done | bytes 344096 | tf_op jit(solution)/shard_map/weights/ppermute | solution.py:596
  46.4 6.3 %collective-permute-done.15 = bf16[4,187,128]{2,1,0:T(8,128)(2,1)S(1)} collective-permute-done((bf16[4,187,128]{2,1,0:T(8,128)(2,1)S(1)}, bf16[4,187,128]{2,1,0:T(8,128)(2,1)S(1)}, u32[]{:S(2)}, u32[]{:S(2)}) %collective-permute-start.15) | collective-permute-done | bytes 191520 | tf_op jit(solution)/shard_map/small_weights/ppermute | solution.py:596
  79.5 19.6 %collective-permute-done.4 = bf16[384,1536]{1,0:T(8,128)(2,1)} collective-permute-done((bf16[384,1536]{1,0:T(8,128)(2,1)}, bf16[384,1536]{1,0:T(8,128)(2,1)}, u32[]{:S(2)}, u32[]{:S(2)}) %collective-permute-start.4) | collective-permute-done | bytes 1179680 | tf_op jit(solution)/shard_map/weights/ppermute | solution.py:596
  113.9 6.3 %collective-permute-done.7.refs_2_ = bf16[128,1536]{1,0:T(8,128)(2,1)S(1)} collective-permute-done((bf16[128,1536]{1,0:T(8,128)(2,1)S(1)}, bf16[128,1536]{1,0:T(8,128)(2,1)S(1)}, u32[]{:S(2)}, u32[]{:S(2)}) %collective-permute-start.7) | collective-permute-done | bytes 393248 | tf_op jit(solution)/shard_map/ppermute | solution.py:592
  120.2 8.8 %collective-permute-done.8.refs_3_ = bf16[128,1536]{1,0:T(8,128)(2,1)} collective-permute-done((bf16[128,1536]{1,0:T(8,128)(2,1)S(1)}, bf16[128,1536]{1,0:T(8,128)(2,1)}, u32[]{:S(2)}, u32[]{:S(2)}) %collective-permute-start.8) | collective-permute-done | bytes 393248 | tf_op jit(solution)/shard_map/ppermute | solution.py:592
  129.4 17.2 %layer_forward.2 = (bf16[128,1536]{1,0:T(8,128)(2,1)}, bf16[128,1536]{1,0:T(8,128)(2,1)}, bf16[128,1536]{1,0:T(8,128)(2,1)}, bf16[128,1536]{1,0:T(8,128)(2,1)}, ...) custom-call(bf16[128,1536]{1,0:T(8,128)(2,1)} %copy-done, ...), custom_call_target="tpu_custom_call" | custom-call | flops 19800000512 | bytes 1048576 | tf_op jit(solution)/shard_map/layer_forward/pallas_call | solution.py:128
  152.4 14.4 %collective-permute-done.19 = f32[1,128]{1,0:T(1,128)S(1)} collective-permute-done((f32[1,128]{1,0:T(1,128)S(1)}, f32[1,128]{1,0:T(1,128)S(1)}, u32[]{:S(2)}, u32[]{:S(2)}) %collective-permute-start.19) | collective-permute-done | bytes 544 | tf_op jit(solution)/shard_map/ppermute | solution.py:592
  182.9 11.3 %collective-permute-done.24.refs_3_ = bf16[128,1536]{1,0:T(8,128)(2,1)} collective-permute-done((bf16[128,1536]{1,0:T(8,128)(2,1)S(1)}, bf16[128,1536]{1,0:T(8,128)(2,1)}, u32[]{:S(2)}, u32[]{:S(2)}) %collective-permute-start.24) | collective-permute-done | bytes 393248 | tf_op jit(solution)/shard_map/ppermute | solution.py:592
  194.1 18.3 %layer_forward.3 = (bf16[128,1536]{1,0:T(8,128)(2,1)}, bf16[128,1536]{1,0:T(8,128)(2,1)}, bf16[128,1536]{1,0:T(8,128)(2,1)}, bf16[128,1536]{1,0:T(8,128)(2,1)}, ...) custom-call(bf16[128,1536]{1,0:T(8,128)(2,1)} %copy-done.3, ...), custom_call_target="tpu_custom_call" | custom-call | flops 19800000512 | bytes 1048576 | tf_op jit(solution)/shard_map/layer_forward/pallas_call | solution.py:128
  217.9 22.9 %backward_1.1 = (bf16[512,768]{1,0:T(8,128)(2,1)}, bf16[512,768]{1,0:T(8,128)(2,1)}, f32[6,8,128]{2,1,0:T(8,128)}, bf16[512,768]{1,0:T(8,128)(2,1)}, bf16[512,38...) custom-call(bf16[128,1536]{1,0:T(8,128)(2,1)} %fusion.11.refs_4_.ref, ...), custom_call_target="tpu_custom_call" | custom-call | flops 30799998976 | bytes 1048576 | tf_op jit(solution)/shard_map/backward_1/pallas_call | solution.py:128
  240.7 9.7 %weight_grads_1.1 = (bf16[16,10,16,1536]{3,2,1,0:T(8,128)(2,1)}, f32[16,1536]{1,0:T(8,128)}) custom-call(bf16[128,1536]{1,0:T(8,128)(2,1)} %fusion.11.refs_4_.refs_0_, bf16[128,1536]{1,0:T(8,128)(2,1)} %collective-permute-done.9.refs_5_.refs_1_, bf16[128,1536]{1,0:T(8,128)(2,1)} %collective-permute-done.10.refs_6_.refs_2_, ...), custom_call_target="tpu_custom_call" | custom-call | flops 8800000000 | bytes 1048576 | tf_op jit(solution)/shard_map/weight_grads_1/pallas_call | solution.py:128
  262.0 8.3 %collective-permute-done.42 = bf16[128,1536]{1,0:T(8,128)(2,1)S(1)} collective-permute-done((bf16[128,1536]{1,0:T(8,128)(2,1)S(1)}, bf16[128,1536]{1,0:T(8,128)(2,1)S(1)}, u32[]{:S(2)}, u32[]{:S(2)}) %collective-permute-start.42) | collective-permute-done | bytes 393248 | tf_op jit(solution)/shard_map/ppermute | solution.py:592
  277.8 9.3 %collective-permute-done.29 = bf16[128,1536]{1,0:T(8,128)(2,1)S(1)} collective-permute-done((bf16[128,1536]{1,0:T(8,128)(2,1)}, bf16[128,1536]{1,0:T(8,128)(2,1)S(1)}, u32[]{:S(2)}, u32[]{:S(2)}) %collective-permute-start.29) | collective-permute-done | bytes 393248 | tf_op jit(solution)/shard_map/ppermute | solution.py:592
  299.9 12.2 %collective-permute-done.34 = f32[8,128]{1,0:T(8,128)S(1)} collective-permute-done((f32[8,128]{1,0:T(8,128)S(1)}, f32[8,128]{1,0:T(8,128)S(1)}, u32[]{:S(2)}, u32[]{:S(2)}) %collective-permute-start.34) | collective-permute-done | bytes 4128 | tf_op jit(solution)/shard_map/ppermute | solution.py:592
  318.6 12.3 %backward_0_gate.1 = (bf16[512,768]{1,0:T(8,128)(2,1)}, bf16[512,768]{1,0:T(8,128)(2,1)}, f32[512,768]{1,0:T(8,128)}, f32[6,8,128]{2,1,0:T(8,128)}, bf16[16,6,16,1536]{3,2,1,0:T(8,128)(2,1)}) custom-call(bf16[128,1536]{1,0:T(8,128)(2,1)} %get-tuple-element.169.refs_0_, bf16[128,1536]{1,0:T(8,128)(2,1)} %copy-done.52, bf16[128,1536]{1,0:T(8,128)(2,1)} %copy-done.53, ...), custom_call_target="tpu_custom_call" | custom-call | flops 15399999488 | bytes 1048576 | tf_op jit(solution)/shard_map/backward_0_gate/pallas_call | solution.py:128
  330.9 16.7 %backward_0_scan.1 = (f32[6,8,128]{2,1,0:T(8,128)}, bf16[512,768]{1,0:T(8,128)(2,1)}, bf16[512,384]{1,0:T(8,128)(2,1)}, f32[2,8,128]{2,1,0:T(8,128)}, f32[8,128]...) custom-call(f32[2,512,768]{2,1,0:T(8,128)} %get-tuple-element.126.refs_6_.refs_0_, ...), custom_call_target="tpu_custom_call" | custom-call | flops 22000001024 | bytes 1048576 | tf_op jit(solution)/shard_map/backward_0_scan/pallas_call | solution.py:128
  373.4 8.2 %collective-permute-done.63 = bf16[2,64,1536]{2,1,0:T(8,128)(2,1)S(1)} collective-permute-done((bf16[2,64,1536]{2,1,0:T(8,128)(2,1)S(1)}, bf16[2,64,1536]{2,1,0:T(8,128)(2,1)S(1)}, u32[]{:S(2)}, u32[]{:S(2)}) %collective-permute-start.63) | collective-permute-done | bytes 393248 | tf_op jit(solution)/shard_map/ppermute | solution.py:653
  386.1 7.2 %collective-permute-done.55 = bf16[2,96,1536]{2,1,0:T(8,128)(2,1)S(1)} collective-permute-done((bf16[2,96,1536]{2,1,0:T(8,128)(2,1)S(1)}, bf16[2,96,1536]{2,1,0:T(8,128)(2,1)S(1)}, u32[]{:S(2)}, u32[]{:S(2)}) %collective-permute-start.55) | collective-permute-done | bytes 589856 | tf_op jit(solution)/shard_map/ppermute | solution.py:653
  394.6 12.3 %collective-permute-done.56 = bf16[2,96,1536]{2,1,0:T(8,128)(2,1)S(1)} collective-permute-done((bf16[2,96,1536]{2,1,0:T(8,128)(2,1)S(1)}, bf16[2,96,1536]{2,1,0:T(8,128)(2,1)S(1)}, u32[]{:S(2)}, u32[]{:S(2)}) %collective-permute-start.56) | collective-permute-done | bytes 589856 | tf_op jit(solution)/shard_map/ppermute | solution.py:653
  436.5 8.4 %backward_0_input.1 = (bf16[128,1536]{1,0:T(8,128)(2,1)}, bf16[128,1536]{1,0:T(8,128)(2,1)}, bf16[128,1536]{1,0:T(8,128)(2,1)}, bf16[128,1536]{1,0:T(8,128)(2,1)}) custom-call(bf16[16,7,16,1536]{3,2,1,0:T(8,128)(2,1)} %bitcast.340, bf16[16,7,16,1536]{3,2,1,0:T(8,128)(2,1)} %bitcast.341, bf16[16,7,16,1536]{3,2,1,0:T(8,128)(2,1)} %bitcast.342, ...), custom_call_target="tpu_custom_call" | custom-call | flops 6600000000 | bytes 1048576 | tf_op jit(solution)/shard_map/backward_0_input/pallas_call | solution.py:128
  449.3 6.3 %collective-permute-start.44 = (bf16[128,1536]{1,0:T(8,128)(2,1)S(1)}, bf16[128,1536]{1,0:T(8,128)(2,1)}, u32[]{:S(2)}, u32[]{:S(2)}) collective-permute-start(bf16[128,1536]{1,0:T(8,128)(2,1)S(1)} %copy-done.15), channel_id=1, source_target_pairs={{0,64},{1,65},{2,66},{3,67},{4,68},{5,69},{6,70},{7,71},{8,72},{9,... | collective-permute-start | bytes 1179656 | tf_op jit(solution)/shard_map/ppermute | solution.py:887
  469.9 6.8 %collective-permute-done.45 = f32[276,128]{1,0:T(8,128)S(1)} collective-permute-done((f32[276,128]{1,0:T(8,128)S(1)}, f32[276,128]{1,0:T(8,128)S(1)}, u32[]{:S(2)}, u32[]{:S(2)}) %collective-permute-start.45) | collective-permute-done | bytes 141344 | tf_op jit(solution)/shard_map/ppermute | solution.py:596
  490.5 9.3 %collective-permute-done.48 = f32[276,128]{1,0:T(8,128)S(1)} collective-permute-done((f32[276,128]{1,0:T(8,128)S(1)}, f32[276,128]{1,0:T(8,128)S(1)}, u32[]{:S(2)}, u32[]{:S(2)}) %collective-permute-start.48) | collective-permute-done | bytes 141344 | tf_op jit(solution)/shard_map/ppermute | solution.py:672
  526.0 10.0 %assemble.1 = (f32[6448,384]{1,0:T(8,128)}, f32[768,1536]{1,0:T(8,128)}) custom-call(bf16[16,592,384]{2,1,0:T(8,128)(2,1)} %bitcast.261, bf16[16,592,384]{2,1,0:T(8,128)(2,1)} %bitcast.262, bf16[16,592,384]{2,1,0:T(8,128)(2,1)} %bitcast.263, f32[48,384]{1,0:T(8,128)} %reshape.467.dt), custom_call_target="tpu_custom_call" | custom-call | tf_op jit(solution)/shard_map/assemble/pallas_call | solution.py:562
  (456 shorter events, 258.9 us)
Async XLA Ops:
  7.2 121.8 %all-gather.7.cloned.1.call-start = ((), (), s32[]{:S(2)}) async-start(), calls=%async_computation.2 | async-start | bytes 5849088 | tf_op jit(solution)/shard_map/weights/all_gather | solution.py:742
  29.3 164.8 %all-gather.9.cloned.1.call-start = ((), (), s32[]{:S(2)}) async-start(), calls=%async_computation.3 | async-start | bytes 5849088 | tf_op jit(solution)/shard_map/all_gather | solution.py:808
  36.8 73.2 %collective-permute-start.10 = (bf16[128,1536]{1,0:T(8,128)(2,1)}, bf16[128,1536]{1,0:T(8,128)(2,1)}, u32[]{:S(2)}, u32[]{:S(2)}) collective-permute-start(bf16[128,1536]{1,0:T(8,128)(2,1)} %fusion.11.refs_4_.refs_0_), channel_id=1, source_target_pairs={{0,2},{1,3},{2,0},{3,1},{4,6},{5,7},{6,4},{7,5},{8,10},{9,11},{10,... | collective-permute-start | bytes 1179656 | tf_op jit(solution)/shard_map/ppermute | solution.py:592
  38.8 75.1 %collective-permute-start.11 = (bf16[128,1536]{1,0:T(8,128)(2,1)}, bf16[128,1536]{1,0:T(8,128)(2,1)}, u32[]{:S(2)}, u32[]{:S(2)}) collective-permute-start(bf16[128,1536]{1,0:T(8,128)(2,1)} %fusion.11.refs_4_.refs_0_), channel_id=1, source_target_pairs={{0,1},{1,2},{2,3},{3,0},{4,5},{5,6},{6,7},{7,4},{8,9},{9,10},{10,1... | collective-permute-start | bytes 1179656 | tf_op jit(solution)/shard_map/ppermute | solution.py:592
  39.3 74.5 %collective-permute-start.9 = (bf16[128,1536]{1,0:T(8,128)(2,1)}, bf16[128,1536]{1,0:T(8,128)(2,1)}, u32[]{:S(2)}, u32[]{:S(2)}) collective-permute-start(bf16[128,1536]{1,0:T(8,128)(2,1)} %fusion.11.refs_4_.refs_0_), channel_id=1, source_target_pairs={{0,3},{1,0},{2,1},{3,2},{4,7},{5,4},{6,5},{7,6},{8,11},{9,8},{10,9... | collective-permute-start | bytes 1179656 | tf_op jit(solution)/shard_map/ppermute | solution.py:592
  46.3 52.9 %collective-permute-start.4 = (bf16[384,1536]{1,0:T(8,128)(2,1)}, bf16[384,1536]{1,0:T(8,128)(2,1)}, u32[]{:S(2)}, u32[]{:S(2)}) collective-permute-start(bf16[384,1536]{1,0:T(8,128)(2,1)} %dynamic-slice_bitcast_fusion), channel_id=1, source_target_pairs={{0,64},{64,0},{1,65},{65,1},{2,66},{66,2},{3,67},{67,3},{4,68},{68... | collective-permute-start | bytes 3538952 | tf_op jit(solution)/shard_map/weights/ppermute | solution.py:596
  52.7 61.2 %collective-permute-start.6 = (bf16[128,1536]{1,0:T(8,128)(2,1)S(1)}, bf16[128,1536]{1,0:T(8,128)(2,1)}, u32[]{:S(2)}, u32[]{:S(2)}) collective-permute-start(bf16[128,1536]{1,0:T(8,128)(2,1)S(1)} %get-tuple-element.91.refs_0_), channel_id=1, source_target_pairs={{0,3},{1,0},{2,1},{3,2},{4,7},{5,4},{6,5},{7,6},{8,11},{9,8},{10,9... | collective-permute-start | bytes 1179656 | tf_op jit(solution)/shard_map/ppermute | solution.py:592
  129.0 283.2 %reduce-scatter.2.cloned.1.call-start = ((), (), s32[]{:S(2)}) async-start(), calls=%async_computation.1 | async-start | bytes 8355840 | tf_op jit(solution)/shard_map/reduce_scatter | solution.py:862
  146.5 23.2 %collective-permute-start.16 = (bf16[128,1536]{1,0:T(8,128)(2,1)}, bf16[128,1536]{1,0:T(8,128)(2,1)S(1)}, u32[]{:S(2)}, u32[]{:S(2)}) collective-permute-start(bf16[128,1536]{1,0:T(8,128)(2,1)} %get-tuple-element.103), channel_id=1, source_target_pairs={{0,1},{1,2},{2,3},{3,0},{4,5},{5,6},{6,7},{7,4},{8,9},{9,10},{10,1... | collective-permute-start | bytes 1179656 | tf_op jit(solution)/shard_map/ppermute | solution.py:592
  146.6 23.2 %collective-permute-start.17 = (bf16[128,1536]{1,0:T(8,128)(2,1)}, bf16[128,1536]{1,0:T(8,128)(2,1)S(1)}, u32[]{:S(2)}, u32[]{:S(2)}) collective-permute-start(bf16[128,1536]{1,0:T(8,128)(2,1)} %get-tuple-element.104), channel_id=1, source_target_pairs={{0,2},{1,3},{2,0},{3,1},{4,6},{5,7},{6,4},{7,5},{8,10},{9,11},{10,... | collective-permute-start | bytes 1179656 | tf_op jit(solution)/shard_map/ppermute | solution.py:592
  147.8 22.0 %collective-permute-start.18 = (bf16[128,1536]{1,0:T(8,128)(2,1)}, bf16[128,1536]{1,0:T(8,128)(2,1)S(1)}, u32[]{:S(2)}, u32[]{:S(2)}) collective-permute-start(bf16[128,1536]{1,0:T(8,128)(2,1)} %get-tuple-element.105), channel_id=1, source_target_pairs={{0,3},{1,0},{2,1},{3,2},{4,7},{5,4},{6,5},{7,6},{8,11},{9,8},{10,9... | collective-permute-start | bytes 1179656 | tf_op jit(solution)/shard_map/ppermute | solution.py:592
  250.5 275.4 %all-gather.11.cloned.1.call-start = ((), (), s32[]{:S(2)}) async-start(), calls=%async_computation.4 | async-start | bytes 7729152 | tf_op jit(solution)/shard_map/all_gather | solution.py:907
  255.1 22.7 %collective-permute-start.28 = (bf16[128,1536]{1,0:T(8,128)(2,1)}, bf16[128,1536]{1,0:T(8,128)(2,1)S(1)}, u32[]{:S(2)}, u32[]{:S(2)}) collective-permute-start(bf16[128,1536]{1,0:T(8,128)(2,1)} %get-tuple-element.123), channel_id=1, source_target_pairs={{0,1},{1,2},{2,3},{3,0},{4,5},{5,6},{6,7},{7,4},{8,9},{9,10},{10,1... | collective-permute-start | bytes 1179656 | tf_op jit(solution)/shard_map/ppermute | solution.py:592
  256.2 30.9 %collective-permute-start.29 = (bf16[128,1536]{1,0:T(8,128)(2,1)}, bf16[128,1536]{1,0:T(8,128)(2,1)S(1)}, u32[]{:S(2)}, u32[]{:S(2)}) collective-permute-start(bf16[128,1536]{1,0:T(8,128)(2,1)} %get-tuple-element.124), channel_id=1, source_target_pairs={{0,2},{1,3},{2,0},{3,1},{4,6},{5,7},{6,4},{7,5},{8,10},{9,11},{10,... | collective-permute-start | bytes 1179656 | tf_op jit(solution)/shard_map/ppermute | solution.py:592
  260.8 27.9 %collective-permute-start.30 = (bf16[128,1536]{1,0:T(8,128)(2,1)}, bf16[128,1536]{1,0:T(8,128)(2,1)S(1)}, u32[]{:S(2)}, u32[]{:S(2)}) collective-permute-start(bf16[128,1536]{1,0:T(8,128)(2,1)} %get-tuple-element.125), channel_id=1, source_target_pairs={{0,3},{1,0},{2,1},{3,2},{4,7},{5,4},{6,5},{7,6},{8,11},{9,8},{10,9... | collective-permute-start | bytes 1179656 | tf_op jit(solution)/shard_map/ppermute | solution.py:592
  292.0 25.5 %collective-permute-start.31 = (bf16[128,1536]{1,0:T(8,128)(2,1)}, bf16[128,1536]{1,0:T(8,128)(2,1)S(1)}, u32[]{:S(2)}, u32[]{:S(2)}) collective-permute-start(bf16[128,1536]{1,0:T(8,128)(2,1)} %get-tuple-element.169.refs_0_), channel_id=1, source_target_pairs={{0,3},{1,0},{2,1},{3,2},{4,7},{5,4},{6,5},{7,6},{8,11},{9,8},{10,9... | collective-permute-start | bytes 1179656 | tf_op jit(solution)/shard_map/ppermute | solution.py:592
  295.3 22.2 %collective-permute-start.32 = (bf16[128,1536]{1,0:T(8,128)(2,1)}, bf16[128,1536]{1,0:T(8,128)(2,1)S(1)}, u32[]{:S(2)}, u32[]{:S(2)}) collective-permute-start(bf16[128,1536]{1,0:T(8,128)(2,1)} %get-tuple-element.169.refs_0_), channel_id=1, source_target_pairs={{0,2},{1,3},{2,0},{3,1},{4,6},{5,7},{6,4},{7,5},{8,10},{9,11},{10,... | collective-permute-start | bytes 1179656 | tf_op jit(solution)/shard_map/ppermute | solution.py:592
  366.7 26.6 %collective-permute-start.55 = (bf16[2,96,1536]{2,1,0:T(8,128)(2,1)S(1)}, bf16[2,96,1536]{2,1,0:T(8,128)(2,1)S(1)}, u32[]{:S(2)}, u32[]{:S(2)}) collective-permute-start(bf16[2,96,1536]{2,1,0:T(8,128)(2,1)S(1)} %get-tuple-element.187), channel_id=1, source_target_pairs={{0,8},{4,12},{8,16},{12,20},{16,24},{20,28},{24,0},{28,4},{32,40},... | collective-permute-start | bytes 1769480 | tf_op jit(solution)/shard_map/ppermute | solution.py:653
  368.2 38.6 %collective-permute-start.56 = (bf16[2,96,1536]{2,1,0:T(8,128)(2,1)S(1)}, bf16[2,96,1536]{2,1,0:T(8,128)(2,1)S(1)}, u32[]{:S(2)}, u32[]{:S(2)}) collective-permute-start(bf16[2,96,1536]{2,1,0:T(8,128)(2,1)S(1)} %get-tuple-element.189), channel_id=1, source_target_pairs={{0,16},{4,20},{8,24},{12,28},{16,0},{20,4},{24,8},{28,12},{32,48},... | collective-permute-start | bytes 1769480 | tf_op jit(solution)/shard_map/ppermute | solution.py:653
  372.2 34.6 %collective-permute-start.57 = (bf16[2,96,1536]{2,1,0:T(8,128)(2,1)S(1)}, bf16[2,96,1536]{2,1,0:T(8,128)(2,1)S(1)}, u32[]{:S(2)}, u32[]{:S(2)}) collective-permute-start(bf16[2,96,1536]{2,1,0:T(8,128)(2,1)S(1)} %get-tuple-element.188), channel_id=1, source_target_pairs={{0,24},{4,28},{8,0},{12,4},{16,8},{20,12},{24,16},{28,20},{32,56},... | collective-permute-start | bytes 1769480 | tf_op jit(solution)/shard_map/ppermute | solution.py:653
  382.5 28.3 %collective-permute-start.65 = (bf16[64,1536]{1,0:T(8,128)(2,1)S(1)}, bf16[64,1536]{1,0:T(8,128)(2,1)S(1)}, u32[]{:S(2)}, u32[]{:S(2)}) collective-permute-start(bf16[64,1536]{1,0:T(8,128)(2,1)S(1)} %get-tuple-element.206), channel_id=1, source_target_pairs={{0,32},{4,36},{8,40},{12,44},{16,48},{20,52},{24,56},{28,60},{96,0... | collective-permute-start | bytes 589832 | tf_op jit(solution)/shard_map/ppermute | solution.py:664
  384.8 27.4 %collective-permute-start.66 = (bf16[64,1536]{1,0:T(8,128)(2,1)S(1)}, bf16[64,1536]{1,0:T(8,128)(2,1)}, u32[]{:S(2)}, u32[]{:S(2)}) collective-permute-start(bf16[64,1536]{1,0:T(8,128)(2,1)S(1)} %get-tuple-element.208), channel_id=1, source_target_pairs={{64,0},{68,4},{72,8},{76,12},{80,16},{84,20},{88,24},{92,28},{96,3... | collective-permute-start | bytes 589832 | tf_op jit(solution)/shard_map/ppermute | solution.py:664
  393.3 24.6 %collective-permute-start.67 = (bf16[64,1536]{1,0:T(8,128)(2,1)}, bf16[64,1536]{1,0:T(8,128)(2,1)}, u32[]{:S(2)}, u32[]{:S(2)}) collective-permute-start(bf16[64,1536]{1,0:T(8,128)(2,1)} %get-tuple-element.207), channel_id=1, source_target_pairs={{32,0},{36,4},{40,8},{44,12},{48,16},{52,20},{56,24},{60,28},{64,3... | collective-permute-start | bytes 589832 | tf_op jit(solution)/shard_map/ppermute | solution.py:664
  449.3 38.4 %collective-permute-start.44 = (bf16[128,1536]{1,0:T(8,128)(2,1)S(1)}, bf16[128,1536]{1,0:T(8,128)(2,1)}, u32[]{:S(2)}, u32[]{:S(2)}) collective-permute-start(bf16[128,1536]{1,0:T(8,128)(2,1)S(1)} %copy-done.15), channel_id=1, source_target_pairs={{0,64},{1,65},{2,66},{3,67},{4,68},{5,69},{6,70},{7,71},{8,72},{9,... | collective-permute-start | bytes 1179656 | tf_op jit(solution)/shard_map/ppermute | solution.py:887
  (113 other events, 1568.0 us)
Sparse Core Ops, SparseCore 0:
  29.4 65.1 all-gather.6
  129.1 39.7 all-gather.8
  250.7 71.8 reduce-scatter.1
  436.5 67.4 all-gather.10

commit v3 on v2

--- a/solution.py
+++ b/solution.py
@@ -128,7 +128,10 @@
     res = pl.pallas_call(
         run,
         grid=(STEPS,),
-        in_specs=[pl.BlockSpec(ins[n][1], ins[n][2]) for n in in_names],
+        in_specs=[
+            pl.BlockSpec(*ins[n][1:]) if len(ins[n]) > 2 else pl.BlockSpec(memory_space=ins[n][1])
+            for n in in_names
+        ],
         out_specs=[pl.BlockSpec(outs[n][2], outs[n][3]) for n in out_names],
         out_shape=[jax.ShapeDtypeStruct(outs[n][0], outs[n][1]) for n in out_names],
         scratch_shapes=[pltpu.VMEM(*scratch[n]) for n in scratch_names],
@@ -170,7 +173,7 @@
     return {
         "wg": (w, half, lambda h: (h, 0, 0, 0)),
         "wv": (w, half, lambda h: (h, 1, 0, 0)),
-        "wbc": (w, (16, 1, 16, w.shape[3]), lambda h: (0, 6, 0, 0)),
+        "wbc": (w, (16, 1, 16, w.shape[3]), lambda h: (0, 9, 0, 0)),
     }
 
 
@@ -189,7 +192,7 @@
     return cv * sigmoid(cv)
 
 
-def forward(x_slots, g_slots, w, dtw, wout, gain, pv, pbcv, dtp):
+def forward(x_slots, g_slots, w, dtw, gain, pv, pbcv, dtp):
     width = x_slots[0].shape[1]
     with_grad = g_slots is not None
 
@@ -213,7 +216,7 @@
         rf.proj[0, :, 0:WIDE] = dot_nt(rf.normed[...], flat_rows(rf.wg))
         rf.proj[0, :, WIDE : 2 * WIDE] = dot_nt(rf.normed[...], flat_rows(rf.wv))
         if with_grad:
-            q_all = dot_nt(rf.g_all[...], rf.wout[pl.ds(pl.multiple_of(h * WIDE, WIDE), WIDE), :])
+            q_all = dot_nt(rf.g_all[...], rf.wout[pl.ds(8 * h, 8)].reshape(WIDE, width))
         for p in range(HALF):
             lanes = pair_lanes(p)
             par = rf.pv[:, lanes]
@@ -247,7 +250,7 @@
         def _finish():
             u = jnp.concatenate([rf.u_all[a] for a in range(STEPS)], axis=1)
             for n in range(0, width, 512):
-                part = dot(u, rf.wout[:, n : n + 512]).astype(BF16)
+                part = dot(u, rf.wout[:, :, :, n : n + 512].reshape(STEPS * WIDE, 512)).astype(BF16)
                 for k in range(SLOTS):
                     getattr(rf, f"out{k}")[:, n : n + 512] = part[slot(k), :]
             ones = jnp.ones((8, LANES), F32)
@@ -261,7 +264,7 @@
         gain=whole(gain),
         **weight_blocks(w),
         dtw=whole(dtw),
-        wout=whole(wout),
+        wout=(w, (16, 3, 16, width), lambda h: (0, 2, 0, 0)),
         pv=lanes_by_step(pv),
         pbcv=whole(pbcv),
         dtp=whole(dtp),
@@ -301,12 +304,24 @@
     return dot(jnp.concatenate([high, low], axis=1), columns)
 
 
+def put_by_core(rf, key, x, at, part):
+    keep, send = getattr(rf, key + "_keep"), getattr(rf, key + "_send")
+    groups = slice(at, at + part.shape[2])
+    for c in range(2):
+
+        @pl.when(rf.core[0] == c)
+        def _store(c=c):
+            for z in range(4):
+                keep[x, z, groups] = part[z, c]
+                send[x, z, groups] = part[z, 1 - c]
+
+
 def backward(stages, name, cost_us, saved, layer, have):
     gate, scan, inp, wgate, wscan = (
         s in stages for s in ("gate", "scan", "input", "wgate", "wscan")
     )
     width = saved["normed"].shape[1]
-    w, dtw, wout, pv, pbcv, dtp = layer
+    w, dtw, pv, pbcv, dtp = layer
     elementwise = gate or scan
 
     def body(rf, h):
@@ -336,7 +351,7 @@
                 rf.total[...] = jnp.zeros_like(rf.total)
 
         if gate:
-            q_all = dot_nt(rf.g_all[...], rf.wout[...])
+            q_all = dot_nt(rf.g_all[...], flat_rows(rf.wout))
         for p in range(HALF if elementwise else 0):
             lanes = pair_lanes(p)
             par = rf.pv[:, lanes]
@@ -399,19 +414,23 @@
                 sums[4] += column_sum(dcv)
                 rf.dv[slot(k), lanes] = conv_back(dcv, par).astype(BF16)
             rf.small[p] = jnp.concatenate(sums, axis=0)
-        if wgate:
-            part = dot_tn(rf.dg[...], rf.normed[...]).astype(BF16)
-            rf.ga[:, 0:3] = part.reshape(8, 3, 16, width)
-            part = dot_tn(rf.u[...], rf.g_all[...]).astype(BF16)
-            rf.ga[:, 3:6] = part.reshape(8, 3, 16, width)
-        if wscan:
+        if wgate and wscan:
+            for at, left, right in (
+                (0, rf.dg, rf.normed),
+                (3, rf.u, rf.g_all),
+                (6, rf.dv, rf.normed),
+            ):
+                part = dot_tn(left[...], right[...]).astype(BF16)
+                rf.ga[:, at : at + 3] = part.reshape(8, 3, 16, width)
+            part = dot_tn(rf.dbc_half[...], rf.normed[...]).astype(BF16)
+            rf.ga[:, 9] = part.reshape(8, 16, width)
+        elif wgate:
+            for at, left, right in ((0, rf.dg, rf.normed), (3, rf.u, rf.g_all)):
+                part = dot_tn(left[...], right[...]).astype(BF16)
+                put_by_core(rf, "ga", h, at, part.reshape(4, 2, 3, 16, width))
+        elif wscan:
             part = dot_tn(rf.dv[...], rf.normed[...]).astype(BF16)
-            if wgate:
-                rf.ga[:, 6:9] = part.reshape(8, 3, 16, width)
-                part = dot_tn(rf.dbc_half[...], rf.normed[...]).astype(BF16)
-                rf.ga[:, 9] = part.reshape(8, 16, width)
-            else:
-                rf.gb[pl.ds(8 * h, 8), 0:3] = part.reshape(8, 3, 16, width)
+            put_by_core(rf, "gb", h, 0, part.reshape(4, 2, 3, 16, width))
         if inp:
             rf.total[...] += dot(rf.dg[...], flat_rows(rf.wg)) + dot(rf.dv[...], flat_rows(rf.wv))
 
@@ -458,7 +477,9 @@
                 rf.small_dt[...] = jnp.concatenate(dt_sums, axis=0)
             if wscan and not wgate:
                 part = dot_tn(rf.dbc[:, 0:256], rf.normed[...]).astype(BF16)
-                rf.gb[:, 3] = part.reshape(16, 16, width)
+                part = part.reshape(2, 4, 2, 1, 16, width)
+                for a in range(2):
+                    put_by_core(rf, "gb", a, 3, part[a])
             if wscan:
                 rf.gdt[...] = dot_tn(rf.dbc[:, 256:384], rf.normed[...])[0:16]
             if inp:
@@ -477,7 +498,7 @@
         scratch["g_all"] = ((ROWS, width), BF16)
     if gate:
         ins["rows"] = whole(have["rows"])
-        ins["wout"] = (wout, (WIDE, width), lambda h: (h, 0))
+        ins["wout"] = (w, (8, 3, 16, width), lambda h: (h, 2, 0, 0))
         scratch["scale_row"] = ((ROWS, LANES), F32)
         scratch["cross_row"] = ((ROWS, LANES), F32)
         outs["u"] = lanes_by_step_out((ROWS, heads_cols), BF16)
@@ -527,10 +548,11 @@
     if wgate and wscan:
         ins["dbc_half"] = (have["dbc"], (ROWS, LANES), lambda h: (0, h))
         outs["ga"] = by_step_out((16, 10, 16, width), BF16, (8, 10, 16, width))
-    elif wgate:
-        outs["ga"] = by_step_out((16, 6, 16, width), BF16, (8, 6, 16, width))
-    elif wscan:
-        outs["gb"] = whole_out((16, 4, 16, width), BF16)
+    elif wgate or wscan:
+        ins["core"] = have["core"]
+        key, groups = ("ga", 6) if wgate else ("gb", 4)
+        for end in ("_keep", "_send"):
+            outs[key + end] = whole_out((2, 4, groups, 16, width), BF16)
     if wscan:
         outs["gdt"] = whole_out((16, width), F32)
     return kernel_call(body, name, ins, outs, scratch, cost_us)
@@ -639,31 +661,35 @@
     return pairs
 
 
-def sum_cores(v):
-    c = lax.axis_index("dp") % 2
-    v = v.reshape((2, 4, 2) + v.shape[1:])
-    moved = lax.ppermute(pick(v, 1 - c, 2), "dp", dp_pairs(lambda x, z, c: (x, z, 1 - c)))
-    return (pick(v, c, 2).astype(F32) + moved.astype(F32)).astype(BF16)
-
-
-def sum_z(v):
+def sum_parts(parts):
+    return sum(p.astype(F32) for p in parts).astype(BF16)
+
+
+def cross_core(v):
+    return lax.ppermute(v, "dp", dp_pairs(lambda x, z, c: (x, z, 1 - c)))
+
+
+def by_distance(parts):
     z = lax.axis_index("dp") // 2 % 4
-    own = pick(v, z, 1).astype(F32)
-    for k in range(1, 4):
-        moved = lax.ppermute(
-            pick(v, (z + k) % 4, 1), "dp", dp_pairs(lambda x, z, c: (x, (z + k) % 4, c))
-        )
-        own = own + moved.astype(F32)
-    return own.astype(BF16)
-
-
-def sum_x(v, layer):
+    return [sum_parts([pick(p, (z + k) % 4, 1) for p in parts]) for k in range(4)]
+
+
+def cross_z(slots):
+    return [slots[0]] + [
+        lax.ppermute(slots[k], "dp", dp_pairs(lambda x, z, c: (x, (z + k) % 4, c)))
+        for k in range(1, 4)
+    ]
+
+
+def sum_x(parts, layer):
     x = lax.axis_index("dp") // 8
-    own = pick(v, x, 0).astype(F32)
-    for k in range(1, 4):
-        moved = lax.ppermute(pick(v, (x + k) % 2, 0), ("section", "dp"), section_pairs(k, layer))
-        own = own + moved.astype(F32)
-    return own.astype(BF16)
+    same = sum_parts([pick(p, x, 0) for p in parts])
+    other = sum_parts([pick(p, 1 - x, 0) for p in parts])
+    moved = [
+        lax.ppermute(same if k == 2 else other, ("section", "dp"), section_pairs(k, layer))
+        for k in range(1, 4)
+    ]
+    return sum_parts([same] + moved)
 
 
 def sum_small(v):
@@ -709,6 +735,7 @@
     n_state = 2 * LANES
     piece = own_cols // 16
     piece_bc = n_state // 16
+    own_core = (core.astype(jnp.int32)[None], pltpu.SMEM)
 
     x_own = pick(tokens, sec, 0)
     cot = pick(cotangent, sec, 0)
@@ -733,22 +760,13 @@
 
         parts = [send_shard(columns_of((j + k) % SLOTS), k) for k in range(SLOTS)]
         w_own = jnp.transpose(in_order(parts, -1), (1, 0, 2)).reshape(-1, width)
+        o_own = lax.dynamic_slice(out_weight[0], (piece * d, 0), (piece, width))
+        w_own = jnp.concatenate([w_own[: 2 * piece], o_own, w_own[2 * piece :]], axis=0)
         w_other = swap_section(w_own)
         w0 = jnp.where(first, w_own, w_other)
         w1 = jnp.where(first, w_other, w_own)
-        w0, x_own, cot, out_weight, norm_gain = lax.optimization_barrier(
-            (w0, x_own, cot, out_weight, norm_gain)
-        )
+        w0, w1, x_own, cot, norm_gain = lax.optimization_barrier((w0, w1, x_own, cot, norm_gain))
         w0 = lax.all_gather(w0, "dp", axis=0, tiled=False)
-        half = own_cols // 2
-        o_half = swap_section(lax.dynamic_slice(out_weight[0], (half * core, 0), (half, width)))
-        o_rest = lax.ppermute(o_half, "dp", dp_pairs(lambda x, z, c: (x, z, 1 - c)))
-        even = core == 0
-        o_other = jnp.concatenate(
-            [jnp.where(even, o_half, o_rest), jnp.where(even, o_rest, o_half)], axis=0
-        )
-        o0 = jnp.where(first, out_weight[0], o_other)
-        o1 = jnp.where(first, o_other, out_weight[0])
 
     with jax.named_scope("small_weights"):
         dt_columns = columns[2 * inner + n_state :]
@@ -802,21 +820,20 @@
     g1 = (mask * cot.astype(F32)).astype(BF16)
     x_slots = gather_slots(x_own)
     g1_slots = gather_slots(g1)
-    w0, o0, o1, x_slots, g1_slots, gain0, params0, gain1, params1, w1 = lax.optimization_barrier(
-        (w0, o0, o1, x_slots, g1_slots, gain0, params0, gain1, params1, w1)
+    w0, x_slots, g1_slots, gain0, params0, gain1, params1, w1 = lax.optimization_barrier(
+        (w0, x_slots, g1_slots, gain0, params0, gain1, params1, w1)
     )
     w1 = lax.all_gather(w1, "dp", axis=0, tiled=False)
-    blocks = lambda v: v.reshape(16, 7, 16, width)
-
-    def layer_of(w, o, params):
-        dtw, pv, pbcv, dtp = params
-        return blocks(w), dtw, o, pv, pbcv, dtp
-
-    def forward_layer(x, g, w, o, gain, params):
-        w, dtw, o, pv, pbcv, dtp = layer_of(w, o, params)
-        return forward(x, g, w, dtw, o, gain, pv, pbcv, dtp)
-
-    parts, saved0 = forward_layer(x_slots, None, w0, o0, gain0, params0)
+    blocks = lambda v: v.reshape(16, 10, 16, width)
+
+    layer0 = (blocks(w0), *params0)
+    layer1 = (blocks(w1), *params1)
+
+    def forward_layer(x, g, gain, layer):
+        w, dtw, pv, pbcv, dtp = layer
+        return forward(x, g, w, dtw, gain, pv, pbcv, dtp)
+
+    parts, saved0 = forward_layer(x_slots, None, gain0, layer0)
     branch = scatter_sum(parts)
     square = scatter_sum([saved0["stats"][0, 0:1, slot(k)] for k in range(SLOTS)])[0]
     scale0 = lax.rsqrt(square / inner + EPS)
@@ -824,7 +841,7 @@
     middle = (x_f + mask * branch0).astype(BF16)
 
     m_slots = gather_slots(middle)
-    parts, saved1 = forward_layer(m_slots, g1_slots, w1, o1, gain1, params1)
+    branch_parts, saved1 = forward_layer(m_slots, g1_slots, gain1, layer1)
     own = saved1["stats"][:, 0].reshape(2, SLOTS, T)
     back = [send_shard(own, k) for k in range(SLOTS)]
     summed = sum(jnp.roll(back[k], -k, axis=1) for k in range(SLOTS))
@@ -839,7 +856,6 @@
         dx = scale * (dn - unit * jnp.mean(dn * unit, axis=1, keepdims=True))
         return dx, jnp.sum(grad * unit, axis=0)
 
-    layer1 = layer_of(w1, o1, params1)
     back1 = backward(
         ("gate", "scan", "input"),
         "backward_1",
@@ -855,9 +871,6 @@
         ("wgate", "wscan"), "weight_grads_1", 8, saved1, layer1, {"g": g1_slots, **back1}
     )
     back1.update(grads1)
-    branch = scatter_sum(parts) * scale1[0][:, None]
-    result = middle.astype(F32) + mask * branch
-
     by_owner = lambda v: v.reshape(16, -1, width)
     owned1 = lax.psum_scatter(by_owner(back1["ga"]), "dp", scatter_dimension=0, tiled=False)
     owned1 = owned1 + lax.ppermute(owned1, "section", [(0, 1)])
@@ -868,17 +881,29 @@
     own = jnp.pad(jnp.stack([scale0, cross0]), ((0, 6), (0, 0)))
     rows0 = jnp.stack(gather_slots(own))
     g0_slots = gather_slots(g0)
-    layer0 = layer_of(w0, o0, params0)
+    g0_slots, branch_parts = lax.optimization_barrier((g0_slots, branch_parts))
+    branch = scatter_sum(branch_parts) * scale1[0][:, None]
+    result = middle.astype(F32) + mask * branch
+
     back0 = backward(
-        ("gate", "wgate"), "backward_0_gate", 14, saved0, layer0, {"g": g0_slots, "rows": rows0}
-    )
-    a0 = sum_cores(by_owner(back0["ga"]))
+        ("gate", "wgate"),
+        "backward_0_gate",
+        14,
+        saved0,
+        layer0,
+        {"g": g0_slots, "rows": rows0, "core": own_core},
+    )
+    a0 = by_distance([back0["ga_keep"], cross_core(back0["ga_send"])])
+    a0, back0["dscan"] = lax.optimization_barrier((a0, back0["dscan"]))
+    a0 = cross_z(a0)
     small_gate = back0["small"]
+    back0["core"] = own_core
     back0.update(backward(("scan", "wscan"), "backward_0_scan", 20, saved0, layer0, back0))
-    a0 = sum_z(a0)
-    b0 = sum_z(sum_cores(by_owner(back0["gb"])))
+    b0 = by_distance([back0["gb_keep"], cross_core(back0["gb_send"])])
+    b0, back0["dv"] = lax.optimization_barrier((b0, back0["dv"]))
+    b0 = cross_z(b0)
     small_scan = back0["small"]
-    back0.update(backward(("input",), "backward_0_input", 6, saved0, layer0, back0))
+    back0.update(backward(("input",), "backward_0_input", 9, saved0, layer0, back0))
     dx, gain_grad0 = norm_back(
         x_f, gain0, scatter_sum([back0[f"out{k}"] for k in range(SLOTS)])
     )
@@ -898,7 +923,7 @@
         v = v.reshape(-1, SLOTS, quarter)
         return in_order([send_shard(pick(v, (j + k) % SLOTS, 1), k) for k in range(SLOTS)], -1)
 
-    owned0 = jnp.concatenate([sum_x(a0, 0), sum_x(b0, 0)], axis=0)
+    owned0 = jnp.concatenate([sum_x(a0, 0), sum_x(b0, 0)], axis=0).reshape(-1, width)
     owned = jnp.where(first, owned0, owned1)
     by_rows = to_rows(jnp.concatenate([owned[:piece], owned[2 * piece :]], axis=0))
     shared = jnp.sum(by_rows[:, 2 * piece :].astype(F32), axis=0).astype(BF16)

time: 552 us -> 512 us (0.928)
  the two profiles are of different devices: /device:TPU:1 before, /device:TPU:4 now
where the time goes in v3:
time: 512 us; the launch traced here: 504 us
  waiting for transfers between devices  214 us (42%)
  Pallas kernels  118 us (23%)
  starting transfers between devices  94.2 us (18%)
  other arithmetic  36.4 us (7%)
  local copies, waits for them, and re-layouts  25.6 us (5%)
  between operations  15.8 us (3%)
    pallas_call x7, Pallas kernels, kernel_call(): pl.pallas_call(run, grid=(STEPS,), in_specs=[pl.BlockSpec(*ins[n][1:]) if...  108 us
    ppermute x45, waiting for transfers between devices, send_shard(): return lax.ppermute(v, 'shard', ring(SLOTS, k)) if k else v  107 us
    ppermute x45, starting transfers between devices, send_shard(): return lax.ppermute(v, 'shard', ring(SLOTS, k)) if k else v  58.8 us
    ppermute x3, waiting for transfers between devices, swap_section(): return lax.ppermute(v, 'section', [(0, 1), (1, 0)])  36.7 us
    ppermute x6, waiting for transfers between devices, cross_z(): lax.ppermute(slots[k], 'dp', dp_pairs(lambda x, z, c: (x, (z + k) % 4, c)))  30 us
    ppermute x6, starting transfers between devices, sum_x(): lax.ppermute(same if k == 2 else other, ('section', 'dp'), section_pairs(...  14.2 us
    ppermute x1, waiting for transfers between devices, shards(): owned1 = owned1 + lax.ppermute(owned1, 'section', [(0, 1)])  12.1 us
    all_gather x1, waiting for transfers between devices, shards(): w0 = lax.all_gather(w0, 'dp', axis=0, tiled=False)  11.2 us
  transfers between devices with their start and end apart: 74, of which 40 were waited for; matrix products, arithmetic and copies ran while one was open for 10% of the time, Pallas kernels for 11%

profile of v3, /device:TPU:4, one launch (start us, length us, event | category | flops | bytes accessed | tf_op | source)
XLA Modules:
  0.0 504.1 jit_solution(7802251437580295969)
XLA Ops:
  22.6 12.1 %collective-permute-done.3 = bf16[160,1536]{1,0:T(8,128)(2,1)S(1)} collective-permute-done((bf16[160,1536]{1,0:T(8,128)(2,1)S(1)}, bf16[160,1536]{1,0:T(8,128)(2,1)S(1)}, u32[]{:S(2)}, u32[]{:S(2)}) %collective-permute-start.3) | collective-permute-done | bytes 491552 | tf_op jit(solution)/shard_map/weights/ppermute | solution.py:618
  49.5 9.4 %collective-permute-done.13 = bf16[4,187,128]{2,1,0:T(8,128)(2,1)S(1)} collective-permute-done((bf16[4,187,128]{2,1,0:T(8,128)(2,1)S(1)}, bf16[4,187,128]{2,1,0:T(8,128)(2,1)S(1)}, u32[]{:S(2)}, u32[]{:S(2)}) %collective-permute-start.13) | collective-permute-done | bytes 191520 | tf_op jit(solution)/shard_map/small_weights/ppermute | solution.py:618
  72.5 5.5 %collective-permute-done.9.refs_7_.refs_3_ = bf16[128,1536]{1,0:T(8,128)(2,1)S(1)} collective-permute-done((bf16[128,1536]{1,0:T(8,128)(2,1)S(1)}, bf16[128,1536]{1,0:T(8,128)(2,1)S(1)}, u32[]{:S(2)}, u32[]{:S(2)}) %collective-permute-start.9) | collective-permute-done | bytes 393248 | tf_op jit(solution)/shard_map/ppermute | solution.py:614
  78.0 11.2 %all-gather.7.cloned.1.call-done = bf16[2560,1536]{1,0:T(8,128)(2,1)} async-done(((bf16[160,1536]{1,0:T(8,128)(2,1)}), bf16[2560,1536]{1,0:T(8,128)(2,1)}) %all-gather.7.cloned.1.call-update) | async-done | bytes 7864336 | tf_op jit(solution)/shard_map/weights/all_gather | solution.py:769
  89.4 17.3 %layer_forward.2 = (bf16[128,1536]{1,0:T(8,128)(2,1)}, bf16[128,1536]{1,0:T(8,128)(2,1)}, bf16[128,1536]{1,0:T(8,128)(2,1)}, bf16[128,1536]{1,0:T(8,128)(2,1)}, ...) custom-call(bf16[128,1536]{1,0:T(8,128)(2,1)} %copy-done.2, ...), custom_call_target="tpu_custom_call" | custom-call | flops 19800000512 | bytes 1048576 | tf_op jit(solution)/shard_map/layer_forward/pallas_call | solution.py:128
  115.6 11.3 %collective-permute-done.19 = f32[1,128]{1,0:T(1,128)S(1)} collective-permute-done((f32[1,128]{1,0:T(1,128)S(1)}, f32[1,128]{1,0:T(1,128)S(1)}, u32[]{:S(2)}, u32[]{:S(2)}) %collective-permute-start.19) | collective-permute-done | bytes 544 | tf_op jit(solution)/shard_map/ppermute | solution.py:614
  138.2 14.6 %collective-permute-done.20.refs_1_ = bf16[128,1536]{1,0:T(8,128)(2,1)S(1)} collective-permute-done((bf16[128,1536]{1,0:T(8,128)(2,1)S(1)}, bf16[128,1536]{1,0:T(8,128)(2,1)S(1)}, u32[]{:S(2)}, u32[]{:S(2)}) %collective-permute-start.20) | collective-permute-done | bytes 393248 | tf_op jit(solution)/shard_map/ppermute | solution.py:614
  157.1 18.4 %layer_forward.3 = (bf16[128,1536]{1,0:T(8,128)(2,1)}, bf16[128,1536]{1,0:T(8,128)(2,1)}, bf16[128,1536]{1,0:T(8,128)(2,1)}, bf16[128,1536]{1,0:T(8,128)(2,1)}, ...) custom-call(bf16[128,1536]{1,0:T(8,128)(2,1)} %copy-done.4, ...), custom_call_target="tpu_custom_call" | custom-call | flops 19800000512 | bytes 1048576 | tf_op jit(solution)/shard_map/layer_forward/pallas_call | solution.py:128
  182.6 22.9 %backward_1.1 = (bf16[512,768]{1,0:T(8,128)(2,1)}, bf16[512,768]{1,0:T(8,128)(2,1)}, f32[6,8,128]{2,1,0:T(8,128)}, bf16[512,768]{1,0:T(8,128)(2,1)}, bf16[512,38...) custom-call(bf16[128,1536]{1,0:T(8,128)(2,1)} %copy-done.15, ...), custom_call_target="tpu_custom_call" | custom-call | flops 30799998976 | bytes 1048576 | tf_op jit(solution)/shard_map/backward_1/pallas_call | solution.py:128
  205.5 9.7 %weight_grads_1.1 = (bf16[16,10,16,1536]{3,2,1,0:T(8,128)(2,1)}, f32[16,1536]{1,0:T(8,128)}) custom-call(bf16[128,1536]{1,0:T(8,128)(2,1)} %copy-done.15, bf16[128,1536]{1,0:T(8,128)(2,1)} %copy-done.51, bf16[128,1536]{1,0:T(8,128)(2,1)} %copy-done.52, bf16[128,1536]{1,0:T(8,128)(2,1)} %copy-done.53, bf16[512,1536]{1,0:T(8,128)(2,1)} %get-tuple-element.180.refs_4_, ...), custom_call_target="tpu_custom_call" | custom-call | flops 8800000000 | bytes 1048576 | tf_op jit(solution)/shard_map/weight_grads_1/pallas_call | solution.py:128
  219.6 14.6 %collective-permute-done.28 = bf16[128,1536]{1,0:T(8,128)(2,1)S(1)} collective-permute-done((bf16[128,1536]{1,0:T(8,128)(2,1)}, bf16[128,1536]{1,0:T(8,128)(2,1)S(1)}, u32[]{:S(2)}, u32[]{:S(2)}) %collective-permute-start.28) | collective-permute-done | bytes 393248 | tf_op jit(solution)/shard_map/ppermute | solution.py:614
  247.3 15.1 %collective-permute-done.34 = f32[8,128]{1,0:T(8,128)S(1)} collective-permute-done((f32[8,128]{1,0:T(8,128)S(1)}, f32[8,128]{1,0:T(8,128)S(1)}, u32[]{:S(2)}, u32[]{:S(2)}) %collective-permute-start.34) | collective-permute-done | bytes 4128 | tf_op jit(solution)/shard_map/ppermute | solution.py:614
  267.6 13.6 %backward_0_gate.1 = (bf16[512,768]{1,0:T(8,128)(2,1)}, bf16[512,768]{1,0:T(8,128)(2,1)}, f32[512,768]{1,0:T(8,128)}, f32[6,8,128]{2,1,0:T(8,128)}, bf16[2,4,6,1...) custom-call(bf16[128,1536]{1,0:T(8,128)(2,1)} %get-tuple-element.146.refs_0_, ...), custom_call_target="tpu_custom_call" | custom-call | flops 15399999488 | bytes 1048576 | tf_op jit(solution)/shard_map/backward_0_gate/pallas_call | solution.py:128
  281.5 4.8 collective-permute-done.35
  291.3 17.2 %backward_0_scan.1 = (f32[6,8,128]{2,1,0:T(8,128)}, bf16[512,768]{1,0:T(8,128)(2,1)}, bf16[512,384]{1,0:T(8,128)(2,1)}, f32[2,8,128]{2,1,0:T(8,128)}, f32[8,128]...) custom-call(f32[2,512,768]{2,1,0:T(8,128)} %get-tuple-element.150.refs, ...), custom_call_target="tpu_custom_call" | custom-call | flops 22000001024 | bytes 1048576 | tf_op jit(solution)/shard_map/backward_0_scan/pallas_call | solution.py:128
  321.7 16.7 %collective-permute-done.56 = bf16[2,6,16,1536]{3,2,1,0:T(8,128)(2,1)} collective-permute-done((bf16[2,6,16,1536]{3,2,1,0:T(8,128)(2,1)}, bf16[2,6,16,1536]{3,2,1,0:T(8,128)(2,1)}, u32[]{:S(2)}, u32[]{:S(2)}) %collective-permute-start.56) | collective-permute-done | bytes 589856 | tf_op jit(solution)/shard_map/ppermute | solution.py:679
  347.5 7.3 %collective-permute-done.62 = bf16[2,4,16,1536]{3,2,1,0:T(8,128)(2,1)} collective-permute-done((bf16[2,4,16,1536]{3,2,1,0:T(8,128)(2,1)}, bf16[2,4,16,1536]{3,2,1,0:T(8,128)(2,1)}, u32[]{:S(2)}, u32[]{:S(2)}) %collective-permute-start.62) | collective-permute-done | bytes 393248 | tf_op jit(solution)/shard_map/ppermute | solution.py:679
  363.0 6.4 %collective-permute-start.64 = (bf16[4,16,1536]{2,1,0:T(8,128)(2,1)S(1)}, bf16[4,16,1536]{2,1,0:T(8,128)(2,1)}, u32[]{:S(2)}, u32[]{:S(2)}) collective-permute-start(bf16[4,16,1536]{2,1,0:T(8,128)(2,1)S(1)} %get-tuple-element.229), channel_id=1, source_target_pairs={{64,0},{68,4},{72,8},{76,12},{80,16},{84,20},{88,24},{92,28},{96,3... | collective-permute-start | bytes 589832 | tf_op jit(solution)/shard_map/ppermute | solution.py:689
  373.6 12.1 %collective-permute-done.66 = bf16[160,1536]{1,0:T(8,128)(2,1)S(1)} collective-permute-done((bf16[160,1536]{1,0:T(8,128)(2,1)}, bf16[160,1536]{1,0:T(8,128)(2,1)S(1)}, u32[]{:S(2)}, u32[]{:S(2)}) %collective-permute-start.66) | collective-permute-done | bytes 491552 | tf_op jit(solution)/shard_map/ppermute | solution.py:876
  401.3 8.4 %backward_0_input.1 = (bf16[128,1536]{1,0:T(8,128)(2,1)}, bf16[128,1536]{1,0:T(8,128)(2,1)}, bf16[128,1536]{1,0:T(8,128)(2,1)}, bf16[128,1536]{1,0:T(8,128)(2,1)}) custom-call(bf16[16,10,16,1536]{3,2,1,0:T(8,128)(2,1)} %bitcast.326, bf16[16,10,16,1536]{3,2,1,0:T(8,128)(2,1)} %bitcast.327, bf16[16,10,16,1536]{3,2,1,0:T(8,128)(2,1)} %bitcast.328, ...), custom_call_target="tpu_custom_call" | custom-call | flops 9900000256 | bytes 1048576 | tf_op jit(solution)/shard_map/backward_0_input/pallas_call | solution.py:128
  415.3 7.3 %collective-permute-done.41 = bf16[128,1536]{1,0:T(8,128)(2,1)} collective-permute-done((bf16[128,1536]{1,0:T(8,128)(2,1)}, bf16[128,1536]{1,0:T(8,128)(2,1)}, u32[]{:S(2)}, u32[]{:S(2)}) %collective-permute-start.41) | collective-permute-done | bytes 393248 | tf_op jit(solution)/shard_map/ppermute | solution.py:614
  436.1 15.3 %collective-permute-done.45 = f32[276,128]{1,0:T(8,128)S(1)} collective-permute-done((f32[276,128]{1,0:T(8,128)S(1)}, f32[276,128]{1,0:T(8,128)S(1)}, u32[]{:S(2)}, u32[]{:S(2)}) %collective-permute-start.45) | collective-permute-done | bytes 141344 | tf_op jit(solution)/shard_map/ppermute | solution.py:618
  460.2 6.4 %collective-permute-done.47 = f32[276,128]{1,0:T(8,128)S(1)} collective-permute-done((f32[276,128]{1,0:T(8,128)S(1)}, f32[276,128]{1,0:T(8,128)S(1)}, u32[]{:S(2)}, u32[]{:S(2)}) %collective-permute-start.47) | collective-permute-done | bytes 141344 | tf_op jit(solution)/shard_map/ppermute | solution.py:698
  487.2 10.1 %assemble.1 = (f32[6448,384]{1,0:T(8,128)}, f32[768,1536]{1,0:T(8,128)}) custom-call(bf16[16,592,384]{2,1,0:T(8,128)(2,1)} %bitcast.247, bf16[16,592,384]{2,1,0:T(8,128)(2,1)} %bitcast.248, bf16[16,592,384]{2,1,0:T(8,128)(2,1)} %bitcast.249, f32[48,384]{1,0:T(8,128)} %reshape.520.dt), custom_call_target="tpu_custom_call" | custom-call | tf_op jit(solution)/shard_map/assemble/pallas_call | solution.py:584
  (449 shorter events, 200.5 us)
Async XLA Ops:
  7.2 82.0 %all-gather.7.cloned.1.call-start = ((), (), s32[]{:S(2)}) async-start(), calls=%async_computation.2 | async-start | bytes 8355840 | tf_op jit(solution)/shard_map/weights/all_gather | solution.py:769
  35.8 120.6 %all-gather.9.cloned.1.call-start = ((), (), s32[]{:S(2)}) async-start(), calls=%async_computation.3 | async-start | bytes 8355840 | tf_op jit(solution)/shard_map/all_gather | solution.py:826
  41.8 22.6 %collective-permute-start.4 = (bf16[128,1536]{1,0:T(8,128)(2,1)S(1)}, bf16[128,1536]{1,0:T(8,128)(2,1)}, u32[]{:S(2)}, u32[]{:S(2)}) collective-permute-start(bf16[128,1536]{1,0:T(8,128)(2,1)S(1)} %get-tuple-element.109.refs_0_), channel_id=1, source_target_pairs={{0,3},{1,0},{2,1},{3,2},{4,7},{5,4},{6,5},{7,6},{8,11},{9,8},{10,9... | collective-permute-start | bytes 1179656 | tf_op jit(solution)/shard_map/ppermute | solution.py:614
  42.6 28.6 %collective-permute-start.5 = (bf16[128,1536]{1,0:T(8,128)(2,1)S(1)}, bf16[128,1536]{1,0:T(8,128)(2,1)}, u32[]{:S(2)}, u32[]{:S(2)}) collective-permute-start(bf16[128,1536]{1,0:T(8,128)(2,1)S(1)} %get-tuple-element.109.refs_0_), channel_id=1, source_target_pairs={{0,2},{1,3},{2,0},{3,1},{4,6},{5,7},{6,4},{7,5},{8,10},{9,11},{10,... | collective-permute-start | bytes 1179656 | tf_op jit(solution)/shard_map/ppermute | solution.py:614
  44.7 26.5 %collective-permute-start.6 = (bf16[128,1536]{1,0:T(8,128)(2,1)S(1)}, bf16[128,1536]{1,0:T(8,128)(2,1)}, u32[]{:S(2)}, u32[]{:S(2)}) collective-permute-start(bf16[128,1536]{1,0:T(8,128)(2,1)S(1)} %get-tuple-element.109.refs_0_), channel_id=1, source_target_pairs={{0,1},{1,2},{2,3},{3,0},{4,5},{5,6},{6,7},{7,4},{8,9},{9,10},{10,1... | collective-permute-start | bytes 1179656 | tf_op jit(solution)/shard_map/ppermute | solution.py:614
  47.5 23.7 %collective-permute-start.7 = (bf16[128,1536]{1,0:T(8,128)(2,1)S(1)}, bf16[128,1536]{1,0:T(8,128)(2,1)S(1)}, u32[]{:S(2)}, u32[]{:S(2)}) collective-permute-start(bf16[128,1536]{1,0:T(8,128)(2,1)S(1)} %fusion.6.refs_4_.refs_0_), channel_id=1, source_target_pairs={{0,3},{1,0},{2,1},{3,2},{4,7},{5,4},{6,5},{7,6},{8,11},{9,8},{10,9... | collective-permute-start | bytes 1179656 | tf_op jit(solution)/shard_map/ppermute | solution.py:614
  89.2 280.4 %reduce-scatter.2.cloned.1.call-start = ((), (), s32[]{:S(2)}) async-start(), calls=%async_computation.1 | async-start | bytes 8355840 | tf_op jit(solution)/shard_map/reduce_scatter | solution.py:875
  106.8 26.0 %collective-permute-start.16 = (bf16[128,1536]{1,0:T(8,128)(2,1)}, bf16[128,1536]{1,0:T(8,128)(2,1)S(1)}, u32[]{:S(2)}, u32[]{:S(2)}) collective-permute-start(bf16[128,1536]{1,0:T(8,128)(2,1)} %get-tuple-element.122), channel_id=1, source_target_pairs={{0,3},{1,0},{2,1},{3,2},{4,7},{5,4},{6,5},{7,6},{8,11},{9,8},{10,9... | collective-permute-start | bytes 1179656 | tf_op jit(solution)/shard_map/ppermute | solution.py:614
  109.4 23.4 %collective-permute-start.15 = (bf16[128,1536]{1,0:T(8,128)(2,1)}, bf16[128,1536]{1,0:T(8,128)(2,1)S(1)}, u32[]{:S(2)}, u32[]{:S(2)}) collective-permute-start(bf16[128,1536]{1,0:T(8,128)(2,1)} %get-tuple-element.121), channel_id=1, source_target_pairs={{0,2},{1,3},{2,0},{3,1},{4,6},{5,7},{6,4},{7,5},{8,10},{9,11},{10,... | collective-permute-start | bytes 1179656 | tf_op jit(solution)/shard_map/ppermute | solution.py:614
  109.6 23.2 %collective-permute-start.14 = (bf16[128,1536]{1,0:T(8,128)(2,1)}, bf16[128,1536]{1,0:T(8,128)(2,1)S(1)}, u32[]{:S(2)}, u32[]{:S(2)}) collective-permute-start(bf16[128,1536]{1,0:T(8,128)(2,1)} %get-tuple-element.120), channel_id=1, source_target_pairs={{0,1},{1,2},{2,3},{3,0},{4,5},{5,6},{6,7},{7,4},{8,9},{9,10},{10,1... | collective-permute-start | bytes 1179656 | tf_op jit(solution)/shard_map/ppermute | solution.py:614
  215.2 272.0 %all-gather.11.cloned.1.call-start = ((), (), s32[]{:S(2)}) async-start(), calls=%async_computation.4 | async-start | bytes 7729152 | tf_op jit(solution)/shard_map/all_gather | solution.py:932
  241.0 25.6 %collective-permute-start.29 = (bf16[128,1536]{1,0:T(8,128)(2,1)}, bf16[128,1536]{1,0:T(8,128)(2,1)S(1)}, u32[]{:S(2)}, u32[]{:S(2)}) collective-permute-start(bf16[128,1536]{1,0:T(8,128)(2,1)} %get-tuple-element.146.refs_0_), channel_id=1, source_target_pairs={{0,3},{1,0},{2,1},{3,2},{4,7},{5,4},{6,5},{7,6},{8,11},{9,8},{10,9... | collective-permute-start | bytes 1179656 | tf_op jit(solution)/shard_map/ppermute | solution.py:614
  241.6 25.0 %collective-permute-start.30 = (bf16[128,1536]{1,0:T(8,128)(2,1)}, bf16[128,1536]{1,0:T(8,128)(2,1)S(1)}, u32[]{:S(2)}, u32[]{:S(2)}) collective-permute-start(bf16[128,1536]{1,0:T(8,128)(2,1)} %get-tuple-element.146.refs_0_), channel_id=1, source_target_pairs={{0,2},{1,3},{2,0},{3,1},{4,6},{5,7},{6,4},{7,5},{8,10},{9,11},{10,... | collective-permute-start | bytes 1179656 | tf_op jit(solution)/shard_map/ppermute | solution.py:614
  242.2 24.4 %collective-permute-start.31 = (bf16[128,1536]{1,0:T(8,128)(2,1)}, bf16[128,1536]{1,0:T(8,128)(2,1)S(1)}, u32[]{:S(2)}, u32[]{:S(2)}) collective-permute-start(bf16[128,1536]{1,0:T(8,128)(2,1)} %get-tuple-element.146.refs_0_), channel_id=1, source_target_pairs={{0,1},{1,2},{2,3},{3,0},{4,5},{5,6},{6,7},{7,4},{8,9},{9,10},{10,1... | collective-permute-start | bytes 1179656 | tf_op jit(solution)/shard_map/ppermute | solution.py:614
  308.6 29.8 %collective-permute-start.56 = (bf16[2,6,16,1536]{3,2,1,0:T(8,128)(2,1)}, bf16[2,6,16,1536]{3,2,1,0:T(8,128)(2,1)}, u32[]{:S(2)}, u32[]{:S(2)}) collective-permute-start(bf16[2,6,16,1536]{3,2,1,0:T(8,128)(2,1)} %fusion.23), channel_id=1, source_target_pairs={{0,24},{4,28},{8,0},{12,4},{16,8},{20,12},{24,16},{28,20},{32,56},... | collective-permute-start | bytes 1769480 | tf_op jit(solution)/shard_map/ppermute | solution.py:679
  311.8 26.6 %collective-permute-start.55 = (bf16[2,6,16,1536]{3,2,1,0:T(8,128)(2,1)S(1)}, bf16[2,6,16,1536]{3,2,1,0:T(8,128)(2,1)}, u32[]{:S(2)}, u32[]{:S(2)}) collective-permute-start(bf16[2,6,16,1536]{3,2,1,0:T(8,128)(2,1)S(1)} %get-tuple-element.188), channel_id=1, source_target_pairs={{0,16},{4,20},{8,24},{12,28},{16,0},{20,4},{24,8},{28,12},{32,48},... | collective-permute-start | bytes 1769480 | tf_op jit(solution)/shard_map/ppermute | solution.py:679
  311.8 29.8 %collective-permute-start.54 = (bf16[2,6,16,1536]{3,2,1,0:T(8,128)(2,1)S(1)}, bf16[2,6,16,1536]{3,2,1,0:T(8,128)(2,1)}, u32[]{:S(2)}, u32[]{:S(2)}) collective-permute-start(bf16[2,6,16,1536]{3,2,1,0:T(8,128)(2,1)S(1)} %get-tuple-element.187), channel_id=1, source_target_pairs={{0,8},{4,12},{8,16},{12,20},{16,24},{20,28},{24,0},{28,4},{32,40},... | collective-permute-start | bytes 1769480 | tf_op jit(solution)/shard_map/ppermute | solution.py:679
  317.1 37.7 %collective-permute-start.62 = (bf16[2,4,16,1536]{3,2,1,0:T(8,128)(2,1)}, bf16[2,4,16,1536]{3,2,1,0:T(8,128)(2,1)}, u32[]{:S(2)}, u32[]{:S(2)}) collective-permute-start(bf16[2,4,16,1536]{3,2,1,0:T(8,128)(2,1)} %fusion.27), channel_id=1, source_target_pairs={{0,24},{4,28},{8,0},{12,4},{16,8},{20,12},{24,16},{28,20},{32,56},... | collective-permute-start | bytes 1179656 | tf_op jit(solution)/shard_map/ppermute | solution.py:679
  319.7 35.8 %collective-permute-start.61 = (bf16[2,4,16,1536]{3,2,1,0:T(8,128)(2,1)}, bf16[2,4,16,1536]{3,2,1,0:T(8,128)(2,1)}, u32[]{:S(2)}, u32[]{:S(2)}) collective-permute-start(bf16[2,4,16,1536]{3,2,1,0:T(8,128)(2,1)} %get-tuple-element.192), channel_id=1, source_target_pairs={{0,16},{4,20},{8,24},{12,28},{16,0},{20,4},{24,8},{28,12},{32,48},... | collective-permute-start | bytes 1179656 | tf_op jit(solution)/shard_map/ppermute | solution.py:679
  338.4 19.9 %collective-permute-start.60 = (bf16[2,4,16,1536]{3,2,1,0:T(8,128)(2,1)}, bf16[2,4,16,1536]{3,2,1,0:T(8,128)(2,1)}, u32[]{:S(2)}, u32[]{:S(2)}) collective-permute-start(bf16[2,4,16,1536]{3,2,1,0:T(8,128)(2,1)} %get-tuple-element.191), channel_id=1, source_target_pairs={{0,8},{4,12},{8,16},{12,20},{16,24},{20,28},{24,0},{28,4},{32,40},... | collective-permute-start | bytes 1179656 | tf_op jit(solution)/shard_map/ppermute | solution.py:679
  345.1 24.3 %collective-permute-start.58 = (bf16[6,16,1536]{2,1,0:T(8,128)(2,1)S(1)}, bf16[6,16,1536]{2,1,0:T(8,128)(2,1)S(1)}, u32[]{:S(2)}, u32[]{:S(2)}) collective-permute-start(bf16[6,16,1536]{2,1,0:T(8,128)(2,1)S(1)} %get-tuple-element.223), channel_id=1, source_target_pairs={{64,0},{68,4},{72,8},{76,12},{80,16},{84,20},{88,24},{92,28},{96,3... | collective-permute-start | bytes 884744 | tf_op jit(solution)/shard_map/ppermute | solution.py:689
  400.2 22.5 %collective-permute-start.41 = (bf16[128,1536]{1,0:T(8,128)(2,1)}, bf16[128,1536]{1,0:T(8,128)(2,1)}, u32[]{:S(2)}, u32[]{:S(2)}) collective-permute-start(bf16[128,1536]{1,0:T(8,128)(2,1)} %get-tuple-element.169), channel_id=1, source_target_pairs={{0,1},{1,2},{2,3},{3,0},{4,5},{5,6},{6,7},{7,4},{8,9},{9,10},{10,1... | collective-permute-start | bytes 1179656 | tf_op jit(solution)/shard_map/ppermute | solution.py:614
  413.4 20.5 %collective-permute-start.37 = (bf16[128,1536]{1,0:T(8,128)(2,1)}, bf16[128,1536]{1,0:T(8,128)(2,1)}, u32[]{:S(2)}, u32[]{:S(2)}) collective-permute-start(bf16[128,1536]{1,0:T(8,128)(2,1)} %get-tuple-element.165), channel_id=1, source_target_pairs={{0,1},{1,2},{2,3},{3,0},{4,5},{5,6},{6,7},{7,4},{8,9},{9,10},{10,1... | collective-permute-start | bytes 1179656 | tf_op jit(solution)/shard_map/ppermute | solution.py:614
  425.0 33.1 %collective-permute-start.44 = (bf16[128,1536]{1,0:T(8,128)(2,1)}, bf16[128,1536]{1,0:T(8,128)(2,1)}, u32[]{:S(2)}, u32[]{:S(2)}) collective-permute-start(bf16[128,1536]{1,0:T(8,128)(2,1)} %get-tuple-element.225), channel_id=1, source_target_pairs={{0,64},{1,65},{2,66},{3,67},{4,68},{5,69},{6,70},{7,71},{8,72},{9,... | collective-permute-start | bytes 1179656 | tf_op jit(solution)/shard_map/ppermute | solution.py:912
  (111 other events, 1478.9 us)
Sparse Core Ops, SparseCore 0:
  35.9 53.2 all-gather.6
  91.5 50.8 all-gather.8
  215.3 75.4 reduce-scatter.1
  397.4 47.7 all-gather.10

commit v4 on v3

--- a/solution.py
+++ b/solution.py
@@ -171,8 +171,8 @@
 def weight_blocks(w):
     half = (8, 3, 16, w.shape[3])
     return {
-        "wg": (w, half, lambda h: (h, 0, 0, 0)),
-        "wv": (w, half, lambda h: (h, 1, 0, 0)),
+        "wg": (w, half, lambda h: (h, 1, 0, 0)),
+        "wv": (w, half, lambda h: (h, 2, 0, 0)),
         "wbc": (w, (16, 1, 16, w.shape[3]), lambda h: (0, 9, 0, 0)),
     }
 
@@ -264,7 +264,7 @@
         gain=whole(gain),
         **weight_blocks(w),
         dtw=whole(dtw),
-        wout=(w, (16, 3, 16, width), lambda h: (0, 2, 0, 0)),
+        wout=(w, (16, 3, 16, width), lambda h: (0, 0, 0, 0)),
         pv=lanes_by_step(pv),
         pbcv=whole(pbcv),
         dtp=whole(dtp),
@@ -498,7 +498,7 @@
         scratch["g_all"] = ((ROWS, width), BF16)
     if gate:
         ins["rows"] = whole(have["rows"])
-        ins["wout"] = (w, (8, 3, 16, width), lambda h: (h, 2, 0, 0))
+        ins["wout"] = (w, (8, 3, 16, width), lambda h: (h, 0, 0, 0))
         scratch["scale_row"] = ((ROWS, LANES), F32)
         scratch["cross_row"] = ((ROWS, LANES), F32)
         outs["u"] = lanes_by_step_out((ROWS, heads_cols), BF16)
@@ -558,12 +558,12 @@
     return kernel_call(body, name, ins, outs, scratch, cost_us)
 
 
-def assemble(parts, dt_rows):
+def assemble(parts, dt_rows, shard):
     quarter = parts.shape[2]
     block = 16 * 48
     total = 8 * block + 16 * 16 + dt_rows.shape[0]
 
-    def body(inw, outw, shared, dt, grad_in, grad_out):
+    def body(_, inw, outw, shared, dt, grad_in, grad_out):
         i = pl.program_id(0)
 
         @pl.when(i < 8)
@@ -581,29 +581,33 @@
             grad_in[256 : 256 + dt_rows.shape[0], :] = dt[...]
 
     last = SLOTS - 1
-    return pl.pallas_call(
-        body,
+    spec = pltpu.PrefetchScalarGridSpec(
+        num_scalar_prefetch=1,
         grid=(9,),
         in_specs=[
             pl.BlockSpec(
                 (16, 48, quarter),
-                lambda i: (0, jnp.where(i < SLOTS, i, jnp.minimum(i + SLOTS, 11)), 0),
+                lambda i, j: (0, jnp.where(i < SLOTS, 0, 8) + (j[0] + 3 * SLOTS - i) % SLOTS, 0),
             ),
-            pl.BlockSpec((16, 48, quarter), lambda i: (0, SLOTS + jnp.minimum(i, last), 0)),
-            pl.BlockSpec((16, 16, quarter), lambda i: (0, 36, 0)),
-            pl.BlockSpec(dt_rows.shape, lambda i: (0, 0)),
+            pl.BlockSpec((16, 48, quarter), lambda i, j: (0, SLOTS + jnp.minimum(i, last), 0)),
+            pl.BlockSpec((16, 16, quarter), lambda i, j: (0, 36, 0)),
+            pl.BlockSpec(dt_rows.shape, lambda i, j: (0, 0)),
         ],
         out_specs=[
-            pl.BlockSpec((block, quarter), lambda i: (i, 0)),
-            pl.BlockSpec((block, quarter), lambda i: (0, jnp.minimum(i, last))),
+            pl.BlockSpec((block, quarter), lambda i, j: (i, 0)),
+            pl.BlockSpec((block, quarter), lambda i, j: (0, jnp.minimum(i, last))),
         ],
+    )
+    return pl.pallas_call(
+        body,
+        grid_spec=spec,
         out_shape=[
             jax.ShapeDtypeStruct((total, quarter), F32),
             jax.ShapeDtypeStruct((block, SLOTS * quarter), F32),
         ],
         compiler_params=pltpu.CompilerParams(vmem_limit_bytes=VMEM_LIMIT),
         name="assemble",
-    )(parts, parts, parts, dt_rows)
+    )(shard.astype(jnp.int32)[None], parts, parts, parts, dt_rows)
 
 
 def ring(n, k):
@@ -612,6 +616,15 @@
 
 def send_shard(v, k):
     return lax.ppermute(v, "shard", ring(SLOTS, k)) if k else v
+
+
+def send_across(v, k):
+    pairs = [
+        (sec * SLOTS + y, (1 - sec) * SLOTS + (y + k) % SLOTS)
+        for sec in range(2)
+        for y in range(SLOTS)
+    ]
+    return lax.ppermute(v, ("section", "shard"), pairs)
 
 
 def swap_section(v):
@@ -681,15 +694,14 @@
     ]
 
 
-def sum_x(parts, layer):
+def cross_x(parts, layer):
     x = lax.axis_index("dp") // 8
     same = sum_parts([pick(p, x, 0) for p in parts])
     other = sum_parts([pick(p, 1 - x, 0) for p in parts])
-    moved = [
+    return [same] + [
         lax.ppermute(same if k == 2 else other, ("section", "dp"), section_pairs(k, layer))
         for k in range(1, 4)
     ]
-    return sum_parts([same] + moved)
 
 
 def sum_small(v):
@@ -758,15 +770,31 @@
                 axis=0,
             )
 
-        parts = [send_shard(columns_of((j + k) % SLOTS), k) for k in range(SLOTS)]
-        w_own = jnp.transpose(in_order(parts, -1), (1, 0, 2)).reshape(-1, width)
+        cuts = [columns_of((j + k) % SLOTS) for k in range(SLOTS)]
         o_own = lax.dynamic_slice(out_weight[0], (piece * d, 0), (piece, width))
-        w_own = jnp.concatenate([w_own[: 2 * piece], o_own, w_own[2 * piece :]], axis=0)
-        w_other = swap_section(w_own)
-        w0 = jnp.where(first, w_own, w_other)
-        w1 = jnp.where(first, w_other, w_own)
-        w0, w1, x_own, cot, norm_gain = lax.optimization_barrier((w0, w1, x_own, cot, norm_gain))
+        o_other = swap_section(o_own)
+
+        w_own = [send_shard(cuts[k], k) for k in range(SLOTS)]
+        w_other = [send_across(cuts[k], k) for k in range(SLOTS)]
+
+        def from_parts(parts, others, o, o_others, own):
+            pieces = [jnp.where(own, p, q) for p, q in zip(parts, others)]
+            lanes = []
+            for y in range(SLOTS):
+                v = pieces[0]
+                for k in range(1, SLOTS):
+                    v = jnp.where((j - y) % SLOTS == k, pieces[k], v)
+                lanes.append(v)
+            return jnp.concatenate(
+                [jnp.where(own, o, o_others), jnp.concatenate(lanes, axis=1)], axis=0
+            )
+
+        w0 = from_parts(w_own, w_other, o_own, o_other, first)
+        w1 = from_parts(w_own, w_other, o_own, o_other, ~first)
+        w0, w1, x_own, cot = lax.optimization_barrier((w0, w1, x_own, cot))
         w0 = lax.all_gather(w0, "dp", axis=0, tiled=False)
+        x_slots = gather_slots(x_own)
+        x_slots, norm_gain = lax.optimization_barrier((x_slots, norm_gain))
 
     with jax.named_scope("small_weights"):
         dt_columns = columns[2 * inner + n_state :]
@@ -818,7 +846,6 @@
 
     x_f = x_own.astype(F32)
     g1 = (mask * cot.astype(F32)).astype(BF16)
-    x_slots = gather_slots(x_own)
     g1_slots = gather_slots(g1)
     w0, x_slots, g1_slots, gain0, params0, gain1, params1, w1 = lax.optimization_barrier(
         (w0, x_slots, g1_slots, gain0, params0, gain1, params1, w1)
@@ -864,16 +891,15 @@
         layer1,
         {"g": g1_slots, "rows": rows1},
     )
-    dx, gain_grad1 = norm_back(
-        middle.astype(F32), gain1, scatter_sum([back1[f"out{k}"] for k in range(SLOTS)])
-    )
+    moved = [send_shard(back1[f"out{k}"], k) for k in range(SLOTS)]
     grads1 = backward(
         ("wgate", "wscan"), "weight_grads_1", 8, saved1, layer1, {"g": g1_slots, **back1}
     )
     back1.update(grads1)
+    moved, back1["ga"] = lax.optimization_barrier((moved, back1["ga"]))
+    dx, gain_grad1 = norm_back(middle.astype(F32), gain1, sum(p.astype(F32) for p in moved))
     by_owner = lambda v: v.reshape(16, -1, width)
     owned1 = lax.psum_scatter(by_owner(back1["ga"]), "dp", scatter_dimension=0, tiled=False)
-    owned1 = owned1 + lax.ppermute(owned1, "section", [(0, 1)])
 
     dmiddle = (cot.astype(F32) + dx).astype(BF16)
     g0 = (mask * dmiddle.astype(F32)).astype(BF16)
@@ -899,14 +925,34 @@
     small_gate = back0["small"]
     back0["core"] = own_core
     back0.update(backward(("scan", "wscan"), "backward_0_scan", 20, saved0, layer0, back0))
-    b0 = by_distance([back0["gb_keep"], cross_core(back0["gb_send"])])
-    b0, back0["dv"] = lax.optimization_barrier((b0, back0["dv"]))
+    a0[1], a0[3], gb_send = lax.optimization_barrier((a0[1], a0[3], back0["gb_send"]))
+    a0, b_moved, owned1 = lax.optimization_barrier((a0, cross_core(gb_send), owned1))
+    b0 = by_distance([back0["gb_keep"], b_moved])
+    b0, back0["dv"], a0 = lax.optimization_barrier((b0, back0["dv"], a0))
     b0 = cross_z(b0)
+    a0 = cross_x(a0, 0)
     small_scan = back0["small"]
     back0.update(backward(("input",), "backward_0_input", 9, saved0, layer0, back0))
-    dx, gain_grad0 = norm_back(
-        x_f, gain0, scatter_sum([back0[f"out{k}"] for k in range(SLOTS)])
-    )
+    outs0 = [back0[f"out{k}"] for k in range(SLOTS)]
+    a0, outs0 = lax.optimization_barrier((a0, outs0))
+    moved0 = [send_shard(outs0[k], k) for k in range(SLOTS)]
+
+    owned1 = (owned1 + lax.ppermute(owned1, "section", [(0, 1)])).reshape(10, 16, width)
+
+    def to_rows(parts, kept):
+        slots = []
+        for k in range(SLOTS):
+            cut = lambda v: lax.dynamic_slice_in_dim(v, quarter * ((j + k) % SLOTS), quarter, 2)
+            mine = jnp.where(first, sum_parts([cut(p) for p in parts]), cut(kept))
+            slots.append(send_shard(mine.reshape(-1, quarter), k))
+        return slots
+
+    gate_rows = to_rows([p[:3] for p in a0], owned1[:3])
+    out_rows = jnp.where(first, sum_parts([p[3:] for p in a0]), owned1[3:6])
+    out_rows = jnp.transpose(out_rows.reshape(piece, SLOTS, quarter), (1, 0, 2))
+    gate_rows, out_rows, b0, moved0 = lax.optimization_barrier((gate_rows, out_rows, b0, moved0))
+    value_rows = to_rows(cross_x(b0, 0), owned1[6:])
+    dx, gain_grad0 = norm_back(x_f, gain0, sum(p.astype(F32) for p in moved0))
     dtokens = dmiddle.astype(F32) + dx
 
     result_moved = lax.ppermute(result.astype(BF16), "section", [(0, 1)]).astype(F32)
@@ -919,24 +965,13 @@
         kept = jnp.where(first, v0, v1).astype(F32)
         return kept + swap_section(jnp.where(first, v1, v0)).astype(F32)
 
-    def to_rows(v):
-        v = v.reshape(-1, SLOTS, quarter)
-        return in_order([send_shard(pick(v, (j + k) % SLOTS, 1), k) for k in range(SLOTS)], -1)
-
-    owned0 = jnp.concatenate([sum_x(a0, 0), sum_x(b0, 0)], axis=0).reshape(-1, width)
-    owned = jnp.where(first, owned0, owned1)
-    by_rows = to_rows(jnp.concatenate([owned[:piece], owned[2 * piece :]], axis=0))
-    shared = jnp.sum(by_rows[:, 2 * piece :].astype(F32), axis=0).astype(BF16)
-    out_rows = jnp.transpose(owned[piece : 2 * piece].reshape(piece, SLOTS, quarter), (1, 0, 2))
-    flat_quarters = lambda v: v.reshape(-1, quarter)
+    shared = sum(v[piece:].astype(F32) for v in value_rows).astype(BF16)
     gathered = lax.all_gather(
         jnp.concatenate(
-            [
-                flat_quarters(by_rows[:, :piece]),
-                flat_quarters(out_rows),
-                flat_quarters(by_rows[:, piece : 2 * piece]),
-                shared,
-            ],
+            gate_rows
+            + [out_rows.reshape(-1, quarter)]
+            + [v[:piece] for v in value_rows]
+            + [shared],
             axis=0,
         ),
         "dp",
@@ -975,7 +1010,7 @@
     conv_own = lax.dynamic_slice(conv_total, (0, channels * j), (5, channels))
     grad_skip = jnp.sum(by_pair[6].reshape(heads, HEAD), axis=1)
 
-    grad_in_weight, grad_out_weight = assemble(gathered, dt_rows)
+    grad_in_weight, grad_out_weight = assemble(gathered, dt_rows, j)
     return (
         ends,
         lax.dynamic_slice(gain_total, (quarter * j,), (quarter,))[None],

time: 512 us -> 518 us (1.012)
  waiting for transfers between devices: 214 us -> 188 us
  starting transfers between devices: 94.2 us -> 120 us
    ppermute x3, waiting for transfers between devices: 36.7 us -> 25.8 us  [swap_section(): return lax.ppermute(v, 'section', [(0, 1), (1, 0)])]
    ppermute x3, starting transfers between devices: 1.26 us -> 11.5 us  [swap_section(): return lax.ppermute(v, 'section', [(0, 1), (1, 0)])]
    ppermute x7 -> x11, starting transfers between devices: 15.6 us -> 25.5 us  [the longest x6 16.8 us: cross_x(): lax.ppermute(same if k == 2 else other, ('section', 'dp'), section_pairs(...]
    ppermute x45 -> x48, starting transfers between devices: 58.8 us -> 67.2 us  [send_shard(): return lax.ppermute(v, 'shard', ring(SLOTS, k)) if k else v]
    all_gather x1, waiting for transfers between devices: 11.2 us -> 2.87 us  [shards(): w0 = lax.all_gather(w0, 'dp', axis=0, tiled=False)]
    ppermute x45 -> x48, waiting for transfers between devices: 107 us -> 101 us  [send_shard(): return lax.ppermute(v, 'shard', ring(SLOTS, k)) if k else v]
    unnamed x138 -> x165, local copies, waits for them, and re-layouts: 4.69 us -> 10 us
    ppermute x7 -> x11, waiting for transfers between devices: 13.3 us -> 9.87 us  [the longest x4 6.79 us: send_across(): return lax.ppermute(v, ('section', 'shard'), pairs)]
  transfers between devices with their start and end apart: 74 -> 81, of which waited for: 40 -> 43; matrix products, arithmetic and copies ran while one was open for 10% -> 9% of each run, Pallas kernels for 11% -> 13%
where the time goes in v4:
time: 518 us; the launch traced here: 508 us
  waiting for transfers between devices  188 us (36%)
  starting transfers between devices  120 us (23%)
  Pallas kernels  117 us (23%)
  other arithmetic  37.4 us (7%)
  local copies, waits for them, and re-layouts  29.4 us (6%)
  between operations  15.7 us (3%)
    pallas_call x7, Pallas kernels, kernel_call(): pl.pallas_call(run, grid=(STEPS,), in_specs=[pl.BlockSpec(*ins[n][1:]) if...  107 us
    ppermute x48, waiting for transfers between devices, send_shard(): return lax.ppermute(v, 'shard', ring(SLOTS, k)) if k else v  101 us
    ppermute x48, starting transfers between devices, send_shard(): return lax.ppermute(v, 'shard', ring(SLOTS, k)) if k else v  67.2 us
    ppermute x6, waiting for transfers between devices, cross_z(): lax.ppermute(slots[k], 'dp', dp_pairs(lambda x, z, c: (x, (z + k) % 4, c)))  32.4 us
    ppermute x3, waiting for transfers between devices, swap_section(): return lax.ppermute(v, 'section', [(0, 1), (1, 0)])  25.8 us
    ppermute x6, starting transfers between devices, cross_x(): lax.ppermute(same if k == 2 else other, ('section', 'dp'), section_pairs(...  16.8 us
    ppermute x3, starting transfers between devices, swap_section(): return lax.ppermute(v, 'section', [(0, 1), (1, 0)])  11.5 us
    convert_element_type x4, other arithmetic, sum_parts(): return sum((p.astype(F32) for p in parts)).astype(BF16)  10.5 us
  transfers between devices with their start and end apart: 81, of which 43 were waited for; matrix products, arithmetic and copies ran while one was open for 9% of the time, Pallas kernels for 13%

profile of v4, /device:TPU:4, one launch (start us, length us, event | category | flops | bytes accessed | tf_op | source)
XLA Modules:
  0.0 508.3 jit_solution(2428643173452380833)
XLA Ops:
  41.8 6.2 %collective-permute-done.8.refs_1_ = bf16[128,1536]{1,0:T(8,128)(2,1)S(1)} collective-permute-done((bf16[128,1536]{1,0:T(8,128)(2,1)S(1)}, bf16[128,1536]{1,0:T(8,128)(2,1)S(1)}, u32[]{:S(2)}, u32[]{:S(2)}) %collective-permute-start.8) | collective-permute-done | bytes 393248 | tf_op jit(solution)/shard_map/weights/ppermute | solution.py:618
  70.7 5.2 %collective-permute-done.17 = bf16[4,187,128]{2,1,0:T(8,128)(2,1)S(1)} collective-permute-done((bf16[4,187,128]{2,1,0:T(8,128)(2,1)S(1)}, bf16[4,187,128]{2,1,0:T(8,128)(2,1)S(1)}, u32[]{:S(2)}, u32[]{:S(2)}) %collective-permute-start.17) | collective-permute-done | bytes 191520 | tf_op jit(solution)/shard_map/small_weights/ppermute | solution.py:631
  91.7 17.3 %layer_forward.2 = (bf16[128,1536]{1,0:T(8,128)(2,1)}, bf16[128,1536]{1,0:T(8,128)(2,1)}, bf16[128,1536]{1,0:T(8,128)(2,1)}, bf16[128,1536]{1,0:T(8,128)(2,1)}, ...) custom-call(bf16[128,1536]{1,0:T(8,128)(2,1)} %copy-done, ...), custom_call_target="tpu_custom_call" | custom-call | flops 19800000512 | bytes 1048576 | tf_op jit(solution)/shard_map/layer_forward/pallas_call | solution.py:128
  118.1 11.3 %collective-permute-done.23 = f32[1,128]{1,0:T(1,128)S(1)} collective-permute-done((f32[1,128]{1,0:T(1,128)S(1)}, f32[1,128]{1,0:T(1,128)S(1)}, u32[]{:S(2)}, u32[]{:S(2)}) %collective-permute-start.23) | collective-permute-done | bytes 544 | tf_op jit(solution)/shard_map/ppermute | solution.py:618
  140.6 14.5 %collective-permute-done.24.refs_1_ = bf16[128,1536]{1,0:T(8,128)(2,1)S(1)} collective-permute-done((bf16[128,1536]{1,0:T(8,128)(2,1)S(1)}, bf16[128,1536]{1,0:T(8,128)(2,1)S(1)}, u32[]{:S(2)}, u32[]{:S(2)}) %collective-permute-start.24) | collective-permute-done | bytes 393248 | tf_op jit(solution)/shard_map/ppermute | solution.py:618
  159.6 18.4 %layer_forward.3 = (bf16[128,1536]{1,0:T(8,128)(2,1)}, bf16[128,1536]{1,0:T(8,128)(2,1)}, bf16[128,1536]{1,0:T(8,128)(2,1)}, bf16[128,1536]{1,0:T(8,128)(2,1)}, ...) custom-call(bf16[128,1536]{1,0:T(8,128)(2,1)} %copy-done.2, ...), custom_call_target="tpu_custom_call" | custom-call | flops 19800000512 | bytes 1048576 | tf_op jit(solution)/shard_map/layer_forward/pallas_call | solution.py:128
  185.0 23.0 %backward_1.1 = (bf16[512,768]{1,0:T(8,128)(2,1)}, bf16[512,768]{1,0:T(8,128)(2,1)}, f32[6,8,128]{2,1,0:T(8,128)}, bf16[512,768]{1,0:T(8,128)(2,1)}, bf16[512,38...) custom-call(bf16[128,1536]{1,0:T(8,128)(2,1)} %copy-done.25, ...), custom_call_target="tpu_custom_call" | custom-call | flops 30799998976 | bytes 1048576 | tf_op jit(solution)/shard_map/backward_1/pallas_call | solution.py:128
  213.0 9.5 %weight_grads_1.1 = (bf16[16,10,16,1536]{3,2,1,0:T(8,128)(2,1)}, f32[16,1536]{1,0:T(8,128)}) custom-call(bf16[128,1536]{1,0:T(8,128)(2,1)} %copy-done.25, bf16[128,1536]{1,0:T(8,128)(2,1)} %copy-done.60, bf16[128,1536]{1,0:T(8,128)(2,1)} %copy-done.61, bf16[128,1536]{1,0:T(8,128)(2,1)} %copy-done.62, bf16[512,1536]{1,0:T(8,128)(2,1)} %get-tuple-element.188.refs_4_, ...), custom_call_target="tpu_custom_call" | custom-call | flops 8800000000 | bytes 1048576 | tf_op jit(solution)/shard_map/weight_grads_1/pallas_call | solution.py:128
  222.5 6.3 %collective-permute-done.31 = bf16[128,1536]{1,0:T(8,128)(2,1)S(1)} collective-permute-done((bf16[128,1536]{1,0:T(8,128)(2,1)}, bf16[128,1536]{1,0:T(8,128)(2,1)S(1)}, u32[]{:S(2)}, u32[]{:S(2)}) %collective-permute-start.31) | collective-permute-done | bytes 393248 | tf_op jit(solution)/shard_map/ppermute | solution.py:618
  240.6 15.6 %collective-permute-done.38 = f32[8,128]{1,0:T(8,128)S(1)} collective-permute-done((f32[8,128]{1,0:T(8,128)S(1)}, f32[8,128]{1,0:T(8,128)S(1)}, u32[]{:S(2)}, u32[]{:S(2)}) %collective-permute-start.38) | collective-permute-done | bytes 4128 | tf_op jit(solution)/shard_map/ppermute | solution.py:618
  261.5 13.7 %backward_0_gate.1 = (bf16[512,768]{1,0:T(8,128)(2,1)}, bf16[512,768]{1,0:T(8,128)(2,1)}, f32[512,768]{1,0:T(8,128)}, f32[6,8,128]{2,1,0:T(8,128)}, bf16[2,4,6,1...) custom-call(bf16[128,1536]{1,0:T(8,128)(2,1)} %get-tuple-element.205.refs_0_, ...), custom_call_target="tpu_custom_call" | custom-call | flops 15399999488 | bytes 1048576 | tf_op jit(solution)/shard_map/backward_0_gate/pallas_call | solution.py:128
  275.4 4.6 collective-permute-done.39
  290.4 16.8 %backward_0_scan.1 = (f32[6,8,128]{2,1,0:T(8,128)}, bf16[512,768]{1,0:T(8,128)(2,1)}, bf16[512,384]{1,0:T(8,128)(2,1)}, f32[2,8,128]{2,1,0:T(8,128)}, f32[8,128]...) custom-call(f32[2,512,768]{2,1,0:T(8,128)} %get-tuple-element.198.refs, ...), custom_call_target="tpu_custom_call" | custom-call | flops 22000001024 | bytes 1048576 | tf_op jit(solution)/shard_map/backward_0_scan/pallas_call | solution.py:128
  312.9 17.6 %collective-permute-done.42 = bf16[2,6,16,1536]{3,2,1,0:T(8,128)(2,1)} collective-permute-done((bf16[2,6,16,1536]{3,2,1,0:T(8,128)(2,1)}, bf16[2,6,16,1536]{3,2,1,0:T(8,128)(2,1)}, u32[]{:S(2)}, u32[]{:S(2)}) %collective-permute-start.42) | collective-permute-done | bytes 589856 | tf_op jit(solution)/shard_map/ppermute | solution.py:692
  342.4 6.1 %collective-permute-start.45 = (bf16[6,16,1536]{2,1,0:T(8,128)(2,1)S(1)}, bf16[6,16,1536]{2,1,0:T(8,128)(2,1)S(1)}, u32[]{:S(2)}, u32[]{:S(2)}) collective-permute-start(bf16[6,16,1536]{2,1,0:T(8,128)(2,1)S(1)} %get-tuple-element.241), channel_id=1, source_target_pairs={{64,0},{68,4},{72,8},{76,12},{80,16},{84,20},{88,24},{92,28},{96,3... | collective-permute-start | bytes 884744 | tf_op jit(solution)/shard_map/ppermute | solution.py:702
  348.8 8.3 %backward_0_input.1 = (bf16[128,1536]{1,0:T(8,128)(2,1)}, bf16[128,1536]{1,0:T(8,128)(2,1)}, bf16[128,1536]{1,0:T(8,128)(2,1)}, bf16[128,1536]{1,0:T(8,128)(2,1)}) custom-call(bf16[16,10,16,1536]{3,2,1,0:T(8,128)(2,1)} %bitcast.314, bf16[16,10,16,1536]{3,2,1,0:T(8,128)(2,1)} %bitcast.315, bf16[16,10,16,1536]{3,2,1,0:T(8,128)(2,1)} %bitcast.316, ...), custom_call_target="tpu_custom_call" | custom-call | flops 9900000256 | bytes 1048576 | tf_op jit(solution)/shard_map/backward_0_input/pallas_call | solution.py:128
  369.1 8.4 %collective-permute-done.53 = bf16[2,4,16,1536]{3,2,1,0:T(8,128)(2,1)S(1)} collective-permute-done((bf16[2,4,16,1536]{3,2,1,0:T(8,128)(2,1)}, bf16[2,4,16,1536]{3,2,1,0:T(8,128)(2,1)S(1)}, u32[]{:S(2)}, u32[]{:S(2)}) %collective-permute-start.53) | collective-permute-done | bytes 393248 | tf_op jit(solution)/shard_map/ppermute | solution.py:692
  388.5 5.6 %collective-permute-start.72 = (bf16[4,16,1536]{2,1,0:T(8,128)(2,1)S(1)}, bf16[4,16,1536]{2,1,0:T(8,128)(2,1)S(1)}, u32[]{:S(2)}, u32[]{:S(2)}) collective-permute-start(bf16[4,16,1536]{2,1,0:T(8,128)(2,1)S(1)} %bitcast.243), channel_id=1, source_target_pairs={{64,0},{68,4},{72,8},{76,12},{80,16},{84,20},{88,24},{92,28},{96,3... | collective-permute-start | bytes 589832 | tf_op jit(solution)/shard_map/ppermute | solution.py:702
  397.8 4.7 collective-permute-start.75
  412.1 5.2 %collective-permute-done.60 = bf16[128,1536]{1,0:T(8,128)(2,1)S(1)} collective-permute-done((bf16[128,1536]{1,0:T(8,128)(2,1)}, bf16[128,1536]{1,0:T(8,128)(2,1)S(1)}, u32[]{:S(2)}, u32[]{:S(2)}) %collective-permute-start.60) | collective-permute-done | bytes 393248 | tf_op jit(solution)/shard_map/ppermute | solution.py:618
  430.0 4.9 collective-permute-start.62
  434.9 19.3 %collective-permute-done.62 = f32[276,128]{1,0:T(8,128)S(1)} collective-permute-done((f32[276,128]{1,0:T(8,128)S(1)}, f32[276,128]{1,0:T(8,128)S(1)}, u32[]{:S(2)}, u32[]{:S(2)}) %collective-permute-start.62) | collective-permute-done | bytes 141344 | tf_op jit(solution)/shard_map/ppermute | solution.py:631
  464.0 6.4 %collective-permute-done.64 = f32[276,128]{1,0:T(8,128)S(1)} collective-permute-done((f32[276,128]{1,0:T(8,128)S(1)}, f32[276,128]{1,0:T(8,128)S(1)}, u32[]{:S(2)}, u32[]{:S(2)}) %collective-permute-start.64) | collective-permute-done | bytes 141344 | tf_op jit(solution)/shard_map/ppermute | solution.py:710
  491.6 10.1 %assemble.1 = (f32[6448,384]{1,0:T(8,128)}, f32[768,1536]{1,0:T(8,128)}) custom-call(s32[1]{0:T(128)} %bitcast.96._, bf16[16,592,384]{2,1,0:T(8,128)(2,1)} %bitcast.238, bf16[16,592,384]{2,1,0:T(8,128)(2,1)} %bitcast.239, bf16[16,592,384]{2,1,0:T(8,128)(2,1)} %bitcast.240, f32[48,384]{1,0:T(8,128)} %reshape.536.dt), custom_call_target="tpu_custom_call" | custom-call | tf_op jit(solution)/shard_map/assemble/pallas_call | solution.py:601
  (480 shorter events, 233.5 us)
Async XLA Ops:
  7.2 84.2 %all-gather.7.cloned.1.call-start = ((), (), s32[]{:S(2)}) async-start(), calls=%async_computation.2 | async-start | bytes 8355840 | tf_op jit(solution)/shard_map/weights/all_gather | solution.py:795
  36.5 122.3 %all-gather.9.cloned.1.call-start = ((), (), s32[]{:S(2)}) async-start(), calls=%async_computation.3 | async-start | bytes 8355840 | tf_op jit(solution)/shard_map/all_gather | solution.py:853
  66.9 18.5 %collective-permute-start.11 = (bf16[128,1536]{1,0:T(8,128)(2,1)S(1)}, bf16[128,1536]{1,0:T(8,128)(2,1)S(1)}, u32[]{:S(2)}, u32[]{:S(2)}) collective-permute-start(bf16[128,1536]{1,0:T(8,128)(2,1)S(1)} %fusion.6.refs_4_.refs_0_), channel_id=1, source_target_pairs={{0,3},{1,0},{2,1},{3,2},{4,7},{5,4},{6,5},{7,6},{8,11},{9,8},{10,9... | collective-permute-start | bytes 1179656 | tf_op jit(solution)/shard_map/ppermute | solution.py:618
  91.4 239.0 %reduce-scatter.2.cloned.1.call-start = ((), (), s32[]{:S(2)}) async-start(), calls=%async_computation.1 | async-start | bytes 8355840 | tf_op jit(solution)/shard_map/reduce_scatter | solution.py:902
  109.0 26.2 %collective-permute-start.20 = (bf16[128,1536]{1,0:T(8,128)(2,1)}, bf16[128,1536]{1,0:T(8,128)(2,1)S(1)}, u32[]{:S(2)}, u32[]{:S(2)}) collective-permute-start(bf16[128,1536]{1,0:T(8,128)(2,1)} %get-tuple-element.168), channel_id=1, source_target_pairs={{0,3},{1,0},{2,1},{3,2},{4,7},{5,4},{6,5},{7,6},{8,11},{9,8},{10,9... | collective-permute-start | bytes 1179656 | tf_op jit(solution)/shard_map/ppermute | solution.py:618
  111.9 23.4 %collective-permute-start.19 = (bf16[128,1536]{1,0:T(8,128)(2,1)}, bf16[128,1536]{1,0:T(8,128)(2,1)S(1)}, u32[]{:S(2)}, u32[]{:S(2)}) collective-permute-start(bf16[128,1536]{1,0:T(8,128)(2,1)} %get-tuple-element.167), channel_id=1, source_target_pairs={{0,2},{1,3},{2,0},{3,1},{4,6},{5,7},{6,4},{7,5},{8,10},{9,11},{10,... | collective-permute-start | bytes 1179656 | tf_op jit(solution)/shard_map/ppermute | solution.py:618
  112.7 22.6 %collective-permute-start.18 = (bf16[128,1536]{1,0:T(8,128)(2,1)}, bf16[128,1536]{1,0:T(8,128)(2,1)S(1)}, u32[]{:S(2)}, u32[]{:S(2)}) collective-permute-start(bf16[128,1536]{1,0:T(8,128)(2,1)} %get-tuple-element.166), channel_id=1, source_target_pairs={{0,1},{1,2},{2,3},{3,0},{4,5},{5,6},{6,7},{7,4},{8,9},{9,10},{10,1... | collective-permute-start | bytes 1179656 | tf_op jit(solution)/shard_map/ppermute | solution.py:618
  139.6 19.2 %collective-permute-start.26 = (bf16[128,1536]{1,0:T(8,128)(2,1)S(1)}, bf16[128,1536]{1,0:T(8,128)(2,1)S(1)}, u32[]{:S(2)}, u32[]{:S(2)}) collective-permute-start(bf16[128,1536]{1,0:T(8,128)(2,1)S(1)} %get-tuple-element.293.refs_0_), channel_id=1, source_target_pairs={{0,1},{1,2},{2,3},{3,0},{4,5},{5,6},{6,7},{7,4},{8,9},{9,10},{10,1... | collective-permute-start | bytes 1179656 | tf_op jit(solution)/shard_map/ppermute | solution.py:618
  210.0 18.7 %collective-permute-start.31 = (bf16[128,1536]{1,0:T(8,128)(2,1)}, bf16[128,1536]{1,0:T(8,128)(2,1)S(1)}, u32[]{:S(2)}, u32[]{:S(2)}) collective-permute-start(bf16[128,1536]{1,0:T(8,128)(2,1)} %get-tuple-element.186), channel_id=1, source_target_pairs={{0,2},{1,3},{2,0},{3,1},{4,6},{5,7},{6,4},{7,5},{8,10},{9,11},{10,... | collective-permute-start | bytes 1179656 | tf_op jit(solution)/shard_map/ppermute | solution.py:618
  228.8 262.8 %all-gather.11.cloned.1.call-start = ((), (), s32[]{:S(2)}) async-start(), calls=%async_computation.4 | async-start | bytes 7729152 | tf_op jit(solution)/shard_map/all_gather | solution.py:969
  233.1 27.4 %collective-permute-start.33 = (bf16[128,1536]{1,0:T(8,128)(2,1)}, bf16[128,1536]{1,0:T(8,128)(2,1)S(1)}, u32[]{:S(2)}, u32[]{:S(2)}) collective-permute-start(bf16[128,1536]{1,0:T(8,128)(2,1)} %get-tuple-element.205.refs_0_), channel_id=1, source_target_pairs={{0,3},{1,0},{2,1},{3,2},{4,7},{5,4},{6,5},{7,6},{8,11},{9,8},{10,9... | collective-permute-start | bytes 1179656 | tf_op jit(solution)/shard_map/ppermute | solution.py:618
  235.2 25.3 %collective-permute-start.34 = (bf16[128,1536]{1,0:T(8,128)(2,1)}, bf16[128,1536]{1,0:T(8,128)(2,1)S(1)}, u32[]{:S(2)}, u32[]{:S(2)}) collective-permute-start(bf16[128,1536]{1,0:T(8,128)(2,1)} %get-tuple-element.205.refs_0_), channel_id=1, source_target_pairs={{0,2},{1,3},{2,0},{3,1},{4,6},{5,7},{6,4},{7,5},{8,10},{9,11},{10,... | collective-permute-start | bytes 1179656 | tf_op jit(solution)/shard_map/ppermute | solution.py:618
  235.8 24.6 %collective-permute-start.35 = (bf16[128,1536]{1,0:T(8,128)(2,1)}, bf16[128,1536]{1,0:T(8,128)(2,1)S(1)}, u32[]{:S(2)}, u32[]{:S(2)}) collective-permute-start(bf16[128,1536]{1,0:T(8,128)(2,1)} %get-tuple-element.205.refs_0_), channel_id=1, source_target_pairs={{0,1},{1,2},{2,3},{3,0},{4,5},{5,6},{6,7},{7,4},{8,9},{9,10},{10,1... | collective-permute-start | bytes 1179656 | tf_op jit(solution)/shard_map/ppermute | solution.py:618
  236.1 20.1 %collective-permute-start.38 = (f32[8,128]{1,0:T(8,128)S(1)}, f32[8,128]{1,0:T(8,128)S(1)}, u32[]{:S(2)}, u32[]{:S(2)}) collective-permute-start(f32[8,128]{1,0:T(8,128)S(1)} %get-tuple-element.379), channel_id=1, source_target_pairs={{0,1},{1,2},{2,3},{3,0},{4,5},{5,6},{6,7},{7,4},{8,9},{9,10},{10,1... | collective-permute-start | bytes 12296 | tf_op jit(solution)/shard_map/ppermute | solution.py:618
  287.0 24.3 %collective-permute-start.40 = (bf16[2,6,16,1536]{3,2,1,0:T(8,128)(2,1)S(1)}, bf16[2,6,16,1536]{3,2,1,0:T(8,128)(2,1)S(1)}, u32[]{:S(2)}, u32[]{:S(2)}) collective-permute-start(bf16[2,6,16,1536]{3,2,1,0:T(8,128)(2,1)S(1)} %get-tuple-element.216), channel_id=1, source_target_pairs={{0,8},{4,12},{8,16},{12,20},{16,24},{20,28},{24,0},{28,4},{32,40},... | collective-permute-start | bytes 1769480 | tf_op jit(solution)/shard_map/ppermute | solution.py:692
  287.0 24.3 %collective-permute-start.41 = (bf16[2,6,16,1536]{3,2,1,0:T(8,128)(2,1)}, bf16[2,6,16,1536]{3,2,1,0:T(8,128)(2,1)S(1)}, u32[]{:S(2)}, u32[]{:S(2)}) collective-permute-start(bf16[2,6,16,1536]{3,2,1,0:T(8,128)(2,1)} %fusion.23), channel_id=1, source_target_pairs={{0,24},{4,28},{8,0},{12,4},{16,8},{20,12},{24,16},{28,20},{32,56},... | collective-permute-start | bytes 1769480 | tf_op jit(solution)/shard_map/ppermute | solution.py:692
  338.0 19.1 %collective-permute-start.44 = (bf16[6,16,1536]{2,1,0:T(8,128)(2,1)S(1)}, bf16[6,16,1536]{2,1,0:T(8,128)(2,1)S(1)}, u32[]{:S(2)}, u32[]{:S(2)}) collective-permute-start(bf16[6,16,1536]{2,1,0:T(8,128)(2,1)S(1)} %get-tuple-element.318), channel_id=1, source_target_pairs={{0,32},{4,36},{8,40},{12,44},{16,48},{20,52},{24,56},{28,60},{96,0... | collective-permute-start | bytes 884744 | tf_op jit(solution)/shard_map/ppermute | solution.py:702
  338.7 21.8 %collective-permute-start.46 = (bf16[6,16,1536]{2,1,0:T(8,128)(2,1)S(1)}, bf16[6,16,1536]{2,1,0:T(8,128)(2,1)S(1)}, u32[]{:S(2)}, u32[]{:S(2)}) collective-permute-start(bf16[6,16,1536]{2,1,0:T(8,128)(2,1)S(1)} %get-tuple-element.318), channel_id=1, source_target_pairs={{32,0},{36,4},{40,8},{44,12},{48,16},{52,20},{56,24},{60,28},{64,3... | collective-permute-start | bytes 884744 | tf_op jit(solution)/shard_map/ppermute | solution.py:702
  341.1 20.5 %collective-permute-start.47 = (bf16[160,1536]{1,0:T(8,128)(2,1)S(1)}, bf16[160,1536]{1,0:T(8,128)(2,1)S(1)}, u32[]{:S(2)}, u32[]{:S(2)}) collective-permute-start(bf16[160,1536]{1,0:T(8,128)(2,1)S(1)} %bitcast.253), channel_id=1, source_target_pairs={{0,64},{1,65},{2,66},{3,67},{4,68},{5,69},{6,70},{7,71},{8,72},{9,... | collective-permute-start | bytes 1474568 | tf_op jit(solution)/shard_map/ppermute | solution.py:940
  361.1 23.2 %collective-permute-start.54 = (bf16[128,1536]{1,0:T(8,128)(2,1)}, bf16[128,1536]{1,0:T(8,128)(2,1)S(1)}, u32[]{:S(2)}, u32[]{:S(2)}) collective-permute-start(bf16[128,1536]{1,0:T(8,128)(2,1)} %get-tuple-element.251), channel_id=1, source_target_pairs={{0,1},{1,2},{2,3},{3,0},{4,5},{5,6},{6,7},{7,4},{8,9},{9,10},{10,1... | collective-permute-start | bytes 1179656 | tf_op jit(solution)/shard_map/ppermute | solution.py:618
  361.6 22.8 %collective-permute-start.55 = (bf16[128,1536]{1,0:T(8,128)(2,1)}, bf16[128,1536]{1,0:T(8,128)(2,1)S(1)}, u32[]{:S(2)}, u32[]{:S(2)}) collective-permute-start(bf16[128,1536]{1,0:T(8,128)(2,1)} %get-tuple-element.252), channel_id=1, source_target_pairs={{0,2},{1,3},{2,0},{3,1},{4,6},{5,7},{6,4},{7,5},{8,10},{9,11},{10,... | collective-permute-start | bytes 1179656 | tf_op jit(solution)/shard_map/ppermute | solution.py:618
  365.2 19.1 %collective-permute-start.56 = (bf16[128,1536]{1,0:T(8,128)(2,1)}, bf16[128,1536]{1,0:T(8,128)(2,1)}, u32[]{:S(2)}, u32[]{:S(2)}) collective-permute-start(bf16[128,1536]{1,0:T(8,128)(2,1)} %get-tuple-element.253), channel_id=1, source_target_pairs={{0,3},{1,0},{2,1},{3,2},{4,7},{5,4},{6,5},{7,6},{8,11},{9,8},{10,9... | collective-permute-start | bytes 1179656 | tf_op jit(solution)/shard_map/ppermute | solution.py:618
  425.6 36.4 %collective-permute-start.61 = (bf16[128,1536]{1,0:T(8,128)(2,1)}, bf16[128,1536]{1,0:T(8,128)(2,1)}, u32[]{:S(2)}, u32[]{:S(2)}) collective-permute-start(bf16[128,1536]{1,0:T(8,128)(2,1)} %get-tuple-element.320), channel_id=1, source_target_pairs={{0,64},{1,65},{2,66},{3,67},{4,68},{5,69},{6,70},{7,71},{8,72},{9,... | collective-permute-start | bytes 1179656 | tf_op jit(solution)/shard_map/ppermute | solution.py:958
  430.0 24.2 %collective-permute-start.62 = (f32[276,128]{1,0:T(8,128)S(1)}, f32[276,128]{1,0:T(8,128)S(1)}, u32[]{:S(2)}, u32[]{:S(2)}) collective-permute-start(f32[276,128]{1,0:T(8,128)S(1)} %broadcast_select_fusion.12), channel_id=1, source_target_pairs={{0,64},{64,0},{1,65},{65,1},{2,66},{66,2},{3,67},{67,3},{4,68},{68... | collective-permute-start | bytes 423944 | tf_op jit(solution)/shard_map/ppermute | solution.py:631
  (131 other events, 1583.3 us)
Sparse Core Ops, SparseCore 0:
  36.6 54.7 all-gather.6
  93.7 50.8 all-gather.8
  228.9 74.0 reduce-scatter.1
  408.1 49.0 all-gather.10

commit v5 on v4

--- a/solution.py
+++ b/solution.py
@@ -19,6 +19,7 @@
 HALF = PAIRS // STEPS
 WIDE = HALF * LANES
 VMEM_LIMIT = 60 * 1024 * 1024
+DP = ("x", "z", "core")
 
 
 def sigmoid(v):
@@ -110,6 +111,21 @@
     left = iota(1) < HEAD
     zero = jnp.zeros_like(v)
     return jnp.concatenate([jnp.where(left, v, zero), jnp.where(left, zero, v)], axis=0)
+
+
+def in_lanes(columns):
+    lane = lax.broadcasted_iota(jnp.int32, (columns[0].shape[0], LANES), 1)
+    out = jnp.zeros(lane.shape, F32)
+    for n, v in enumerate(columns):
+        for k in range(3):
+            part = v.astype(BF16).astype(F32)
+            out = jnp.where(lane == 3 * n + k, part, out)
+            v = v - part
+    return out.astype(BF16)
+
+
+def from_lanes(v, n):
+    return sum(v[:, 3 * n + k : 3 * n + k + 1].astype(F32) for k in range(3))
 
 
 class Refs:
@@ -253,6 +269,9 @@
                 part = dot(u, rf.wout[:, :, :, n : n + 512].reshape(STEPS * WIDE, 512)).astype(BF16)
                 for k in range(SLOTS):
                     getattr(rf, f"out{k}")[:, n : n + 512] = part[slot(k), :]
+            for k in range(SLOTS):
+                total = jnp.sum(rf.square[slot(k), :], axis=1, keepdims=True)
+                getattr(rf, f"out{k}")[:, width:] = in_lanes([total])
             ones = jnp.ones((8, LANES), F32)
             rf.stats[0] = dot_nt(ones, rf.square[...], HI)
             rf.stats[1] = dot_nt(ones, rf.cross[...], HI)
@@ -269,7 +288,7 @@
         pbcv=whole(pbcv),
         dtp=whole(dtp),
     )
-    outs = {f"out{k}": whole_out((T, width), BF16) for k in range(SLOTS)}
+    outs = {f"out{k}": whole_out((T, width + LANES), BF16) for k in range(SLOTS)}
     outs.update(
         stats=whole_out((2, 8, ROWS), F32),
         normed=whole_out((ROWS, width), BF16),
@@ -332,9 +351,13 @@
                     rf.g_all[slot(k), :] = getattr(rf, f"g{k}")[...]
                 if gate:
                     for row, ref in ((0, rf.scale_row), (1, rf.cross_row)):
-                        ref[slot(k), :] = jnp.transpose(
-                            jnp.broadcast_to(rf.rows[k, row : row + 1, :], (T, LANES))
-                        )
+                        if "rows" in have:
+                            ref[slot(k), :] = jnp.transpose(
+                                jnp.broadcast_to(rf.rows[k, row : row + 1, :], (T, LANES))
+                            )
+                        else:
+                            column = from_lanes(getattr(rf, f"e{k}")[...], row)
+                            ref[slot(k), :] = jnp.broadcast_to(column, (T, LANES))
                 if scan:
                     inbound, outbound = mixed_bc(rf, k, 0), mixed_bc(rf, k, 1)
                     rf.mixed[0, slot(k), :] = inbound
@@ -494,10 +517,15 @@
     ins, outs, scratch = {}, {}, {}
     heads_cols = STEPS * WIDE
     if gate or wgate:
-        ins.update({f"g{k}": whole(v) for k, v in enumerate(have["g"])})
+        for k, v in enumerate(have["g"]):
+            ins[f"g{k}"] = (v, (T, width), lambda h: (0, 0))
         scratch["g_all"] = ((ROWS, width), BF16)
     if gate:
-        ins["rows"] = whole(have["rows"])
+        if "rows" in have:
+            ins["rows"] = whole(have["rows"])
+        else:
+            for k, v in enumerate(have["g"]):
+                ins[f"e{k}"] = (v, (T, LANES), lambda h: (0, width // LANES))
         ins["wout"] = (w, (8, 3, 16, width), lambda h: (h, 0, 0, 0))
         scratch["scale_row"] = ((ROWS, LANES), F32)
         scratch["cross_row"] = ((ROWS, LANES), F32)
@@ -657,59 +685,16 @@
     return sum(p.astype(F32) for p in parts)
 
 
-def section_pairs(k, layer):
-    pairs = []
-    for chip in range(4):
-        to = (chip + k) % 4
-        if to // 2 != layer:
-            continue
-        for z in range(4):
-            for c in range(2):
-                pairs.append(
-                    (
-                        (chip // 2) * 16 + dp_index(chip % 2, z, c),
-                        (to // 2) * 16 + dp_index(to % 2, z, c),
-                    )
-                )
-    return pairs
-
-
-def sum_parts(parts):
-    return sum(p.astype(F32) for p in parts).astype(BF16)
-
-
 def cross_core(v):
-    return lax.ppermute(v, "dp", dp_pairs(lambda x, z, c: (x, z, 1 - c)))
-
-
-def by_distance(parts):
-    z = lax.axis_index("dp") // 2 % 4
-    return [sum_parts([pick(p, (z + k) % 4, 1) for p in parts]) for k in range(4)]
-
-
-def cross_z(slots):
-    return [slots[0]] + [
-        lax.ppermute(slots[k], "dp", dp_pairs(lambda x, z, c: (x, (z + k) % 4, c)))
-        for k in range(1, 4)
-    ]
-
-
-def cross_x(parts, layer):
-    x = lax.axis_index("dp") // 8
-    same = sum_parts([pick(p, x, 0) for p in parts])
-    other = sum_parts([pick(p, 1 - x, 0) for p in parts])
-    return [same] + [
-        lax.ppermute(same if k == 2 else other, ("section", "dp"), section_pairs(k, layer))
-        for k in range(1, 4)
-    ]
+    return lax.ppermute(v, DP, dp_pairs(lambda x, z, c: (x, z, 1 - c)))
 
 
 def sum_small(v):
-    v = v + lax.ppermute(v, "dp", dp_pairs(lambda x, z, c: (x, z, 1 - c)))
+    v = v + lax.ppermute(v, DP, dp_pairs(lambda x, z, c: (x, z, 1 - c)))
     v = v + sum(
-        lax.ppermute(v, "dp", dp_pairs(lambda x, z, c: (x, (z + k) % 4, c))) for k in range(1, 4)
-    )
-    return v + lax.ppermute(v, "dp", dp_pairs(lambda x, z, c: (1 - x, z, c)))
+        lax.ppermute(v, DP, dp_pairs(lambda x, z, c: (x, (z + k) % 4, c))) for k in range(1, 4)
+    )
+    return v + lax.ppermute(v, DP, dp_pairs(lambda x, z, c: (1 - x, z, c)))
 
 
 def in_order(parts, sign):
@@ -733,7 +718,7 @@
     out_weight,
 ):
     sec = lax.axis_index("section")
-    d = lax.axis_index("dp")
+    d = lax.axis_index(DP)
     j = lax.axis_index("shard")
     core = d % 2
     first = sec == 0
@@ -792,7 +777,7 @@
         w0 = from_parts(w_own, w_other, o_own, o_other, first)
         w1 = from_parts(w_own, w_other, o_own, o_other, ~first)
         w0, w1, x_own, cot = lax.optimization_barrier((w0, w1, x_own, cot))
-        w0 = lax.all_gather(w0, "dp", axis=0, tiled=False)
+        w0 = lax.all_gather(w0, DP, axis=0, tiled=False)
         x_slots = gather_slots(x_own)
         x_slots, norm_gain = lax.optimization_barrier((x_slots, norm_gain))
 
@@ -850,7 +835,7 @@
     w0, x_slots, g1_slots, gain0, params0, gain1, params1, w1 = lax.optimization_barrier(
         (w0, x_slots, g1_slots, gain0, params0, gain1, params1, w1)
     )
-    w1 = lax.all_gather(w1, "dp", axis=0, tiled=False)
+    w1 = lax.all_gather(w1, DP, axis=0, tiled=False)
     blocks = lambda v: v.reshape(16, 10, 16, width)
 
     layer0 = (blocks(w0), *params0)
@@ -862,9 +847,9 @@
 
     parts, saved0 = forward_layer(x_slots, None, gain0, layer0)
     branch = scatter_sum(parts)
-    square = scatter_sum([saved0["stats"][0, 0:1, slot(k)] for k in range(SLOTS)])[0]
+    square = jnp.sum(branch[:, width : width + 3], axis=1, keepdims=True)
     scale0 = lax.rsqrt(square / inner + EPS)
-    branch0 = branch * scale0[:, None]
+    branch0 = branch[:, :width] * scale0
     middle = (x_f + mask * branch0).astype(BF16)
 
     m_slots = gather_slots(middle)
@@ -899,16 +884,14 @@
     moved, back1["ga"] = lax.optimization_barrier((moved, back1["ga"]))
     dx, gain_grad1 = norm_back(middle.astype(F32), gain1, sum(p.astype(F32) for p in moved))
     by_owner = lambda v: v.reshape(16, -1, width)
-    owned1 = lax.psum_scatter(by_owner(back1["ga"]), "dp", scatter_dimension=0, tiled=False)
+    owned1 = lax.psum_scatter(by_owner(back1["ga"]), DP, scatter_dimension=0, tiled=False)
 
     dmiddle = (cot.astype(F32) + dx).astype(BF16)
     g0 = (mask * dmiddle.astype(F32)).astype(BF16)
-    cross0 = scale0 * scale0 * jnp.sum(g0.astype(F32) * branch0, axis=1) / inner
-    own = jnp.pad(jnp.stack([scale0, cross0]), ((0, 6), (0, 0)))
-    rows0 = jnp.stack(gather_slots(own))
-    g0_slots = gather_slots(g0)
+    cross0 = scale0 * scale0 * jnp.sum(g0.astype(F32) * branch0, axis=1, keepdims=True) / inner
+    g0_slots = gather_slots(jnp.concatenate([g0, in_lanes([scale0, cross0])], axis=1))
     g0_slots, branch_parts = lax.optimization_barrier((g0_slots, branch_parts))
-    branch = scatter_sum(branch_parts) * scale1[0][:, None]
+    branch = scatter_sum(branch_parts)[:, :width] * scale1[0][:, None]
     result = middle.astype(F32) + mask * branch
 
     back0 = backward(
@@ -917,44 +900,45 @@
         14,
         saved0,
         layer0,
-        {"g": g0_slots, "rows": rows0, "core": own_core},
-    )
-    a0 = by_distance([back0["ga_keep"], cross_core(back0["ga_send"])])
-    a0, back0["dscan"] = lax.optimization_barrier((a0, back0["dscan"]))
-    a0 = cross_z(a0)
+        {"g": g0_slots, "core": own_core},
+    )
+    both = lambda kept, moved: (kept.astype(F32) + moved.astype(F32)).astype(BF16)
+    a_moved = cross_core(back0["ga_send"])
     small_gate = back0["small"]
     back0["core"] = own_core
     back0.update(backward(("scan", "wscan"), "backward_0_scan", 20, saved0, layer0, back0))
-    a0[1], a0[3], gb_send = lax.optimization_barrier((a0[1], a0[3], back0["gb_send"]))
-    a0, b_moved, owned1 = lax.optimization_barrier((a0, cross_core(gb_send), owned1))
-    b0 = by_distance([back0["gb_keep"], b_moved])
-    b0, back0["dv"], a0 = lax.optimization_barrier((b0, back0["dv"], a0))
-    b0 = cross_z(b0)
-    a0 = cross_x(a0, 0)
+    gb_send, a_moved = lax.optimization_barrier((back0["gb_send"], a_moved))
+    a0 = both(back0["ga_keep"], a_moved)
+    b0 = both(back0["gb_keep"], cross_core(gb_send))
+    owned0 = jnp.pad(a0, ((0, 0), (0, 0), (0, 4), (0, 0), (0, 0)))
+    owned0 = lax.dynamic_update_slice(owned0, b0, (0, 0, 6, 0, 0)).reshape(8, -1, width)
+    owned0 = lax.psum_scatter(owned0, ("x", "z"), scatter_dimension=0, tiled=False)
     small_scan = back0["small"]
     back0.update(backward(("input",), "backward_0_input", 9, saved0, layer0, back0))
-    outs0 = [back0[f"out{k}"] for k in range(SLOTS)]
-    a0, outs0 = lax.optimization_barrier((a0, outs0))
-    moved0 = [send_shard(outs0[k], k) for k in range(SLOTS)]
-
-    owned1 = (owned1 + lax.ppermute(owned1, "section", [(0, 1)])).reshape(10, 16, width)
-
-    def to_rows(parts, kept):
-        slots = []
-        for k in range(SLOTS):
-            cut = lambda v: lax.dynamic_slice_in_dim(v, quarter * ((j + k) % SLOTS), quarter, 2)
-            mine = jnp.where(first, sum_parts([cut(p) for p in parts]), cut(kept))
-            slots.append(send_shard(mine.reshape(-1, quarter), k))
-        return slots
-
-    gate_rows = to_rows([p[:3] for p in a0], owned1[:3])
-    out_rows = jnp.where(first, sum_parts([p[3:] for p in a0]), owned1[3:6])
-    out_rows = jnp.transpose(out_rows.reshape(piece, SLOTS, quarter), (1, 0, 2))
-    gate_rows, out_rows, b0, moved0 = lax.optimization_barrier((gate_rows, out_rows, b0, moved0))
-    value_rows = to_rows(cross_x(b0, 0), owned1[6:])
+    moved0 = [send_shard(back0[f"out{k}"], k) for k in range(SLOTS)]
     dx, gain_grad0 = norm_back(x_f, gain0, sum(p.astype(F32) for p in moved0))
     dtokens = dmiddle.astype(F32) + dx
-
+    owned1 = owned1 + lax.ppermute(owned1, "section", [(0, 1)])
+    owned0, owned1, gain_grad0, dtokens, result = lax.optimization_barrier(
+        (owned0, owned1, gain_grad0, dtokens, result)
+    )
+
+    kept = jnp.where(first, owned0, owned1).reshape(10, 16, width)
+    arrived = lax.ppermute(owned0, "section", [(1, 0)]).reshape(10, 16, width)
+
+    def total_of(cut):
+        return (cut(kept).astype(F32) + cut(arrived).astype(F32)).astype(BF16)
+
+    row_slots = []
+    for k in range(SLOTS):
+
+        def cut(v):
+            v = lax.dynamic_slice_in_dim(v, quarter * ((j + k) % SLOTS), quarter, 2)
+            return jnp.concatenate([v[:3], v[6:]], axis=0)
+
+        row_slots.append(send_shard(total_of(cut).reshape(-1, quarter), k))
+    out_rows = total_of(lambda v: v[3:6])
+    out_rows = jnp.transpose(out_rows.reshape(piece, SLOTS, quarter), (1, 0, 2))
     result_moved = lax.ppermute(result.astype(BF16), "section", [(0, 1)]).astype(F32)
     dtokens_moved = lax.ppermute(dtokens.astype(BF16), "section", [(1, 0)]).astype(F32)
     ends = jnp.where(
@@ -965,16 +949,16 @@
         kept = jnp.where(first, v0, v1).astype(F32)
         return kept + swap_section(jnp.where(first, v1, v0)).astype(F32)
 
-    shared = sum(v[piece:].astype(F32) for v in value_rows).astype(BF16)
+    shared = sum(v[2 * piece :].astype(F32) for v in row_slots).astype(BF16)
     gathered = lax.all_gather(
         jnp.concatenate(
-            gate_rows
+            [v[:piece] for v in row_slots]
             + [out_rows.reshape(-1, quarter)]
-            + [v[:piece] for v in value_rows]
+            + [v[piece : 2 * piece] for v in row_slots]
             + [shared],
             axis=0,
         ),
-        "dp",
+        DP,
         tiled=False,
     )
 
@@ -1026,13 +1010,17 @@
 
 
 def solution(mesh):
+    sections, copies, owners = mesh.devices.shape
+    fine = jax.sharding.Mesh(
+        mesh.devices.reshape(sections, 2, copies // 4, 2, owners), ("section", *DP, "shard")
+    )
     return jax.shard_map(
         shards,
-        mesh=mesh,
+        mesh=fine,
         in_specs=(
-            P(("dp", "shard"), None, None),
-            P(("dp", "shard"), None, None),
-            P(("dp", "shard")),
+            P((*DP, "shard"), None, None),
+            P((*DP, "shard"), None, None),
+            P((*DP, "shard")),
             P("section", "shard"),
             P("section", "shard", None),
             P("section", None, "shard"),
@@ -1044,7 +1032,7 @@
             P("section", "shard", None),
         ),
         out_specs=(
-            P("section", ("dp", "shard"), None, None),
+            P("section", (*DP, "shard"), None, None),
             P("section", "shard"),
             P("section", "shard", None),
             P("section", None, "shard"),

time: 518 us -> 471 us (0.909)
  starting transfers between devices: 120 us -> 92.6 us
  other arithmetic: 37.4 us -> 25.8 us
  local copies, waits for them, and re-layouts: 29.4 us -> 23.5 us
    ppermute x48 -> x39, waiting for transfers between devices: 101 us -> 122 us  [send_shard(): return lax.ppermute(v, 'shard', ring(SLOTS, k)) if k else v]
    ppermute x20 -> x9, waiting for transfers between devices: 52.1 us -> 34.2 us  [the longest x1 11.7 us: shards(): owned1 = owned1 + lax.ppermute(owned1, 'section', [(0, 1)])]
    ppermute x48 -> x39, starting transfers between devices: 67.2 us -> 52.4 us  [send_shard(): return lax.ppermute(v, 'shard', ring(SLOTS, k)) if k else v]
    ppermute x3, waiting for transfers between devices: 25.8 us -> 11.6 us  [swap_section(): return lax.ppermute(v, 'section', [(0, 1), (1, 0)])]
    ppermute x20 -> x9, starting transfers between devices: 31 us -> 17.4 us  [the longest x1 10.4 us: shards(): arrived = lax.ppermute(owned0, 'section', [(1, 0)]).reshape(10, 16, width)]
    ppermute x1, waiting for transfers between devices: 0.01 us -> 10.2 us  [shards(): lax.ppermute(result.astype(BF16), 'section', [(0, 1)]).astype(F32)]
    convert_element_type x4 -> x12, other arithmetic: 10.5 us -> 4.31 us  [the longest x2 3.93 us: shards(): (kept.astype(F32) + moved.astype(F32)).astype(BF16)]
    ppermute x3, starting transfers between devices: 11.5 us -> 5.98 us  [swap_section(): return lax.ppermute(v, 'section', [(0, 1), (1, 0)])]
  transfers between devices with their start and end apart: 81 -> 62, of which waited for: 43 -> 35; matrix products, arithmetic and copies ran while one was open for 9% -> 9% of each run, Pallas kernels for 13% -> 14%
where the time goes in v5:
time: 471 us; the launch traced here: 463 us
  waiting for transfers between devices  188 us (40%)
  Pallas kernels  118 us (25%)
  starting transfers between devices  92.6 us (20%)
  other arithmetic  25.8 us (5%)
  local copies, waits for them, and re-layouts  23.5 us (5%)
  between operations  15.9 us (3%)
    ppermute x39, waiting for transfers between devices, send_shard(): return lax.ppermute(v, 'shard', ring(SLOTS, k)) if k else v  122 us
    pallas_call x7, Pallas kernels, kernel_call(): pl.pallas_call(run, grid=(STEPS,), in_specs=[pl.BlockSpec(*ins[n][1:]) if...  108 us
    ppermute x39, starting transfers between devices, send_shard(): return lax.ppermute(v, 'shard', ring(SLOTS, k)) if k else v  52.4 us
    ppermute x1, waiting for transfers between devices, shards(): owned1 = owned1 + lax.ppermute(owned1, 'section', [(0, 1)])  11.7 us
    ppermute x3, waiting for transfers between devices, swap_section(): return lax.ppermute(v, 'section', [(0, 1), (1, 0)])  11.6 us
    ppermute x1, waiting for transfers between devices, shards(): arrived = lax.ppermute(owned0, 'section', [(1, 0)]).reshape(10, 16, width)  10.6 us
    ppermute x1, starting transfers between devices, shards(): arrived = lax.ppermute(owned0, 'section', [(1, 0)]).reshape(10, 16, width)  10.4 us
    ppermute x1, waiting for transfers between devices, shards(): lax.ppermute(result.astype(BF16), 'section', [(0, 1)]).astype(F32)  10.2 us
  transfers between devices with their start and end apart: 62, of which 35 were waited for; matrix products, arithmetic and copies ran while one was open for 9% of the time, Pallas kernels for 14%

profile of v5, /device:TPU:4, one launch (start us, length us, event | category | flops | bytes accessed | tf_op | source)
XLA Modules:
  0.0 463.3 jit_solution(11512817153994405692)
XLA Ops:
  13.0 5.7 %collective-permute-start.4 = (bf16[112,384]{1,0:T(8,128)(2,1)S(1)}, bf16[112,384]{1,0:T(8,128)(2,1)S(1)}, u32[]{:S(2)}, u32[]{:S(2)}) collective-permute-start(bf16[112,384]{1,0:T(8,128)(2,1)S(1)} %get-tuple-element.284), channel_id=1, source_target_pairs={{0,66},{1,67},{2,64},{3,65},{64,2},{65,3},{66,0},{67,1},{4,70},{5,... | collective-permute-start | bytes 258056 | tf_op jit(solution)/shard_map/weights/ppermute | solution.py:655
  67.1 7.7 %collective-permute-done.17 = bf16[4,187,128]{2,1,0:T(8,128)(2,1)S(1)} collective-permute-done((bf16[4,187,128]{2,1,0:T(8,128)(2,1)S(1)}, bf16[4,187,128]{2,1,0:T(8,128)(2,1)S(1)}, u32[]{:S(2)}, u32[]{:S(2)}) %collective-permute-start.17) | collective-permute-done | bytes 191520 | tf_op jit(solution)/shard_map/small_weights/ppermute | solution.py:659
  84.3 5.9 %all-gather.7.cloned.1.call-done = bf16[2560,1536]{1,0:T(8,128)(2,1)} async-done(((bf16[160,1536]{1,0:T(8,128)(2,1)}), bf16[2560,1536]{1,0:T(8,128)(2,1)}) %all-gather.7.cloned.1.call-update) | async-done | bytes 7864336 | tf_op jit(solution)/shard_map/weights/all_gather | solution.py:780
  90.4 17.4 %layer_forward.2 = (bf16[128,1664]{1,0:T(8,128)(2,1)}, bf16[128,1664]{1,0:T(8,128)(2,1)}, bf16[128,1664]{1,0:T(8,128)(2,1)}, bf16[128,1664]{1,0:T(8,128)(2,1)}, ...) custom-call(bf16[128,1536]{1,0:T(8,128)(2,1)} %copy-done, ...), custom_call_target="tpu_custom_call" | custom-call | flops 19800000512 | bytes 1048576 | tf_op jit(solution)/shard_map/layer_forward/pallas_call | solution.py:144
  113.6 7.7 %collective-permute-done.18 = bf16[128,1664]{1,0:T(8,128)(2,1)S(1)} collective-permute-done((bf16[128,1664]{1,0:T(8,128)(2,1)}, bf16[128,1664]{1,0:T(8,128)(2,1)S(1)}, u32[]{:S(2)}, u32[]{:S(2)}) %collective-permute-start.18) | collective-permute-done | bytes 426016 | tf_op jit(solution)/shard_map/ppermute | solution.py:646
  121.3 10.1 %collective-permute-done.19 = bf16[128,1664]{1,0:T(8,128)(2,1)S(1)} collective-permute-done((bf16[128,1664]{1,0:T(8,128)(2,1)}, bf16[128,1664]{1,0:T(8,128)(2,1)S(1)}, u32[]{:S(2)}, u32[]{:S(2)}) %collective-permute-start.19) | collective-permute-done | bytes 426016 | tf_op jit(solution)/shard_map/ppermute | solution.py:646
  137.4 15.0 %collective-permute-done.21.refs_1_ = bf16[128,1536]{1,0:T(8,128)(2,1)S(1)} collective-permute-done((bf16[128,1536]{1,0:T(8,128)(2,1)S(1)}, bf16[128,1536]{1,0:T(8,128)(2,1)S(1)}, u32[]{:S(2)}, u32[]{:S(2)}) %collective-permute-start.21) | collective-permute-done | bytes 393248 | tf_op jit(solution)/shard_map/ppermute | solution.py:646
  156.8 18.5 %layer_forward.3 = (bf16[128,1664]{1,0:T(8,128)(2,1)}, bf16[128,1664]{1,0:T(8,128)(2,1)}, bf16[128,1664]{1,0:T(8,128)(2,1)}, bf16[128,1664]{1,0:T(8,128)(2,1)}, ...) custom-call(bf16[128,1536]{1,0:T(8,128)(2,1)} %copy-done.2, ...), custom_call_target="tpu_custom_call" | custom-call | flops 19800000512 | bytes 1048576 | tf_op jit(solution)/shard_map/layer_forward/pallas_call | solution.py:144
  182.3 22.9 %backward_1.1 = (bf16[512,768]{1,0:T(8,128)(2,1)}, bf16[512,768]{1,0:T(8,128)(2,1)}, f32[6,8,128]{2,1,0:T(8,128)}, bf16[512,768]{1,0:T(8,128)(2,1)}, bf16[512,38...) custom-call(bf16[128,1536]{1,0:T(8,128)(2,1)} %copy-done.11, ...), custom_call_target="tpu_custom_call" | custom-call | flops 30799998976 | bytes 1048576 | tf_op jit(solution)/shard_map/backward_1/pallas_call | solution.py:144
  210.4 9.5 %weight_grads_1.1 = (bf16[16,10,16,1536]{3,2,1,0:T(8,128)(2,1)}, f32[16,1536]{1,0:T(8,128)}) custom-call(bf16[128,1536]{1,0:T(8,128)(2,1)} %copy-done.11, bf16[128,1536]{1,0:T(8,128)(2,1)} %copy-done.36, bf16[128,1536]{1,0:T(8,128)(2,1)} %copy-done.37, bf16[128,1536]{1,0:T(8,128)(2,1)} %copy-done.38, bf16[512,1536]{1,0:T(8,128)(2,1)} %get-tuple-element.149.refs_4_, ...), custom_call_target="tpu_custom_call" | custom-call | flops 8800000000 | bytes 1048576 | tf_op jit(solution)/shard_map/weight_grads_1/pallas_call | solution.py:144
  219.9 6.3 %collective-permute-done.28 = bf16[128,1536]{1,0:T(8,128)(2,1)S(1)} collective-permute-done((bf16[128,1536]{1,0:T(8,128)(2,1)}, bf16[128,1536]{1,0:T(8,128)(2,1)S(1)}, u32[]{:S(2)}, u32[]{:S(2)}) %collective-permute-start.28) | collective-permute-done | bytes 393248 | tf_op jit(solution)/shard_map/ppermute | solution.py:646
  235.2 17.4 %collective-permute-done.30.refs_1_.refs_5_ = bf16[128,1664]{1,0:T(8,128)(2,1)S(1)} collective-permute-done((bf16[128,1664]{1,0:T(8,128)(2,1)S(1)}, bf16[128,1664]{1,0:T(8,128)(2,1)S(1)}, u32[]{:S(2)}, u32[]{:S(2)}) %collective-permute-start.30) | collective-permute-done | bytes 426016 | tf_op jit(solution)/shard_map/ppermute | solution.py:646
  256.4 14.3 %backward_0_gate.1 = (bf16[512,768]{1,0:T(8,128)(2,1)}, bf16[512,768]{1,0:T(8,128)(2,1)}, f32[512,768]{1,0:T(8,128)}, f32[6,8,128]{2,1,0:T(8,128)}, bf16[2,4,6,1...) custom-call(bf16[128,1664]{1,0:T(8,128)(2,1)} %copy-done.10, bf16[128,1664]{1,0:T(8,128)(2,1)} %copy-done.34, ...), custom_call_target="tpu_custom_call" | custom-call | flops 15399999488 | bytes 1048576 | tf_op jit(solution)/shard_map/backward_0_gate/pallas_call | solution.py:144
  271.1 16.8 %backward_0_scan.1 = (f32[6,8,128]{2,1,0:T(8,128)}, bf16[512,768]{1,0:T(8,128)(2,1)}, bf16[512,384]{1,0:T(8,128)(2,1)}, f32[2,8,128]{2,1,0:T(8,128)}, f32[8,128]...) custom-call(f32[2,512,768]{2,1,0:T(8,128)} %get-tuple-element.167.refs, ...), custom_call_target="tpu_custom_call" | custom-call | flops 22000001024 | bytes 1048576 | tf_op jit(solution)/shard_map/backward_0_scan/pallas_call | solution.py:144
  295.5 8.3 %backward_0_input.1 = (bf16[128,1536]{1,0:T(8,128)(2,1)}, bf16[128,1536]{1,0:T(8,128)(2,1)}, bf16[128,1536]{1,0:T(8,128)(2,1)}, bf16[128,1536]{1,0:T(8,128)(2,1)}) custom-call(bf16[16,10,16,1536]{3,2,1,0:T(8,128)(2,1)} %bitcast.247, bf16[16,10,16,1536]{3,2,1,0:T(8,128)(2,1)} %bitcast.248, bf16[16,10,16,1536]{3,2,1,0:T(8,128)(2,1)} %bitcast.249, ...), custom_call_target="tpu_custom_call" | custom-call | flops 9900000256 | bytes 1048576 | tf_op jit(solution)/shard_map/backward_0_input/pallas_call | solution.py:144
  310.1 15.5 %collective-permute-done.36 = bf16[128,1536]{1,0:T(8,128)(2,1)S(1)} collective-permute-done((bf16[128,1536]{1,0:T(8,128)(2,1)}, bf16[128,1536]{1,0:T(8,128)(2,1)S(1)}, u32[]{:S(2)}, u32[]{:S(2)}) %collective-permute-start.36) | collective-permute-done | bytes 393248 | tf_op jit(solution)/shard_map/ppermute | solution.py:646
  331.0 12.3 %collective-permute-done.39 = bf16[128,1664]{1,0:T(8,128)(2,1)S(1)} collective-permute-done((bf16[128,1664]{1,0:T(8,128)(2,1)}, bf16[128,1664]{1,0:T(8,128)(2,1)S(1)}, u32[]{:S(2)}, u32[]{:S(2)}) %collective-permute-start.39) | collective-permute-done | bytes 426016 | tf_op jit(solution)/shard_map/ppermute | solution.py:646
  345.3 11.7 %collective-permute-done.35 = bf16[160,1536]{1,0:T(8,128)(2,1)S(1)} collective-permute-done((bf16[160,1536]{1,0:T(8,128)(2,1)}, bf16[160,1536]{1,0:T(8,128)(2,1)S(1)}, u32[]{:S(2)}, u32[]{:S(2)}) %collective-permute-start.35) | collective-permute-done | bytes 491552 | tf_op jit(solution)/shard_map/ppermute | solution.py:921
  357.2 10.4 %collective-permute-start.53 = (bf16[160,1536]{1,0:T(8,128)(2,1)}, bf16[160,1536]{1,0:T(8,128)(2,1)S(1)}, u32[]{:S(2)}, u32[]{:S(2)}) collective-permute-start(bf16[160,1536]{1,0:T(8,128)(2,1)} %bitcast.194), channel_id=1, source_target_pairs={{64,0},{65,1},{66,2},{67,3},{68,4},{69,5},{70,6},{71,7},{72,8},{73... | collective-permute-start | bytes 1474568 | tf_op jit(solution)/shard_map/ppermute | solution.py:927
  367.8 10.6 %collective-permute-done.53 = bf16[160,1536]{1,0:T(8,128)(2,1)S(1)} collective-permute-done((bf16[160,1536]{1,0:T(8,128)(2,1)}, bf16[160,1536]{1,0:T(8,128)(2,1)S(1)}, u32[]{:S(2)}, u32[]{:S(2)}) %collective-permute-start.53) | collective-permute-done | bytes 491552 | tf_op jit(solution)/shard_map/ppermute | solution.py:927
  397.6 5.5 %collective-permute-start.42 = (bf16[128,1536]{1,0:T(8,128)(2,1)S(1)}, bf16[128,1536]{1,0:T(8,128)(2,1)S(1)}, u32[]{:S(2)}, u32[]{:S(2)}) collective-permute-start(bf16[128,1536]{1,0:T(8,128)(2,1)S(1)} %convert_element_type.406), channel_id=1, source_target_pairs={{64,0},{65,1},{66,2},{67,3},{68,4},{69,5},{70,6},{71,7},{72,8},{73... | collective-permute-start | bytes 1179656 | tf_op jit(solution)/shard_map/ppermute | solution.py:943
  406.4 10.2 %collective-permute-done.43 = bf16[128,1536]{1,0:T(8,128)(2,1)S(1)} collective-permute-done((bf16[128,1536]{1,0:T(8,128)(2,1)S(1)}, bf16[128,1536]{1,0:T(8,128)(2,1)S(1)}, u32[]{:S(2)}, u32[]{:S(2)}) %collective-permute-start.43) | collective-permute-done | bytes 393248 | tf_op jit(solution)/shard_map/ppermute | solution.py:942
  422.0 7.9 %collective-permute-done.49 = f32[276,128]{1,0:T(8,128)S(1)} collective-permute-done((f32[276,128]{1,0:T(8,128)S(1)}, f32[276,128]{1,0:T(8,128)S(1)}, u32[]{:S(2)}, u32[]{:S(2)}) %collective-permute-start.49) | collective-permute-done | bytes 141344 | tf_op jit(solution)/shard_map/ppermute | solution.py:697
  446.2 10.1 %assemble.1 = (f32[6448,384]{1,0:T(8,128)}, f32[768,1536]{1,0:T(8,128)}) custom-call(s32[1]{0:T(128)} %bitcast.71._, bf16[16,592,384]{2,1,0:T(8,128)(2,1)} %bitcast.175, bf16[16,592,384]{2,1,0:T(8,128)(2,1)} %bitcast.176, bf16[16,592,384]{2,1,0:T(8,128)(2,1)} %bitcast.177, f32[48,384]{1,0:T(8,128)} %reshape.526.dt), custom_call_target="tpu_custom_call" | custom-call | tf_op jit(solution)/shard_map/assemble/pallas_call | solution.py:629
  (396 shorter events, 169.6 us)
Async XLA Ops:
  7.2 83.0 %all-gather.7.cloned.1.call-start = ((), (), s32[]{:S(2)}) async-start(), calls=%async_computation.4 | async-start | bytes 8355840 | tf_op jit(solution)/shard_map/weights/all_gather | solution.py:780
  34.0 122.1 %all-gather.9.cloned.1.call-start = ((), (), s32[]{:S(2)}) async-start(), calls=%async_computation.5 | async-start | bytes 8355840 | tf_op jit(solution)/shard_map/all_gather | solution.py:838
  64.8 19.5 %collective-permute-start.11 = (bf16[128,1536]{1,0:T(8,128)(2,1)S(1)}, bf16[128,1536]{1,0:T(8,128)(2,1)S(1)}, u32[]{:S(2)}, u32[]{:S(2)}) collective-permute-start(bf16[128,1536]{1,0:T(8,128)(2,1)S(1)} %fusion.6.refs_4_.refs_0_), channel_id=1, source_target_pairs={{0,3},{1,0},{2,1},{3,2},{4,7},{5,4},{6,5},{7,6},{8,11},{9,8},{10,9... | collective-permute-start | bytes 1179656 | tf_op jit(solution)/shard_map/ppermute | solution.py:646
  64.9 19.4 %collective-permute-start.12 = (bf16[128,1536]{1,0:T(8,128)(2,1)S(1)}, bf16[128,1536]{1,0:T(8,128)(2,1)S(1)}, u32[]{:S(2)}, u32[]{:S(2)}) collective-permute-start(bf16[128,1536]{1,0:T(8,128)(2,1)S(1)} %fusion.6.refs_4_.refs_0_), channel_id=1, source_target_pairs={{0,2},{1,3},{2,0},{3,1},{4,6},{5,7},{6,4},{7,5},{8,10},{9,11},{10,... | collective-permute-start | bytes 1179656 | tf_op jit(solution)/shard_map/ppermute | solution.py:646
  90.2 239.3 %reduce-scatter.5.cloned.1.call-start = ((), (), s32[]{:S(2)}) async-start(), calls=%async_computation.3 | async-start | bytes 8355840 | tf_op jit(solution)/shard_map/reduce_scatter | solution.py:887
  109.4 22.0 %collective-permute-start.19 = (bf16[128,1664]{1,0:T(8,128)(2,1)}, bf16[128,1664]{1,0:T(8,128)(2,1)S(1)}, u32[]{:S(2)}, u32[]{:S(2)}) collective-permute-start(bf16[128,1664]{1,0:T(8,128)(2,1)} %get-tuple-element.129), channel_id=1, source_target_pairs={{0,2},{1,3},{2,0},{3,1},{4,6},{5,7},{6,4},{7,5},{8,10},{9,11},{10,... | collective-permute-start | bytes 1277960 | tf_op jit(solution)/shard_map/ppermute | solution.py:646
  112.2 19.3 %collective-permute-start.20 = (bf16[128,1664]{1,0:T(8,128)(2,1)}, bf16[128,1664]{1,0:T(8,128)(2,1)S(1)}, u32[]{:S(2)}, u32[]{:S(2)}) collective-permute-start(bf16[128,1664]{1,0:T(8,128)(2,1)} %get-tuple-element.130), channel_id=1, source_target_pairs={{0,3},{1,0},{2,1},{3,2},{4,7},{5,4},{6,5},{7,6},{8,11},{9,8},{10,9... | collective-permute-start | bytes 1277960 | tf_op jit(solution)/shard_map/ppermute | solution.py:646
  133.1 19.3 %collective-permute-start.21 = (bf16[128,1536]{1,0:T(8,128)(2,1)S(1)}, bf16[128,1536]{1,0:T(8,128)(2,1)S(1)}, u32[]{:S(2)}, u32[]{:S(2)}) collective-permute-start(bf16[128,1536]{1,0:T(8,128)(2,1)S(1)} %get-tuple-element.218.refs_0_), channel_id=1, source_target_pairs={{0,3},{1,0},{2,1},{3,2},{4,7},{5,4},{6,5},{7,6},{8,11},{9,8},{10,9... | collective-permute-start | bytes 1179656 | tf_op jit(solution)/shard_map/ppermute | solution.py:646
  136.6 19.5 %collective-permute-start.23 = (bf16[128,1536]{1,0:T(8,128)(2,1)S(1)}, bf16[128,1536]{1,0:T(8,128)(2,1)S(1)}, u32[]{:S(2)}, u32[]{:S(2)}) collective-permute-start(bf16[128,1536]{1,0:T(8,128)(2,1)S(1)} %get-tuple-element.218.refs_0_), channel_id=1, source_target_pairs={{0,1},{1,2},{2,3},{3,0},{4,5},{5,6},{6,7},{7,4},{8,9},{9,10},{10,1... | collective-permute-start | bytes 1179656 | tf_op jit(solution)/shard_map/ppermute | solution.py:646
  207.3 18.9 %collective-permute-start.28 = (bf16[128,1536]{1,0:T(8,128)(2,1)}, bf16[128,1536]{1,0:T(8,128)(2,1)S(1)}, u32[]{:S(2)}, u32[]{:S(2)}) collective-permute-start(bf16[128,1536]{1,0:T(8,128)(2,1)} %get-tuple-element.147), channel_id=1, source_target_pairs={{0,2},{1,3},{2,0},{3,1},{4,6},{5,7},{6,4},{7,5},{8,10},{9,11},{10,... | collective-permute-start | bytes 1179656 | tf_op jit(solution)/shard_map/ppermute | solution.py:646
  226.9 130.2 %reduce-scatter.3.cloned.1.call-start = ((), (), s32[]{:S(2)}) async-start(), calls=%async_computation.2 | async-start | bytes 4423680 | tf_op jit(solution)/shard_map/reduce_scatter | solution.py:915
  232.0 20.6 %collective-permute-start.30 = (bf16[128,1664]{1,0:T(8,128)(2,1)S(1)}, bf16[128,1664]{1,0:T(8,128)(2,1)S(1)}, u32[]{:S(2)}, u32[]{:S(2)}) collective-permute-start(bf16[128,1664]{1,0:T(8,128)(2,1)S(1)} %pad_maximum_fusion.2.refs_0_.refs_4_), channel_id=1, source_target_pairs={{0,3},{1,0},{2,1},{3,2},{4,7},{5,4},{6,5},{7,6},{8,11},{9,8},{10,9... | collective-permute-start | bytes 1277960 | tf_op jit(solution)/shard_map/ppermute | solution.py:646
  234.8 21.6 %collective-permute-start.32 = (bf16[128,1664]{1,0:T(8,128)(2,1)S(1)}, bf16[128,1664]{1,0:T(8,128)(2,1)}, u32[]{:S(2)}, u32[]{:S(2)}) collective-permute-start(bf16[128,1664]{1,0:T(8,128)(2,1)S(1)} %pad_maximum_fusion.2.refs_0_.refs_4_), channel_id=1, source_target_pairs={{0,1},{1,2},{2,3},{3,0},{4,5},{5,6},{6,7},{7,4},{8,9},{9,10},{10,1... | collective-permute-start | bytes 1277960 | tf_op jit(solution)/shard_map/ppermute | solution.py:646
  294.8 151.5 %all-gather.11.cloned.1.call-start = ((), (), s32[]{:S(2)}) async-start(), calls=%async_computation.6 | async-start | bytes 7729152 | tf_op jit(solution)/shard_map/all_gather | solution.py:953
  303.8 21.8 %collective-permute-start.36 = (bf16[128,1536]{1,0:T(8,128)(2,1)}, bf16[128,1536]{1,0:T(8,128)(2,1)S(1)}, u32[]{:S(2)}, u32[]{:S(2)}) collective-permute-start(bf16[128,1536]{1,0:T(8,128)(2,1)} %get-tuple-element.183), channel_id=1, source_target_pairs={{0,1},{1,2},{2,3},{3,0},{4,5},{5,6},{6,7},{7,4},{8,9},{9,10},{10,1... | collective-permute-start | bytes 1179656 | tf_op jit(solution)/shard_map/ppermute | solution.py:646
  303.8 21.8 %collective-permute-start.37 = (bf16[128,1536]{1,0:T(8,128)(2,1)}, bf16[128,1536]{1,0:T(8,128)(2,1)S(1)}, u32[]{:S(2)}, u32[]{:S(2)}) collective-permute-start(bf16[128,1536]{1,0:T(8,128)(2,1)} %get-tuple-element.184), channel_id=1, source_target_pairs={{0,2},{1,3},{2,0},{3,1},{4,6},{5,7},{6,4},{7,5},{8,10},{9,11},{10,... | collective-permute-start | bytes 1179656 | tf_op jit(solution)/shard_map/ppermute | solution.py:646
  306.1 20.4 %collective-permute-start.38 = (bf16[128,1536]{1,0:T(8,128)(2,1)}, bf16[128,1536]{1,0:T(8,128)(2,1)S(1)}, u32[]{:S(2)}, u32[]{:S(2)}) collective-permute-start(bf16[128,1536]{1,0:T(8,128)(2,1)} %get-tuple-element.185), channel_id=1, source_target_pairs={{0,3},{1,0},{2,1},{3,2},{4,7},{5,4},{6,5},{7,6},{8,11},{9,8},{10,9... | collective-permute-start | bytes 1179656 | tf_op jit(solution)/shard_map/ppermute | solution.py:646
  307.1 36.2 %collective-permute-start.39 = (bf16[128,1664]{1,0:T(8,128)(2,1)}, bf16[128,1664]{1,0:T(8,128)(2,1)S(1)}, u32[]{:S(2)}, u32[]{:S(2)}) collective-permute-start(bf16[128,1664]{1,0:T(8,128)(2,1)} %get-tuple-element.187), channel_id=1, source_target_pairs={{0,1},{1,2},{2,3},{3,0},{4,5},{5,6},{6,7},{7,4},{8,9},{9,10},{10,1... | collective-permute-start | bytes 1277960 | tf_op jit(solution)/shard_map/ppermute | solution.py:646
  308.2 35.1 %collective-permute-start.40 = (bf16[128,1664]{1,0:T(8,128)(2,1)}, bf16[128,1664]{1,0:T(8,128)(2,1)S(1)}, u32[]{:S(2)}, u32[]{:S(2)}) collective-permute-start(bf16[128,1664]{1,0:T(8,128)(2,1)} %get-tuple-element.188), channel_id=1, source_target_pairs={{0,2},{1,3},{2,0},{3,1},{4,6},{5,7},{6,4},{7,5},{8,10},{9,11},{10,... | collective-permute-start | bytes 1277960 | tf_op jit(solution)/shard_map/ppermute | solution.py:646
  325.6 18.4 %collective-permute-start.41 = (bf16[128,1664]{1,0:T(8,128)(2,1)}, bf16[128,1664]{1,0:T(8,128)(2,1)}, u32[]{:S(2)}, u32[]{:S(2)}) collective-permute-start(bf16[128,1664]{1,0:T(8,128)(2,1)} %get-tuple-element.189), channel_id=1, source_target_pairs={{0,3},{1,0},{2,1},{3,2},{4,7},{5,4},{6,5},{7,6},{8,11},{9,8},{10,9... | collective-permute-start | bytes 1277960 | tf_op jit(solution)/shard_map/ppermute | solution.py:646
  329.5 27.5 %collective-permute-start.35 = (bf16[160,1536]{1,0:T(8,128)(2,1)}, bf16[160,1536]{1,0:T(8,128)(2,1)S(1)}, u32[]{:S(2)}, u32[]{:S(2)}) collective-permute-start(bf16[160,1536]{1,0:T(8,128)(2,1)} %bitcast.193), channel_id=1, source_target_pairs={{0,64},{1,65},{2,66},{3,67},{4,68},{5,69},{6,70},{7,71},{8,72},{9,... | collective-permute-start | bytes 1474568 | tf_op jit(solution)/shard_map/ppermute | solution.py:921
  357.2 21.3 %collective-permute-start.53 = (bf16[160,1536]{1,0:T(8,128)(2,1)}, bf16[160,1536]{1,0:T(8,128)(2,1)S(1)}, u32[]{:S(2)}, u32[]{:S(2)}) collective-permute-start(bf16[160,1536]{1,0:T(8,128)(2,1)} %bitcast.194), channel_id=1, source_target_pairs={{64,0},{65,1},{66,2},{67,3},{68,4},{69,5},{70,6},{71,7},{72,8},{73... | collective-permute-start | bytes 1474568 | tf_op jit(solution)/shard_map/ppermute | solution.py:927
  394.3 22.3 %collective-permute-start.43 = (bf16[128,1536]{1,0:T(8,128)(2,1)S(1)}, bf16[128,1536]{1,0:T(8,128)(2,1)S(1)}, u32[]{:S(2)}, u32[]{:S(2)}) collective-permute-start(bf16[128,1536]{1,0:T(8,128)(2,1)S(1)} %convert_element_type.407), channel_id=1, source_target_pairs={{0,64},{1,65},{2,66},{3,67},{4,68},{5,69},{6,70},{7,71},{8,72},{9,... | collective-permute-start | bytes 1179656 | tf_op jit(solution)/shard_map/ppermute | solution.py:942
  397.6 24.4 %collective-permute-start.42 = (bf16[128,1536]{1,0:T(8,128)(2,1)S(1)}, bf16[128,1536]{1,0:T(8,128)(2,1)S(1)}, u32[]{:S(2)}, u32[]{:S(2)}) collective-permute-start(bf16[128,1536]{1,0:T(8,128)(2,1)S(1)} %convert_element_type.406), channel_id=1, source_target_pairs={{64,0},{65,1},{66,2},{67,3},{68,4},{69,5},{70,6},{71,7},{72,8},{73... | collective-permute-start | bytes 1179656 | tf_op jit(solution)/shard_map/ppermute | solution.py:943
  (84 other events, 1066.2 us)
Sparse Core Ops, SparseCore 0:
  34.1 55.9 all-gather.6
  92.5 50.8 all-gather.8
  227.1 74.1 reduce-scatter.4
  304.1 50.1 reduce-scatter.2
  389.6 56.6 all-gather.10

commit v6 on v5

--- a/solution.py
+++ b/solution.py
@@ -18,7 +18,7 @@
 STEPS = 2
 HALF = PAIRS // STEPS
 WIDE = HALF * LANES
-VMEM_LIMIT = 60 * 1024 * 1024
+VMEM_LIMIT = 34 * 1024 * 1024
 DP = ("x", "z", "core")
 
 
@@ -881,7 +881,7 @@
         ("wgate", "wscan"), "weight_grads_1", 8, saved1, layer1, {"g": g1_slots, **back1}
     )
     back1.update(grads1)
-    moved, back1["ga"] = lax.optimization_barrier((moved, back1["ga"]))
+    moved[1], back1["ga"] = lax.optimization_barrier((moved[1], back1["ga"]))
     dx, gain_grad1 = norm_back(middle.astype(F32), gain1, sum(p.astype(F32) for p in moved))
     by_owner = lambda v: v.reshape(16, -1, width)
     owned1 = lax.psum_scatter(by_owner(back1["ga"]), DP, scatter_dimension=0, tiled=False)

time: 471 us -> 464 us (0.985)
  Pallas kernels: 118 us -> 84.9 us
  local copies, waits for them, and re-layouts: 23.5 us -> 54.2 us
  waiting for transfers between devices: 188 us -> 197 us
  starting transfers between devices: 92.6 us -> 85 us
  other arithmetic: 25.8 us -> 19 us
    unnamed x111 -> x139, local copies, waits for them, and re-layouts: 5.37 us -> 40.1 us
    pallas_call x7, Pallas kernels: 108 us -> 77.5 us  [kernel_call(): pl.pallas_call(run, grid=(STEPS,), in_specs=[pl.BlockSpec(*ins[n][1:]) if...]
    ppermute x39, waiting for transfers between devices: 122 us -> 132 us  [send_shard(): return lax.ppermute(v, 'shard', ring(SLOTS, k)) if k else v]
    ppermute x1, starting transfers between devices: 10.4 us -> 1.58 us  [shards(): arrived = lax.ppermute(owned0, 'section', [(1, 0)]).reshape(10, 16, width)]
    ppermute x1, waiting for transfers between devices: 11.7 us -> 4.33 us  [shards(): owned1 = owned1 + lax.ppermute(owned1, 'section', [(0, 1)])]
  transfers between devices with their start and end apart: 62 -> 62, of which waited for: 35 -> 39; matrix products, arithmetic and copies ran while one was open for 9% -> 7% of each run, Pallas kernels for 14% -> 10%
where the time goes in v6:
time: 464 us; the launch traced here: 456 us
  waiting for transfers between devices  197 us (42%)
  starting transfers between devices  85 us (18%)
  Pallas kernels  84.9 us (18%)
  local copies, waits for them, and re-layouts  54.2 us (12%)
  other arithmetic  19 us (4%)
  between operations  15.9 us (3%)
    ppermute x39, waiting for transfers between devices, send_shard(): return lax.ppermute(v, 'shard', ring(SLOTS, k)) if k else v  132 us
    pallas_call x7, Pallas kernels, kernel_call(): pl.pallas_call(run, grid=(STEPS,), in_specs=[pl.BlockSpec(*ins[n][1:]) if...  77.5 us
    ppermute x39, starting transfers between devices, send_shard(): return lax.ppermute(v, 'shard', ring(SLOTS, k)) if k else v  53.7 us
    unnamed x139, local copies, waits for them, and re-layouts  40.1 us
    ppermute x3, waiting for transfers between devices, swap_section(): return lax.ppermute(v, 'section', [(0, 1), (1, 0)])  11.6 us
    ppermute x1, waiting for transfers between devices, shards(): arrived = lax.ppermute(owned0, 'section', [(1, 0)]).reshape(10, 16, width)  9.95 us
    ppermute x4, starting transfers between devices, send_across(): return lax.ppermute(v, ('section', 'shard'), pairs)  9.45 us
  transfers between devices with their start and end apart: 62, of which 39 were waited for; matrix products, arithmetic and copies ran while one was open for 7% of the time, Pallas kernels for 10%

profile of v6, /device:TPU:4, one launch (start us, length us, event | category | flops | bytes accessed | tf_op | source)
XLA Modules:
  0.0 455.6 jit_solution(5459331655344838844)
XLA Ops:
  13.0 5.7 %collective-permute-start.4 = (bf16[112,384]{1,0:T(8,128)(2,1)S(1)}, bf16[112,384]{1,0:T(8,128)(2,1)S(1)}, u32[]{:S(2)}, u32[]{:S(2)}) collective-permute-start(bf16[112,384]{1,0:T(8,128)(2,1)S(1)} %get-tuple-element.278), channel_id=1, source_target_pairs={{0,66},{1,67},{2,64},{3,65},{64,2},{65,3},{66,0},{67,1},{4,70},{5,... | collective-permute-start | bytes 258056 | tf_op jit(solution)/shard_map/weights/ppermute | solution.py:655
  41.2 5.3 %collective-permute-done.10.refs_3_ = bf16[128,1536]{1,0:T(8,128)(2,1)S(1)} collective-permute-done((bf16[128,1536]{1,0:T(8,128)(2,1)S(1)}, bf16[128,1536]{1,0:T(8,128)(2,1)S(1)}, u32[]{:S(2)}, u32[]{:S(2)}) %collective-permute-start.10) | collective-permute-done | bytes 393248 | tf_op jit(solution)/shard_map/weights/ppermute | solution.py:646
  67.1 7.7 %collective-permute-done.17 = bf16[4,187,128]{2,1,0:T(8,128)(2,1)S(1)} collective-permute-done((bf16[4,187,128]{2,1,0:T(8,128)(2,1)S(1)}, bf16[4,187,128]{2,1,0:T(8,128)(2,1)S(1)}, u32[]{:S(2)}, u32[]{:S(2)}) %collective-permute-start.17) | collective-permute-done | bytes 191520 | tf_op jit(solution)/shard_map/small_weights/ppermute | solution.py:659
  81.1 9.1 %all-gather.7.cloned.1.call-done = bf16[2560,1536]{1,0:T(8,128)(2,1)} async-done(((bf16[160,1536]{1,0:T(8,128)(2,1)}), bf16[2560,1536]{1,0:T(8,128)(2,1)}) %all-gather.7.cloned.1.call-update) | async-done | bytes 7864336 | tf_op jit(solution)/shard_map/weights/all_gather | solution.py:780
  95.7 12.4 %layer_forward.2 = (bf16[128,1664]{1,0:T(8,128)(2,1)S(1)}, bf16[128,1664]{1,0:T(8,128)(2,1)S(1)}, bf16[128,1664]{1,0:T(8,128)(2,1)S(1)}, bf16[128,1664]{1,0:T(8,...) custom-call(bf16[128,1536]{1,0:T(8,128)(2,1)S(1)} %get-tuple-element, ...), custom_call_target="tpu_custom_call" | custom-call | flops 19800000512 | bytes 1048576 | tf_op jit(solution)/shard_map/layer_forward/pallas_call | solution.py:144
  116.1 7.5 %collective-permute-done.18 = bf16[128,1664]{1,0:T(8,128)(2,1)S(1)} collective-permute-done((bf16[128,1664]{1,0:T(8,128)(2,1)S(1)}, bf16[128,1664]{1,0:T(8,128)(2,1)S(1)}, u32[]{:S(2)}, u32[]{:S(2)}) %collective-permute-start.18) | collective-permute-done | bytes 426016 | tf_op jit(solution)/shard_map/ppermute | solution.py:646
  123.6 10.1 %collective-permute-done.19 = bf16[128,1664]{1,0:T(8,128)(2,1)S(1)} collective-permute-done((bf16[128,1664]{1,0:T(8,128)(2,1)S(1)}, bf16[128,1664]{1,0:T(8,128)(2,1)S(1)}, u32[]{:S(2)}, u32[]{:S(2)}) %collective-permute-start.19) | collective-permute-done | bytes 426016 | tf_op jit(solution)/shard_map/ppermute | solution.py:646
  138.7 15.0 %collective-permute-done.21.refs_1_ = bf16[128,1536]{1,0:T(8,128)(2,1)S(1)} collective-permute-done((bf16[128,1536]{1,0:T(8,128)(2,1)S(1)}, bf16[128,1536]{1,0:T(8,128)(2,1)S(1)}, u32[]{:S(2)}, u32[]{:S(2)}) %collective-permute-start.21) | collective-permute-done | bytes 393248 | tf_op jit(solution)/shard_map/ppermute | solution.py:646
  166.3 13.1 %layer_forward.3 = (bf16[128,1664]{1,0:T(8,128)(2,1)S(1)}, bf16[128,1664]{1,0:T(8,128)(2,1)}, bf16[128,1664]{1,0:T(8,128)(2,1)S(1)}, bf16[128,1664]{1,0:T(8,128)...) custom-call(bf16[128,1536]{1,0:T(8,128)(2,1)S(1)} %get-tuple-element, ...), custom_call_target="tpu_custom_call" | custom-call | flops 19800000512 | bytes 1048576 | tf_op jit(solution)/shard_map/layer_forward/pallas_call | solution.py:144
  186.0 18.3 %backward_1.1 = (bf16[512,768]{1,0:T(8,128)(2,1)S(1)}, bf16[512,768]{1,0:T(8,128)(2,1)S(1)}, f32[6,8,128]{2,1,0:T(8,128)S(1)}, bf16[512,768]{1,0:T(8,128)(2,1)S(...) custom-call(bf16[128,1536]{1,0:T(8,128)(2,1)S(1)} %fusion.6.refs_4_., ...), custom_call_target="tpu_custom_call" | custom-call | flops 30799998976 | bytes 1048576 | tf_op jit(solution)/shard_map/backward_1/pallas_call | solution.py:144
  206.4 5.3 %weight_grads_1.1 = (bf16[16,10,16,1536]{3,2,1,0:T(8,128)(2,1)S(1)}, f32[16,1536]{1,0:T(8,128)S(1)}) custom-call(bf16[128,1536]{1,0:T(8,128)(2,1)S(1)} %fusion.6.refs_4_.refs_0_, bf16[128,1536]{1,0:T(8,128)(2,1)S(1)} %copy-done.9, bf16[128,1536]{1,0:T(8,128)(2,1)S(1)} %copy-done.11, bf16[128,1536]{1,0:T(8,128)(2,1)S(1)} %copy-done.14, ...), custom_call_target="tpu_custom_call" | custom-call | flops 8800000000 | bytes 1048576 | tf_op jit(solution)/shard_map/weight_grads_1/pallas_call | solution.py:144
  220.2 7.3 %collective-permute-done.28 = bf16[128,1536]{1,0:T(8,128)(2,1)} collective-permute-done((bf16[128,1536]{1,0:T(8,128)(2,1)S(1)}, bf16[128,1536]{1,0:T(8,128)(2,1)}, u32[]{:S(2)}, u32[]{:S(2)}) %collective-permute-start.28) | collective-permute-done | bytes 393248 | tf_op jit(solution)/shard_map/ppermute | solution.py:646
  227.6 7.4 %collective-permute-done.29 = bf16[128,1536]{1,0:T(8,128)(2,1)} collective-permute-done((bf16[128,1536]{1,0:T(8,128)(2,1)S(1)}, bf16[128,1536]{1,0:T(8,128)(2,1)}, u32[]{:S(2)}, u32[]{:S(2)}) %collective-permute-start.29) | collective-permute-done | bytes 393248 | tf_op jit(solution)/shard_map/ppermute | solution.py:646
  243.2 17.4 %collective-permute-done.30.refs_1_.refs_5_ = bf16[128,1664]{1,0:T(8,128)(2,1)S(1)} collective-permute-done((bf16[128,1664]{1,0:T(8,128)(2,1)S(1)}, bf16[128,1664]{1,0:T(8,128)(2,1)S(1)}, u32[]{:S(2)}, u32[]{:S(2)}) %collective-permute-start.30) | collective-permute-done | bytes 426016 | tf_op jit(solution)/shard_map/ppermute | solution.py:646
  269.3 10.9 %backward_0_gate.1 = (bf16[512,768]{1,0:T(8,128)(2,1)}, bf16[512,768]{1,0:T(8,128)(2,1)S(1)}, f32[512,768]{1,0:T(8,128)S(1)}, f32[6,8,128]{2,1,0:T(8,128)S(1)}, ...) custom-call(bf16[128,1664]{1,0:T(8,128)(2,1)S(1)} %pad_maximum_fusion.2.refs_0_.refs_4_, ...), custom_call_target="tpu_custom_call" | custom-call | flops 15399999488 | bytes 1048576 | tf_op jit(solution)/shard_map/backward_0_gate/pallas_call | solution.py:144
  281.3 12.1 %backward_0_scan.1 = (f32[6,8,128]{2,1,0:T(8,128)S(1)}, bf16[512,768]{1,0:T(8,128)(2,1)S(1)}, bf16[512,384]{1,0:T(8,128)(2,1)S(1)}, f32[2,8,128]{2,1,0:T(8,128)S...) custom-call(f32[2,512,768]{2,1,0:T(8,128)S(1)} %copy-done.33, ...), custom_call_target="tpu_custom_call" | custom-call | flops 22000001024 | bytes 1048576 | tf_op jit(solution)/shard_map/backward_0_scan/pallas_call | solution.py:144
  305.7 5.4 %backward_0_input.1 = (bf16[128,1536]{1,0:T(8,128)(2,1)S(1)}, bf16[128,1536]{1,0:T(8,128)(2,1)S(1)}, bf16[128,1536]{1,0:T(8,128)(2,1)S(1)}, bf16[128,1536]{1,0:T(8,128)(2,1)S(1)}) custom-call(bf16[16,10,16,1536]{3,2,1,0:T(8,128)(2,1)S(1)} %bitcast.191, bf16[16,10,16,1536]{3,2,1,0:T(8,128)(2,1)S(1)} %bitcast.192, bf16[16,10,16,1536]{3,2,1,0:T(8,128)(2,1)S(1)} %bitcast.193, ...), custom_call_target="tpu_custom_call" | custom-call | flops 9900000256 | bytes 1048576 | tf_op jit(solution)/shard_map/backward_0_input/pallas_call | solution.py:144
  317.4 15.3 %collective-permute-done.36 = bf16[128,1536]{1,0:T(8,128)(2,1)S(1)} collective-permute-done((bf16[128,1536]{1,0:T(8,128)(2,1)S(1)}, bf16[128,1536]{1,0:T(8,128)(2,1)S(1)}, u32[]{:S(2)}, u32[]{:S(2)}) %collective-permute-start.36) | collective-permute-done | bytes 393248 | tf_op jit(solution)/shard_map/ppermute | solution.py:646
  336.9 13.7 %collective-permute-done.39 = bf16[128,1664]{1,0:T(8,128)(2,1)} collective-permute-done((bf16[128,1664]{1,0:T(8,128)(2,1)}, bf16[128,1664]{1,0:T(8,128)(2,1)}, u32[]{:S(2)}, u32[]{:S(2)}) %collective-permute-start.39) | collective-permute-done | bytes 426016 | tf_op jit(solution)/shard_map/ppermute | solution.py:646
  358.9 10.0 %collective-permute-done.53 = bf16[160,1536]{1,0:T(8,128)(2,1)S(1)} collective-permute-done((bf16[160,1536]{1,0:T(8,128)(2,1)}, bf16[160,1536]{1,0:T(8,128)(2,1)S(1)}, u32[]{:S(2)}, u32[]{:S(2)}) %collective-permute-start.53) | collective-permute-done | bytes 491552 | tf_op jit(solution)/shard_map/ppermute | solution.py:927
  388.3 5.5 %collective-permute-start.42 = (bf16[128,1536]{1,0:T(8,128)(2,1)S(1)}, bf16[128,1536]{1,0:T(8,128)(2,1)S(1)}, u32[]{:S(2)}, u32[]{:S(2)}) collective-permute-start(bf16[128,1536]{1,0:T(8,128)(2,1)S(1)} %convert_element_type.406), channel_id=1, source_target_pairs={{64,0},{65,1},{66,2},{67,3},{68,4},{69,5},{70,6},{71,7},{72,8},{73... | collective-permute-start | bytes 1179656 | tf_op jit(solution)/shard_map/ppermute | solution.py:943
  397.1 9.0 %collective-permute-done.43 = bf16[128,1536]{1,0:T(8,128)(2,1)S(1)} collective-permute-done((bf16[128,1536]{1,0:T(8,128)(2,1)S(1)}, bf16[128,1536]{1,0:T(8,128)(2,1)S(1)}, u32[]{:S(2)}, u32[]{:S(2)}) %collective-permute-start.43) | collective-permute-done | bytes 393248 | tf_op jit(solution)/shard_map/ppermute | solution.py:942
  412.8 7.8 %collective-permute-done.49 = f32[276,128]{1,0:T(8,128)S(1)} collective-permute-done((f32[276,128]{1,0:T(8,128)S(1)}, f32[276,128]{1,0:T(8,128)S(1)}, u32[]{:S(2)}, u32[]{:S(2)}) %collective-permute-start.49) | collective-permute-done | bytes 141344 | tf_op jit(solution)/shard_map/ppermute | solution.py:697
  441.2 7.4 %assemble.1 = (f32[6448,384]{1,0:T(8,128)}, f32[768,1536]{1,0:T(8,128)}) custom-call(s32[1]{0:T(128)} %bitcast.71._, bf16[16,592,384]{2,1,0:T(8,128)(2,1)S(1)} %bitcast.175, bf16[16,592,384]{2,1,0:T(8,128)(2,1)S(1)} %bitcast.176, bf16[16,592,384]{2,1,0:T(8,128)(2,1)S(1)} %bitcast.177, f32[48,384]{1,0:T(8,128)S(1)} %reshape.526.dt), custom_call_target="tpu_custom_call" | custom-call | tf_op jit(solution)/shard_map/assemble/pallas_call | solution.py:629
  (424 shorter events, 201.1 us)
Async XLA Ops:
  7.2 83.0 %all-gather.7.cloned.1.call-start = ((), (), s32[]{:S(2)}) async-start(), calls=%async_computation.4 | async-start | bytes 8355840 | tf_op jit(solution)/shard_map/weights/all_gather | solution.py:780
  34.0 124.1 %all-gather.9.cloned.1.call-start = ((), (), s32[]{:S(2)}) async-start(), calls=%async_computation.5 | async-start | bytes 8355840 | tf_op jit(solution)/shard_map/all_gather | solution.py:838
  34.7 16.8 %collective-permute-start.8 = (bf16[128,1536]{1,0:T(8,128)(2,1)S(1)}, bf16[128,1536]{1,0:T(8,128)(2,1)S(1)}, u32[]{:S(2)}, u32[]{:S(2)}) collective-permute-start(bf16[128,1536]{1,0:T(8,128)(2,1)S(1)} %get-tuple-element.114.refs_0_), channel_id=1, source_target_pairs={{0,3},{1,0},{2,1},{3,2},{4,7},{5,4},{6,5},{7,6},{8,11},{9,8},{10,9... | collective-permute-start | bytes 1179656 | tf_op jit(solution)/shard_map/weights/ppermute | solution.py:646
  90.2 245.2 %reduce-scatter.5.cloned.1.call-start = ((), (), s32[]{:S(2)}) async-start(), calls=%async_computation.3 | async-start | bytes 8355840 | tf_op jit(solution)/shard_map/reduce_scatter | solution.py:887
  111.9 21.8 %collective-permute-start.19 = (bf16[128,1664]{1,0:T(8,128)(2,1)S(1)}, bf16[128,1664]{1,0:T(8,128)(2,1)S(1)}, u32[]{:S(2)}, u32[]{:S(2)}) collective-permute-start(bf16[128,1664]{1,0:T(8,128)(2,1)S(1)} %get-tuple-element.126), channel_id=1, source_target_pairs={{0,2},{1,3},{2,0},{3,1},{4,6},{5,7},{6,4},{7,5},{8,10},{9,11},{10,... | collective-permute-start | bytes 1277960 | tf_op jit(solution)/shard_map/ppermute | solution.py:646
  114.6 19.1 %collective-permute-start.20 = (bf16[128,1664]{1,0:T(8,128)(2,1)S(1)}, bf16[128,1664]{1,0:T(8,128)(2,1)S(1)}, u32[]{:S(2)}, u32[]{:S(2)}) collective-permute-start(bf16[128,1664]{1,0:T(8,128)(2,1)S(1)} %get-tuple-element.127), channel_id=1, source_target_pairs={{0,3},{1,0},{2,1},{3,2},{4,7},{5,4},{6,5},{7,6},{8,11},{9,8},{10,9... | collective-permute-start | bytes 1277960 | tf_op jit(solution)/shard_map/ppermute | solution.py:646
  134.3 19.3 %collective-permute-start.21 = (bf16[128,1536]{1,0:T(8,128)(2,1)S(1)}, bf16[128,1536]{1,0:T(8,128)(2,1)S(1)}, u32[]{:S(2)}, u32[]{:S(2)}) collective-permute-start(bf16[128,1536]{1,0:T(8,128)(2,1)S(1)} %get-tuple-element.212.refs_0_), channel_id=1, source_target_pairs={{0,3},{1,0},{2,1},{3,2},{4,7},{5,4},{6,5},{7,6},{8,11},{9,8},{10,9... | collective-permute-start | bytes 1179656 | tf_op jit(solution)/shard_map/ppermute | solution.py:646
  136.7 17.0 %collective-permute-start.22 = (bf16[128,1536]{1,0:T(8,128)(2,1)S(1)}, bf16[128,1536]{1,0:T(8,128)(2,1)S(1)}, u32[]{:S(2)}, u32[]{:S(2)}) collective-permute-start(bf16[128,1536]{1,0:T(8,128)(2,1)S(1)} %get-tuple-element.212.refs_0_), channel_id=1, source_target_pairs={{0,2},{1,3},{2,0},{3,1},{4,6},{5,7},{6,4},{7,5},{8,10},{9,11},{10,... | collective-permute-start | bytes 1179656 | tf_op jit(solution)/shard_map/ppermute | solution.py:646
  137.8 19.5 %collective-permute-start.23 = (bf16[128,1536]{1,0:T(8,128)(2,1)S(1)}, bf16[128,1536]{1,0:T(8,128)(2,1)S(1)}, u32[]{:S(2)}, u32[]{:S(2)}) collective-permute-start(bf16[128,1536]{1,0:T(8,128)(2,1)S(1)} %get-tuple-element.212.refs_0_), channel_id=1, source_target_pairs={{0,1},{1,2},{2,3},{3,0},{4,5},{5,6},{6,7},{7,4},{8,9},{9,10},{10,1... | collective-permute-start | bytes 1179656 | tf_op jit(solution)/shard_map/ppermute | solution.py:646
  216.3 140.9 %reduce-scatter.3.cloned.1.call-start = ((), (), s32[]{:S(2)}) async-start(), calls=%async_computation.2 | async-start | bytes 4423680 | tf_op jit(solution)/shard_map/reduce_scatter | solution.py:915
  239.6 21.1 %collective-permute-start.30 = (bf16[128,1664]{1,0:T(8,128)(2,1)S(1)}, bf16[128,1664]{1,0:T(8,128)(2,1)S(1)}, u32[]{:S(2)}, u32[]{:S(2)}) collective-permute-start(bf16[128,1664]{1,0:T(8,128)(2,1)S(1)} %pad_maximum_fusion.2.refs_0_.refs_4_), channel_id=1, source_target_pairs={{0,3},{1,0},{2,1},{3,2},{4,7},{5,4},{6,5},{7,6},{8,11},{9,8},{10,9... | collective-permute-start | bytes 1277960 | tf_op jit(solution)/shard_map/ppermute | solution.py:646
  242.3 18.4 %collective-permute-start.31 = (bf16[128,1664]{1,0:T(8,128)(2,1)S(1)}, bf16[128,1664]{1,0:T(8,128)(2,1)}, u32[]{:S(2)}, u32[]{:S(2)}) collective-permute-start(bf16[128,1664]{1,0:T(8,128)(2,1)S(1)} %pad_maximum_fusion.2.refs_0_.refs_4_), channel_id=1, source_target_pairs={{0,2},{1,3},{2,0},{3,1},{4,6},{5,7},{6,4},{7,5},{8,10},{9,11},{10,... | collective-permute-start | bytes 1277960 | tf_op jit(solution)/shard_map/ppermute | solution.py:646
  242.8 21.6 %collective-permute-start.32 = (bf16[128,1664]{1,0:T(8,128)(2,1)S(1)}, bf16[128,1664]{1,0:T(8,128)(2,1)}, u32[]{:S(2)}, u32[]{:S(2)}) collective-permute-start(bf16[128,1664]{1,0:T(8,128)(2,1)S(1)} %pad_maximum_fusion.2.refs_0_.refs_4_), channel_id=1, source_target_pairs={{0,1},{1,2},{2,3},{3,0},{4,5},{5,6},{6,7},{7,4},{8,9},{9,10},{10,1... | collective-permute-start | bytes 1277960 | tf_op jit(solution)/shard_map/ppermute | solution.py:646
  299.8 138.3 %all-gather.11.cloned.1.call-start = ((), (), s32[]{:S(2)}) async-start(), calls=%async_computation.6 | async-start | bytes 7729152 | tf_op jit(solution)/shard_map/all_gather | solution.py:953
  311.1 21.6 %collective-permute-start.36 = (bf16[128,1536]{1,0:T(8,128)(2,1)S(1)}, bf16[128,1536]{1,0:T(8,128)(2,1)S(1)}, u32[]{:S(2)}, u32[]{:S(2)}) collective-permute-start(bf16[128,1536]{1,0:T(8,128)(2,1)S(1)} %get-tuple-element.177), channel_id=1, source_target_pairs={{0,1},{1,2},{2,3},{3,0},{4,5},{5,6},{6,7},{7,4},{8,9},{9,10},{10,1... | collective-permute-start | bytes 1179656 | tf_op jit(solution)/shard_map/ppermute | solution.py:646
  311.2 21.6 %collective-permute-start.37 = (bf16[128,1536]{1,0:T(8,128)(2,1)S(1)}, bf16[128,1536]{1,0:T(8,128)(2,1)S(1)}, u32[]{:S(2)}, u32[]{:S(2)}) collective-permute-start(bf16[128,1536]{1,0:T(8,128)(2,1)S(1)} %get-tuple-element.178), channel_id=1, source_target_pairs={{0,2},{1,3},{2,0},{3,1},{4,6},{5,7},{6,4},{7,5},{8,10},{9,11},{10,... | collective-permute-start | bytes 1179656 | tf_op jit(solution)/shard_map/ppermute | solution.py:646
  313.2 20.5 %collective-permute-start.38 = (bf16[128,1536]{1,0:T(8,128)(2,1)S(1)}, bf16[128,1536]{1,0:T(8,128)(2,1)S(1)}, u32[]{:S(2)}, u32[]{:S(2)}) collective-permute-start(bf16[128,1536]{1,0:T(8,128)(2,1)S(1)} %get-tuple-element.179), channel_id=1, source_target_pairs={{0,3},{1,0},{2,1},{3,2},{4,7},{5,4},{6,5},{7,6},{8,11},{9,8},{10,9... | collective-permute-start | bytes 1179656 | tf_op jit(solution)/shard_map/ppermute | solution.py:646
  314.4 36.1 %collective-permute-start.39 = (bf16[128,1664]{1,0:T(8,128)(2,1)}, bf16[128,1664]{1,0:T(8,128)(2,1)}, u32[]{:S(2)}, u32[]{:S(2)}) collective-permute-start(bf16[128,1664]{1,0:T(8,128)(2,1)} %get-tuple-element.181), channel_id=1, source_target_pairs={{0,1},{1,2},{2,3},{3,0},{4,5},{5,6},{6,7},{7,4},{8,9},{9,10},{10,1... | collective-permute-start | bytes 1277960 | tf_op jit(solution)/shard_map/ppermute | solution.py:646
  315.3 35.2 %collective-permute-start.40 = (bf16[128,1664]{1,0:T(8,128)(2,1)S(1)}, bf16[128,1664]{1,0:T(8,128)(2,1)}, u32[]{:S(2)}, u32[]{:S(2)}) collective-permute-start(bf16[128,1664]{1,0:T(8,128)(2,1)S(1)} %copy-done.6), channel_id=1, source_target_pairs={{0,2},{1,3},{2,0},{3,1},{4,6},{5,7},{6,4},{7,5},{8,10},{9,11},{10,... | collective-permute-start | bytes 1277960 | tf_op jit(solution)/shard_map/ppermute | solution.py:646
  332.7 18.5 %collective-permute-start.41 = (bf16[128,1664]{1,0:T(8,128)(2,1)S(1)}, bf16[128,1664]{1,0:T(8,128)(2,1)}, u32[]{:S(2)}, u32[]{:S(2)}) collective-permute-start(bf16[128,1664]{1,0:T(8,128)(2,1)S(1)} %get-tuple-element.183), channel_id=1, source_target_pairs={{0,3},{1,0},{2,1},{3,2},{4,7},{5,4},{6,5},{7,6},{8,11},{9,8},{10,9... | collective-permute-start | bytes 1277960 | tf_op jit(solution)/shard_map/ppermute | solution.py:646
  335.4 21.6 %collective-permute-start.35 = (bf16[160,1536]{1,0:T(8,128)(2,1)}, bf16[160,1536]{1,0:T(8,128)(2,1)S(1)}, u32[]{:S(2)}, u32[]{:S(2)}) collective-permute-start(bf16[160,1536]{1,0:T(8,128)(2,1)} %bitcast.216), channel_id=1, source_target_pairs={{0,64},{1,65},{2,66},{3,67},{4,68},{5,69},{6,70},{7,71},{8,72},{9,... | collective-permute-start | bytes 1474568 | tf_op jit(solution)/shard_map/ppermute | solution.py:921
  385.1 21.1 %collective-permute-start.43 = (bf16[128,1536]{1,0:T(8,128)(2,1)S(1)}, bf16[128,1536]{1,0:T(8,128)(2,1)S(1)}, u32[]{:S(2)}, u32[]{:S(2)}) collective-permute-start(bf16[128,1536]{1,0:T(8,128)(2,1)S(1)} %convert_element_type.407), channel_id=1, source_target_pairs={{0,64},{1,65},{2,66},{3,67},{4,68},{5,69},{6,70},{7,71},{8,72},{9,... | collective-permute-start | bytes 1179656 | tf_op jit(solution)/shard_map/ppermute | solution.py:942
  388.3 24.5 %collective-permute-start.42 = (bf16[128,1536]{1,0:T(8,128)(2,1)S(1)}, bf16[128,1536]{1,0:T(8,128)(2,1)S(1)}, u32[]{:S(2)}, u32[]{:S(2)}) collective-permute-start(bf16[128,1536]{1,0:T(8,128)(2,1)S(1)} %convert_element_type.406), channel_id=1, source_target_pairs={{64,0},{65,1},{66,2},{67,3},{68,4},{69,5},{70,6},{71,7},{72,8},{73... | collective-permute-start | bytes 1179656 | tf_op jit(solution)/shard_map/ppermute | solution.py:943
  393.9 16.6 %collective-permute-start.47 = (f32[276,128]{1,0:T(8,128)S(1)}, f32[276,128]{1,0:T(8,128)S(1)}, u32[]{:S(2)}, u32[]{:S(2)}) collective-permute-start(f32[276,128]{1,0:T(8,128)S(1)} %add.513), channel_id=1, source_target_pairs={{0,16},{4,20},{8,24},{12,28},{16,0},{20,4},{24,8},{28,12},{32,48},... | collective-permute-start | bytes 423944 | tf_op jit(solution)/shard_map/ppermute | solution.py:695
  (98 other events, 966.8 us)
Sparse Core Ops, SparseCore 0:
  34.2 55.9 all-gather.6
  92.5 50.8 all-gather.8
  216.4 74.5 reduce-scatter.4
  300.0 49.3 reduce-scatter.2
  380.4 57.7 all-gather.10

commit v7 on v6

--- a/solution.py
+++ b/solution.py
@@ -19,6 +19,7 @@
 HALF = PAIRS // STEPS
 WIDE = HALF * LANES
 VMEM_LIMIT = 34 * 1024 * 1024
+VMEM_MOST = 60 * 1024 * 1024
 DP = ("x", "z", "core")
 
 
@@ -132,26 +133,37 @@
     pass
 
 
-def kernel_call(body, name, ins, outs, scratch, cost_us):
+def kernel_call(body, name, ins, outs, scratch, cost_us, limit=VMEM_LIMIT):
     in_names, out_names, scratch_names = list(ins), list(outs), list(scratch)
 
     def run(*refs):
-        rf = Refs()
-        for key, ref in zip(in_names + out_names + scratch_names, refs):
-            setattr(rf, key, ref)
-        body(rf, pl.program_id(0))
+        for h in range(STEPS):
+            rf = Refs()
+            for key, ref in zip(in_names + out_names + scratch_names, refs):
+                spec = ins.get(key) or outs.get(key)
+                blocks = spec[-2:] if spec and len(spec) > 2 else None
+                if blocks and blocks[1](1) != blocks[1](0):
+                    at = [
+                        slice(n * size, (n + 1) * size) if n else slice(0, size)
+                        for n, size in zip(blocks[1](h), blocks[0])
+                    ]
+                    ref = ref.at[tuple(at)]
+                setattr(rf, key, ref)
+            body(rf, h)
 
     res = pl.pallas_call(
         run,
-        grid=(STEPS,),
         in_specs=[
-            pl.BlockSpec(*ins[n][1:]) if len(ins[n]) > 2 else pl.BlockSpec(memory_space=ins[n][1])
+            pl.BlockSpec(memory_space=pltpu.VMEM if len(ins[n]) > 2 else ins[n][1])
             for n in in_names
         ],
-        out_specs=[pl.BlockSpec(outs[n][2], outs[n][3]) for n in out_names],
+        out_specs=[pl.BlockSpec(memory_space=pltpu.VMEM) for n in out_names],
         out_shape=[jax.ShapeDtypeStruct(outs[n][0], outs[n][1]) for n in out_names],
-        scratch_shapes=[pltpu.VMEM(*scratch[n]) for n in scratch_names],
-        compiler_params=pltpu.CompilerParams(vmem_limit_bytes=VMEM_LIMIT),
+        scratch_shapes=[
+            pltpu.VMEM(*scratch[n]) if isinstance(scratch[n], tuple) else scratch[n]
+            for n in scratch_names
+        ],
+        compiler_params=pltpu.CompilerParams(vmem_limit_bytes=limit),
         cost_estimate=pl.CostEstimate(
             flops=int(cost_us * 1.1e9), bytes_accessed=1 << 20, transcendentals=0
         ),
@@ -160,6 +172,10 @@
     return dict(zip(out_names, res))
 
 
+def when(condition):
+    return (lambda f: f()) if condition else (lambda f: None)
+
+
 def whole(v):
     return (v, v.shape, lambda h: (0,) * v.ndim)
 
@@ -184,13 +200,42 @@
     return (shape, dtype, (shape[0], WIDE), lambda h: (0, h))
 
 
-def weight_blocks(w):
-    half = (8, 3, 16, w.shape[3])
-    return {
-        "wg": (w, half, lambda h: (h, 1, 0, 0)),
-        "wv": (w, half, lambda h: (h, 2, 0, 0)),
-        "wbc": (w, (16, 1, 16, w.shape[3]), lambda h: (0, 9, 0, 0)),
-    }
+def in_hbm(v):
+    return (v, pltpu.HBM)
+
+
+WEIGHT_GROUPS = {"wo": (0, 3), "wg": (3, 3), "wv": (6, 3), "ws": (9, 1)}
+
+
+class Copies:
+    def __init__(self, sems):
+        self.sems, self.copies = sems, {}
+
+    def add(self, key, source, target):
+        self.copies[key] = (source, target, self.sems.at[len(self.copies)])
+
+    def add_weights(self, rf, keys):
+        for key in keys:
+            at, count = WEIGHT_GROUPS[key]
+            self.add(key, rf.w.at[:, pl.ds(at, count)], getattr(rf, key))
+
+    def start(self):
+        for copy in self.copies.values():
+            pltpu.make_async_copy(*copy).start()
+
+    def wait(self, *keys):
+        for key in keys:
+            pltpu.make_async_copy(*self.copies[key]).wait()
+
+
+def weight_scratch(scratch, keys, width):
+    for key in keys:
+        scratch[key] = ((16, WEIGHT_GROUPS[key][1], 16, width), BF16)
+
+
+def half_rows(ref, h):
+    v = ref[pl.ds(8 * h, 8)]
+    return v.reshape(WIDE, v.shape[-1])
 
 
 def pair_lanes(p):
@@ -213,26 +258,38 @@
     with_grad = g_slots is not None
 
     def body(rf, h):
-        @pl.when(h == 0)
+        copies = Copies(rf.sems)
+        for k in range(SLOTS):
+            copies.add(f"x{k}", getattr(rf, f"x{k}"), rf.x_all.at[k])
+        copies.add_weights(rf, ("ws", "wg", "wv", "wo"))
+        if with_grad:
+            for k in range(SLOTS):
+                copies.add(f"g{k}", getattr(rf, f"g{k}"), rf.g_all.at[slot(k)])
+
+        @when(h == 0)
         def _prep():
+            copies.start()
             for k in range(SLOTS):
-                x = getattr(rf, f"x{k}")[...].astype(F32)
+                copies.wait(f"x{k}")
+                x = rf.x_all[k].astype(F32)
                 scale = lax.rsqrt(jnp.mean(x * x, axis=1, keepdims=True) + EPS)
                 rf.normed[slot(k), :] = (x * scale * rf.gain[...]).astype(BF16)
-                if with_grad:
-                    rf.g_all[slot(k), :] = getattr(rf, f"g{k}")[...]
-            rf.pbc[:, 0:256] = dot_nt(rf.normed[...], flat_rows(rf.wbc))
+            copies.wait("ws")
+            rf.pbc[:, 0:256] = dot_nt(rf.normed[...], flat_rows(rf.ws))
             rf.pbc[:, 256:384] = dot_nt(rf.normed[...], rf.dtw[...])
             for k in range(SLOTS):
                 rf.scores[k] = dot_nt(mixed_bc(rf, k, 1), mixed_bc(rf, k, 0), HI) * tri(True)
                 step_prep(k, rf.pbc, rf.dtp, rf.run_col, rf.run_row, rf.step_wide)
             rf.square[...] = jnp.zeros_like(rf.square)
             rf.cross[...] = jnp.zeros_like(rf.cross)
-
-        rf.proj[0, :, 0:WIDE] = dot_nt(rf.normed[...], flat_rows(rf.wg))
-        rf.proj[0, :, WIDE : 2 * WIDE] = dot_nt(rf.normed[...], flat_rows(rf.wv))
+            copies.wait("wg", "wv", "wo")
+            if with_grad:
+                copies.wait(*[f"g{k}" for k in range(SLOTS)])
+
+        rf.proj[0, :, 0:WIDE] = dot_nt(rf.normed[...], half_rows(rf.wg, h))
+        rf.proj[0, :, WIDE : 2 * WIDE] = dot_nt(rf.normed[...], half_rows(rf.wv, h))
         if with_grad:
-            q_all = dot_nt(rf.g_all[...], rf.wout[pl.ds(8 * h, 8)].reshape(WIDE, width))
+            q_all = dot_nt(rf.g_all[...], half_rows(rf.wo, h))
         for p in range(HALF):
             lanes = pair_lanes(p)
             par = rf.pv[:, lanes]
@@ -262,11 +319,11 @@
                 if with_grad:
                     rf.cross[slot(k), :] += q_all[slot(k), lanes] * scaled_out
 
-        @pl.when(h == STEPS - 1)
+        @when(h == STEPS - 1)
         def _finish():
             u = jnp.concatenate([rf.u_all[a] for a in range(STEPS)], axis=1)
             for n in range(0, width, 512):
-                part = dot(u, rf.wout[:, :, :, n : n + 512].reshape(STEPS * WIDE, 512)).astype(BF16)
+                part = dot(u, rf.wo[:, :, :, n : n + 512].reshape(STEPS * WIDE, 512)).astype(BF16)
                 for k in range(SLOTS):
                     getattr(rf, f"out{k}")[:, n : n + 512] = part[slot(k), :]
             for k in range(SLOTS):
@@ -276,14 +333,13 @@
             rf.stats[0] = dot_nt(ones, rf.square[...], HI)
             rf.stats[1] = dot_nt(ones, rf.cross[...], HI)
 
-    ins = {f"x{k}": whole(v) for k, v in enumerate(x_slots)}
+    ins = {f"x{k}": in_hbm(v) for k, v in enumerate(x_slots)}
     if with_grad:
-        ins.update({f"g{k}": whole(v) for k, v in enumerate(g_slots)})
+        ins.update({f"g{k}": in_hbm(v) for k, v in enumerate(g_slots)})
     ins.update(
         gain=whole(gain),
-        **weight_blocks(w),
+        w=in_hbm(w),
         dtw=whole(dtw),
-        wout=(w, (16, 3, 16, width), lambda h: (0, 0, 0, 0)),
         pv=lanes_by_step(pv),
         pbcv=whole(pbcv),
         dtp=whole(dtp),
@@ -304,10 +360,14 @@
         u_all=((STEPS, ROWS, WIDE), BF16),
         square=((ROWS, LANES), F32),
         cross=((ROWS, LANES), F32),
-    )
+        x_all=((SLOTS, T, width), BF16),
+        sems=pltpu.SemaphoreType.DMA((2 * SLOTS + 4,)),
+    )
+    weight_scratch(scratch, ("ws", "wg", "wv", "wo"), width)
     if with_grad:
         scratch["g_all"] = ((ROWS, width), BF16)
-    res = kernel_call(body, "layer_forward", ins, outs, scratch, 18)
+    limit = VMEM_LIMIT if with_grad else VMEM_MOST
+    res = kernel_call(body, "layer_forward", ins, outs, scratch, 18, limit)
     return [res[f"out{k}"] for k in range(SLOTS)], res
 
 
@@ -342,13 +402,29 @@
     width = saved["normed"].shape[1]
     w, dtw, pv, pbcv, dtp = layer
     elementwise = gate or scan
+    fetched = (("wo",) if gate else ()) + (("wg", "wv", "ws") if inp else ())
+    in_slots = gate and "rows" not in have
 
     def body(rf, h):
-        @pl.when(h == 0)
+        copies = Copies(rf.sems) if gate or wgate or inp else None
+        if gate or wgate:
+            for k in range(SLOTS):
+                source = getattr(rf, f"g{k}")
+                copies.add(f"g{k}", source.at[:, pl.ds(0, width)], rf.g_all.at[slot(k)])
+                if in_slots:
+                    copies.add(f"e{k}", source.at[:, pl.ds(width, LANES)], rf.e_all.at[k])
+        if copies:
+            copies.add_weights(rf, fetched)
+
+        @when(h == 0)
         def _prep():
+            if copies:
+                copies.start()
             for k in range(SLOTS):
                 if gate or wgate:
-                    rf.g_all[slot(k), :] = getattr(rf, f"g{k}")[...]
+                    copies.wait(f"g{k}")
+                if in_slots:
+                    copies.wait(f"e{k}")
                 if gate:
                     for row, ref in ((0, rf.scale_row), (1, rf.cross_row)):
                         if "rows" in have:
@@ -356,7 +432,7 @@
                                 jnp.broadcast_to(rf.rows[k, row : row + 1, :], (T, LANES))
                             )
                         else:
-                            column = from_lanes(getattr(rf, f"e{k}")[...], row)
+                            column = from_lanes(rf.e_all[k], row)
                             ref[slot(k), :] = jnp.broadcast_to(column, (T, LANES))
                 if scan:
                     inbound, outbound = mixed_bc(rf, k, 0), mixed_bc(rf, k, 1)
@@ -372,9 +448,11 @@
                 rf.drun[...] = jnp.zeros_like(rf.drun)
             if inp:
                 rf.total[...] = jnp.zeros_like(rf.total)
+            if copies:
+                copies.wait(*fetched)
 
         if gate:
-            q_all = dot_nt(rf.g_all[...], flat_rows(rf.wout))
+            q_all = dot_nt(rf.g_all[...], half_rows(rf.wo, h))
         for p in range(HALF if elementwise else 0):
             lanes = pair_lanes(p)
             par = rf.pv[:, lanes]
@@ -455,9 +533,11 @@
             part = dot_tn(rf.dv[...], rf.normed[...]).astype(BF16)
             put_by_core(rf, "gb", h, 0, part.reshape(4, 2, 3, 16, width))
         if inp:
-            rf.total[...] += dot(rf.dg[...], flat_rows(rf.wg)) + dot(rf.dv[...], flat_rows(rf.wv))
-
-        @pl.when(h == STEPS - 1)
+            rf.total[...] += dot(rf.dg[...], half_rows(rf.wg, h)) + dot(
+                rf.dv[...], half_rows(rf.wv, h)
+            )
+
+        @when(h == STEPS - 1)
         def _finish():
             if scan:
                 sums = [[jnp.zeros((1, LANES), F32) for _ in range(8)] for _ in range(2)]
@@ -508,7 +588,7 @@
             if inp:
                 final = (
                     rf.total[...]
-                    + dot(rf.dbc[:, 0:256], flat_rows(rf.wbc))
+                    + dot(rf.dbc[:, 0:256], flat_rows(rf.ws))
                     + dot(rf.dbc[:, 256:384], rf.dtw[...])
                 )
                 for k in range(SLOTS):
@@ -518,15 +598,13 @@
     heads_cols = STEPS * WIDE
     if gate or wgate:
         for k, v in enumerate(have["g"]):
-            ins[f"g{k}"] = (v, (T, width), lambda h: (0, 0))
+            ins[f"g{k}"] = in_hbm(v)
         scratch["g_all"] = ((ROWS, width), BF16)
     if gate:
-        if "rows" in have:
+        if in_slots:
+            scratch["e_all"] = ((SLOTS, T, LANES), BF16)
+        else:
             ins["rows"] = whole(have["rows"])
-        else:
-            for k, v in enumerate(have["g"]):
-                ins[f"e{k}"] = (v, (T, LANES), lambda h: (0, width // LANES))
-        ins["wout"] = (w, (8, 3, 16, width), lambda h: (h, 0, 0, 0))
         scratch["scale_row"] = ((ROWS, LANES), F32)
         scratch["cross_row"] = ((ROWS, LANES), F32)
         outs["u"] = lanes_by_step_out((ROWS, heads_cols), BF16)
@@ -560,10 +638,14 @@
             drun=((ROWS, LANES), F32),
         )
     if inp:
-        ins.update(weight_blocks(w))
         ins["dtw"] = whole(dtw)
         scratch["total"] = ((ROWS, width), F32)
         outs.update({f"out{k}": whole_out((T, width), BF16) for k in range(SLOTS)})
+    if fetched:
+        ins["w"] = in_hbm(w)
+        weight_scratch(scratch, fetched, width)
+    if gate or wgate or inp:
+        scratch["sems"] = pltpu.SemaphoreType.DMA((2 * SLOTS + 4,))
     if wgate or wscan:
         ins["normed"] = whole(saved["normed"])
     if not gate and (wgate or inp):
@@ -633,7 +715,7 @@
             jax.ShapeDtypeStruct((total, quarter), F32),
             jax.ShapeDtypeStruct((block, SLOTS * quarter), F32),
         ],
-        compiler_params=pltpu.CompilerParams(vmem_limit_bytes=VMEM_LIMIT),
+        compiler_params=pltpu.CompilerParams(vmem_limit_bytes=VMEM_MOST),
         name="assemble",
     )(shard.astype(jnp.int32)[None], parts, parts, parts, dt_rows)
 
@@ -881,7 +963,7 @@
         ("wgate", "wscan"), "weight_grads_1", 8, saved1, layer1, {"g": g1_slots, **back1}
     )
     back1.update(grads1)
-    moved[1], back1["ga"] = lax.optimization_barrier((moved[1], back1["ga"]))
+    moved, back1["ga"] = lax.optimization_barrier((moved, back1["ga"]))
     dx, gain_grad1 = norm_back(middle.astype(F32), gain1, sum(p.astype(F32) for p in moved))
     by_owner = lambda v: v.reshape(16, -1, width)
     owned1 = lax.psum_scatter(by_owner(back1["ga"]), DP, scatter_dimension=0, tiled=False)

time: 464 us -> 468 us (level)
  starting transfers between devices: 85 us -> 93.6 us
  local copies, waits for them, and re-layouts: 54.2 us -> 47.2 us
  Pallas kernels: 84.9 us -> 89.9 us
  waiting for transfers between devices: 197 us -> 192 us
    ppermute x1, starting transfers between devices: 1.58 us -> 12.9 us  [shards(): arrived = lax.ppermute(owned0, 'section', [(1, 0)]).reshape(10, 16, width)]
    unnamed x139 -> x135, local copies, waits for them, and re-layouts: 40.1 us -> 31.1 us
    ppermute x39, waiting for transfers between devices: 132 us -> 123 us  [send_shard(): return lax.ppermute(v, 'shard', ring(SLOTS, k)) if k else v]
    ppermute x1, waiting for transfers between devices: 4.33 us -> 9.44 us  [shards(): owned1 = owned1 + lax.ppermute(owned1, 'section', [(0, 1)])]
  transfers between devices with their start and end apart: 62 -> 62, of which waited for: 39 -> 36; matrix products, arithmetic and copies ran while one was open for 7% -> 7% of each run, Pallas kernels for 10% -> 10%
where the time goes in v7:
time: 468 us; the launch traced here: 459 us
  waiting for transfers between devices  192 us (41%)
  starting transfers between devices  93.6 us (20%)
  Pallas kernels  89.9 us (19%)
  local copies, waits for them, and re-layouts  47.2 us (10%)
  other arithmetic  20.5 us (4%)
  between operations  15.9 us (3%)
    ppermute x39, waiting for transfers between devices, send_shard(): return lax.ppermute(v, 'shard', ring(SLOTS, k)) if k else v  123 us
    pallas_call x7, Pallas kernels, kernel_call(): pl.pallas_call(run, in_specs=[pl.BlockSpec(memory_space=pltpu.VMEM if len...  79.8 us
    ppermute x39, starting transfers between devices, send_shard(): return lax.ppermute(v, 'shard', ring(SLOTS, k)) if k else v  51.2 us
    unnamed x135, local copies, waits for them, and re-layouts  31.1 us
    ppermute x1, starting transfers between devices, shards(): arrived = lax.ppermute(owned0, 'section', [(1, 0)]).reshape(10, 16, width)  12.9 us
    ppermute x3, waiting for transfers between devices, swap_section(): return lax.ppermute(v, 'section', [(0, 1), (1, 0)])  11.7 us
    ppermute x1, waiting for transfers between devices, shards(): arrived = lax.ppermute(owned0, 'section', [(1, 0)]).reshape(10, 16, width)  10.6 us
    ppermute x1, waiting for transfers between devices, shards(): lax.ppermute(result.astype(BF16), 'section', [(0, 1)]).astype(F32)  10.3 us
  transfers between devices with their start and end apart: 62, of which 36 were waited for; matrix products, arithmetic and copies ran while one was open for 7% of the time, Pallas kernels for 10%

profile of v7, /device:TPU:4, one launch (start us, length us, event | category | flops | bytes accessed | tf_op | source)
XLA Modules:
  0.0 459.5 jit_solution(8712590090308375691)
XLA Ops:
  13.0 5.7 %collective-permute-start.4 = (bf16[112,384]{1,0:T(8,128)(2,1)S(1)}, bf16[112,384]{1,0:T(8,128)(2,1)S(1)}, u32[]{:S(2)}, u32[]{:S(2)}) collective-permute-start(bf16[112,384]{1,0:T(8,128)(2,1)S(1)} %get-tuple-element.284), channel_id=1, source_target_pairs={{0,66},{1,67},{2,64},{3,65},{64,2},{65,3},{66,0},{67,1},{4,70},{5,... | collective-permute-start | bytes 258056 | tf_op jit(solution)/shard_map/weights/ppermute | solution.py:737
  41.2 5.3 %collective-permute-done.10.refs_3_ = bf16[128,1536]{1,0:T(8,128)(2,1)S(1)} collective-permute-done((bf16[128,1536]{1,0:T(8,128)(2,1)S(1)}, bf16[128,1536]{1,0:T(8,128)(2,1)S(1)}, u32[]{:S(2)}, u32[]{:S(2)}) %collective-permute-start.10) | collective-permute-done | bytes 393248 | tf_op jit(solution)/shard_map/weights/ppermute | solution.py:728
  67.1 7.7 %collective-permute-done.17 = bf16[4,187,128]{2,1,0:T(8,128)(2,1)S(1)} collective-permute-done((bf16[4,187,128]{2,1,0:T(8,128)(2,1)S(1)}, bf16[4,187,128]{2,1,0:T(8,128)(2,1)S(1)}, u32[]{:S(2)}, u32[]{:S(2)}) %collective-permute-start.17) | collective-permute-done | bytes 191520 | tf_op jit(solution)/shard_map/small_weights/ppermute | solution.py:741
  81.2 9.0 %all-gather.7.cloned.1.call-done = bf16[2560,1536]{1,0:T(8,128)(2,1)} async-done(((bf16[160,1536]{1,0:T(8,128)(2,1)}), bf16[2560,1536]{1,0:T(8,128)(2,1)}) %all-gather.7.cloned.1.call-update) | async-done | bytes 7864336 | tf_op jit(solution)/shard_map/weights/all_gather | solution.py:862
  90.8 14.3 %layer_forward.2 = (bf16[128,1664]{1,0:T(8,128)(2,1)}, bf16[128,1664]{1,0:T(8,128)(2,1)}, bf16[128,1664]{1,0:T(8,128)(2,1)}, bf16[128,1664]{1,0:T(8,128)(2,1)}, ...) custom-call(bf16[128,1536]{1,0:T(8,128)(2,1)} %copy-done.31, ...), custom_call_target="tpu_custom_call" | custom-call | flops 19800000512 | bytes 1048576 | tf_op jit(solution)/shard_map/layer_forward/pallas_call | solution.py:154
  110.8 7.7 %collective-permute-done.18 = bf16[128,1664]{1,0:T(8,128)(2,1)S(1)} collective-permute-done((bf16[128,1664]{1,0:T(8,128)(2,1)}, bf16[128,1664]{1,0:T(8,128)(2,1)S(1)}, u32[]{:S(2)}, u32[]{:S(2)}) %collective-permute-start.18) | collective-permute-done | bytes 426016 | tf_op jit(solution)/shard_map/ppermute | solution.py:728
  118.5 10.1 %collective-permute-done.19 = bf16[128,1664]{1,0:T(8,128)(2,1)S(1)} collective-permute-done((bf16[128,1664]{1,0:T(8,128)(2,1)}, bf16[128,1664]{1,0:T(8,128)(2,1)S(1)}, u32[]{:S(2)}, u32[]{:S(2)}) %collective-permute-start.19) | collective-permute-done | bytes 426016 | tf_op jit(solution)/shard_map/ppermute | solution.py:728
  135.0 15.0 %collective-permute-done.21.refs_1_ = bf16[128,1536]{1,0:T(8,128)(2,1)S(1)} collective-permute-done((bf16[128,1536]{1,0:T(8,128)(2,1)S(1)}, bf16[128,1536]{1,0:T(8,128)(2,1)S(1)}, u32[]{:S(2)}, u32[]{:S(2)}) %collective-permute-start.21) | collective-permute-done | bytes 393248 | tf_op jit(solution)/shard_map/ppermute | solution.py:728
  162.7 14.4 %layer_forward.3 = (bf16[128,1664]{1,0:T(8,128)(2,1)S(1)}, bf16[128,1664]{1,0:T(8,128)(2,1)S(1)}, bf16[128,1664]{1,0:T(8,128)(2,1)S(1)}, bf16[128,1664]{1,0:T(8,...) custom-call(bf16[128,1536]{1,0:T(8,128)(2,1)S(1)} %get-tuple-element, ...), custom_call_target="tpu_custom_call" | custom-call | flops 19800000512 | bytes 1048576 | tf_op jit(solution)/shard_map/layer_forward/pallas_call | solution.py:154
  184.2 19.5 %backward_1.1 = (bf16[512,768]{1,0:T(8,128)(2,1)S(1)}, bf16[512,768]{1,0:T(8,128)(2,1)S(1)}, f32[6,8,128]{2,1,0:T(8,128)S(1)}, bf16[512,768]{1,0:T(8,128)(2,1)S(...) custom-call(bf16[128,1536]{1,0:T(8,128)(2,1)S(1)} %fusion.6.refs_4_., ...), custom_call_target="tpu_custom_call" | custom-call | flops 30799998976 | bytes 1048576 | tf_op jit(solution)/shard_map/backward_1/pallas_call | solution.py:154
  208.0 5.3 %weight_grads_1.1 = (bf16[16,10,16,1536]{3,2,1,0:T(8,128)(2,1)S(1)}, f32[16,1536]{1,0:T(8,128)S(1)}) custom-call(bf16[128,1536]{1,0:T(8,128)(2,1)S(1)} %fusion.6.refs_4_.refs_0_, bf16[128,1536]{1,0:T(8,128)(2,1)S(1)} %copy-done.8, bf16[128,1536]{1,0:T(8,128)(2,1)S(1)} %copy-done.11, bf16[128,1536]{1,0:T(8,128)(2,1)S(1)} %copy-done.13, ...), custom_call_target="tpu_custom_call" | custom-call | flops 8800000000 | bytes 1048576 | tf_op jit(solution)/shard_map/weight_grads_1/pallas_call | solution.py:154
  216.5 7.2 %collective-permute-done.28 = bf16[128,1536]{1,0:T(8,128)(2,1)S(1)} collective-permute-done((bf16[128,1536]{1,0:T(8,128)(2,1)S(1)}, bf16[128,1536]{1,0:T(8,128)(2,1)S(1)}, u32[]{:S(2)}, u32[]{:S(2)}) %collective-permute-start.28) | collective-permute-done | bytes 393248 | tf_op jit(solution)/shard_map/ppermute | solution.py:728
  233.3 17.4 %collective-permute-done.30.refs_1_ = bf16[128,1664]{1,0:T(8,128)(2,1)S(1)} collective-permute-done((bf16[128,1664]{1,0:T(8,128)(2,1)S(1)}, bf16[128,1664]{1,0:T(8,128)(2,1)S(1)}, u32[]{:S(2)}, u32[]{:S(2)}) %collective-permute-start.30) | collective-permute-done | bytes 426016 | tf_op jit(solution)/shard_map/ppermute | solution.py:728
  259.3 10.7 %backward_0_gate.1 = (bf16[512,768]{1,0:T(8,128)(2,1)}, bf16[512,768]{1,0:T(8,128)(2,1)S(1)}, f32[512,768]{1,0:T(8,128)S(1)}, f32[6,8,128]{2,1,0:T(8,128)S(1)}, ...) custom-call(bf16[128,1664]{1,0:T(8,128)(2,1)S(1)} %pad_maximum_fusion.2.refs_0_, ...), custom_call_target="tpu_custom_call" | custom-call | flops 15399999488 | bytes 1048576 | tf_op jit(solution)/shard_map/backward_0_gate/pallas_call | solution.py:154
  270.2 10.8 %backward_0_scan.1 = (f32[6,8,128]{2,1,0:T(8,128)S(1)}, bf16[512,768]{1,0:T(8,128)(2,1)S(1)}, bf16[512,384]{1,0:T(8,128)(2,1)S(1)}, f32[2,8,128]{2,1,0:T(8,128)S...) custom-call(f32[2,512,768]{2,1,0:T(8,128)S(1)} %copy-done.20, ...), custom_call_target="tpu_custom_call" | custom-call | flops 22000001024 | bytes 1048576 | tf_op jit(solution)/shard_map/backward_0_scan/pallas_call | solution.py:154
  306.5 15.1 %collective-permute-done.36 = bf16[128,1536]{1,0:T(8,128)(2,1)S(1)} collective-permute-done((bf16[128,1536]{1,0:T(8,128)(2,1)S(1)}, bf16[128,1536]{1,0:T(8,128)(2,1)S(1)}, u32[]{:S(2)}, u32[]{:S(2)}) %collective-permute-start.36) | collective-permute-done | bytes 393248 | tf_op jit(solution)/shard_map/ppermute | solution.py:728
  324.9 14.5 %collective-permute-done.39 = bf16[128,1664]{1,0:T(8,128)(2,1)} collective-permute-done((bf16[128,1664]{1,0:T(8,128)(2,1)S(1)}, bf16[128,1664]{1,0:T(8,128)(2,1)}, u32[]{:S(2)}, u32[]{:S(2)}) %collective-permute-start.39) | collective-permute-done | bytes 426016 | tf_op jit(solution)/shard_map/ppermute | solution.py:728
  341.6 9.4 %collective-permute-done.35 = bf16[160,1536]{1,0:T(8,128)(2,1)S(1)} collective-permute-done((bf16[160,1536]{1,0:T(8,128)(2,1)}, bf16[160,1536]{1,0:T(8,128)(2,1)S(1)}, u32[]{:S(2)}, u32[]{:S(2)}) %collective-permute-start.35) | collective-permute-done | bytes 491552 | tf_op jit(solution)/shard_map/ppermute | solution.py:1003
  351.1 12.9 %collective-permute-start.53 = (bf16[160,1536]{1,0:T(8,128)(2,1)}, bf16[160,1536]{1,0:T(8,128)(2,1)S(1)}, u32[]{:S(2)}, u32[]{:S(2)}) collective-permute-start(bf16[160,1536]{1,0:T(8,128)(2,1)} %bitcast.204), channel_id=1, source_target_pairs={{64,0},{65,1},{66,2},{67,3},{68,4},{69,5},{70,6},{71,7},{72,8},{73... | collective-permute-start | bytes 1474568 | tf_op jit(solution)/shard_map/ppermute | solution.py:1009
  364.1 10.6 %collective-permute-done.53 = bf16[160,1536]{1,0:T(8,128)(2,1)S(1)} collective-permute-done((bf16[160,1536]{1,0:T(8,128)(2,1)}, bf16[160,1536]{1,0:T(8,128)(2,1)S(1)}, u32[]{:S(2)}, u32[]{:S(2)}) %collective-permute-start.53) | collective-permute-done | bytes 491552 | tf_op jit(solution)/shard_map/ppermute | solution.py:1009
  393.8 5.5 %collective-permute-start.42 = (bf16[128,1536]{1,0:T(8,128)(2,1)S(1)}, bf16[128,1536]{1,0:T(8,128)(2,1)S(1)}, u32[]{:S(2)}, u32[]{:S(2)}) collective-permute-start(bf16[128,1536]{1,0:T(8,128)(2,1)S(1)} %convert_element_type.406), channel_id=1, source_target_pairs={{64,0},{65,1},{66,2},{67,3},{68,4},{69,5},{70,6},{71,7},{72,8},{73... | collective-permute-start | bytes 1179656 | tf_op jit(solution)/shard_map/ppermute | solution.py:1025
  402.6 10.3 %collective-permute-done.43 = bf16[128,1536]{1,0:T(8,128)(2,1)S(1)} collective-permute-done((bf16[128,1536]{1,0:T(8,128)(2,1)S(1)}, bf16[128,1536]{1,0:T(8,128)(2,1)S(1)}, u32[]{:S(2)}, u32[]{:S(2)}) %collective-permute-start.43) | collective-permute-done | bytes 393248 | tf_op jit(solution)/shard_map/ppermute | solution.py:1024
  418.2 7.8 %collective-permute-done.49 = f32[276,128]{1,0:T(8,128)S(1)} collective-permute-done((f32[276,128]{1,0:T(8,128)S(1)}, f32[276,128]{1,0:T(8,128)S(1)}, u32[]{:S(2)}, u32[]{:S(2)}) %collective-permute-start.49) | collective-permute-done | bytes 141344 | tf_op jit(solution)/shard_map/ppermute | solution.py:779
  442.4 10.1 %assemble.1 = (f32[6448,384]{1,0:T(8,128)}, f32[768,1536]{1,0:T(8,128)}) custom-call(s32[1]{0:T(128)} %bitcast.71._, bf16[16,592,384]{2,1,0:T(8,128)(2,1)} %bitcast.186, bf16[16,592,384]{2,1,0:T(8,128)(2,1)} %bitcast.187, bf16[16,592,384]{2,1,0:T(8,128)(2,1)} %bitcast.188, f32[48,384]{1,0:T(8,128)} %reshape.526.dt), custom_call_target="tpu_custom_call" | custom-call | tf_op jit(solution)/shard_map/assemble/pallas_call | solution.py:711
  (420 shorter events, 187.2 us)
Async XLA Ops:
  7.2 83.0 %all-gather.7.cloned.1.call-start = ((), (), s32[]{:S(2)}) async-start(), calls=%async_computation.4 | async-start | bytes 8355840 | tf_op jit(solution)/shard_map/weights/all_gather | solution.py:862
  34.1 120.4 %all-gather.9.cloned.1.call-start = ((), (), s32[]{:S(2)}) async-start(), calls=%async_computation.5 | async-start | bytes 8355840 | tf_op jit(solution)/shard_map/all_gather | solution.py:920
  90.2 233.2 %reduce-scatter.5.cloned.1.call-start = ((), (), s32[]{:S(2)}) async-start(), calls=%async_computation.3 | async-start | bytes 8355840 | tf_op jit(solution)/shard_map/reduce_scatter | solution.py:969
  106.6 22.0 %collective-permute-start.19 = (bf16[128,1664]{1,0:T(8,128)(2,1)}, bf16[128,1664]{1,0:T(8,128)(2,1)S(1)}, u32[]{:S(2)}, u32[]{:S(2)}) collective-permute-start(bf16[128,1664]{1,0:T(8,128)(2,1)} %get-tuple-element.129), channel_id=1, source_target_pairs={{0,2},{1,3},{2,0},{3,1},{4,6},{5,7},{6,4},{7,5},{8,10},{9,11},{10,... | collective-permute-start | bytes 1277960 | tf_op jit(solution)/shard_map/ppermute | solution.py:728
  109.3 19.3 %collective-permute-start.20 = (bf16[128,1664]{1,0:T(8,128)(2,1)}, bf16[128,1664]{1,0:T(8,128)(2,1)S(1)}, u32[]{:S(2)}, u32[]{:S(2)}) collective-permute-start(bf16[128,1664]{1,0:T(8,128)(2,1)} %get-tuple-element.130), channel_id=1, source_target_pairs={{0,3},{1,0},{2,1},{3,2},{4,7},{5,4},{6,5},{7,6},{8,11},{9,8},{10,9... | collective-permute-start | bytes 1277960 | tf_op jit(solution)/shard_map/ppermute | solution.py:728
  130.7 19.3 %collective-permute-start.21 = (bf16[128,1536]{1,0:T(8,128)(2,1)S(1)}, bf16[128,1536]{1,0:T(8,128)(2,1)S(1)}, u32[]{:S(2)}, u32[]{:S(2)}) collective-permute-start(bf16[128,1536]{1,0:T(8,128)(2,1)S(1)} %get-tuple-element.218.refs_0_), channel_id=1, source_target_pairs={{0,3},{1,0},{2,1},{3,2},{4,7},{5,4},{6,5},{7,6},{8,11},{9,8},{10,9... | collective-permute-start | bytes 1179656 | tf_op jit(solution)/shard_map/ppermute | solution.py:728
  133.0 17.7 %collective-permute-start.22 = (bf16[128,1536]{1,0:T(8,128)(2,1)S(1)}, bf16[128,1536]{1,0:T(8,128)(2,1)S(1)}, u32[]{:S(2)}, u32[]{:S(2)}) collective-permute-start(bf16[128,1536]{1,0:T(8,128)(2,1)S(1)} %get-tuple-element.218.refs_0_), channel_id=1, source_target_pairs={{0,2},{1,3},{2,0},{3,1},{4,6},{5,7},{6,4},{7,5},{8,10},{9,11},{10,... | collective-permute-start | bytes 1179656 | tf_op jit(solution)/shard_map/ppermute | solution.py:728
  134.2 19.5 %collective-permute-start.23 = (bf16[128,1536]{1,0:T(8,128)(2,1)S(1)}, bf16[128,1536]{1,0:T(8,128)(2,1)S(1)}, u32[]{:S(2)}, u32[]{:S(2)}) collective-permute-start(bf16[128,1536]{1,0:T(8,128)(2,1)S(1)} %get-tuple-element.218.refs_0_), channel_id=1, source_target_pairs={{0,1},{1,2},{2,3},{3,0},{4,5},{5,6},{6,7},{7,4},{8,9},{9,10},{10,1... | collective-permute-start | bytes 1179656 | tf_op jit(solution)/shard_map/ppermute | solution.py:728
  205.0 18.7 %collective-permute-start.28 = (bf16[128,1536]{1,0:T(8,128)(2,1)S(1)}, bf16[128,1536]{1,0:T(8,128)(2,1)S(1)}, u32[]{:S(2)}, u32[]{:S(2)}) collective-permute-start(bf16[128,1536]{1,0:T(8,128)(2,1)S(1)} %get-tuple-element.147), channel_id=1, source_target_pairs={{0,2},{1,3},{2,0},{3,1},{4,6},{5,7},{6,4},{7,5},{8,10},{9,11},{10,... | collective-permute-start | bytes 1179656 | tf_op jit(solution)/shard_map/ppermute | solution.py:728
  224.6 126.5 %reduce-scatter.3.cloned.1.call-start = ((), (), s32[]{:S(2)}) async-start(), calls=%async_computation.2 | async-start | bytes 4423680 | tf_op jit(solution)/shard_map/reduce_scatter | solution.py:997
  230.2 20.5 %collective-permute-start.30 = (bf16[128,1664]{1,0:T(8,128)(2,1)S(1)}, bf16[128,1664]{1,0:T(8,128)(2,1)S(1)}, u32[]{:S(2)}, u32[]{:S(2)}) collective-permute-start(bf16[128,1664]{1,0:T(8,128)(2,1)S(1)} %pad_maximum_fusion.2.refs_0_), channel_id=1, source_target_pairs={{0,3},{1,0},{2,1},{3,2},{4,7},{5,4},{6,5},{7,6},{8,11},{9,8},{10,9... | collective-permute-start | bytes 1277960 | tf_op jit(solution)/shard_map/ppermute | solution.py:728
  232.3 18.4 %collective-permute-start.31 = (bf16[128,1664]{1,0:T(8,128)(2,1)S(1)}, bf16[128,1664]{1,0:T(8,128)(2,1)}, u32[]{:S(2)}, u32[]{:S(2)}) collective-permute-start(bf16[128,1664]{1,0:T(8,128)(2,1)S(1)} %pad_maximum_fusion.2.refs_0_), channel_id=1, source_target_pairs={{0,2},{1,3},{2,0},{3,1},{4,6},{5,7},{6,4},{7,5},{8,10},{9,11},{10,... | collective-permute-start | bytes 1277960 | tf_op jit(solution)/shard_map/ppermute | solution.py:728
  232.9 21.6 %collective-permute-start.32 = (bf16[128,1664]{1,0:T(8,128)(2,1)S(1)}, bf16[128,1664]{1,0:T(8,128)(2,1)}, u32[]{:S(2)}, u32[]{:S(2)}) collective-permute-start(bf16[128,1664]{1,0:T(8,128)(2,1)S(1)} %pad_maximum_fusion.2.refs_0_), channel_id=1, source_target_pairs={{0,1},{1,2},{2,3},{3,0},{4,5},{5,6},{6,7},{7,4},{8,9},{9,10},{10,1... | collective-permute-start | bytes 1277960 | tf_op jit(solution)/shard_map/ppermute | solution.py:728
  287.5 154.8 %all-gather.11.cloned.1.call-start = ((), (), s32[]{:S(2)}) async-start(), calls=%async_computation.6 | async-start | bytes 7729152 | tf_op jit(solution)/shard_map/all_gather | solution.py:1035
  299.9 21.6 %collective-permute-start.36 = (bf16[128,1536]{1,0:T(8,128)(2,1)S(1)}, bf16[128,1536]{1,0:T(8,128)(2,1)S(1)}, u32[]{:S(2)}, u32[]{:S(2)}) collective-permute-start(bf16[128,1536]{1,0:T(8,128)(2,1)S(1)} %get-tuple-element.183), channel_id=1, source_target_pairs={{0,1},{1,2},{2,3},{3,0},{4,5},{5,6},{6,7},{7,4},{8,9},{9,10},{10,1... | collective-permute-start | bytes 1179656 | tf_op jit(solution)/shard_map/ppermute | solution.py:728
  300.0 21.6 %collective-permute-start.37 = (bf16[128,1536]{1,0:T(8,128)(2,1)S(1)}, bf16[128,1536]{1,0:T(8,128)(2,1)S(1)}, u32[]{:S(2)}, u32[]{:S(2)}) collective-permute-start(bf16[128,1536]{1,0:T(8,128)(2,1)S(1)} %get-tuple-element.184), channel_id=1, source_target_pairs={{0,2},{1,3},{2,0},{3,1},{4,6},{5,7},{6,4},{7,5},{8,10},{9,11},{10,... | collective-permute-start | bytes 1179656 | tf_op jit(solution)/shard_map/ppermute | solution.py:728
  301.9 20.6 %collective-permute-start.38 = (bf16[128,1536]{1,0:T(8,128)(2,1)S(1)}, bf16[128,1536]{1,0:T(8,128)(2,1)S(1)}, u32[]{:S(2)}, u32[]{:S(2)}) collective-permute-start(bf16[128,1536]{1,0:T(8,128)(2,1)S(1)} %get-tuple-element.185), channel_id=1, source_target_pairs={{0,3},{1,0},{2,1},{3,2},{4,7},{5,4},{6,5},{7,6},{8,11},{9,8},{10,9... | collective-permute-start | bytes 1179656 | tf_op jit(solution)/shard_map/ppermute | solution.py:728
  303.2 36.1 %collective-permute-start.39 = (bf16[128,1664]{1,0:T(8,128)(2,1)S(1)}, bf16[128,1664]{1,0:T(8,128)(2,1)}, u32[]{:S(2)}, u32[]{:S(2)}) collective-permute-start(bf16[128,1664]{1,0:T(8,128)(2,1)S(1)} %get-tuple-element.187), channel_id=1, source_target_pairs={{0,1},{1,2},{2,3},{3,0},{4,5},{5,6},{6,7},{7,4},{8,9},{9,10},{10,1... | collective-permute-start | bytes 1277960 | tf_op jit(solution)/shard_map/ppermute | solution.py:728
  304.2 35.2 %collective-permute-start.40 = (bf16[128,1664]{1,0:T(8,128)(2,1)S(1)}, bf16[128,1664]{1,0:T(8,128)(2,1)}, u32[]{:S(2)}, u32[]{:S(2)}) collective-permute-start(bf16[128,1664]{1,0:T(8,128)(2,1)S(1)} %get-tuple-element.188), channel_id=1, source_target_pairs={{0,2},{1,3},{2,0},{3,1},{4,6},{5,7},{6,4},{7,5},{8,10},{9,11},{10,... | collective-permute-start | bytes 1277960 | tf_op jit(solution)/shard_map/ppermute | solution.py:728
  321.6 18.5 %collective-permute-start.41 = (bf16[128,1664]{1,0:T(8,128)(2,1)S(1)}, bf16[128,1664]{1,0:T(8,128)(2,1)}, u32[]{:S(2)}, u32[]{:S(2)}) collective-permute-start(bf16[128,1664]{1,0:T(8,128)(2,1)S(1)} %get-tuple-element.189), channel_id=1, source_target_pairs={{0,3},{1,0},{2,1},{3,2},{4,7},{5,4},{6,5},{7,6},{8,11},{9,8},{10,9... | collective-permute-start | bytes 1277960 | tf_op jit(solution)/shard_map/ppermute | solution.py:728
  323.4 27.6 %collective-permute-start.35 = (bf16[160,1536]{1,0:T(8,128)(2,1)}, bf16[160,1536]{1,0:T(8,128)(2,1)S(1)}, u32[]{:S(2)}, u32[]{:S(2)}) collective-permute-start(bf16[160,1536]{1,0:T(8,128)(2,1)} %bitcast.203), channel_id=1, source_target_pairs={{0,64},{1,65},{2,66},{3,67},{4,68},{5,69},{6,70},{7,71},{8,72},{9,... | collective-permute-start | bytes 1474568 | tf_op jit(solution)/shard_map/ppermute | solution.py:1003
  351.1 23.7 %collective-permute-start.53 = (bf16[160,1536]{1,0:T(8,128)(2,1)}, bf16[160,1536]{1,0:T(8,128)(2,1)S(1)}, u32[]{:S(2)}, u32[]{:S(2)}) collective-permute-start(bf16[160,1536]{1,0:T(8,128)(2,1)} %bitcast.204), channel_id=1, source_target_pairs={{64,0},{65,1},{66,2},{67,3},{68,4},{69,5},{70,6},{71,7},{72,8},{73... | collective-permute-start | bytes 1474568 | tf_op jit(solution)/shard_map/ppermute | solution.py:1009
  390.6 22.3 %collective-permute-start.43 = (bf16[128,1536]{1,0:T(8,128)(2,1)S(1)}, bf16[128,1536]{1,0:T(8,128)(2,1)S(1)}, u32[]{:S(2)}, u32[]{:S(2)}) collective-permute-start(bf16[128,1536]{1,0:T(8,128)(2,1)S(1)} %convert_element_type.407), channel_id=1, source_target_pairs={{0,64},{1,65},{2,66},{3,67},{4,68},{5,69},{6,70},{7,71},{8,72},{9,... | collective-permute-start | bytes 1179656 | tf_op jit(solution)/shard_map/ppermute | solution.py:1024
  393.8 24.4 %collective-permute-start.42 = (bf16[128,1536]{1,0:T(8,128)(2,1)S(1)}, bf16[128,1536]{1,0:T(8,128)(2,1)S(1)}, u32[]{:S(2)}, u32[]{:S(2)}) collective-permute-start(bf16[128,1536]{1,0:T(8,128)(2,1)S(1)} %convert_element_type.406), channel_id=1, source_target_pairs={{64,0},{65,1},{66,2},{67,3},{68,4},{69,5},{70,6},{71,7},{72,8},{73... | collective-permute-start | bytes 1179656 | tf_op jit(solution)/shard_map/ppermute | solution.py:1025
  (96 other events, 1053.6 us)
Sparse Core Ops, SparseCore 0:
  34.2 55.9 all-gather.6
  92.5 50.8 all-gather.8
  224.7 73.9 reduce-scatter.4
  301.6 49.0 reduce-scatter.2
  385.9 56.4 all-gather.10

commit v8 on v7

--- a/solution.py
+++ b/solution.py
@@ -20,6 +20,7 @@
 WIDE = HALF * LANES
 VMEM_LIMIT = 34 * 1024 * 1024
 VMEM_MOST = 60 * 1024 * 1024
+VMEM_BACK = 56 * 1024 * 1024
 DP = ("x", "z", "core")
 
 
@@ -147,6 +148,7 @@
                         slice(n * size, (n + 1) * size) if n else slice(0, size)
                         for n, size in zip(blocks[1](h), blocks[0])
                     ]
+                    setattr(rf, key + "_whole", ref)
                     ref = ref.at[tuple(at)]
                 setattr(rf, key, ref)
             body(rf, h)
@@ -366,8 +368,7 @@
     weight_scratch(scratch, ("ws", "wg", "wv", "wo"), width)
     if with_grad:
         scratch["g_all"] = ((ROWS, width), BF16)
-    limit = VMEM_LIMIT if with_grad else VMEM_MOST
-    res = kernel_call(body, "layer_forward", ins, outs, scratch, 18, limit)
+    res = kernel_call(body, "layer_forward", ins, outs, scratch, 18, VMEM_MOST)
     return [res[f"out{k}"] for k in range(SLOTS)], res
 
 
@@ -395,7 +396,7 @@
                 send[x, z, groups] = part[z, 1 - c]
 
 
-def backward(stages, name, cost_us, saved, layer, have):
+def backward(stages, name, cost_us, saved, layer, have, limit=VMEM_LIMIT):
     gate, scan, inp, wgate, wscan = (
         s in stages for s in ("gate", "scan", "input", "wgate", "wscan")
     )
@@ -523,8 +524,9 @@
             ):
                 part = dot_tn(left[...], right[...]).astype(BF16)
                 rf.ga[:, at : at + 3] = part.reshape(8, 3, 16, width)
-            part = dot_tn(rf.dbc_half[...], rf.normed[...]).astype(BF16)
-            rf.ga[:, 9] = part.reshape(8, 16, width)
+            if not scan:
+                part = dot_tn(rf.dbc_half[...], rf.normed[...]).astype(BF16)
+                rf.ga[:, 9] = part.reshape(8, 16, width)
         elif wgate:
             for at, left, right in ((0, rf.dg, rf.normed), (3, rf.u, rf.g_all)):
                 part = dot_tn(left[...], right[...]).astype(BF16)
@@ -578,6 +580,9 @@
                 rf.small_bc[1] = jnp.concatenate(sums[1], axis=0)
                 dt_sums[1] = dt_sums[1] * rf.dtp[1:2, :]
                 rf.small_dt[...] = jnp.concatenate(dt_sums, axis=0)
+            if wscan and wgate and scan:
+                part = dot_tn(rf.dbc[:, 0:256], rf.normed[...]).astype(BF16)
+                rf.ga_whole[:, 9] = part.reshape(16, 16, width)
             if wscan and not wgate:
                 part = dot_tn(rf.dbc[:, 0:256], rf.normed[...]).astype(BF16)
                 part = part.reshape(2, 4, 2, 1, 16, width)
@@ -656,7 +661,8 @@
         ins["dv"] = lanes_by_step(have["dv"])
         ins["dbc"] = whole(have["dbc"])
     if wgate and wscan:
-        ins["dbc_half"] = (have["dbc"], (ROWS, LANES), lambda h: (0, h))
+        if not scan:
+            ins["dbc_half"] = (have["dbc"], (ROWS, LANES), lambda h: (0, h))
         outs["ga"] = by_step_out((16, 10, 16, width), BF16, (8, 10, 16, width))
     elif wgate or wscan:
         ins["core"] = have["core"]
@@ -665,7 +671,7 @@
             outs[key + end] = whole_out((2, 4, groups, 16, width), BF16)
     if wscan:
         outs["gdt"] = whole_out((16, width), F32)
-    return kernel_call(body, name, ins, outs, scratch, cost_us)
+    return kernel_call(body, name, ins, outs, scratch, cost_us, limit)
 
 
 def assemble(parts, dt_rows, shard):
@@ -951,19 +957,15 @@
         return dx, jnp.sum(grad * unit, axis=0)
 
     back1 = backward(
-        ("gate", "scan", "input"),
+        ("gate", "scan", "input", "wgate", "wscan"),
         "backward_1",
         28,
         saved1,
         layer1,
         {"g": g1_slots, "rows": rows1},
+        VMEM_BACK,
     )
     moved = [send_shard(back1[f"out{k}"], k) for k in range(SLOTS)]
-    grads1 = backward(
-        ("wgate", "wscan"), "weight_grads_1", 8, saved1, layer1, {"g": g1_slots, **back1}
-    )
-    back1.update(grads1)
-    moved, back1["ga"] = lax.optimization_barrier((moved, back1["ga"]))
     dx, gain_grad1 = norm_back(middle.astype(F32), gain1, sum(p.astype(F32) for p in moved))
     by_owner = lambda v: v.reshape(16, -1, width)
     owned1 = lax.psum_scatter(by_owner(back1["ga"]), DP, scatter_dimension=0, tiled=False)

time: 468 us -> 452 us (0.966)
  local copies, waits for them, and re-layouts: 47.2 us -> 30.3 us
  starting transfers between devices: 93.6 us -> 86.2 us
    unnamed x135 -> x103, local copies, waits for them, and re-layouts: 31.1 us -> 12.3 us
    ppermute x1, starting transfers between devices: 12.9 us -> 3.38 us  [shards(): arrived = lax.ppermute(owned0, 'section', [(1, 0)]).reshape(10, 16, width)]
    ppermute x39, waiting for transfers between devices: 123 us -> 132 us  [send_shard(): return lax.ppermute(v, 'shard', ring(SLOTS, k)) if k else v]
    pallas_call x7 -> x6, Pallas kernels: 79.8 us -> 84.5 us  [kernel_call(): pl.pallas_call(run, in_specs=[pl.BlockSpec(memory_space=pltpu.VMEM if len...]
  transfers between devices with their start and end apart: 62 -> 62, of which waited for: 36 -> 36; matrix products, arithmetic and copies ran while one was open for 7% -> 8% of each run, Pallas kernels for 10% -> 9%
where the time goes in v8:
time: 452 us; the launch traced here: 444 us
  waiting for transfers between devices  195 us (43%)
  Pallas kernels  94.5 us (21%)
  starting transfers between devices  86.2 us (19%)
  local copies, waits for them, and re-layouts  30.3 us (7%)
  other arithmetic  21.7 us (5%)
  between operations  15.8 us (3%)
    ppermute x39, waiting for transfers between devices, send_shard(): return lax.ppermute(v, 'shard', ring(SLOTS, k)) if k else v  132 us
    pallas_call x6, Pallas kernels, kernel_call(): pl.pallas_call(run, in_specs=[pl.BlockSpec(memory_space=pltpu.VMEM if len...  84.5 us
    ppermute x39, starting transfers between devices, send_shard(): return lax.ppermute(v, 'shard', ring(SLOTS, k)) if k else v  54.4 us
    unnamed x103, local copies, waits for them, and re-layouts  12.3 us
    ppermute x3, waiting for transfers between devices, swap_section(): return lax.ppermute(v, 'section', [(0, 1), (1, 0)])  11.7 us
    ppermute x1, waiting for transfers between devices, shards(): lax.ppermute(result.astype(BF16), 'section', [(0, 1)]).astype(F32)  10.7 us
    ppermute x1, waiting for transfers between devices, shards(): arrived = lax.ppermute(owned0, 'section', [(1, 0)]).reshape(10, 16, width)  10.2 us
    pallas_call x1, Pallas kernels, assemble(): pl.pallas_call(body, grid_spec=spec, out_shape=[jax.ShapeDtypeStruct((tot...  10 us
  transfers between devices with their start and end apart: 62, of which 36 were waited for; matrix products, arithmetic and copies ran while one was open for 8% of the time, Pallas kernels for 9%

profile of v8, /device:TPU:4, one launch (start us, length us, event | category | flops | bytes accessed | tf_op | source)
XLA Modules:
  0.0 443.8 jit_solution(9476650576729355154)
XLA Ops:
  13.0 5.7 %collective-permute-start.4 = (bf16[112,384]{1,0:T(8,128)(2,1)S(1)}, bf16[112,384]{1,0:T(8,128)(2,1)S(1)}, u32[]{:S(2)}, u32[]{:S(2)}) collective-permute-start(bf16[112,384]{1,0:T(8,128)(2,1)S(1)} %get-tuple-element.266), channel_id=1, source_target_pairs={{0,66},{1,67},{2,64},{3,65},{64,2},{65,3},{66,0},{67,1},{4,70},{5,... | collective-permute-start | bytes 258056 | tf_op jit(solution)/shard_map/weights/ppermute | solution.py:743
  41.2 5.3 %collective-permute-done.10.refs_3_ = bf16[128,1536]{1,0:T(8,128)(2,1)S(1)} collective-permute-done((bf16[128,1536]{1,0:T(8,128)(2,1)S(1)}, bf16[128,1536]{1,0:T(8,128)(2,1)S(1)}, u32[]{:S(2)}, u32[]{:S(2)}) %collective-permute-start.10) | collective-permute-done | bytes 393248 | tf_op jit(solution)/shard_map/weights/ppermute | solution.py:734
  46.5 5.0 %collective-permute-done.8.refs_1_ = bf16[128,1536]{1,0:T(8,128)(2,1)S(1)} collective-permute-done((bf16[128,1536]{1,0:T(8,128)(2,1)S(1)}, bf16[128,1536]{1,0:T(8,128)(2,1)S(1)}, u32[]{:S(2)}, u32[]{:S(2)}) %collective-permute-start.8) | collective-permute-done | bytes 393248 | tf_op jit(solution)/shard_map/weights/ppermute | solution.py:734
  67.2 7.7 %collective-permute-done.17 = bf16[4,187,128]{2,1,0:T(8,128)(2,1)S(1)} collective-permute-done((bf16[4,187,128]{2,1,0:T(8,128)(2,1)S(1)}, bf16[4,187,128]{2,1,0:T(8,128)(2,1)S(1)}, u32[]{:S(2)}, u32[]{:S(2)}) %collective-permute-start.17) | collective-permute-done | bytes 191520 | tf_op jit(solution)/shard_map/small_weights/ppermute | solution.py:747
  84.4 5.8 %all-gather.7.cloned.1.call-done = bf16[2560,1536]{1,0:T(8,128)(2,1)} async-done(((bf16[160,1536]{1,0:T(8,128)(2,1)}), bf16[2560,1536]{1,0:T(8,128)(2,1)}) %all-gather.7.cloned.1.call-update) | async-done | bytes 7864336 | tf_op jit(solution)/shard_map/weights/all_gather | solution.py:868
  90.8 14.3 %layer_forward.2 = (bf16[128,1664]{1,0:T(8,128)(2,1)}, bf16[128,1664]{1,0:T(8,128)(2,1)}, bf16[128,1664]{1,0:T(8,128)(2,1)}, bf16[128,1664]{1,0:T(8,128)(2,1)}, ...) custom-call(bf16[128,1536]{1,0:T(8,128)(2,1)} %copy-done.11, ...), custom_call_target="tpu_custom_call" | custom-call | flops 19800000512 | bytes 1048576 | tf_op jit(solution)/shard_map/layer_forward/pallas_call | solution.py:156
  110.8 7.7 %collective-permute-done.18 = bf16[128,1664]{1,0:T(8,128)(2,1)S(1)} collective-permute-done((bf16[128,1664]{1,0:T(8,128)(2,1)}, bf16[128,1664]{1,0:T(8,128)(2,1)S(1)}, u32[]{:S(2)}, u32[]{:S(2)}) %collective-permute-start.18) | collective-permute-done | bytes 426016 | tf_op jit(solution)/shard_map/ppermute | solution.py:734
  118.5 10.1 %collective-permute-done.19 = bf16[128,1664]{1,0:T(8,128)(2,1)S(1)} collective-permute-done((bf16[128,1664]{1,0:T(8,128)(2,1)}, bf16[128,1664]{1,0:T(8,128)(2,1)S(1)}, u32[]{:S(2)}, u32[]{:S(2)}) %collective-permute-start.19) | collective-permute-done | bytes 426016 | tf_op jit(solution)/shard_map/ppermute | solution.py:734
  134.6 15.0 %collective-permute-done.21.refs_1_ = bf16[128,1536]{1,0:T(8,128)(2,1)S(1)} collective-permute-done((bf16[128,1536]{1,0:T(8,128)(2,1)S(1)}, bf16[128,1536]{1,0:T(8,128)(2,1)S(1)}, u32[]{:S(2)}, u32[]{:S(2)}) %collective-permute-start.21) | collective-permute-done | bytes 393248 | tf_op jit(solution)/shard_map/ppermute | solution.py:734
  154.1 15.0 %layer_forward.3 = (bf16[128,1664]{1,0:T(8,128)(2,1)}, bf16[128,1664]{1,0:T(8,128)(2,1)}, bf16[128,1664]{1,0:T(8,128)(2,1)}, bf16[128,1664]{1,0:T(8,128)(2,1)}, ...) custom-call(bf16[128,1536]{1,0:T(8,128)(2,1)} %copy-done.13, ...), custom_call_target="tpu_custom_call" | custom-call | flops 19800000512 | bytes 1048576 | tf_op jit(solution)/shard_map/layer_forward/pallas_call | solution.py:156
  175.9 28.9 %backward_1.1 = (bf16[512,768]{1,0:T(8,128)(2,1)}, bf16[512,768]{1,0:T(8,128)(2,1)}, f32[6,8,128]{2,1,0:T(8,128)}, bf16[512,768]{1,0:T(8,128)(2,1)}, bf16[512,38...) custom-call(bf16[128,1536]{1,0:T(8,128)(2,1)} %copy-done.19, ...), custom_call_target="tpu_custom_call" | custom-call | flops 30799998976 | bytes 1048576 | tf_op jit(solution)/shard_map/backward_1/pallas_call | solution.py:156
  209.9 7.8 %collective-permute-done.27 = bf16[128,1536]{1,0:T(8,128)(2,1)S(1)} collective-permute-done((bf16[128,1536]{1,0:T(8,128)(2,1)}, bf16[128,1536]{1,0:T(8,128)(2,1)S(1)}, u32[]{:S(2)}, u32[]{:S(2)}) %collective-permute-start.27) | collective-permute-done | bytes 393248 | tf_op jit(solution)/shard_map/ppermute | solution.py:734
  217.8 8.1 %collective-permute-done.28 = bf16[128,1536]{1,0:T(8,128)(2,1)S(1)} collective-permute-done((bf16[128,1536]{1,0:T(8,128)(2,1)}, bf16[128,1536]{1,0:T(8,128)(2,1)S(1)}, u32[]{:S(2)}, u32[]{:S(2)}) %collective-permute-start.28) | collective-permute-done | bytes 393248 | tf_op jit(solution)/shard_map/ppermute | solution.py:734
  233.3 17.3 %collective-permute-done.30.refs_1_ = bf16[128,1664]{1,0:T(8,128)(2,1)S(1)} collective-permute-done((bf16[128,1664]{1,0:T(8,128)(2,1)S(1)}, bf16[128,1664]{1,0:T(8,128)(2,1)S(1)}, u32[]{:S(2)}, u32[]{:S(2)}) %collective-permute-start.30) | collective-permute-done | bytes 426016 | tf_op jit(solution)/shard_map/ppermute | solution.py:734
  259.1 10.5 %backward_0_gate.1 = (bf16[512,768]{1,0:T(8,128)(2,1)}, bf16[512,768]{1,0:T(8,128)(2,1)S(1)}, f32[512,768]{1,0:T(8,128)S(1)}, f32[6,8,128]{2,1,0:T(8,128)S(1)}, ...) custom-call(bf16[128,1664]{1,0:T(8,128)(2,1)S(1)} %pad_maximum_fusion.2.refs_0_, ...), custom_call_target="tpu_custom_call" | custom-call | flops 15399999488 | bytes 1048576 | tf_op jit(solution)/shard_map/backward_0_gate/pallas_call | solution.py:156
  269.9 11.1 %backward_0_scan.1 = (f32[6,8,128]{2,1,0:T(8,128)S(1)}, bf16[512,768]{1,0:T(8,128)(2,1)S(1)}, bf16[512,384]{1,0:T(8,128)(2,1)S(1)}, f32[2,8,128]{2,1,0:T(8,128)S...) custom-call(f32[2,512,768]{2,1,0:T(8,128)S(1)} %copy-done.6, ...), custom_call_target="tpu_custom_call" | custom-call | flops 22000001024 | bytes 1048576 | tf_op jit(solution)/shard_map/backward_0_scan/pallas_call | solution.py:156
  302.7 15.3 %collective-permute-done.36 = bf16[128,1536]{1,0:T(8,128)(2,1)S(1)} collective-permute-done((bf16[128,1536]{1,0:T(8,128)(2,1)S(1)}, bf16[128,1536]{1,0:T(8,128)(2,1)S(1)}, u32[]{:S(2)}, u32[]{:S(2)}) %collective-permute-start.36) | collective-permute-done | bytes 393248 | tf_op jit(solution)/shard_map/ppermute | solution.py:734
  321.4 14.5 %collective-permute-done.39 = bf16[128,1664]{1,0:T(8,128)(2,1)} collective-permute-done((bf16[128,1664]{1,0:T(8,128)(2,1)}, bf16[128,1664]{1,0:T(8,128)(2,1)}, u32[]{:S(2)}, u32[]{:S(2)}) %collective-permute-start.39) | collective-permute-done | bytes 426016 | tf_op jit(solution)/shard_map/ppermute | solution.py:734
  338.2 6.4 %collective-permute-done.35 = bf16[160,1536]{1,0:T(8,128)(2,1)S(1)} collective-permute-done((bf16[160,1536]{1,0:T(8,128)(2,1)}, bf16[160,1536]{1,0:T(8,128)(2,1)S(1)}, u32[]{:S(2)}, u32[]{:S(2)}) %collective-permute-start.35) | collective-permute-done | bytes 491552 | tf_op jit(solution)/shard_map/ppermute | solution.py:1005
  348.2 10.2 %collective-permute-done.53 = bf16[160,1536]{1,0:T(8,128)(2,1)S(1)} collective-permute-done((bf16[160,1536]{1,0:T(8,128)(2,1)}, bf16[160,1536]{1,0:T(8,128)(2,1)S(1)}, u32[]{:S(2)}, u32[]{:S(2)}) %collective-permute-start.53) | collective-permute-done | bytes 491552 | tf_op jit(solution)/shard_map/ppermute | solution.py:1011
  378.5 5.5 %collective-permute-start.42 = (bf16[128,1536]{1,0:T(8,128)(2,1)S(1)}, bf16[128,1536]{1,0:T(8,128)(2,1)S(1)}, u32[]{:S(2)}, u32[]{:S(2)}) collective-permute-start(bf16[128,1536]{1,0:T(8,128)(2,1)S(1)} %convert_element_type.406), channel_id=1, source_target_pairs={{64,0},{65,1},{66,2},{67,3},{68,4},{69,5},{70,6},{71,7},{72,8},{73... | collective-permute-start | bytes 1179656 | tf_op jit(solution)/shard_map/ppermute | solution.py:1027
  387.4 10.7 %collective-permute-done.43 = bf16[128,1536]{1,0:T(8,128)(2,1)S(1)} collective-permute-done((bf16[128,1536]{1,0:T(8,128)(2,1)S(1)}, bf16[128,1536]{1,0:T(8,128)(2,1)S(1)}, u32[]{:S(2)}, u32[]{:S(2)}) %collective-permute-start.43) | collective-permute-done | bytes 393248 | tf_op jit(solution)/shard_map/ppermute | solution.py:1026
  401.9 8.9 %collective-permute-done.49 = f32[276,128]{1,0:T(8,128)S(1)} collective-permute-done((f32[276,128]{1,0:T(8,128)S(1)}, f32[276,128]{1,0:T(8,128)S(1)}, u32[]{:S(2)}, u32[]{:S(2)}) %collective-permute-start.49) | collective-permute-done | bytes 141344 | tf_op jit(solution)/shard_map/ppermute | solution.py:785
  426.8 10.0 %assemble.1 = (f32[6448,384]{1,0:T(8,128)}, f32[768,1536]{1,0:T(8,128)}) custom-call(s32[1]{0:T(128)} %bitcast.71._, bf16[16,592,384]{2,1,0:T(8,128)(2,1)} %bitcast.179, bf16[16,592,384]{2,1,0:T(8,128)(2,1)} %bitcast.180, bf16[16,592,384]{2,1,0:T(8,128)(2,1)} %bitcast.181, f32[48,384]{1,0:T(8,128)} %reshape.526.dt), custom_call_target="tpu_custom_call" | custom-call | tf_op jit(solution)/shard_map/assemble/pallas_call | solution.py:717
  (387 shorter events, 171.1 us)
Async XLA Ops:
  7.2 83.0 %all-gather.7.cloned.1.call-start = ((), (), s32[]{:S(2)}) async-start(), calls=%async_computation.4 | async-start | bytes 8355840 | tf_op jit(solution)/shard_map/weights/all_gather | solution.py:868
  34.0 119.3 %all-gather.9.cloned.1.call-start = ((), (), s32[]{:S(2)}) async-start(), calls=%async_computation.5 | async-start | bytes 8355840 | tf_op jit(solution)/shard_map/all_gather | solution.py:926
  64.9 19.4 %collective-permute-start.11 = (bf16[128,1536]{1,0:T(8,128)(2,1)S(1)}, bf16[128,1536]{1,0:T(8,128)(2,1)S(1)}, u32[]{:S(2)}, u32[]{:S(2)}) collective-permute-start(bf16[128,1536]{1,0:T(8,128)(2,1)S(1)} %fusion.6.refs_4_.refs_0_), channel_id=1, source_target_pairs={{0,3},{1,0},{2,1},{3,2},{4,7},{5,4},{6,5},{7,6},{8,11},{9,8},{10,9... | collective-permute-start | bytes 1179656 | tf_op jit(solution)/shard_map/ppermute | solution.py:734
  65.0 19.4 %collective-permute-start.12 = (bf16[128,1536]{1,0:T(8,128)(2,1)S(1)}, bf16[128,1536]{1,0:T(8,128)(2,1)S(1)}, u32[]{:S(2)}, u32[]{:S(2)}) collective-permute-start(bf16[128,1536]{1,0:T(8,128)(2,1)S(1)} %fusion.6.refs_4_.refs_0_), channel_id=1, source_target_pairs={{0,2},{1,3},{2,0},{3,1},{4,6},{5,7},{6,4},{7,5},{8,10},{9,11},{10,... | collective-permute-start | bytes 1179656 | tf_op jit(solution)/shard_map/ppermute | solution.py:734
  90.2 229.7 %reduce-scatter.5.cloned.1.call-start = ((), (), s32[]{:S(2)}) async-start(), calls=%async_computation.3 | async-start | bytes 8355840 | tf_op jit(solution)/shard_map/reduce_scatter | solution.py:971
  106.6 22.0 %collective-permute-start.19 = (bf16[128,1664]{1,0:T(8,128)(2,1)}, bf16[128,1664]{1,0:T(8,128)(2,1)S(1)}, u32[]{:S(2)}, u32[]{:S(2)}) collective-permute-start(bf16[128,1664]{1,0:T(8,128)(2,1)} %get-tuple-element.120), channel_id=1, source_target_pairs={{0,2},{1,3},{2,0},{3,1},{4,6},{5,7},{6,4},{7,5},{8,10},{9,11},{10,... | collective-permute-start | bytes 1277960 | tf_op jit(solution)/shard_map/ppermute | solution.py:734
  109.3 19.3 %collective-permute-start.20 = (bf16[128,1664]{1,0:T(8,128)(2,1)}, bf16[128,1664]{1,0:T(8,128)(2,1)S(1)}, u32[]{:S(2)}, u32[]{:S(2)}) collective-permute-start(bf16[128,1664]{1,0:T(8,128)(2,1)} %get-tuple-element.121), channel_id=1, source_target_pairs={{0,3},{1,0},{2,1},{3,2},{4,7},{5,4},{6,5},{7,6},{8,11},{9,8},{10,9... | collective-permute-start | bytes 1277960 | tf_op jit(solution)/shard_map/ppermute | solution.py:734
  130.3 19.3 %collective-permute-start.21 = (bf16[128,1536]{1,0:T(8,128)(2,1)S(1)}, bf16[128,1536]{1,0:T(8,128)(2,1)S(1)}, u32[]{:S(2)}, u32[]{:S(2)}) collective-permute-start(bf16[128,1536]{1,0:T(8,128)(2,1)S(1)} %get-tuple-element.200.refs_0_), channel_id=1, source_target_pairs={{0,3},{1,0},{2,1},{3,2},{4,7},{5,4},{6,5},{7,6},{8,11},{9,8},{10,9... | collective-permute-start | bytes 1179656 | tf_op jit(solution)/shard_map/ppermute | solution.py:734
  133.8 19.5 %collective-permute-start.23 = (bf16[128,1536]{1,0:T(8,128)(2,1)S(1)}, bf16[128,1536]{1,0:T(8,128)(2,1)S(1)}, u32[]{:S(2)}, u32[]{:S(2)}) collective-permute-start(bf16[128,1536]{1,0:T(8,128)(2,1)S(1)} %get-tuple-element.200.refs_0_), channel_id=1, source_target_pairs={{0,1},{1,2},{2,3},{3,0},{4,5},{5,6},{6,7},{7,4},{8,9},{9,10},{10,1... | collective-permute-start | bytes 1179656 | tf_op jit(solution)/shard_map/ppermute | solution.py:734
  204.9 139.8 %reduce-scatter.3.cloned.1.call-start = ((), (), s32[]{:S(2)}) async-start(), calls=%async_computation.2 | async-start | bytes 4423680 | tf_op jit(solution)/shard_map/reduce_scatter | solution.py:999
  206.9 18.9 %collective-permute-start.28 = (bf16[128,1536]{1,0:T(8,128)(2,1)}, bf16[128,1536]{1,0:T(8,128)(2,1)S(1)}, u32[]{:S(2)}, u32[]{:S(2)}) collective-permute-start(bf16[128,1536]{1,0:T(8,128)(2,1)} %get-tuple-element.139), channel_id=1, source_target_pairs={{0,2},{1,3},{2,0},{3,1},{4,6},{5,7},{6,4},{7,5},{8,10},{9,11},{10,... | collective-permute-start | bytes 1179656 | tf_op jit(solution)/shard_map/ppermute | solution.py:734
  229.8 20.7 %collective-permute-start.30 = (bf16[128,1664]{1,0:T(8,128)(2,1)S(1)}, bf16[128,1664]{1,0:T(8,128)(2,1)S(1)}, u32[]{:S(2)}, u32[]{:S(2)}) collective-permute-start(bf16[128,1664]{1,0:T(8,128)(2,1)S(1)} %pad_maximum_fusion.2.refs_0_), channel_id=1, source_target_pairs={{0,3},{1,0},{2,1},{3,2},{4,7},{5,4},{6,5},{7,6},{8,11},{9,8},{10,9... | collective-permute-start | bytes 1277960 | tf_op jit(solution)/shard_map/ppermute | solution.py:734
  232.2 18.4 %collective-permute-start.31 = (bf16[128,1664]{1,0:T(8,128)(2,1)S(1)}, bf16[128,1664]{1,0:T(8,128)(2,1)S(1)}, u32[]{:S(2)}, u32[]{:S(2)}) collective-permute-start(bf16[128,1664]{1,0:T(8,128)(2,1)S(1)} %pad_maximum_fusion.2.refs_0_), channel_id=1, source_target_pairs={{0,2},{1,3},{2,0},{3,1},{4,6},{5,7},{6,4},{7,5},{8,10},{9,11},{10,... | collective-permute-start | bytes 1277960 | tf_op jit(solution)/shard_map/ppermute | solution.py:734
  232.7 21.5 %collective-permute-start.32 = (bf16[128,1664]{1,0:T(8,128)(2,1)S(1)}, bf16[128,1664]{1,0:T(8,128)(2,1)S(1)}, u32[]{:S(2)}, u32[]{:S(2)}) collective-permute-start(bf16[128,1664]{1,0:T(8,128)(2,1)S(1)} %pad_maximum_fusion.2.refs_0_), channel_id=1, source_target_pairs={{0,1},{1,2},{2,3},{3,0},{4,5},{5,6},{6,7},{7,4},{8,9},{9,10},{10,1... | collective-permute-start | bytes 1277960 | tf_op jit(solution)/shard_map/ppermute | solution.py:734
  287.4 139.3 %all-gather.11.cloned.1.call-start = ((), (), s32[]{:S(2)}) async-start(), calls=%async_computation.6 | async-start | bytes 7729152 | tf_op jit(solution)/shard_map/all_gather | solution.py:1037
  296.4 21.7 %collective-permute-start.36 = (bf16[128,1536]{1,0:T(8,128)(2,1)S(1)}, bf16[128,1536]{1,0:T(8,128)(2,1)S(1)}, u32[]{:S(2)}, u32[]{:S(2)}) collective-permute-start(bf16[128,1536]{1,0:T(8,128)(2,1)S(1)} %get-tuple-element.165), channel_id=1, source_target_pairs={{0,1},{1,2},{2,3},{3,0},{4,5},{5,6},{6,7},{7,4},{8,9},{9,10},{10,1... | collective-permute-start | bytes 1179656 | tf_op jit(solution)/shard_map/ppermute | solution.py:734
  296.5 21.9 %collective-permute-start.37 = (bf16[128,1536]{1,0:T(8,128)(2,1)S(1)}, bf16[128,1536]{1,0:T(8,128)(2,1)S(1)}, u32[]{:S(2)}, u32[]{:S(2)}) collective-permute-start(bf16[128,1536]{1,0:T(8,128)(2,1)S(1)} %get-tuple-element.166), channel_id=1, source_target_pairs={{0,2},{1,3},{2,0},{3,1},{4,6},{5,7},{6,4},{7,5},{8,10},{9,11},{10,... | collective-permute-start | bytes 1179656 | tf_op jit(solution)/shard_map/ppermute | solution.py:734
  298.5 20.4 %collective-permute-start.38 = (bf16[128,1536]{1,0:T(8,128)(2,1)S(1)}, bf16[128,1536]{1,0:T(8,128)(2,1)S(1)}, u32[]{:S(2)}, u32[]{:S(2)}) collective-permute-start(bf16[128,1536]{1,0:T(8,128)(2,1)S(1)} %get-tuple-element.167), channel_id=1, source_target_pairs={{0,3},{1,0},{2,1},{3,2},{4,7},{5,4},{6,5},{7,6},{8,11},{9,8},{10,9... | collective-permute-start | bytes 1179656 | tf_op jit(solution)/shard_map/ppermute | solution.py:734
  299.7 36.1 %collective-permute-start.39 = (bf16[128,1664]{1,0:T(8,128)(2,1)}, bf16[128,1664]{1,0:T(8,128)(2,1)}, u32[]{:S(2)}, u32[]{:S(2)}) collective-permute-start(bf16[128,1664]{1,0:T(8,128)(2,1)} %get-tuple-element.169), channel_id=1, source_target_pairs={{0,1},{1,2},{2,3},{3,0},{4,5},{5,6},{6,7},{7,4},{8,9},{9,10},{10,1... | collective-permute-start | bytes 1277960 | tf_op jit(solution)/shard_map/ppermute | solution.py:734
  300.6 35.2 %collective-permute-start.40 = (bf16[128,1664]{1,0:T(8,128)(2,1)}, bf16[128,1664]{1,0:T(8,128)(2,1)}, u32[]{:S(2)}, u32[]{:S(2)}) collective-permute-start(bf16[128,1664]{1,0:T(8,128)(2,1)} %get-tuple-element.170), channel_id=1, source_target_pairs={{0,2},{1,3},{2,0},{3,1},{4,6},{5,7},{6,4},{7,5},{8,10},{9,11},{10,... | collective-permute-start | bytes 1277960 | tf_op jit(solution)/shard_map/ppermute | solution.py:734
  318.0 18.5 %collective-permute-start.41 = (bf16[128,1664]{1,0:T(8,128)(2,1)}, bf16[128,1664]{1,0:T(8,128)(2,1)}, u32[]{:S(2)}, u32[]{:S(2)}) collective-permute-start(bf16[128,1664]{1,0:T(8,128)(2,1)} %get-tuple-element.171), channel_id=1, source_target_pairs={{0,3},{1,0},{2,1},{3,2},{4,7},{5,4},{6,5},{7,6},{8,11},{9,8},{10,9... | collective-permute-start | bytes 1277960 | tf_op jit(solution)/shard_map/ppermute | solution.py:734
  319.9 24.6 %collective-permute-start.35 = (bf16[160,1536]{1,0:T(8,128)(2,1)}, bf16[160,1536]{1,0:T(8,128)(2,1)S(1)}, u32[]{:S(2)}, u32[]{:S(2)}) collective-permute-start(bf16[160,1536]{1,0:T(8,128)(2,1)} %bitcast.197), channel_id=1, source_target_pairs={{0,64},{1,65},{2,66},{3,67},{4,68},{5,69},{6,70},{7,71},{8,72},{9,... | collective-permute-start | bytes 1474568 | tf_op jit(solution)/shard_map/ppermute | solution.py:1005
  375.3 22.7 %collective-permute-start.43 = (bf16[128,1536]{1,0:T(8,128)(2,1)S(1)}, bf16[128,1536]{1,0:T(8,128)(2,1)S(1)}, u32[]{:S(2)}, u32[]{:S(2)}) collective-permute-start(bf16[128,1536]{1,0:T(8,128)(2,1)S(1)} %convert_element_type.407), channel_id=1, source_target_pairs={{0,64},{1,65},{2,66},{3,67},{4,68},{5,69},{6,70},{7,71},{8,72},{9,... | collective-permute-start | bytes 1179656 | tf_op jit(solution)/shard_map/ppermute | solution.py:1026
  378.5 23.3 %collective-permute-start.42 = (bf16[128,1536]{1,0:T(8,128)(2,1)S(1)}, bf16[128,1536]{1,0:T(8,128)(2,1)S(1)}, u32[]{:S(2)}, u32[]{:S(2)}) collective-permute-start(bf16[128,1536]{1,0:T(8,128)(2,1)S(1)} %convert_element_type.406), channel_id=1, source_target_pairs={{64,0},{65,1},{66,2},{67,3},{68,4},{69,5},{70,6},{71,7},{72,8},{73... | collective-permute-start | bytes 1179656 | tf_op jit(solution)/shard_map/ppermute | solution.py:1027
  (80 other events, 960.0 us)
Sparse Core Ops, SparseCore 0:
  34.2 55.9 all-gather.6
  92.5 50.8 all-gather.8
  205.0 75.6 reduce-scatter.4
  287.5 49.2 reduce-scatter.2
  370.6 56.1 all-gather.10

commit v9 on v8

--- a/solution.py
+++ b/solution.py
@@ -92,8 +92,8 @@
     return (iota(0) <= iota(1)).astype(F32)
 
 
-def step_prep(k, pbc, dtp, run_col, run_row, step_wide):
-    step = softplus(pbc[slot(k), 256:384] + dtp[0:1, :])
+def step_prep(k, pbc, at, dtp, run_col, run_row, step_wide):
+    step = softplus(pbc[slot(at), 256:384] + dtp[0:1, :])
     run = jnp.dot(tri(True), step * dtp[1:2, :], precision=HI, preferred_element_type=F32)
     run_row[k] = jnp.transpose(run)
     left = iota(1) < HEAD
@@ -249,29 +249,31 @@
     return v.reshape(-1, v.shape[-1])
 
 
-def mixed_bc(rf, k, c):
+def mixed_bc(pbc, pbcv, k, c):
     lanes = slice(c * LANES, (c + 1) * LANES)
-    cv = conv_sum(conv_taps(rf.pbc[slot(k), lanes]), rf.pbcv[:, lanes])
+    cv = conv_sum(conv_taps(pbc[slot(k), lanes]), pbcv[:, lanes])
     return cv * sigmoid(cv)
 
 
 def forward(x_slots, g_slots, w, dtw, gain, pv, pbcv, dtp):
     width = x_slots[0].shape[1]
     with_grad = g_slots is not None
+    slots = len(x_slots)
+    rows = slots * T
 
     def body(rf, h):
         copies = Copies(rf.sems)
-        for k in range(SLOTS):
+        for k in range(slots):
             copies.add(f"x{k}", getattr(rf, f"x{k}"), rf.x_all.at[k])
         copies.add_weights(rf, ("ws", "wg", "wv", "wo"))
         if with_grad:
-            for k in range(SLOTS):
+            for k in range(slots):
                 copies.add(f"g{k}", getattr(rf, f"g{k}"), rf.g_all.at[slot(k)])
 
         @when(h == 0)
         def _prep():
             copies.start()
-            for k in range(SLOTS):
+            for k in range(slots):
                 copies.wait(f"x{k}")
                 x = rf.x_all[k].astype(F32)
                 scale = lax.rsqrt(jnp.mean(x * x, axis=1, keepdims=True) + EPS)
@@ -279,14 +281,16 @@
             copies.wait("ws")
             rf.pbc[:, 0:256] = dot_nt(rf.normed[...], flat_rows(rf.ws))
             rf.pbc[:, 256:384] = dot_nt(rf.normed[...], rf.dtw[...])
-            for k in range(SLOTS):
-                rf.scores[k] = dot_nt(mixed_bc(rf, k, 1), mixed_bc(rf, k, 0), HI) * tri(True)
-                step_prep(k, rf.pbc, rf.dtp, rf.run_col, rf.run_row, rf.step_wide)
+            for k in range(slots):
+                rf.scores[k] = dot_nt(
+                    mixed_bc(rf.pbc, rf.pbcv, k, 1), mixed_bc(rf.pbc, rf.pbcv, k, 0), HI
+                ) * tri(True)
+                step_prep(k, rf.pbc, k, rf.dtp, rf.run_col, rf.run_row, rf.step_wide)
             rf.square[...] = jnp.zeros_like(rf.square)
             rf.cross[...] = jnp.zeros_like(rf.cross)
             copies.wait("wg", "wv", "wo")
             if with_grad:
-                copies.wait(*[f"g{k}" for k in range(SLOTS)])
+                copies.wait(*[f"g{k}" for k in range(slots)])
 
         rf.proj[0, :, 0:WIDE] = dot_nt(rf.normed[...], half_rows(rf.wg, h))
         rf.proj[0, :, WIDE : 2 * WIDE] = dot_nt(rf.normed[...], half_rows(rf.wv, h))
@@ -296,7 +300,7 @@
             lanes = pair_lanes(p)
             par = rf.pv[:, lanes]
             pair = HALF * h + p
-            for k in range(SLOTS):
+            for k in range(slots):
                 gate = rf.proj[0, slot(k), lanes]
                 cv = conv_sum(
                     conv_taps(rf.proj[0, slot(k), WIDE + p * LANES : WIDE + (p + 1) * LANES]), par
@@ -326,9 +330,9 @@
             u = jnp.concatenate([rf.u_all[a] for a in range(STEPS)], axis=1)
             for n in range(0, width, 512):
                 part = dot(u, rf.wo[:, :, :, n : n + 512].reshape(STEPS * WIDE, 512)).astype(BF16)
-                for k in range(SLOTS):
+                for k in range(slots):
                     getattr(rf, f"out{k}")[:, n : n + 512] = part[slot(k), :]
-            for k in range(SLOTS):
+            for k in range(slots):
                 total = jnp.sum(rf.square[slot(k), :], axis=1, keepdims=True)
                 getattr(rf, f"out{k}")[:, width:] = in_lanes([total])
             ones = jnp.ones((8, LANES), F32)
@@ -346,30 +350,30 @@
         pbcv=whole(pbcv),
         dtp=whole(dtp),
     )
-    outs = {f"out{k}": whole_out((T, width + LANES), BF16) for k in range(SLOTS)}
+    outs = {f"out{k}": whole_out((T, width + LANES), BF16) for k in range(slots)}
     outs.update(
-        stats=whole_out((2, 8, ROWS), F32),
-        normed=whole_out((ROWS, width), BF16),
-        proj=by_step_out((STEPS, ROWS, 2 * WIDE), F32, (1, ROWS, 2 * WIDE)),
-        y=by_step_out((STEPS, ROWS, WIDE), F32, (1, ROWS, WIDE)),
-        pbc=whole_out((ROWS, 384), F32),
+        stats=whole_out((2, 8, rows), F32),
+        normed=whole_out((rows, width), BF16),
+        proj=by_step_out((STEPS, rows, 2 * WIDE), F32, (1, rows, 2 * WIDE)),
+        y=by_step_out((STEPS, rows, WIDE), F32, (1, rows, WIDE)),
+        pbc=whole_out((rows, 384), F32),
     )
     scratch = dict(
-        scores=((SLOTS, T, T), F32),
-        run_col=((2 * PAIRS, ROWS, LANES), F32),
-        run_row=((SLOTS, T, LANES), F32),
-        step_wide=((PAIRS, ROWS, LANES), F32),
-        u_all=((STEPS, ROWS, WIDE), BF16),
-        square=((ROWS, LANES), F32),
-        cross=((ROWS, LANES), F32),
-        x_all=((SLOTS, T, width), BF16),
-        sems=pltpu.SemaphoreType.DMA((2 * SLOTS + 4,)),
+        scores=((slots, T, T), F32),
+        run_col=((2 * PAIRS, rows, LANES), F32),
+        run_row=((slots, T, LANES), F32),
+        step_wide=((PAIRS, rows, LANES), F32),
+        u_all=((STEPS, rows, WIDE), BF16),
+        square=((rows, LANES), F32),
+        cross=((rows, LANES), F32),
+        x_all=((slots, T, width), BF16),
+        sems=pltpu.SemaphoreType.DMA((2 * slots + 4,)),
     )
     weight_scratch(scratch, ("ws", "wg", "wv", "wo"), width)
     if with_grad:
-        scratch["g_all"] = ((ROWS, width), BF16)
-    res = kernel_call(body, "layer_forward", ins, outs, scratch, 18, VMEM_MOST)
-    return [res[f"out{k}"] for k in range(SLOTS)], res
+        scratch["g_all"] = ((rows, width), BF16)
+    res = kernel_call(body, "layer_forward", ins, outs, scratch, 4 * slots, VMEM_MOST)
+    return [res[f"out{k}"] for k in range(slots)], res
 
 
 def head_columns(pair):
@@ -400,11 +404,14 @@
     gate, scan, inp, wgate, wscan = (
         s in stages for s in ("gate", "scan", "input", "wgate", "wscan")
     )
-    width = saved["normed"].shape[1]
+    width = saved[0]["normed"].shape[1]
+    per = SLOTS // len(saved)
     w, dtw, pv, pbcv, dtp = layer
     elementwise = gate or scan
     fetched = (("wo",) if gate else ()) + (("wg", "wv", "ws") if inp else ())
     in_slots = gate and "rows" not in have
+    part_of = lambda rf, key, k: getattr(rf, f"{key}{k // per}")
+    mixed = lambda rf, k, c: mixed_bc(part_of(rf, "pbc", k), rf.pbcv, k % per, c)
 
     def body(rf, h):
         copies = Copies(rf.sems) if gate or wgate or inp else None
@@ -416,6 +423,10 @@
                     copies.add(f"e{k}", source.at[:, pl.ds(width, LANES)], rf.e_all.at[k])
         if copies:
             copies.add_weights(rf, fetched)
+            if (wgate or wscan) and len(saved) > 1:
+                for n in range(len(saved)):
+                    rows = pl.ds(n * per * T, per * T)
+                    copies.add(f"n{n}", getattr(rf, f"normed{n}"), rf.normed.at[rows])
 
         @when(h == 0)
         def _prep():
@@ -436,12 +447,12 @@
                             column = from_lanes(rf.e_all[k], row)
                             ref[slot(k), :] = jnp.broadcast_to(column, (T, LANES))
                 if scan:
-                    inbound, outbound = mixed_bc(rf, k, 0), mixed_bc(rf, k, 1)
-                    rf.mixed[0, slot(k), :] = inbound
-                    rf.mixed[1, slot(k), :] = outbound
+                    inbound, outbound = mixed(rf, k, 0), mixed(rf, k, 1)
+                    rf.mixed_all[0, slot(k), :] = inbound
+                    rf.mixed_all[1, slot(k), :] = outbound
                     rf.scores[k] = dot_nt(inbound, outbound, HI) * tri(False)
                     rf.step_all[slot(k), :] = step_prep(
-                        k, rf.pbc, rf.dtp, rf.run_col, rf.run_row, rf.step_wide
+                        k, part_of(rf, "pbc", k), k % per, rf.dtp, rf.run_col, rf.run_row, rf.step_wide
                     )
             if scan:
                 rf.dscores[...] = jnp.zeros_like(rf.dscores)
@@ -451,6 +462,8 @@
                 rf.total[...] = jnp.zeros_like(rf.total)
             if copies:
                 copies.wait(*fetched)
+                if (wgate or wscan) and len(saved) > 1:
+                    copies.wait(*[f"n{n}" for n in range(len(saved))])
 
         if gate:
             q_all = dot_nt(rf.g_all[...], half_rows(rf.wo, h))
@@ -462,13 +475,13 @@
             if scan:
                 columns = head_columns(pair)
             for k in range(SLOTS):
-                taps = conv_taps(rf.proj[0, slot(k), WIDE + p * LANES : WIDE + (p + 1) * LANES])
+                taps = conv_taps(part_of(rf, "proj", k)[0, slot(k % per), WIDE + p * LANES : WIDE + (p + 1) * LANES])
                 cv = conv_sum(taps, par)
                 sig_c = sigmoid(cv)
                 values = cv * sig_c
-                y = rf.y[0, slot(k), lanes]
+                y = part_of(rf, "y", k)[0, slot(k % per), lanes]
                 if gate:
-                    gate_in = rf.proj[0, slot(k), lanes]
+                    gate_in = part_of(rf, "proj", k)[0, slot(k % per), lanes]
                     sig_g = sigmoid(gate_in)
                     silu_g = gate_in * sig_g
                     scanned = y + par[6:7, :] * values
@@ -550,16 +563,16 @@
                     dmixed = (
                         jnp.dot(
                             dscore,
-                            rf.mixed[1, slot(k), :],
+                            rf.mixed_all[1, slot(k), :],
                             precision=HI,
                             preferred_element_type=F32,
                         ),
-                        dot_tn(dscore, rf.mixed[0, slot(k), :], HI),
+                        dot_tn(dscore, rf.mixed_all[0, slot(k), :], HI),
                     )
                     for c in range(2):
                         lanes = slice(c * LANES, (c + 1) * LANES)
                         par = rf.pbcv[:, lanes]
-                        taps = conv_taps(rf.pbc[slot(k), lanes])
+                        taps = conv_taps(part_of(rf, "pbc", k)[slot(k % per), lanes])
                         cv = conv_sum(taps, par)
                         sig = sigmoid(cv)
                         dcv = dmixed[c] * (sig * (1.0 + cv * (1.0 - sig)))
@@ -572,7 +585,7 @@
                     )
                     grad_step = rf.dstep[slot(k), :] + dlog * rf.dtp[1:2, :]
                     dt_sums[1] += column_sum(dlog * rf.step_all[slot(k), :])
-                    draw = grad_step * sigmoid(rf.pbc[slot(k), 256:384] + rf.dtp[0:1, :])
+                    draw = grad_step * sigmoid(part_of(rf, "pbc", k)[slot(k % per), 256:384] + rf.dtp[0:1, :])
                     draw = jnp.where(live, draw, 0.0)
                     dt_sums[0] += column_sum(draw)
                     rf.dbc[slot(k), 256:384] = draw.astype(BF16)
@@ -617,12 +630,14 @@
         if not scan:
             outs["dscan"] = lanes_by_step_out((ROWS, heads_cols), F32)
     if elementwise:
-        ins["proj"] = by_step(saved["proj"], (1, ROWS, 2 * WIDE))
-        ins["y"] = by_step(saved["y"], (1, ROWS, WIDE))
+        for n, part in enumerate(saved):
+            ins[f"proj{n}"] = by_step(part["proj"], (1, per * T, 2 * WIDE))
+            ins[f"y{n}"] = by_step(part["y"], (1, per * T, WIDE))
         ins["pv"] = lanes_by_step(pv)
         outs["small"] = by_step_out((PAIRS, 8, LANES), F32, (HALF, 8, LANES))
     if scan:
-        ins["pbc"] = whole(saved["pbc"])
+        for n, part in enumerate(saved):
+            ins[f"pbc{n}"] = whole(part["pbc"])
         ins["pbcv"] = whole(pbcv)
         ins["dtp"] = whole(dtp)
         if not gate:
@@ -632,7 +647,7 @@
         outs["small_bc"] = whole_out((2, 8, LANES), F32)
         outs["small_dt"] = whole_out((8, LANES), F32)
         scratch.update(
-            mixed=((2, ROWS, LANES), F32),
+            mixed_all=((2, ROWS, LANES), F32),
             scores=((SLOTS, T, T), F32),
             run_col=((2 * PAIRS, ROWS, LANES), F32),
             run_row=((SLOTS, T, LANES), F32),
@@ -652,7 +667,12 @@
     if gate or wgate or inp:
         scratch["sems"] = pltpu.SemaphoreType.DMA((2 * SLOTS + 4,))
     if wgate or wscan:
-        ins["normed"] = whole(saved["normed"])
+        if len(saved) == 1:
+            ins["normed"] = whole(saved[0]["normed"])
+        else:
+            for n, part in enumerate(saved):
+                ins[f"normed{n}"] = in_hbm(part["normed"])
+            scratch["normed"] = ((ROWS, width), BF16)
     if not gate and (wgate or inp):
         ins["dg"] = lanes_by_step(have["dg"])
     if wgate and not gate:
@@ -672,6 +692,42 @@
     if wscan:
         outs["gdt"] = whole_out((16, width), F32)
     return kernel_call(body, name, ins, outs, scratch, cost_us, limit)
+
+
+def owner_back(parts, x, gain, cot, branch, scale_out, mask, inner):
+    rows, width = x.shape
+
+    def body(*refs):
+        moved = refs[: len(parts)]
+        x, gain, cot, branch, scale_out, mask, sent, dmiddle, gain_grad = refs[len(parts) :]
+        grad = moved[0][...].astype(F32)
+        for p in moved[1:]:
+            grad = grad + p[...].astype(F32)
+        v = x[...].astype(F32)
+        scale = lax.rsqrt(jnp.mean(v * v, axis=1, keepdims=True) + EPS)
+        unit = v * scale
+        gain_grad[...] = column_sum(grad * unit)
+        dn = grad * gain[...]
+        dx = scale * (dn - unit * jnp.mean(dn * unit, axis=1, keepdims=True))
+        dm = (cot[...].astype(F32) + dx).astype(BF16)
+        dmiddle[...] = dm
+        g = mask[...] * dm.astype(F32)
+        sent[:, 0:width] = g.astype(BF16)
+        r = scale_out[...]
+        cross = r * r * jnp.sum(g * branch[...], axis=1, keepdims=True) / inner
+        sent[:, width:] = in_lanes([r, cross])
+
+    return pl.pallas_call(
+        body,
+        out_shape=[
+            jax.ShapeDtypeStruct((rows, width + LANES), BF16),
+            jax.ShapeDtypeStruct((rows, width), BF16),
+            jax.ShapeDtypeStruct((1, width), F32),
+        ],
+        compiler_params=pltpu.CompilerParams(vmem_limit_bytes=VMEM_MOST),
+        cost_estimate=pl.CostEstimate(flops=1 << 30, bytes_accessed=1 << 20, transcendentals=0),
+        name="owner_back",
+    )(*parts, x, gain, cot, branch, scale_out, mask)
 
 
 def assemble(parts, dt_rows, shard):
@@ -845,10 +901,14 @@
 
         cuts = [columns_of((j + k) % SLOTS) for k in range(SLOTS)]
         o_own = lax.dynamic_slice(out_weight[0], (piece * d, 0), (piece, width))
-        o_other = swap_section(o_own)
+        o_cut = jnp.transpose(o_own.reshape(piece, SLOTS, quarter), (1, 0, 2))
+        first_cut = jnp.concatenate([cuts[0], o_cut.reshape(-1, quarter)], axis=0)
 
         w_own = [send_shard(cuts[k], k) for k in range(SLOTS)]
-        w_other = [send_across(cuts[k], k) for k in range(SLOTS)]
+        w_other = [send_across(first_cut if k == 0 else cuts[k], k) for k in range(SLOTS)]
+        w_other[0], o_other = w_other[0][: cuts[0].shape[0]], w_other[0][cuts[0].shape[0] :]
+        o_other = jnp.transpose(o_other.reshape(SLOTS, piece, quarter), (1, 0, 2))
+        o_other = o_other.reshape(piece, width)
 
         def from_parts(parts, others, o, o_others, own):
             pieces = [jnp.where(own, p, q) for p, q in zip(parts, others)]
@@ -939,10 +999,17 @@
     scale0 = lax.rsqrt(square / inner + EPS)
     branch0 = branch[:, :width] * scale0
     middle = (x_f + mask * branch0).astype(BF16)
+    saved0 = [saved0]
 
     m_slots = gather_slots(middle)
-    branch_parts, saved1 = forward_layer(m_slots, g1_slots, gain1, layer1)
-    own = saved1["stats"][:, 0].reshape(2, SLOTS, T)
+    branch_parts, saved1 = forward_layer(m_slots[:2], g1_slots[:2], gain1, layer1)
+    m_slots[2], m_slots[3], saved1["stats"] = lax.optimization_barrier(
+        (m_slots[2], m_slots[3], saved1["stats"])
+    )
+    more_parts, more1 = forward_layer(m_slots[2:], g1_slots[2:], gain1, layer1)
+    branch_parts = branch_parts + more_parts
+    saved1 = [saved1, more1]
+    own = jnp.concatenate([v["stats"][:, 0].reshape(2, 2, T) for v in saved1], axis=1)
     back = [send_shard(own, k) for k in range(SLOTS)]
     summed = sum(jnp.roll(back[k], -k, axis=1) for k in range(SLOTS))
     scale1 = lax.rsqrt(summed[0] / inner + EPS)
@@ -966,14 +1033,12 @@
         VMEM_BACK,
     )
     moved = [send_shard(back1[f"out{k}"], k) for k in range(SLOTS)]
-    dx, gain_grad1 = norm_back(middle.astype(F32), gain1, sum(p.astype(F32) for p in moved))
-    by_owner = lambda v: v.reshape(16, -1, width)
-    owned1 = lax.psum_scatter(by_owner(back1["ga"]), DP, scatter_dimension=0, tiled=False)
-
-    dmiddle = (cot.astype(F32) + dx).astype(BF16)
-    g0 = (mask * dmiddle.astype(F32)).astype(BF16)
-    cross0 = scale0 * scale0 * jnp.sum(g0.astype(F32) * branch0, axis=1, keepdims=True) / inner
-    g0_slots = gather_slots(jnp.concatenate([g0, in_lanes([scale0, cross0])], axis=1))
+    sent, dmiddle, gain_grad1 = owner_back(
+        moved, middle, gain1, cot, branch0, scale0, mask, inner
+    )
+    owned1 = back1["ga"].reshape(16, -1, width)
+    owned1 = lax.psum_scatter(owned1, DP, scatter_dimension=0, tiled=False)
+    g0_slots = gather_slots(sent)
     g0_slots, branch_parts = lax.optimization_barrier((g0_slots, branch_parts))
     branch = scatter_sum(branch_parts)[:, :width] * scale1[0][:, None]
     result = middle.astype(F32) + mask * branch

time: 452 us -> 459 us (1.015)
  starting transfers between devices: 86.2 us -> 79.6 us
  Pallas kernels: 94.5 us -> 101 us
  waiting for transfers between devices: 195 us -> 200 us
    ppermute x4, waiting for transfers between devices: 3.37 us -> 10.1 us  [send_across(): return lax.ppermute(v, ('section', 'shard'), pairs)]
    ppermute x39, starting transfers between devices: 54.4 us -> 49 us  [send_shard(): return lax.ppermute(v, 'shard', ring(SLOTS, k)) if k else v]
    unnamed x103 -> x126, local copies, waits for them, and re-layouts: 12.3 us -> 15.9 us
    pallas_call x6 -> x7, Pallas kernels: 84.5 us -> 87.5 us  [kernel_call(): pl.pallas_call(run, in_specs=[pl.BlockSpec(memory_space=pltpu.VMEM if len...]
    ppermute x3 -> x2, waiting for transfers between devices: 11.7 us -> 8.75 us  [swap_section(): return lax.ppermute(v, 'section', [(0, 1), (1, 0)])]
  transfers between devices with their start and end apart: 62 -> 61, of which waited for: 36 -> 39; matrix products, arithmetic and copies ran while one was open for 8% -> 8% of each run, Pallas kernels for 9% -> 12%
where the time goes in v9:
time: 459 us; the launch traced here: 451 us
  waiting for transfers between devices  200 us (44%)
  Pallas kernels  101 us (22%)
  starting transfers between devices  79.6 us (17%)
  local copies, waits for them, and re-layouts  34.4 us (7%)
  other arithmetic  19.6 us (4%)
  between operations  15.9 us (3%)
    ppermute x39, waiting for transfers between devices, send_shard(): return lax.ppermute(v, 'shard', ring(SLOTS, k)) if k else v  135 us
    pallas_call x7, Pallas kernels, kernel_call(): pl.pallas_call(run, in_specs=[pl.BlockSpec(memory_space=pltpu.VMEM if len...  87.5 us
    ppermute x39, starting transfers between devices, send_shard(): return lax.ppermute(v, 'shard', ring(SLOTS, k)) if k else v  49 us
    unnamed x126, local copies, waits for them, and re-layouts  15.9 us
    ppermute x1, waiting for transfers between devices, shards(): lax.ppermute(result.astype(BF16), 'section', [(0, 1)]).astype(F32)  10.7 us
    ppermute x1, waiting for transfers between devices, shards(): arrived = lax.ppermute(owned0, 'section', [(1, 0)]).reshape(10, 16, width)  10.1 us
    pallas_call x1, Pallas kernels, assemble(): pl.pallas_call(body, grid_spec=spec, out_shape=[jax.ShapeDtypeStruct((tot...  10.1 us
    ppermute x4, waiting for transfers between devices, send_across(): return lax.ppermute(v, ('section', 'shard'), pairs)  10.1 us
  transfers between devices with their start and end apart: 61, of which 39 were waited for; matrix products, arithmetic and copies ran while one was open for 8% of the time, Pallas kernels for 12%

profile of v9, /device:TPU:4, one launch (start us, length us, event | category | flops | bytes accessed | tf_op | source)
XLA Modules:
  0.0 450.8 jit_solution(18199367897404684338)
XLA Ops:
  13.1 5.7 %collective-permute-start.4 = (bf16[112,384]{1,0:T(8,128)(2,1)S(1)}, bf16[112,384]{1,0:T(8,128)(2,1)S(1)}, u32[]{:S(2)}, u32[]{:S(2)}) collective-permute-start(bf16[112,384]{1,0:T(8,128)(2,1)S(1)} %get-tuple-element.279), channel_id=1, source_target_pairs={{0,66},{1,67},{2,64},{3,65},{64,2},{65,3},{66,0},{67,1},{4,70},{5,... | collective-permute-start | bytes 258056 | tf_op jit(solution)/shard_map/weights/ppermute | solution.py:799
  20.6 7.1 %collective-permute-done = bf16[304,384]{1,0:T(8,128)(2,1)S(1)} collective-permute-done((bf16[304,384]{1,0:T(8,128)(2,1)S(1)}, bf16[304,384]{1,0:T(8,128)(2,1)S(1)}, u32[]{:S(2)}, u32[]{:S(2)}) %collective-permute-start) | collective-permute-done | bytes 233504 | tf_op jit(solution)/shard_map/weights/ppermute | solution.py:799
  42.5 8.1 %collective-permute-done.7.refs_1_ = bf16[128,1536]{1,0:T(8,128)(2,1)S(1)} collective-permute-done((bf16[128,1536]{1,0:T(8,128)(2,1)S(1)}, bf16[128,1536]{1,0:T(8,128)(2,1)S(1)}, u32[]{:S(2)}, u32[]{:S(2)}) %collective-permute-start.7) | collective-permute-done | bytes 393248 | tf_op jit(solution)/shard_map/weights/ppermute | solution.py:790
  69.9 7.0 %collective-permute-done.16 = bf16[4,187,128]{2,1,0:T(8,128)(2,1)S(1)} collective-permute-done((bf16[4,187,128]{2,1,0:T(8,128)(2,1)S(1)}, bf16[4,187,128]{2,1,0:T(8,128)(2,1)S(1)}, u32[]{:S(2)}, u32[]{:S(2)}) %collective-permute-start.16) | collective-permute-done | bytes 191520 | tf_op jit(solution)/shard_map/small_weights/ppermute | solution.py:803
  92.7 14.3 %layer_forward.3 = (bf16[128,1664]{1,0:T(8,128)(2,1)}, bf16[128,1664]{1,0:T(8,128)(2,1)}, bf16[128,1664]{1,0:T(8,128)(2,1)}, bf16[128,1664]{1,0:T(8,128)(2,1)}, ...) custom-call(bf16[128,1536]{1,0:T(8,128)(2,1)} %copy-done.11, ...), custom_call_target="tpu_custom_call" | custom-call | flops 17600000000 | bytes 1048576 | tf_op jit(solution)/shard_map/layer_forward/pallas_call | solution.py:156
  112.8 7.7 %collective-permute-done.17 = bf16[128,1664]{1,0:T(8,128)(2,1)S(1)} collective-permute-done((bf16[128,1664]{1,0:T(8,128)(2,1)}, bf16[128,1664]{1,0:T(8,128)(2,1)S(1)}, u32[]{:S(2)}, u32[]{:S(2)}) %collective-permute-start.17) | collective-permute-done | bytes 426016 | tf_op jit(solution)/shard_map/ppermute | solution.py:790
  120.5 10.1 %collective-permute-done.18 = bf16[128,1664]{1,0:T(8,128)(2,1)S(1)} collective-permute-done((bf16[128,1664]{1,0:T(8,128)(2,1)}, bf16[128,1664]{1,0:T(8,128)(2,1)S(1)}, u32[]{:S(2)}, u32[]{:S(2)}) %collective-permute-start.18) | collective-permute-done | bytes 426016 | tf_op jit(solution)/shard_map/ppermute | solution.py:790
  137.2 15.0 %collective-permute-done.22.refs_1_ = bf16[128,1536]{1,0:T(8,128)(2,1)S(1)} collective-permute-done((bf16[128,1536]{1,0:T(8,128)(2,1)S(1)}, bf16[128,1536]{1,0:T(8,128)(2,1)S(1)}, u32[]{:S(2)}, u32[]{:S(2)}) %collective-permute-start.22) | collective-permute-done | bytes 393248 | tf_op jit(solution)/shard_map/ppermute | solution.py:790
  153.0 9.4 %layer_forward.4 = (bf16[128,1664]{1,0:T(8,128)(2,1)}, bf16[128,1664]{1,0:T(8,128)(2,1)}, f32[2,8,256]{2,1,0:T(8,128)}, bf16[256,1536]{1,0:T(8,128)(2,1)}, f32[2...) custom-call(bf16[128,1536]{1,0:T(8,128)(2,1)} %copy-done.13, bf16[128,1536]{1,0:T(8,128)(2,1)} %copy-done.51, ...), custom_call_target="tpu_custom_call" | custom-call | flops 8800000000 | bytes 1048576 | tf_op jit(solution)/shard_map/layer_forward/pallas_call | solution.py:156
  163.3 9.4 %layer_forward.5 = (bf16[128,1664]{1,0:T(8,128)(2,1)}, bf16[128,1664]{1,0:T(8,128)(2,1)}, f32[2,8,256]{2,1,0:T(8,128)}, bf16[256,1536]{1,0:T(8,128)(2,1)}, f32[2...) custom-call(bf16[128,1536]{1,0:T(8,128)(2,1)} %copy-done.46, bf16[128,1536]{1,0:T(8,128)(2,1)} %copy-done.48, ...), custom_call_target="tpu_custom_call" | custom-call | flops 8800000000 | bytes 1048576 | tf_op jit(solution)/shard_map/layer_forward/pallas_call | solution.py:156
  183.2 28.3 %backward_1.1 = (bf16[512,768]{1,0:T(8,128)(2,1)}, bf16[512,768]{1,0:T(8,128)(2,1)}, f32[6,8,128]{2,1,0:T(8,128)}, bf16[512,768]{1,0:T(8,128)(2,1)}, bf16[512,38...) custom-call(bf16[128,1536]{1,0:T(8,128)(2,1)} %copy-done.18, ...), custom_call_target="tpu_custom_call" | custom-call | flops 30799998976 | bytes 1048576 | tf_op jit(solution)/shard_map/backward_1/pallas_call | solution.py:156
  217.9 12.8 %collective-permute-done.26.refs_1_ = bf16[128,1536]{1,0:T(8,128)(2,1)S(1)} collective-permute-done((bf16[128,1536]{1,0:T(8,128)(2,1)S(1)}, bf16[128,1536]{1,0:T(8,128)(2,1)S(1)}, u32[]{:S(2)}, u32[]{:S(2)}) %collective-permute-start.26) | collective-permute-done | bytes 393248 | tf_op jit(solution)/shard_map/ppermute | solution.py:790
  239.1 17.5 %collective-permute-done.29.refs_1_ = bf16[128,1664]{1,0:T(8,128)(2,1)S(1)} collective-permute-done((bf16[128,1664]{1,0:T(8,128)(2,1)}, bf16[128,1664]{1,0:T(8,128)(2,1)S(1)}, u32[]{:S(2)}, u32[]{:S(2)}) %collective-permute-start.29) | collective-permute-done | bytes 426016 | tf_op jit(solution)/shard_map/ppermute | solution.py:790
  265.8 10.5 %backward_0_gate.1 = (bf16[512,768]{1,0:T(8,128)(2,1)}, bf16[512,768]{1,0:T(8,128)(2,1)S(1)}, f32[512,768]{1,0:T(8,128)S(1)}, f32[6,8,128]{2,1,0:T(8,128)S(1)}, ...) custom-call(bf16[128,1664]{1,0:T(8,128)(2,1)S(1)} %copy-done.5, ...), custom_call_target="tpu_custom_call" | custom-call | flops 15399999488 | bytes 1048576 | tf_op jit(solution)/shard_map/backward_0_gate/pallas_call | solution.py:156
  276.5 10.9 %backward_0_scan.1 = (f32[6,8,128]{2,1,0:T(8,128)S(1)}, bf16[512,768]{1,0:T(8,128)(2,1)S(1)}, bf16[512,384]{1,0:T(8,128)(2,1)S(1)}, f32[2,8,128]{2,1,0:T(8,128)S...) custom-call(f32[2,512,768]{2,1,0:T(8,128)S(1)} %copy-done.7, ...), custom_call_target="tpu_custom_call" | custom-call | flops 22000001024 | bytes 1048576 | tf_op jit(solution)/shard_map/backward_0_scan/pallas_call | solution.py:156
  298.0 4.8 %backward_0_input.1 = (bf16[128,1536]{1,0:T(8,128)(2,1)S(1)}, bf16[128,1536]{1,0:T(8,128)(2,1)S(1)}, bf16[128,1536]{1,0:T(8,128)(2,1)S(1)}, bf16[128,1536]{1,0:T(8,128)(2,1)S(1)}) custom-call(bf16[128,1536]{1,0:T(8,128)(2,1)S(1)} %copy-done, bf16[16,10,16,1536]{3,2,1,0:T(8,128)(2,1)S(1)} %bitcast.186, bf16[512,768]{1,0:T(8,128)(2,1)S(1)} %get-tuple-element.181.refs_2_, ...), custom_call_target="tpu_custom_call" | custom-call | flops 9900000256 | bytes 1048576 | tf_op jit(solution)/shard_map/backward_0_input/pallas_call | solution.py:156
  309.5 15.0 %collective-permute-done.35 = bf16[128,1536]{1,0:T(8,128)(2,1)S(1)} collective-permute-done((bf16[128,1536]{1,0:T(8,128)(2,1)S(1)}, bf16[128,1536]{1,0:T(8,128)(2,1)S(1)}, u32[]{:S(2)}, u32[]{:S(2)}) %collective-permute-start.35) | collective-permute-done | bytes 393248 | tf_op jit(solution)/shard_map/ppermute | solution.py:790
  327.8 14.5 %collective-permute-done.38 = bf16[128,1664]{1,0:T(8,128)(2,1)} collective-permute-done((bf16[128,1664]{1,0:T(8,128)(2,1)S(1)}, bf16[128,1664]{1,0:T(8,128)(2,1)}, u32[]{:S(2)}, u32[]{:S(2)}) %collective-permute-start.38) | collective-permute-done | bytes 426016 | tf_op jit(solution)/shard_map/ppermute | solution.py:790
  344.5 6.7 %collective-permute-done.34 = bf16[160,1536]{1,0:T(8,128)(2,1)S(1)} collective-permute-done((bf16[160,1536]{1,0:T(8,128)(2,1)}, bf16[160,1536]{1,0:T(8,128)(2,1)S(1)}, u32[]{:S(2)}, u32[]{:S(2)}) %collective-permute-start.34) | collective-permute-done | bytes 491552 | tf_op jit(solution)/shard_map/ppermute | solution.py:1070
  355.0 10.1 %collective-permute-done.52 = bf16[160,1536]{1,0:T(8,128)(2,1)S(1)} collective-permute-done((bf16[160,1536]{1,0:T(8,128)(2,1)}, bf16[160,1536]{1,0:T(8,128)(2,1)S(1)}, u32[]{:S(2)}, u32[]{:S(2)}) %collective-permute-start.52) | collective-permute-done | bytes 491552 | tf_op jit(solution)/shard_map/ppermute | solution.py:1076
  385.3 5.5 %collective-permute-start.41 = (bf16[128,1536]{1,0:T(8,128)(2,1)S(1)}, bf16[128,1536]{1,0:T(8,128)(2,1)S(1)}, u32[]{:S(2)}, u32[]{:S(2)}) collective-permute-start(bf16[128,1536]{1,0:T(8,128)(2,1)S(1)} %convert_element_type.234), channel_id=1, source_target_pairs={{64,0},{65,1},{66,2},{67,3},{68,4},{69,5},{70,6},{71,7},{72,8},{73... | collective-permute-start | bytes 1179656 | tf_op jit(solution)/shard_map/ppermute | solution.py:1092
  394.1 10.7 %collective-permute-done.42 = bf16[128,1536]{1,0:T(8,128)(2,1)S(1)} collective-permute-done((bf16[128,1536]{1,0:T(8,128)(2,1)S(1)}, bf16[128,1536]{1,0:T(8,128)(2,1)S(1)}, u32[]{:S(2)}, u32[]{:S(2)}) %collective-permute-start.42) | collective-permute-done | bytes 393248 | tf_op jit(solution)/shard_map/ppermute | solution.py:1091
  408.6 8.9 %collective-permute-done.48 = f32[276,128]{1,0:T(8,128)S(1)} collective-permute-done((f32[276,128]{1,0:T(8,128)S(1)}, f32[276,128]{1,0:T(8,128)S(1)}, u32[]{:S(2)}, u32[]{:S(2)}) %collective-permute-start.48) | collective-permute-done | bytes 141344 | tf_op jit(solution)/shard_map/ppermute | solution.py:841
  433.7 10.1 %assemble.1 = (f32[6448,384]{1,0:T(8,128)}, f32[768,1536]{1,0:T(8,128)}) custom-call(s32[1]{0:T(128)} %bitcast.78._, bf16[16,592,384]{2,1,0:T(8,128)(2,1)} %bitcast.187, bf16[16,592,384]{2,1,0:T(8,128)(2,1)} %bitcast.188, bf16[16,592,384]{2,1,0:T(8,128)(2,1)} %bitcast.189, f32[48,384]{1,0:T(8,128)} %reshape.494.dt), custom_call_target="tpu_custom_call" | custom-call | tf_op jit(solution)/shard_map/assemble/pallas_call | solution.py:773
  (408 shorter events, 174.9 us)
Async XLA Ops:
  7.2 85.0 %all-gather.7.cloned.1.call-start = ((), (), s32[]{:S(2)}) async-start(), calls=%async_computation.4 | async-start | bytes 8355840 | tf_op jit(solution)/shard_map/weights/all_gather | solution.py:928
  9.1 20.1 %collective-permute-start.1 = (bf16[112,384]{1,0:T(8,128)(2,1)S(1)}, bf16[112,384]{1,0:T(8,128)(2,1)S(1)}, u32[]{:S(2)}, u32[]{:S(2)}) collective-permute-start(bf16[112,384]{1,0:T(8,128)(2,1)S(1)} %get-tuple-element.278), channel_id=1, source_target_pairs={{0,3},{1,0},{2,1},{3,2},{4,7},{5,4},{6,5},{7,6},{8,11},{9,8},{10,9... | collective-permute-start | bytes 258056 | tf_op jit(solution)/shard_map/weights/ppermute | solution.py:790
  12.2 19.0 %collective-permute-start.2 = (bf16[112,384]{1,0:T(8,128)(2,1)S(1)}, bf16[112,384]{1,0:T(8,128)(2,1)S(1)}, u32[]{:S(2)}, u32[]{:S(2)}) collective-permute-start(bf16[112,384]{1,0:T(8,128)(2,1)S(1)} %get-tuple-element.278), channel_id=1, source_target_pairs={{0,67},{1,64},{2,65},{3,66},{64,3},{65,0},{66,1},{67,2},{4,71},{5,... | collective-permute-start | bytes 258056 | tf_op jit(solution)/shard_map/weights/ppermute | solution.py:799
  38.7 113.5 %all-gather.9.cloned.1.call-start = ((), (), s32[]{:S(2)}) async-start(), calls=%async_computation.5 | async-start | bytes 8355840 | tf_op jit(solution)/shard_map/all_gather | solution.py:986
  67.0 19.4 %collective-permute-start.10 = (bf16[128,1536]{1,0:T(8,128)(2,1)S(1)}, bf16[128,1536]{1,0:T(8,128)(2,1)S(1)}, u32[]{:S(2)}, u32[]{:S(2)}) collective-permute-start(bf16[128,1536]{1,0:T(8,128)(2,1)S(1)} %multiply_convert_fusion.refs_2_.refs_0_), channel_id=1, source_target_pairs={{0,3},{1,0},{2,1},{3,2},{4,7},{5,4},{6,5},{7,6},{8,11},{9,8},{10,9... | collective-permute-start | bytes 1179656 | tf_op jit(solution)/shard_map/ppermute | solution.py:790
  92.2 234.1 %reduce-scatter.5.cloned.1.call-start = ((), (), s32[]{:S(2)}) async-start(), calls=%async_computation.3 | async-start | bytes 8355840 | tf_op jit(solution)/shard_map/reduce_scatter | solution.py:1040
  108.6 22.0 %collective-permute-start.18 = (bf16[128,1664]{1,0:T(8,128)(2,1)}, bf16[128,1664]{1,0:T(8,128)(2,1)S(1)}, u32[]{:S(2)}, u32[]{:S(2)}) collective-permute-start(bf16[128,1664]{1,0:T(8,128)(2,1)} %get-tuple-element.135), channel_id=1, source_target_pairs={{0,2},{1,3},{2,0},{3,1},{4,6},{5,7},{6,4},{7,5},{8,10},{9,11},{10,... | collective-permute-start | bytes 1277960 | tf_op jit(solution)/shard_map/ppermute | solution.py:790
  111.3 19.3 %collective-permute-start.19 = (bf16[128,1664]{1,0:T(8,128)(2,1)}, bf16[128,1664]{1,0:T(8,128)(2,1)S(1)}, u32[]{:S(2)}, u32[]{:S(2)}) collective-permute-start(bf16[128,1664]{1,0:T(8,128)(2,1)} %get-tuple-element.136), channel_id=1, source_target_pairs={{0,3},{1,0},{2,1},{3,2},{4,7},{5,4},{6,5},{7,6},{8,11},{9,8},{10,9... | collective-permute-start | bytes 1277960 | tf_op jit(solution)/shard_map/ppermute | solution.py:790
  133.0 19.3 %collective-permute-start.22 = (bf16[128,1536]{1,0:T(8,128)(2,1)S(1)}, bf16[128,1536]{1,0:T(8,128)(2,1)S(1)}, u32[]{:S(2)}, u32[]{:S(2)}) collective-permute-start(bf16[128,1536]{1,0:T(8,128)(2,1)S(1)} %get-tuple-element.214.refs_0_.refs_4_), channel_id=1, source_target_pairs={{0,3},{1,0},{2,1},{3,2},{4,7},{5,4},{6,5},{7,6},{8,11},{9,8},{10,9... | collective-permute-start | bytes 1179656 | tf_op jit(solution)/shard_map/ppermute | solution.py:790
  135.3 27.1 %collective-permute-start.20 = (bf16[128,1536]{1,0:T(8,128)(2,1)S(1)}, bf16[128,1536]{1,0:T(8,128)(2,1)S(1)}, u32[]{:S(2)}, u32[]{:S(2)}) collective-permute-start(bf16[128,1536]{1,0:T(8,128)(2,1)S(1)} %get-tuple-element.214.refs_0_.refs_4_), channel_id=1, source_target_pairs={{0,2},{1,3},{2,0},{3,1},{4,6},{5,7},{6,4},{7,5},{8,10},{9,11},{10,... | collective-permute-start | bytes 1179656 | tf_op jit(solution)/shard_map/ppermute | solution.py:790
  136.4 26.0 %collective-permute-start.21 = (bf16[128,1536]{1,0:T(8,128)(2,1)S(1)}, bf16[128,1536]{1,0:T(8,128)(2,1)S(1)}, u32[]{:S(2)}, u32[]{:S(2)}) collective-permute-start(bf16[128,1536]{1,0:T(8,128)(2,1)S(1)} %get-tuple-element.214.refs_0_.refs_4_), channel_id=1, source_target_pairs={{0,1},{1,2},{2,3},{3,0},{4,5},{5,6},{6,7},{7,4},{8,9},{9,10},{10,1... | collective-permute-start | bytes 1179656 | tf_op jit(solution)/shard_map/ppermute | solution.py:790
  211.6 139.7 %reduce-scatter.3.cloned.1.call-start = ((), (), s32[]{:S(2)}) async-start(), calls=%async_computation.2 | async-start | bytes 4423680 | tf_op jit(solution)/shard_map/reduce_scatter | solution.py:1064
  235.6 21.0 %collective-permute-start.29 = (bf16[128,1664]{1,0:T(8,128)(2,1)}, bf16[128,1664]{1,0:T(8,128)(2,1)S(1)}, u32[]{:S(2)}, u32[]{:S(2)}) collective-permute-start(bf16[128,1664]{1,0:T(8,128)(2,1)} %get-tuple-element.165.refs_0_), channel_id=1, source_target_pairs={{0,3},{1,0},{2,1},{3,2},{4,7},{5,4},{6,5},{7,6},{8,11},{9,8},{10,9... | collective-permute-start | bytes 1277960 | tf_op jit(solution)/shard_map/ppermute | solution.py:790
  238.0 18.5 %collective-permute-start.30 = (bf16[128,1664]{1,0:T(8,128)(2,1)}, bf16[128,1664]{1,0:T(8,128)(2,1)S(1)}, u32[]{:S(2)}, u32[]{:S(2)}) collective-permute-start(bf16[128,1664]{1,0:T(8,128)(2,1)} %get-tuple-element.165.refs_0_), channel_id=1, source_target_pairs={{0,2},{1,3},{2,0},{3,1},{4,6},{5,7},{6,4},{7,5},{8,10},{9,11},{10,... | collective-permute-start | bytes 1277960 | tf_op jit(solution)/shard_map/ppermute | solution.py:790
  238.0 22.0 %collective-permute-start.31 = (bf16[128,1664]{1,0:T(8,128)(2,1)}, bf16[128,1664]{1,0:T(8,128)(2,1)S(1)}, u32[]{:S(2)}, u32[]{:S(2)}) collective-permute-start(bf16[128,1664]{1,0:T(8,128)(2,1)} %get-tuple-element.165.refs_0_), channel_id=1, source_target_pairs={{0,1},{1,2},{2,3},{3,0},{4,5},{5,6},{6,7},{7,4},{8,9},{9,10},{10,1... | collective-permute-start | bytes 1277960 | tf_op jit(solution)/shard_map/ppermute | solution.py:790
  293.8 139.9 %all-gather.11.cloned.1.call-start = ((), (), s32[]{:S(2)}) async-start(), calls=%async_computation.6 | async-start | bytes 7729152 | tf_op jit(solution)/shard_map/all_gather | solution.py:1102
  302.8 21.6 %collective-permute-start.35 = (bf16[128,1536]{1,0:T(8,128)(2,1)S(1)}, bf16[128,1536]{1,0:T(8,128)(2,1)S(1)}, u32[]{:S(2)}, u32[]{:S(2)}) collective-permute-start(bf16[128,1536]{1,0:T(8,128)(2,1)S(1)} %get-tuple-element.185), channel_id=1, source_target_pairs={{0,1},{1,2},{2,3},{3,0},{4,5},{5,6},{6,7},{7,4},{8,9},{9,10},{10,1... | collective-permute-start | bytes 1179656 | tf_op jit(solution)/shard_map/ppermute | solution.py:790
  302.9 21.6 %collective-permute-start.36 = (bf16[128,1536]{1,0:T(8,128)(2,1)S(1)}, bf16[128,1536]{1,0:T(8,128)(2,1)S(1)}, u32[]{:S(2)}, u32[]{:S(2)}) collective-permute-start(bf16[128,1536]{1,0:T(8,128)(2,1)S(1)} %get-tuple-element.186), channel_id=1, source_target_pairs={{0,2},{1,3},{2,0},{3,1},{4,6},{5,7},{6,4},{7,5},{8,10},{9,11},{10,... | collective-permute-start | bytes 1179656 | tf_op jit(solution)/shard_map/ppermute | solution.py:790
  305.1 20.3 %collective-permute-start.37 = (bf16[128,1536]{1,0:T(8,128)(2,1)S(1)}, bf16[128,1536]{1,0:T(8,128)(2,1)S(1)}, u32[]{:S(2)}, u32[]{:S(2)}) collective-permute-start(bf16[128,1536]{1,0:T(8,128)(2,1)S(1)} %get-tuple-element.187), channel_id=1, source_target_pairs={{0,3},{1,0},{2,1},{3,2},{4,7},{5,4},{6,5},{7,6},{8,11},{9,8},{10,9... | collective-permute-start | bytes 1179656 | tf_op jit(solution)/shard_map/ppermute | solution.py:790
  306.1 36.1 %collective-permute-start.38 = (bf16[128,1664]{1,0:T(8,128)(2,1)S(1)}, bf16[128,1664]{1,0:T(8,128)(2,1)}, u32[]{:S(2)}, u32[]{:S(2)}) collective-permute-start(bf16[128,1664]{1,0:T(8,128)(2,1)S(1)} %copy-done.36), channel_id=1, source_target_pairs={{0,1},{1,2},{2,3},{3,0},{4,5},{5,6},{6,7},{7,4},{8,9},{9,10},{10,1... | collective-permute-start | bytes 1277960 | tf_op jit(solution)/shard_map/ppermute | solution.py:790
  307.2 35.1 %collective-permute-start.39 = (bf16[128,1664]{1,0:T(8,128)(2,1)}, bf16[128,1664]{1,0:T(8,128)(2,1)}, u32[]{:S(2)}, u32[]{:S(2)}) collective-permute-start(bf16[128,1664]{1,0:T(8,128)(2,1)} %get-tuple-element.191), channel_id=1, source_target_pairs={{0,2},{1,3},{2,0},{3,1},{4,6},{5,7},{6,4},{7,5},{8,10},{9,11},{10,... | collective-permute-start | bytes 1277960 | tf_op jit(solution)/shard_map/ppermute | solution.py:790
  326.3 24.9 %collective-permute-start.34 = (bf16[160,1536]{1,0:T(8,128)(2,1)}, bf16[160,1536]{1,0:T(8,128)(2,1)S(1)}, u32[]{:S(2)}, u32[]{:S(2)}) collective-permute-start(bf16[160,1536]{1,0:T(8,128)(2,1)} %bitcast.210), channel_id=1, source_target_pairs={{0,64},{1,65},{2,66},{3,67},{4,68},{5,69},{6,70},{7,71},{8,72},{9,... | collective-permute-start | bytes 1474568 | tf_op jit(solution)/shard_map/ppermute | solution.py:1070
  382.1 22.7 %collective-permute-start.42 = (bf16[128,1536]{1,0:T(8,128)(2,1)S(1)}, bf16[128,1536]{1,0:T(8,128)(2,1)S(1)}, u32[]{:S(2)}, u32[]{:S(2)}) collective-permute-start(bf16[128,1536]{1,0:T(8,128)(2,1)S(1)} %convert_element_type.235), channel_id=1, source_target_pairs={{0,64},{1,65},{2,66},{3,67},{4,68},{5,69},{6,70},{7,71},{8,72},{9,... | collective-permute-start | bytes 1179656 | tf_op jit(solution)/shard_map/ppermute | solution.py:1091
  385.3 23.3 %collective-permute-start.41 = (bf16[128,1536]{1,0:T(8,128)(2,1)S(1)}, bf16[128,1536]{1,0:T(8,128)(2,1)S(1)}, u32[]{:S(2)}, u32[]{:S(2)}) collective-permute-start(bf16[128,1536]{1,0:T(8,128)(2,1)S(1)} %convert_element_type.234), channel_id=1, source_target_pairs={{64,0},{65,1},{66,2},{67,3},{68,4},{69,5},{70,6},{71,7},{72,8},{73... | collective-permute-start | bytes 1179656 | tf_op jit(solution)/shard_map/ppermute | solution.py:1092
  (90 other events, 1143.8 us)
Sparse Core Ops, SparseCore 0:
  38.8 53.3 all-gather.6
  94.5 50.8 all-gather.8
  211.7 73.1 reduce-scatter.4
  293.9 49.4 reduce-scatter.2
  377.3 56.3 all-gather.10

commit v10 on v8

--- a/solution.py
+++ b/solution.py
@@ -674,12 +674,12 @@
     return kernel_call(body, name, ins, outs, scratch, cost_us, limit)
 
 
-def assemble(parts, dt_rows, shard):
+def assemble(parts, dt_rows):
     quarter = parts.shape[2]
     block = 16 * 48
     total = 8 * block + 16 * 16 + dt_rows.shape[0]
 
-    def body(_, inw, outw, shared, dt, grad_in, grad_out):
+    def body(inw, outw, shared, dt, grad_in, grad_out):
         i = pl.program_id(0)
 
         @pl.when(i < 8)
@@ -697,33 +697,29 @@
             grad_in[256 : 256 + dt_rows.shape[0], :] = dt[...]
 
     last = SLOTS - 1
-    spec = pltpu.PrefetchScalarGridSpec(
-        num_scalar_prefetch=1,
+    return pl.pallas_call(
+        body,
         grid=(9,),
         in_specs=[
             pl.BlockSpec(
                 (16, 48, quarter),
-                lambda i, j: (0, jnp.where(i < SLOTS, 0, 8) + (j[0] + 3 * SLOTS - i) % SLOTS, 0),
+                lambda i: (0, jnp.where(i < SLOTS, i, jnp.minimum(i + SLOTS, 11)), 0),
             ),
-            pl.BlockSpec((16, 48, quarter), lambda i, j: (0, SLOTS + jnp.minimum(i, last), 0)),
-            pl.BlockSpec((16, 16, quarter), lambda i, j: (0, 36, 0)),
-            pl.BlockSpec(dt_rows.shape, lambda i, j: (0, 0)),
+            pl.BlockSpec((16, 48, quarter), lambda i: (0, SLOTS + jnp.minimum(i, last), 0)),
+            pl.BlockSpec((16, 16, quarter), lambda i: (0, 36, 0)),
+            pl.BlockSpec(dt_rows.shape, lambda i: (0, 0)),
         ],
         out_specs=[
-            pl.BlockSpec((block, quarter), lambda i, j: (i, 0)),
-            pl.BlockSpec((block, quarter), lambda i, j: (0, jnp.minimum(i, last))),
+            pl.BlockSpec((block, quarter), lambda i: (i, 0)),
+            pl.BlockSpec((block, quarter), lambda i: (0, jnp.minimum(i, last))),
         ],
-    )
-    return pl.pallas_call(
-        body,
-        grid_spec=spec,
         out_shape=[
             jax.ShapeDtypeStruct((total, quarter), F32),
             jax.ShapeDtypeStruct((block, SLOTS * quarter), F32),
         ],
         compiler_params=pltpu.CompilerParams(vmem_limit_bytes=VMEM_MOST),
         name="assemble",
-    )(shard.astype(jnp.int32)[None], parts, parts, parts, dt_rows)
+    )(parts, parts, parts, dt_rows)
 
 
 def ring(n, k):
@@ -734,13 +730,8 @@
     return lax.ppermute(v, "shard", ring(SLOTS, k)) if k else v
 
 
-def send_across(v, k):
-    pairs = [
-        (sec * SLOTS + y, (1 - sec) * SLOTS + (y + k) % SLOTS)
-        for sec in range(2)
-        for y in range(SLOTS)
-    ]
-    return lax.ppermute(v, ("section", "shard"), pairs)
+def across(v):
+    return lax.all_to_all(v, ("section", "shard"), 0, 0)
 
 
 def swap_section(v):
@@ -843,27 +834,17 @@
                 axis=0,
             )
 
-        cuts = [columns_of((j + k) % SLOTS) for k in range(SLOTS)]
+        cuts = jnp.stack([columns_of(y) for y in range(SLOTS)])
+        got = across(jnp.concatenate([cuts, cuts], axis=0))
         o_own = lax.dynamic_slice(out_weight[0], (piece * d, 0), (piece, width))
         o_other = swap_section(o_own)
 
-        w_own = [send_shard(cuts[k], k) for k in range(SLOTS)]
-        w_other = [send_across(cuts[k], k) for k in range(SLOTS)]
-
-        def from_parts(parts, others, o, o_others, own):
-            pieces = [jnp.where(own, p, q) for p, q in zip(parts, others)]
-            lanes = []
-            for y in range(SLOTS):
-                v = pieces[0]
-                for k in range(1, SLOTS):
-                    v = jnp.where((j - y) % SLOTS == k, pieces[k], v)
-                lanes.append(v)
-            return jnp.concatenate(
-                [jnp.where(own, o, o_others), jnp.concatenate(lanes, axis=1)], axis=0
-            )
-
-        w0 = from_parts(w_own, w_other, o_own, o_other, first)
-        w1 = from_parts(w_own, w_other, o_own, o_other, ~first)
+        def whole_rows(layer, own):
+            rows = jnp.concatenate([got[SLOTS * layer + y] for y in range(SLOTS)], axis=1)
+            return jnp.concatenate([jnp.where(own, o_own, o_other), rows], axis=0)
+
+        w0 = whole_rows(0, first)
+        w1 = whole_rows(1, ~first)
         w0, w1, x_own, cot = lax.optimization_barrier((w0, w1, x_own, cot))
         w0 = lax.all_gather(w0, DP, axis=0, tiled=False)
         x_slots = gather_slots(x_own)
@@ -1002,27 +983,10 @@
     moved0 = [send_shard(back0[f"out{k}"], k) for k in range(SLOTS)]
     dx, gain_grad0 = norm_back(x_f, gain0, sum(p.astype(F32) for p in moved0))
     dtokens = dmiddle.astype(F32) + dx
-    owned1 = owned1 + lax.ppermute(owned1, "section", [(0, 1)])
     owned0, owned1, gain_grad0, dtokens, result = lax.optimization_barrier(
         (owned0, owned1, gain_grad0, dtokens, result)
     )
 
-    kept = jnp.where(first, owned0, owned1).reshape(10, 16, width)
-    arrived = lax.ppermute(owned0, "section", [(1, 0)]).reshape(10, 16, width)
-
-    def total_of(cut):
-        return (cut(kept).astype(F32) + cut(arrived).astype(F32)).astype(BF16)
-
-    row_slots = []
-    for k in range(SLOTS):
-
-        def cut(v):
-            v = lax.dynamic_slice_in_dim(v, quarter * ((j + k) % SLOTS), quarter, 2)
-            return jnp.concatenate([v[:3], v[6:]], axis=0)
-
-        row_slots.append(send_shard(total_of(cut).reshape(-1, quarter), k))
-    out_rows = total_of(lambda v: v[3:6])
-    out_rows = jnp.transpose(out_rows.reshape(piece, SLOTS, quarter), (1, 0, 2))
     result_moved = lax.ppermute(result.astype(BF16), "section", [(0, 1)]).astype(F32)
     dtokens_moved = lax.ppermute(dtokens.astype(BF16), "section", [(1, 0)]).astype(F32)
     ends = jnp.where(
@@ -1033,13 +997,24 @@
         kept = jnp.where(first, v0, v1).astype(F32)
         return kept + swap_section(jnp.where(first, v1, v0)).astype(F32)
 
-    shared = sum(v[2 * piece :].astype(F32) for v in row_slots).astype(BF16)
+    def by_row(v):
+        rows = jnp.concatenate([v[:piece], v[2 * piece :]], axis=0)
+        return jnp.transpose(rows.reshape(-1, SLOTS, quarter), (1, 0, 2))
+
+    got = across(jnp.concatenate([by_row(owned0), by_row(owned1)], axis=0))
+    out_rows = to_section(owned0[piece : 2 * piece], owned1[piece : 2 * piece]).astype(BF16)
+    out_rows = jnp.transpose(out_rows.reshape(piece, SLOTS, quarter), (1, 0, 2))
+    rows = got[:SLOTS].astype(F32) + got[SLOTS:].astype(F32)
+    shared = jnp.sum(rows[:, 2 * piece :], axis=0).astype(BF16)
+    rows = rows.astype(BF16)
     gathered = lax.all_gather(
         jnp.concatenate(
-            [v[:piece] for v in row_slots]
-            + [out_rows.reshape(-1, quarter)]
-            + [v[piece : 2 * piece] for v in row_slots]
-            + [shared],
+            [
+                rows[:, :piece].reshape(-1, quarter),
+                out_rows.reshape(-1, quarter),
+                rows[:, piece : 2 * piece].reshape(-1, quarter),
+                shared,
+            ],
             axis=0,
         ),
         DP,
@@ -1078,7 +1053,7 @@
     conv_own = lax.dynamic_slice(conv_total, (0, channels * j), (5, channels))
     grad_skip = jnp.sum(by_pair[6].reshape(heads, HEAD), axis=1)
 
-    grad_in_weight, grad_out_weight = assemble(gathered, dt_rows, j)
+    grad_in_weight, grad_out_weight = assemble(gathered, dt_rows)
     return (
         ends,
         lax.dynamic_slice(gain_total, (quarter * j,), (quarter,))[None],

time: 452 us -> 515 us (1.14)
  waiting for transfers between devices: 195 us -> 265 us
  starting transfers between devices: 86.2 us -> 74.2 us
  other arithmetic: 21.7 us -> 29 us
    reduce_scatter x1, waiting for transfers between devices: 0.02 us -> 75.6 us  [shards(): lax.psum_scatter(by_owner(back1['ga']), DP, scatter_dimension=0, tiled=Fa...]
    ppermute x6 -> x0, waiting for transfers between devices: 19.9 us -> none  [the longest x1 10.2 us: shards(): arrived = lax.ppermute(owned0, 'section', [(1, 0)]).reshape(10, 16, width)]
    all_to_all x0 -> x2, starting transfers between devices: none -> 14.8 us  [across(): return lax.all_to_all(v, ('section', 'shard'), 0, 0)]
    ppermute x6 -> x0, starting transfers between devices: 14.2 us -> none  [the longest x4 9.45 us: send_across(): return lax.ppermute(v, ('section', 'shard'), pairs)]
    ppermute x39 -> x33, starting transfers between devices: 54.4 us -> 42.5 us  [send_shard(): return lax.ppermute(v, 'shard', ring(SLOTS, k)) if k else v]
    ppermute x3 -> x4, waiting for transfers between devices: 11.7 us -> 19.8 us  [swap_section(): return lax.ppermute(v, 'section', [(0, 1), (1, 0)])]
    all_to_all x0 -> x2, waiting for transfers between devices: none -> 6.96 us  [across(): return lax.all_to_all(v, ('section', 'shard'), 0, 0)]
    ppermute x39 -> x33, waiting for transfers between devices: 132 us -> 135 us  [send_shard(): return lax.ppermute(v, 'shard', ring(SLOTS, k)) if k else v]
  transfers between devices with their start and end apart: 62 -> 53, of which waited for: 36 -> 36; matrix products, arithmetic and copies ran while one was open for 8% -> 6% of each run, Pallas kernels for 9% -> 6%
where the time goes in v10:
time: 515 us; the launch traced here: 509 us
  waiting for transfers between devices  265 us (51%)
  Pallas kernels  94.5 us (18%)
  starting transfers between devices  74.2 us (14%)
  local copies, waits for them, and re-layouts  30.8 us (6%)
  other arithmetic  29 us (6%)
  between operations  15.5 us (3%)
    ppermute x33, waiting for transfers between devices, send_shard(): return lax.ppermute(v, 'shard', ring(SLOTS, k)) if k else v  135 us
    pallas_call x6, Pallas kernels, kernel_call(): pl.pallas_call(run, in_specs=[pl.BlockSpec(memory_space=pltpu.VMEM if len...  84.6 us
    reduce_scatter x1, waiting for transfers between devices, shards(): lax.psum_scatter(by_owner(back1['ga']), DP, scatter_dimension=0, tiled=Fa...  75.6 us
    ppermute x33, starting transfers between devices, send_shard(): return lax.ppermute(v, 'shard', ring(SLOTS, k)) if k else v  42.5 us
    ppermute x4, waiting for transfers between devices, swap_section(): return lax.ppermute(v, 'section', [(0, 1), (1, 0)])  19.8 us
    all_to_all x2, starting transfers between devices, across(): return lax.all_to_all(v, ('section', 'shard'), 0, 0)  14.8 us
    unnamed x100, local copies, waits for them, and re-layouts  10.9 us
  transfers between devices with their start and end apart: 53, of which 36 were waited for; matrix products, arithmetic and copies ran while one was open for 6% of the time, Pallas kernels for 6%

profile of v10, /device:TPU:4, one launch (start us, length us, event | category | flops | bytes accessed | tf_op | source)
XLA Modules:
  0.0 508.7 jit_solution(10452722425167071196)
XLA Ops:
  14.1 7.4 %all-to-all-start = ((bf16[8,112,384]{2,1,0:T(8,128)(2,1)}), bf16[8,112,384]{2,1,0:T(8,128)(2,1)S(1)}, u32[]{:S(2)}, u32[]{:S(2)}) async-start(bf16[8,112,384]{2,1,0:T(8,128)(2,1)} %fusion.25), calls=%async_computation | async-start | bytes 1376256 | tf_op jit(solution)/shard_map/weights/all_to_all | solution.py:734
  23.7 8.9 %collective-permute-done = bf16[48,1536]{1,0:T(8,128)(2,1)S(1)} collective-permute-done((bf16[48,1536]{1,0:T(8,128)(2,1)S(1)}, bf16[48,1536]{1,0:T(8,128)(2,1)S(1)}, u32[]{:S(2)}, u32[]{:S(2)}) %collective-permute-start) | collective-permute-done | bytes 147488 | tf_op jit(solution)/shard_map/weights/ppermute | solution.py:738
  41.2 12.3 %collective-permute-done.1.refs_1_ = bf16[128,1536]{1,0:T(8,128)(2,1)S(1)} collective-permute-done((bf16[128,1536]{1,0:T(8,128)(2,1)S(1)}, bf16[128,1536]{1,0:T(8,128)(2,1)S(1)}, u32[]{:S(2)}, u32[]{:S(2)}) %collective-permute-start.1) | collective-permute-done | bytes 393248 | tf_op jit(solution)/shard_map/weights/ppermute | solution.py:730
  71.2 6.5 %collective-permute-done.10 = bf16[4,187,128]{2,1,0:T(8,128)(2,1)S(1)} collective-permute-done((bf16[4,187,128]{2,1,0:T(8,128)(2,1)S(1)}, bf16[4,187,128]{2,1,0:T(8,128)(2,1)S(1)}, u32[]{:S(2)}, u32[]{:S(2)}) %collective-permute-start.10) | collective-permute-done | bytes 191520 | tf_op jit(solution)/shard_map/small_weights/ppermute | solution.py:738
  91.3 14.3 %layer_forward.2 = (bf16[128,1664]{1,0:T(8,128)(2,1)}, bf16[128,1664]{1,0:T(8,128)(2,1)}, bf16[128,1664]{1,0:T(8,128)(2,1)}, bf16[128,1664]{1,0:T(8,128)(2,1)}, ...) custom-call(bf16[128,1536]{1,0:T(8,128)(2,1)} %copy-done.11, ...), custom_call_target="tpu_custom_call" | custom-call | flops 19800000512 | bytes 1048576 | tf_op jit(solution)/shard_map/layer_forward/pallas_call | solution.py:156
  111.4 7.7 %collective-permute-done.11 = bf16[128,1664]{1,0:T(8,128)(2,1)S(1)} collective-permute-done((bf16[128,1664]{1,0:T(8,128)(2,1)}, bf16[128,1664]{1,0:T(8,128)(2,1)S(1)}, u32[]{:S(2)}, u32[]{:S(2)}) %collective-permute-start.11) | collective-permute-done | bytes 426016 | tf_op jit(solution)/shard_map/ppermute | solution.py:730
  119.1 10.1 %collective-permute-done.12 = bf16[128,1664]{1,0:T(8,128)(2,1)S(1)} collective-permute-done((bf16[128,1664]{1,0:T(8,128)(2,1)}, bf16[128,1664]{1,0:T(8,128)(2,1)S(1)}, u32[]{:S(2)}, u32[]{:S(2)}) %collective-permute-start.12) | collective-permute-done | bytes 426016 | tf_op jit(solution)/shard_map/ppermute | solution.py:730
  135.2 15.0 %collective-permute-done.14.refs_1_ = bf16[128,1536]{1,0:T(8,128)(2,1)S(1)} collective-permute-done((bf16[128,1536]{1,0:T(8,128)(2,1)S(1)}, bf16[128,1536]{1,0:T(8,128)(2,1)S(1)}, u32[]{:S(2)}, u32[]{:S(2)}) %collective-permute-start.14) | collective-permute-done | bytes 393248 | tf_op jit(solution)/shard_map/ppermute | solution.py:730
  154.7 15.0 %layer_forward.3 = (bf16[128,1664]{1,0:T(8,128)(2,1)}, bf16[128,1664]{1,0:T(8,128)(2,1)}, bf16[128,1664]{1,0:T(8,128)(2,1)}, bf16[128,1664]{1,0:T(8,128)(2,1)}, ...) custom-call(bf16[128,1536]{1,0:T(8,128)(2,1)} %copy-done.13, ...), custom_call_target="tpu_custom_call" | custom-call | flops 19800000512 | bytes 1048576 | tf_op jit(solution)/shard_map/layer_forward/pallas_call | solution.py:156
  176.5 29.0 %backward_1.1 = (bf16[512,768]{1,0:T(8,128)(2,1)}, bf16[512,768]{1,0:T(8,128)(2,1)}, f32[6,8,128]{2,1,0:T(8,128)}, bf16[512,768]{1,0:T(8,128)(2,1)}, bf16[512,38...) custom-call(bf16[128,1536]{1,0:T(8,128)(2,1)} %copy-done.16, ...), custom_call_target="tpu_custom_call" | custom-call | flops 30799998976 | bytes 1048576 | tf_op jit(solution)/shard_map/backward_1/pallas_call | solution.py:156
  210.5 7.8 %collective-permute-done.20 = bf16[128,1536]{1,0:T(8,128)(2,1)S(1)} collective-permute-done((bf16[128,1536]{1,0:T(8,128)(2,1)}, bf16[128,1536]{1,0:T(8,128)(2,1)S(1)}, u32[]{:S(2)}, u32[]{:S(2)}) %collective-permute-start.20) | collective-permute-done | bytes 393248 | tf_op jit(solution)/shard_map/ppermute | solution.py:730
  218.3 8.1 %collective-permute-done.21 = bf16[128,1536]{1,0:T(8,128)(2,1)S(1)} collective-permute-done((bf16[128,1536]{1,0:T(8,128)(2,1)}, bf16[128,1536]{1,0:T(8,128)(2,1)S(1)}, u32[]{:S(2)}, u32[]{:S(2)}) %collective-permute-start.21) | collective-permute-done | bytes 393248 | tf_op jit(solution)/shard_map/ppermute | solution.py:730
  233.7 17.3 %collective-permute-done.23.refs_1_ = bf16[128,1664]{1,0:T(8,128)(2,1)S(1)} collective-permute-done((bf16[128,1664]{1,0:T(8,128)(2,1)S(1)}, bf16[128,1664]{1,0:T(8,128)(2,1)S(1)}, u32[]{:S(2)}, u32[]{:S(2)}) %collective-permute-start.23) | collective-permute-done | bytes 426016 | tf_op jit(solution)/shard_map/ppermute | solution.py:730
  259.5 10.5 %backward_0_gate.1 = (bf16[512,768]{1,0:T(8,128)(2,1)}, bf16[512,768]{1,0:T(8,128)(2,1)S(1)}, f32[512,768]{1,0:T(8,128)S(1)}, f32[6,8,128]{2,1,0:T(8,128)S(1)}, ...) custom-call(bf16[128,1664]{1,0:T(8,128)(2,1)S(1)} %pad_maximum_fusion.4.refs_0_, ...), custom_call_target="tpu_custom_call" | custom-call | flops 15399999488 | bytes 1048576 | tf_op jit(solution)/shard_map/backward_0_gate/pallas_call | solution.py:156
  270.1 11.1 %backward_0_scan.1 = (f32[6,8,128]{2,1,0:T(8,128)S(1)}, bf16[512,768]{1,0:T(8,128)(2,1)S(1)}, bf16[512,384]{1,0:T(8,128)(2,1)S(1)}, f32[2,8,128]{2,1,0:T(8,128)S...) custom-call(f32[2,512,768]{2,1,0:T(8,128)S(1)} %copy-done.6, ...), custom_call_target="tpu_custom_call" | custom-call | flops 22000001024 | bytes 1048576 | tf_op jit(solution)/shard_map/backward_0_scan/pallas_call | solution.py:156
  303.5 15.0 %collective-permute-done.28 = bf16[128,1536]{1,0:T(8,128)(2,1)S(1)} collective-permute-done((bf16[128,1536]{1,0:T(8,128)(2,1)S(1)}, bf16[128,1536]{1,0:T(8,128)(2,1)S(1)}, u32[]{:S(2)}, u32[]{:S(2)}) %collective-permute-start.28) | collective-permute-done | bytes 393248 | tf_op jit(solution)/shard_map/ppermute | solution.py:730
  320.3 15.9 %collective-permute-done.31 = bf16[128,1664]{1,0:T(8,128)(2,1)S(1)} collective-permute-done((bf16[128,1664]{1,0:T(8,128)(2,1)S(1)}, bf16[128,1664]{1,0:T(8,128)(2,1)S(1)}, u32[]{:S(2)}, u32[]{:S(2)}) %collective-permute-start.31) | collective-permute-done | bytes 426016 | tf_op jit(solution)/shard_map/ppermute | solution.py:730
  337.3 75.6 %reduce-scatter.5.cloned.1.call-done = bf16[1,160,1536]{2,1,0:T(8,128)(2,1)} async-done(((bf16[16,160,1536]{2,1,0:T(8,128)(2,1)}), bf16[1,160,1536]{2,1,0:T(8,128)(2,1)}) %reduce-scatter.5.cloned.1.call-update) | async-done | bytes 491536 | tf_op jit(solution)/shard_map/reduce_scatter | solution.py:952
  418.1 7.4 %all-to-all-start.1 = ((bf16[8,112,384]{2,1,0:T(8,128)(2,1)}), bf16[8,112,384]{2,1,0:T(8,128)(2,1)S(1)}, u32[]{:S(2)}, u32[]{:S(2)}) async-start(bf16[8,112,384]{2,1,0:T(8,128)(2,1)} %pad_maximum_fusion.1), calls=%async_computation.3 | async-start | bytes 1376256 | tf_op jit(solution)/shard_map/all_to_all | solution.py:734
  426.6 7.0 %all-to-all-done.1 = bf16[8,112,384]{2,1,0:T(8,128)(2,1)S(1)} async-done(((bf16[8,112,384]{2,1,0:T(8,128)(2,1)}), bf16[8,112,384]{2,1,0:T(8,128)(2,1)S(1)}, u32[]{:S(2)}, u32[]{:S(2)}) %all-to-all-start.1) | async-done | bytes 688160 | tf_op jit(solution)/shard_map/all_to_all | solution.py:734
  449.8 7.2 %collective-permute-done.35 = bf16[128,1536]{1,0:T(8,128)(2,1)S(1)} collective-permute-done((bf16[128,1536]{1,0:T(8,128)(2,1)S(1)}, bf16[128,1536]{1,0:T(8,128)(2,1)S(1)}, u32[]{:S(2)}, u32[]{:S(2)}) %collective-permute-start.35) | collective-permute-done | bytes 393248 | tf_op jit(solution)/shard_map/ppermute | solution.py:990
  457.2 6.1 %collective-permute-done.39 = f32[276,128]{1,0:T(8,128)S(1)} collective-permute-done((f32[276,128]{1,0:T(8,128)S(1)}, f32[276,128]{1,0:T(8,128)S(1)}, u32[]{:S(2)}, u32[]{:S(2)}) %collective-permute-start.39) | collective-permute-done | bytes 141344 | tf_op jit(solution)/shard_map/ppermute | solution.py:774
  465.8 7.5 %collective-permute-done.41 = f32[276,128]{1,0:T(8,128)S(1)} collective-permute-done((f32[276,128]{1,0:T(8,128)S(1)}, f32[276,128]{1,0:T(8,128)S(1)}, u32[]{:S(2)}, u32[]{:S(2)}) %collective-permute-start.41) | collective-permute-done | bytes 141344 | tf_op jit(solution)/shard_map/ppermute | solution.py:776
  491.8 9.9 %assemble.1 = (f32[6448,384]{1,0:T(8,128)}, f32[768,1536]{1,0:T(8,128)}) custom-call(bf16[16,592,384]{2,1,0:T(8,128)(2,1)} %bitcast.221, bf16[16,592,384]{2,1,0:T(8,128)(2,1)} %bitcast.222, bf16[16,592,384]{2,1,0:T(8,128)(2,1)} %bitcast.223, f32[48,384]{1,0:T(8,128)} %reshape.502.dt), custom_call_target="tpu_custom_call" | custom-call | tf_op jit(solution)/shard_map/assemble/pallas_call | solution.py:700
  (371 shorter events, 160.6 us)
Async XLA Ops:
  14.1 19.5 %all-to-all-start = ((bf16[8,112,384]{2,1,0:T(8,128)(2,1)}), bf16[8,112,384]{2,1,0:T(8,128)(2,1)S(1)}, u32[]{:S(2)}, u32[]{:S(2)}) async-start(bf16[8,112,384]{2,1,0:T(8,128)(2,1)} %fusion.25), calls=%async_computation | async-start | bytes 1376256 | tf_op jit(solution)/shard_map/weights/all_to_all | solution.py:734
  21.5 69.3 %all-gather.7.cloned.1.call-start = ((), (), s32[]{:S(2)}) async-start(), calls=%async_computation.6 | async-start | bytes 8355840 | tf_op jit(solution)/shard_map/weights/all_gather | solution.py:849
  34.8 119.2 %all-gather.9.cloned.1.call-start = ((), (), s32[]{:S(2)}) async-start(), calls=%async_computation.7 | async-start | bytes 8355840 | tf_op jit(solution)/shard_map/all_gather | solution.py:907
  34.8 18.7 %collective-permute-start.1 = (bf16[128,1536]{1,0:T(8,128)(2,1)S(1)}, bf16[128,1536]{1,0:T(8,128)(2,1)S(1)}, u32[]{:S(2)}, u32[]{:S(2)}) collective-permute-start(bf16[128,1536]{1,0:T(8,128)(2,1)S(1)} %get-tuple-element.108.refs_0_), channel_id=1, source_target_pairs={{0,3},{1,0},{2,1},{3,2},{4,7},{5,4},{6,5},{7,6},{8,11},{9,8},{10,9... | collective-permute-start | bytes 1179656 | tf_op jit(solution)/shard_map/weights/ppermute | solution.py:730
  38.7 18.4 %collective-permute-start.3 = (bf16[128,1536]{1,0:T(8,128)(2,1)S(1)}, bf16[128,1536]{1,0:T(8,128)(2,1)S(1)}, u32[]{:S(2)}, u32[]{:S(2)}) collective-permute-start(bf16[128,1536]{1,0:T(8,128)(2,1)S(1)} %get-tuple-element.108.refs_0_), channel_id=1, source_target_pairs={{0,1},{1,2},{2,3},{3,0},{4,5},{5,6},{6,7},{7,4},{8,9},{9,10},{10,1... | collective-permute-start | bytes 1179656 | tf_op jit(solution)/shard_map/weights/ppermute | solution.py:730
  68.3 18.9 %collective-permute-start.4 = (bf16[128,1536]{1,0:T(8,128)(2,1)S(1)}, bf16[128,1536]{1,0:T(8,128)(2,1)S(1)}, u32[]{:S(2)}, u32[]{:S(2)}) collective-permute-start(bf16[128,1536]{1,0:T(8,128)(2,1)S(1)} %fusion.6.refs_4_.refs_0_), channel_id=1, source_target_pairs={{0,3},{1,0},{2,1},{3,2},{4,7},{5,4},{6,5},{7,6},{8,11},{9,8},{10,9... | collective-permute-start | bytes 1179656 | tf_op jit(solution)/shard_map/ppermute | solution.py:730
  90.8 246.5 %reduce-scatter.3.cloned.1.call-start = ((), (), s32[]{:S(2)}) async-start(), calls=%async_computation.4 | async-start | bytes 4423680 | tf_op jit(solution)/shard_map/reduce_scatter | solution.py:980
  107.2 22.0 %collective-permute-start.12 = (bf16[128,1664]{1,0:T(8,128)(2,1)}, bf16[128,1664]{1,0:T(8,128)(2,1)S(1)}, u32[]{:S(2)}, u32[]{:S(2)}) collective-permute-start(bf16[128,1664]{1,0:T(8,128)(2,1)} %get-tuple-element.120), channel_id=1, source_target_pairs={{0,2},{1,3},{2,0},{3,1},{4,6},{5,7},{6,4},{7,5},{8,10},{9,11},{10,... | collective-permute-start | bytes 1277960 | tf_op jit(solution)/shard_map/ppermute | solution.py:730
  109.9 19.3 %collective-permute-start.13 = (bf16[128,1664]{1,0:T(8,128)(2,1)}, bf16[128,1664]{1,0:T(8,128)(2,1)S(1)}, u32[]{:S(2)}, u32[]{:S(2)}) collective-permute-start(bf16[128,1664]{1,0:T(8,128)(2,1)} %get-tuple-element.121), channel_id=1, source_target_pairs={{0,3},{1,0},{2,1},{3,2},{4,7},{5,4},{6,5},{7,6},{8,11},{9,8},{10,9... | collective-permute-start | bytes 1277960 | tf_op jit(solution)/shard_map/ppermute | solution.py:730
  130.9 19.3 %collective-permute-start.14 = (bf16[128,1536]{1,0:T(8,128)(2,1)S(1)}, bf16[128,1536]{1,0:T(8,128)(2,1)S(1)}, u32[]{:S(2)}, u32[]{:S(2)}) collective-permute-start(bf16[128,1536]{1,0:T(8,128)(2,1)S(1)} %get-tuple-element.200.refs_0_), channel_id=1, source_target_pairs={{0,3},{1,0},{2,1},{3,2},{4,7},{5,4},{6,5},{7,6},{8,11},{9,8},{10,9... | collective-permute-start | bytes 1179656 | tf_op jit(solution)/shard_map/ppermute | solution.py:730
  134.4 19.5 %collective-permute-start.16 = (bf16[128,1536]{1,0:T(8,128)(2,1)S(1)}, bf16[128,1536]{1,0:T(8,128)(2,1)S(1)}, u32[]{:S(2)}, u32[]{:S(2)}) collective-permute-start(bf16[128,1536]{1,0:T(8,128)(2,1)S(1)} %get-tuple-element.200.refs_0_), channel_id=1, source_target_pairs={{0,1},{1,2},{2,3},{3,0},{4,5},{5,6},{6,7},{7,4},{8,9},{9,10},{10,1... | collective-permute-start | bytes 1179656 | tf_op jit(solution)/shard_map/ppermute | solution.py:730
  207.5 18.9 %collective-permute-start.21 = (bf16[128,1536]{1,0:T(8,128)(2,1)}, bf16[128,1536]{1,0:T(8,128)(2,1)S(1)}, u32[]{:S(2)}, u32[]{:S(2)}) collective-permute-start(bf16[128,1536]{1,0:T(8,128)(2,1)} %get-tuple-element.139), channel_id=1, source_target_pairs={{0,2},{1,3},{2,0},{3,1},{4,6},{5,7},{6,4},{7,5},{8,10},{9,11},{10,... | collective-permute-start | bytes 1179656 | tf_op jit(solution)/shard_map/ppermute | solution.py:730
  230.4 20.6 %collective-permute-start.23 = (bf16[128,1664]{1,0:T(8,128)(2,1)S(1)}, bf16[128,1664]{1,0:T(8,128)(2,1)S(1)}, u32[]{:S(2)}, u32[]{:S(2)}) collective-permute-start(bf16[128,1664]{1,0:T(8,128)(2,1)S(1)} %pad_maximum_fusion.4.refs_0_), channel_id=1, source_target_pairs={{0,3},{1,0},{2,1},{3,2},{4,7},{5,4},{6,5},{7,6},{8,11},{9,8},{10,9... | collective-permute-start | bytes 1277960 | tf_op jit(solution)/shard_map/ppermute | solution.py:730
  232.6 18.4 %collective-permute-start.24 = (bf16[128,1664]{1,0:T(8,128)(2,1)S(1)}, bf16[128,1664]{1,0:T(8,128)(2,1)S(1)}, u32[]{:S(2)}, u32[]{:S(2)}) collective-permute-start(bf16[128,1664]{1,0:T(8,128)(2,1)S(1)} %pad_maximum_fusion.4.refs_0_), channel_id=1, source_target_pairs={{0,2},{1,3},{2,0},{3,1},{4,6},{5,7},{6,4},{7,5},{8,10},{9,11},{10,... | collective-permute-start | bytes 1277960 | tf_op jit(solution)/shard_map/ppermute | solution.py:730
  233.2 21.5 %collective-permute-start.25 = (bf16[128,1664]{1,0:T(8,128)(2,1)S(1)}, bf16[128,1664]{1,0:T(8,128)(2,1)S(1)}, u32[]{:S(2)}, u32[]{:S(2)}) collective-permute-start(bf16[128,1664]{1,0:T(8,128)(2,1)S(1)} %pad_maximum_fusion.4.refs_0_), channel_id=1, source_target_pairs={{0,1},{1,2},{2,3},{3,0},{4,5},{5,6},{6,7},{7,4},{8,9},{9,10},{10,1... | collective-permute-start | bytes 1277960 | tf_op jit(solution)/shard_map/ppermute | solution.py:730
  287.7 125.2 %reduce-scatter.5.cloned.1.call-start = ((), (), s32[]{:S(2)}) async-start(), calls=%async_computation.5 | async-start | bytes 8355840 | tf_op jit(solution)/shard_map/reduce_scatter | solution.py:952
  296.8 21.7 %collective-permute-start.28 = (bf16[128,1536]{1,0:T(8,128)(2,1)S(1)}, bf16[128,1536]{1,0:T(8,128)(2,1)S(1)}, u32[]{:S(2)}, u32[]{:S(2)}) collective-permute-start(bf16[128,1536]{1,0:T(8,128)(2,1)S(1)} %get-tuple-element.165), channel_id=1, source_target_pairs={{0,1},{1,2},{2,3},{3,0},{4,5},{5,6},{6,7},{7,4},{8,9},{9,10},{10,1... | collective-permute-start | bytes 1179656 | tf_op jit(solution)/shard_map/ppermute | solution.py:730
  296.9 21.6 %collective-permute-start.29 = (bf16[128,1536]{1,0:T(8,128)(2,1)S(1)}, bf16[128,1536]{1,0:T(8,128)(2,1)S(1)}, u32[]{:S(2)}, u32[]{:S(2)}) collective-permute-start(bf16[128,1536]{1,0:T(8,128)(2,1)S(1)} %get-tuple-element.166), channel_id=1, source_target_pairs={{0,2},{1,3},{2,0},{3,1},{4,6},{5,7},{6,4},{7,5},{8,10},{9,11},{10,... | collective-permute-start | bytes 1179656 | tf_op jit(solution)/shard_map/ppermute | solution.py:730
  298.9 20.4 %collective-permute-start.30 = (bf16[128,1536]{1,0:T(8,128)(2,1)S(1)}, bf16[128,1536]{1,0:T(8,128)(2,1)S(1)}, u32[]{:S(2)}, u32[]{:S(2)}) collective-permute-start(bf16[128,1536]{1,0:T(8,128)(2,1)S(1)} %get-tuple-element.167), channel_id=1, source_target_pairs={{0,3},{1,0},{2,1},{3,2},{4,7},{5,4},{6,5},{7,6},{8,11},{9,8},{10,9... | collective-permute-start | bytes 1179656 | tf_op jit(solution)/shard_map/ppermute | solution.py:730
  300.1 36.0 %collective-permute-start.31 = (bf16[128,1664]{1,0:T(8,128)(2,1)S(1)}, bf16[128,1664]{1,0:T(8,128)(2,1)S(1)}, u32[]{:S(2)}, u32[]{:S(2)}) collective-permute-start(bf16[128,1664]{1,0:T(8,128)(2,1)S(1)} %copy-done.34), channel_id=1, source_target_pairs={{0,1},{1,2},{2,3},{3,0},{4,5},{5,6},{6,7},{7,4},{8,9},{9,10},{10,1... | collective-permute-start | bytes 1277960 | tf_op jit(solution)/shard_map/ppermute | solution.py:730
  301.1 35.1 %collective-permute-start.32 = (bf16[128,1664]{1,0:T(8,128)(2,1)S(1)}, bf16[128,1664]{1,0:T(8,128)(2,1)S(1)}, u32[]{:S(2)}, u32[]{:S(2)}) collective-permute-start(bf16[128,1664]{1,0:T(8,128)(2,1)S(1)} %copy-done.33), channel_id=1, source_target_pairs={{0,2},{1,3},{2,0},{3,1},{4,6},{5,7},{6,4},{7,5},{8,10},{9,11},{10,... | collective-permute-start | bytes 1277960 | tf_op jit(solution)/shard_map/ppermute | solution.py:730
  425.4 66.3 %all-gather.11.cloned.1.call-start = ((), (), s32[]{:S(2)}) async-start(), calls=%async_computation.8 | async-start | bytes 7729152 | tf_op jit(solution)/shard_map/all_gather | solution.py:1010
  437.8 19.3 %collective-permute-start.35 = (bf16[128,1536]{1,0:T(8,128)(2,1)S(1)}, bf16[128,1536]{1,0:T(8,128)(2,1)S(1)}, u32[]{:S(2)}, u32[]{:S(2)}) collective-permute-start(bf16[128,1536]{1,0:T(8,128)(2,1)S(1)} %convert_element_type.333), channel_id=1, source_target_pairs={{0,64},{1,65},{2,66},{3,67},{4,68},{5,69},{6,70},{7,71},{8,72},{9,... | collective-permute-start | bytes 1179656 | tf_op jit(solution)/shard_map/ppermute | solution.py:990
  443.6 22.1 %collective-permute-start.34 = (bf16[128,1536]{1,0:T(8,128)(2,1)S(1)}, bf16[128,1536]{1,0:T(8,128)(2,1)S(1)}, u32[]{:S(2)}, u32[]{:S(2)}) collective-permute-start(bf16[128,1536]{1,0:T(8,128)(2,1)S(1)} %convert_element_type.332), channel_id=1, source_target_pairs={{64,0},{65,1},{66,2},{67,3},{68,4},{69,5},{70,6},{71,7},{72,8},{73... | collective-permute-start | bytes 1179656 | tf_op jit(solution)/shard_map/ppermute | solution.py:991
  (74 other events, 991.7 us)
Sparse Core Ops, SparseCore 0:
  34.9 55.8 all-gather.6
  93.1 50.8 all-gather.8
  287.9 49.3 reduce-scatter.2
  340.1 72.7 reduce-scatter.4
  434.6 57.1 all-gather.10

commit v11 on v10

--- a/solution.py
+++ b/solution.py
@@ -730,6 +730,15 @@
     return lax.ppermute(v, "shard", ring(SLOTS, k)) if k else v
 
 
+def send_across(v, k):
+    pairs = [
+        (sec * SLOTS + y, (1 - sec) * SLOTS + (y + k) % SLOTS)
+        for sec in range(2)
+        for y in range(SLOTS)
+    ]
+    return lax.ppermute(v, ("section", "shard"), pairs)
+
+
 def across(v):
     return lax.all_to_all(v, ("section", "shard"), 0, 0)
 
@@ -834,17 +843,27 @@
                 axis=0,
             )
 
-        cuts = jnp.stack([columns_of(y) for y in range(SLOTS)])
-        got = across(jnp.concatenate([cuts, cuts], axis=0))
+        cuts = [columns_of((j + k) % SLOTS) for k in range(SLOTS)]
         o_own = lax.dynamic_slice(out_weight[0], (piece * d, 0), (piece, width))
         o_other = swap_section(o_own)
 
-        def whole_rows(layer, own):
-            rows = jnp.concatenate([got[SLOTS * layer + y] for y in range(SLOTS)], axis=1)
-            return jnp.concatenate([jnp.where(own, o_own, o_other), rows], axis=0)
-
-        w0 = whole_rows(0, first)
-        w1 = whole_rows(1, ~first)
+        w_own = [send_shard(cuts[k], k) for k in range(SLOTS)]
+        w_other = [send_across(cuts[k], k) for k in range(SLOTS)]
+
+        def from_parts(parts, others, o, o_others, own):
+            pieces = [jnp.where(own, p, q) for p, q in zip(parts, others)]
+            lanes = []
+            for y in range(SLOTS):
+                v = pieces[0]
+                for k in range(1, SLOTS):
+                    v = jnp.where((j - y) % SLOTS == k, pieces[k], v)
+                lanes.append(v)
+            return jnp.concatenate(
+                [jnp.where(own, o, o_others), jnp.concatenate(lanes, axis=1)], axis=0
+            )
+
+        w0 = from_parts(w_own, w_other, o_own, o_other, first)
+        w1 = from_parts(w_own, w_other, o_own, o_other, ~first)
         w0, w1, x_own, cot = lax.optimization_barrier((w0, w1, x_own, cot))
         w0 = lax.all_gather(w0, DP, axis=0, tiled=False)
         x_slots = gather_slots(x_own)
@@ -974,7 +993,8 @@
     back0.update(backward(("scan", "wscan"), "backward_0_scan", 20, saved0, layer0, back0))
     gb_send, a_moved = lax.optimization_barrier((back0["gb_send"], a_moved))
     a0 = both(back0["ga_keep"], a_moved)
-    b0 = both(back0["gb_keep"], cross_core(gb_send))
+    b_moved, owned1 = lax.optimization_barrier((cross_core(gb_send), owned1))
+    b0 = both(back0["gb_keep"], b_moved)
     owned0 = jnp.pad(a0, ((0, 0), (0, 0), (0, 4), (0, 0), (0, 0)))
     owned0 = lax.dynamic_update_slice(owned0, b0, (0, 0, 6, 0, 0)).reshape(8, -1, width)
     owned0 = lax.psum_scatter(owned0, ("x", "z"), scatter_dimension=0, tiled=False)
@@ -983,8 +1003,13 @@
     moved0 = [send_shard(back0[f"out{k}"], k) for k in range(SLOTS)]
     dx, gain_grad0 = norm_back(x_f, gain0, sum(p.astype(F32) for p in moved0))
     dtokens = dmiddle.astype(F32) + dx
-    owned0, owned1, gain_grad0, dtokens, result = lax.optimization_barrier(
-        (owned0, owned1, gain_grad0, dtokens, result)
+    def by_row(v):
+        rows = jnp.concatenate([v[:piece], v[2 * piece :]], axis=0)
+        return jnp.transpose(rows.reshape(-1, SLOTS, quarter), (1, 0, 2))
+
+    rows1 = by_row(owned1)
+    owned0, owned1, rows1, gain_grad0, dtokens, result = lax.optimization_barrier(
+        (owned0, owned1, rows1, gain_grad0, dtokens, result)
     )
 
     result_moved = lax.ppermute(result.astype(BF16), "section", [(0, 1)]).astype(F32)
@@ -997,11 +1022,7 @@
         kept = jnp.where(first, v0, v1).astype(F32)
         return kept + swap_section(jnp.where(first, v1, v0)).astype(F32)
 
-    def by_row(v):
-        rows = jnp.concatenate([v[:piece], v[2 * piece :]], axis=0)
-        return jnp.transpose(rows.reshape(-1, SLOTS, quarter), (1, 0, 2))
-
-    got = across(jnp.concatenate([by_row(owned0), by_row(owned1)], axis=0))
+    got = across(jnp.concatenate([by_row(owned0), rows1], axis=0))
     out_rows = to_section(owned0[piece : 2 * piece], owned1[piece : 2 * piece]).astype(BF16)
     out_rows = jnp.transpose(out_rows.reshape(piece, SLOTS, quarter), (1, 0, 2))
     rows = got[:SLOTS].astype(F32) + got[SLOTS:].astype(F32)

time: 515 us -> 443 us (0.86)
  waiting for transfers between devices: 265 us -> 186 us
    reduce_scatter x1, waiting for transfers between devices: 75.6 us -> 0.01 us  [shards(): lax.psum_scatter(by_owner(back1['ga']), DP, scatter_dimension=0, tiled=Fa...]
    ppermute x0 -> x4, starting transfers between devices: none -> 9.45 us  [send_across(): return lax.ppermute(v, ('section', 'shard'), pairs)]
    all_to_all x2 -> x1, starting transfers between devices: 14.8 us -> 6.58 us  [across(): return lax.all_to_all(v, ('section', 'shard'), 0, 0)]
    ppermute x33 -> x36, waiting for transfers between devices: 135 us -> 129 us  [send_shard(): return lax.ppermute(v, 'shard', ring(SLOTS, k)) if k else v]
    ppermute x33 -> x36, starting transfers between devices: 42.5 us -> 47.8 us  [send_shard(): return lax.ppermute(v, 'shard', ring(SLOTS, k)) if k else v]
    unnamed x100 -> x112, local copies, waits for them, and re-layouts: 10.9 us -> 12.6 us
  transfers between devices with their start and end apart: 53 -> 59, of which waited for: 36 -> 32; matrix products, arithmetic and copies ran while one was open for 6% -> 8% of each run, Pallas kernels for 6% -> 9%
where the time goes in v11:
time: 443 us; the launch traced here: 435 us
  waiting for transfers between devices  186 us (42%)
  Pallas kernels  94.1 us (21%)
  starting transfers between devices  78.6 us (18%)
  local copies, waits for them, and re-layouts  34.4 us (8%)
  other arithmetic  25.9 us (6%)
  between operations  15.6 us (4%)
    ppermute x36, waiting for transfers between devices, send_shard(): return lax.ppermute(v, 'shard', ring(SLOTS, k)) if k else v  129 us
    pallas_call x6, Pallas kernels, kernel_call(): pl.pallas_call(run, in_specs=[pl.BlockSpec(memory_space=pltpu.VMEM if len...  84.1 us
    ppermute x36, starting transfers between devices, send_shard(): return lax.ppermute(v, 'shard', ring(SLOTS, k)) if k else v  47.8 us
    ppermute x4, waiting for transfers between devices, swap_section(): return lax.ppermute(v, 'section', [(0, 1), (1, 0)])  16 us
    unnamed x112, local copies, waits for them, and re-layouts  12.6 us
    pallas_call x1, Pallas kernels, assemble(): pl.pallas_call(body, grid=(9,), in_specs=[pl.BlockSpec((16, 48, quarter),...  9.95 us
    ppermute x4, starting transfers between devices, send_across(): return lax.ppermute(v, ('section', 'shard'), pairs)  9.45 us
    ppermute x1, waiting for transfers between devices, shards(): lax.ppermute(result.astype(BF16), 'section', [(0, 1)]).astype(F32)  9.16 us
  transfers between devices with their start and end apart: 59, of which 32 were waited for; matrix products, arithmetic and copies ran while one was open for 8% of the time, Pallas kernels for 9%

profile of v11, /device:TPU:4, one launch (start us, length us, event | category | flops | bytes accessed | tf_op | source)
XLA Modules:
  0.0 434.8 jit_solution(5837316466096102496)
XLA Ops:
  13.0 5.7 %collective-permute-start.4 = (bf16[112,384]{1,0:T(8,128)(2,1)S(1)}, bf16[112,384]{1,0:T(8,128)(2,1)S(1)}, u32[]{:S(2)}, u32[]{:S(2)}) collective-permute-start(bf16[112,384]{1,0:T(8,128)(2,1)S(1)} %get-tuple-element.260), channel_id=1, source_target_pairs={{0,66},{1,67},{2,64},{3,65},{64,2},{65,3},{66,0},{67,1},{4,70},{5,... | collective-permute-start | bytes 258056 | tf_op jit(solution)/shard_map/weights/ppermute | solution.py:739
  41.2 5.3 %collective-permute-done.10.refs_3_ = bf16[128,1536]{1,0:T(8,128)(2,1)S(1)} collective-permute-done((bf16[128,1536]{1,0:T(8,128)(2,1)S(1)}, bf16[128,1536]{1,0:T(8,128)(2,1)S(1)}, u32[]{:S(2)}, u32[]{:S(2)}) %collective-permute-start.10) | collective-permute-done | bytes 393248 | tf_op jit(solution)/shard_map/weights/ppermute | solution.py:730
  46.5 5.0 %collective-permute-done.8.refs_1_ = bf16[128,1536]{1,0:T(8,128)(2,1)S(1)} collective-permute-done((bf16[128,1536]{1,0:T(8,128)(2,1)S(1)}, bf16[128,1536]{1,0:T(8,128)(2,1)S(1)}, u32[]{:S(2)}, u32[]{:S(2)}) %collective-permute-start.8) | collective-permute-done | bytes 393248 | tf_op jit(solution)/shard_map/weights/ppermute | solution.py:730
  67.1 7.7 %collective-permute-done.17 = bf16[4,187,128]{2,1,0:T(8,128)(2,1)S(1)} collective-permute-done((bf16[4,187,128]{2,1,0:T(8,128)(2,1)S(1)}, bf16[4,187,128]{2,1,0:T(8,128)(2,1)S(1)}, u32[]{:S(2)}, u32[]{:S(2)}) %collective-permute-start.17) | collective-permute-done | bytes 191520 | tf_op jit(solution)/shard_map/small_weights/ppermute | solution.py:747
  84.3 5.9 %all-gather.7.cloned.1.call-done = bf16[2560,1536]{1,0:T(8,128)(2,1)} async-done(((bf16[160,1536]{1,0:T(8,128)(2,1)}), bf16[2560,1536]{1,0:T(8,128)(2,1)}) %all-gather.7.cloned.1.call-update) | async-done | bytes 7864336 | tf_op jit(solution)/shard_map/weights/all_gather | solution.py:868
  90.7 14.3 %layer_forward.2 = (bf16[128,1664]{1,0:T(8,128)(2,1)}, bf16[128,1664]{1,0:T(8,128)(2,1)}, bf16[128,1664]{1,0:T(8,128)(2,1)}, bf16[128,1664]{1,0:T(8,128)(2,1)}, ...) custom-call(bf16[128,1536]{1,0:T(8,128)(2,1)} %copy-done.14, ...), custom_call_target="tpu_custom_call" | custom-call | flops 19800000512 | bytes 1048576 | tf_op jit(solution)/shard_map/layer_forward/pallas_call | solution.py:156
  110.8 7.7 %collective-permute-done.18 = bf16[128,1664]{1,0:T(8,128)(2,1)S(1)} collective-permute-done((bf16[128,1664]{1,0:T(8,128)(2,1)}, bf16[128,1664]{1,0:T(8,128)(2,1)S(1)}, u32[]{:S(2)}, u32[]{:S(2)}) %collective-permute-start.18) | collective-permute-done | bytes 426016 | tf_op jit(solution)/shard_map/ppermute | solution.py:730
  118.5 10.1 %collective-permute-done.19 = bf16[128,1664]{1,0:T(8,128)(2,1)S(1)} collective-permute-done((bf16[128,1664]{1,0:T(8,128)(2,1)}, bf16[128,1664]{1,0:T(8,128)(2,1)S(1)}, u32[]{:S(2)}, u32[]{:S(2)}) %collective-permute-start.19) | collective-permute-done | bytes 426016 | tf_op jit(solution)/shard_map/ppermute | solution.py:730
  134.5 15.0 %collective-permute-done.21.refs_1_ = bf16[128,1536]{1,0:T(8,128)(2,1)S(1)} collective-permute-done((bf16[128,1536]{1,0:T(8,128)(2,1)S(1)}, bf16[128,1536]{1,0:T(8,128)(2,1)S(1)}, u32[]{:S(2)}, u32[]{:S(2)}) %collective-permute-start.21) | collective-permute-done | bytes 393248 | tf_op jit(solution)/shard_map/ppermute | solution.py:730
  154.0 14.9 %layer_forward.3 = (bf16[128,1664]{1,0:T(8,128)(2,1)}, bf16[128,1664]{1,0:T(8,128)(2,1)}, bf16[128,1664]{1,0:T(8,128)(2,1)}, bf16[128,1664]{1,0:T(8,128)(2,1)}, ...) custom-call(bf16[128,1536]{1,0:T(8,128)(2,1)} %copy-done.17, ...), custom_call_target="tpu_custom_call" | custom-call | flops 19800000512 | bytes 1048576 | tf_op jit(solution)/shard_map/layer_forward/pallas_call | solution.py:156
  175.8 28.9 %backward_1.1 = (bf16[512,768]{1,0:T(8,128)(2,1)}, bf16[512,768]{1,0:T(8,128)(2,1)}, f32[6,8,128]{2,1,0:T(8,128)}, bf16[512,768]{1,0:T(8,128)(2,1)}, bf16[512,38...) custom-call(bf16[128,1536]{1,0:T(8,128)(2,1)} %copy-done.23, ...), custom_call_target="tpu_custom_call" | custom-call | flops 30799998976 | bytes 1048576 | tf_op jit(solution)/shard_map/backward_1/pallas_call | solution.py:156
  209.9 7.8 %collective-permute-done.27 = bf16[128,1536]{1,0:T(8,128)(2,1)S(1)} collective-permute-done((bf16[128,1536]{1,0:T(8,128)(2,1)}, bf16[128,1536]{1,0:T(8,128)(2,1)S(1)}, u32[]{:S(2)}, u32[]{:S(2)}) %collective-permute-start.27) | collective-permute-done | bytes 393248 | tf_op jit(solution)/shard_map/ppermute | solution.py:730
  217.7 8.1 %collective-permute-done.28 = bf16[128,1536]{1,0:T(8,128)(2,1)S(1)} collective-permute-done((bf16[128,1536]{1,0:T(8,128)(2,1)}, bf16[128,1536]{1,0:T(8,128)(2,1)S(1)}, u32[]{:S(2)}, u32[]{:S(2)}) %collective-permute-start.28) | collective-permute-done | bytes 393248 | tf_op jit(solution)/shard_map/ppermute | solution.py:730
  231.6 17.3 %collective-permute-done.30.refs_1_ = bf16[128,1664]{1,0:T(8,128)(2,1)S(1)} collective-permute-done((bf16[128,1664]{1,0:T(8,128)(2,1)S(1)}, bf16[128,1664]{1,0:T(8,128)(2,1)S(1)}, u32[]{:S(2)}, u32[]{:S(2)}) %collective-permute-start.30) | collective-permute-done | bytes 426016 | tf_op jit(solution)/shard_map/ppermute | solution.py:730
  257.4 10.5 %backward_0_gate.1 = (bf16[512,768]{1,0:T(8,128)(2,1)}, bf16[512,768]{1,0:T(8,128)(2,1)S(1)}, f32[512,768]{1,0:T(8,128)S(1)}, f32[6,8,128]{2,1,0:T(8,128)S(1)}, ...) custom-call(bf16[128,1664]{1,0:T(8,128)(2,1)S(1)} %pad_maximum_fusion.4.refs_0_, ...), custom_call_target="tpu_custom_call" | custom-call | flops 15399999488 | bytes 1048576 | tf_op jit(solution)/shard_map/backward_0_gate/pallas_call | solution.py:156
  268.0 10.8 %backward_0_scan.1 = (f32[6,8,128]{2,1,0:T(8,128)S(1)}, bf16[512,768]{1,0:T(8,128)(2,1)S(1)}, bf16[512,384]{1,0:T(8,128)(2,1)S(1)}, f32[2,8,128]{2,1,0:T(8,128)S...) custom-call(f32[2,512,768]{2,1,0:T(8,128)S(1)} %copy-done.6, ...), custom_call_target="tpu_custom_call" | custom-call | flops 22000001024 | bytes 1048576 | tf_op jit(solution)/shard_map/backward_0_scan/pallas_call | solution.py:156
  303.8 15.0 %collective-permute-done.35 = bf16[128,1536]{1,0:T(8,128)(2,1)S(1)} collective-permute-done((bf16[128,1536]{1,0:T(8,128)(2,1)S(1)}, bf16[128,1536]{1,0:T(8,128)(2,1)S(1)}, u32[]{:S(2)}, u32[]{:S(2)}) %collective-permute-start.35) | collective-permute-done | bytes 393248 | tf_op jit(solution)/shard_map/ppermute | solution.py:730
  321.1 15.3 %collective-permute-done.38 = bf16[128,1664]{1,0:T(8,128)(2,1)S(1)} collective-permute-done((bf16[128,1664]{1,0:T(8,128)(2,1)S(1)}, bf16[128,1664]{1,0:T(8,128)(2,1)S(1)}, u32[]{:S(2)}, u32[]{:S(2)}) %collective-permute-start.38) | collective-permute-done | bytes 426016 | tf_op jit(solution)/shard_map/ppermute | solution.py:730
  341.5 6.6 %all-to-all-start = ((bf16[8,112,384]{2,1,0:T(8,128)(2,1)}), bf16[8,112,384]{2,1,0:T(8,128)(2,1)S(1)}, u32[]{:S(2)}, u32[]{:S(2)}) async-start(bf16[8,112,384]{2,1,0:T(8,128)(2,1)} %pad_maximum_fusion.1), calls=%async_computation.2 | async-start | bytes 1376256 | tf_op jit(solution)/shard_map/all_to_all | solution.py:743
  349.1 8.9 %all-to-all-done = bf16[8,112,384]{2,1,0:T(8,128)(2,1)S(1)} async-done(((bf16[8,112,384]{2,1,0:T(8,128)(2,1)}), bf16[8,112,384]{2,1,0:T(8,128)(2,1)S(1)}, u32[]{:S(2)}, u32[]{:S(2)}) %all-to-all-start) | async-done | bytes 688160 | tf_op jit(solution)/shard_map/all_to_all | solution.py:743
  366.2 6.1 %collective-permute-done.43 = f32[276,128]{1,0:T(8,128)S(1)} collective-permute-done((f32[276,128]{1,0:T(8,128)S(1)}, f32[276,128]{1,0:T(8,128)S(1)}, u32[]{:S(2)}, u32[]{:S(2)}) %collective-permute-start.43) | collective-permute-done | bytes 141344 | tf_op jit(solution)/shard_map/ppermute | solution.py:747
  378.9 9.2 %collective-permute-done.42 = bf16[128,1536]{1,0:T(8,128)(2,1)S(1)} collective-permute-done((bf16[128,1536]{1,0:T(8,128)(2,1)S(1)}, bf16[128,1536]{1,0:T(8,128)(2,1)S(1)}, u32[]{:S(2)}, u32[]{:S(2)}) %collective-permute-start.42) | collective-permute-done | bytes 393248 | tf_op jit(solution)/shard_map/ppermute | solution.py:1015
  393.1 8.6 %collective-permute-done.48 = f32[276,128]{1,0:T(8,128)S(1)} collective-permute-done((f32[276,128]{1,0:T(8,128)S(1)}, f32[276,128]{1,0:T(8,128)S(1)}, u32[]{:S(2)}, u32[]{:S(2)}) %collective-permute-start.48) | collective-permute-done | bytes 141344 | tf_op jit(solution)/shard_map/ppermute | solution.py:785
  417.9 10.0 %assemble.1 = (f32[6448,384]{1,0:T(8,128)}, f32[768,1536]{1,0:T(8,128)}) custom-call(bf16[16,592,384]{2,1,0:T(8,128)(2,1)} %bitcast.181, bf16[16,592,384]{2,1,0:T(8,128)(2,1)} %bitcast.182, bf16[16,592,384]{2,1,0:T(8,128)(2,1)} %bitcast.183, f32[48,384]{1,0:T(8,128)} %reshape.502.dt), custom_call_target="tpu_custom_call" | custom-call | tf_op jit(solution)/shard_map/assemble/pallas_call | solution.py:700
  (391 shorter events, 164.5 us)
Async XLA Ops:
  7.2 83.0 %all-gather.7.cloned.1.call-start = ((), (), s32[]{:S(2)}) async-start(), calls=%async_computation.5 | async-start | bytes 8355840 | tf_op jit(solution)/shard_map/weights/all_gather | solution.py:868
  34.0 119.3 %all-gather.9.cloned.1.call-start = ((), (), s32[]{:S(2)}) async-start(), calls=%async_computation.6 | async-start | bytes 8355840 | tf_op jit(solution)/shard_map/all_gather | solution.py:926
  64.8 19.5 %collective-permute-start.11 = (bf16[128,1536]{1,0:T(8,128)(2,1)S(1)}, bf16[128,1536]{1,0:T(8,128)(2,1)S(1)}, u32[]{:S(2)}, u32[]{:S(2)}) collective-permute-start(bf16[128,1536]{1,0:T(8,128)(2,1)S(1)} %fusion.6.refs_4_.refs_0_), channel_id=1, source_target_pairs={{0,3},{1,0},{2,1},{3,2},{4,7},{5,4},{6,5},{7,6},{8,11},{9,8},{10,9... | collective-permute-start | bytes 1179656 | tf_op jit(solution)/shard_map/ppermute | solution.py:730
  64.9 19.4 %collective-permute-start.12 = (bf16[128,1536]{1,0:T(8,128)(2,1)S(1)}, bf16[128,1536]{1,0:T(8,128)(2,1)S(1)}, u32[]{:S(2)}, u32[]{:S(2)}) collective-permute-start(bf16[128,1536]{1,0:T(8,128)(2,1)S(1)} %fusion.6.refs_4_.refs_0_), channel_id=1, source_target_pairs={{0,2},{1,3},{2,0},{3,1},{4,6},{5,7},{6,4},{7,5},{8,10},{9,11},{10,... | collective-permute-start | bytes 1179656 | tf_op jit(solution)/shard_map/ppermute | solution.py:730
  90.2 192.3 %reduce-scatter.3.cloned.1.call-start = ((), (), s32[]{:S(2)}) async-start(), calls=%async_computation.3 | async-start | bytes 8355840 | tf_op jit(solution)/shard_map/reduce_scatter | solution.py:971
  106.6 22.0 %collective-permute-start.19 = (bf16[128,1664]{1,0:T(8,128)(2,1)}, bf16[128,1664]{1,0:T(8,128)(2,1)S(1)}, u32[]{:S(2)}, u32[]{:S(2)}) collective-permute-start(bf16[128,1664]{1,0:T(8,128)(2,1)} %get-tuple-element.123), channel_id=1, source_target_pairs={{0,2},{1,3},{2,0},{3,1},{4,6},{5,7},{6,4},{7,5},{8,10},{9,11},{10,... | collective-permute-start | bytes 1277960 | tf_op jit(solution)/shard_map/ppermute | solution.py:730
  109.3 19.3 %collective-permute-start.20 = (bf16[128,1664]{1,0:T(8,128)(2,1)}, bf16[128,1664]{1,0:T(8,128)(2,1)S(1)}, u32[]{:S(2)}, u32[]{:S(2)}) collective-permute-start(bf16[128,1664]{1,0:T(8,128)(2,1)} %get-tuple-element.124), channel_id=1, source_target_pairs={{0,3},{1,0},{2,1},{3,2},{4,7},{5,4},{6,5},{7,6},{8,11},{9,8},{10,9... | collective-permute-start | bytes 1277960 | tf_op jit(solution)/shard_map/ppermute | solution.py:730
  130.2 19.3 %collective-permute-start.21 = (bf16[128,1536]{1,0:T(8,128)(2,1)S(1)}, bf16[128,1536]{1,0:T(8,128)(2,1)S(1)}, u32[]{:S(2)}, u32[]{:S(2)}) collective-permute-start(bf16[128,1536]{1,0:T(8,128)(2,1)S(1)} %get-tuple-element.206.refs_0_), channel_id=1, source_target_pairs={{0,3},{1,0},{2,1},{3,2},{4,7},{5,4},{6,5},{7,6},{8,11},{9,8},{10,9... | collective-permute-start | bytes 1179656 | tf_op jit(solution)/shard_map/ppermute | solution.py:730
  133.7 19.5 %collective-permute-start.23 = (bf16[128,1536]{1,0:T(8,128)(2,1)S(1)}, bf16[128,1536]{1,0:T(8,128)(2,1)S(1)}, u32[]{:S(2)}, u32[]{:S(2)}) collective-permute-start(bf16[128,1536]{1,0:T(8,128)(2,1)S(1)} %get-tuple-element.206.refs_0_), channel_id=1, source_target_pairs={{0,1},{1,2},{2,3},{3,0},{4,5},{5,6},{6,7},{7,4},{8,9},{9,10},{10,1... | collective-permute-start | bytes 1179656 | tf_op jit(solution)/shard_map/ppermute | solution.py:730
  204.8 132.8 %reduce-scatter.5.cloned.1.call-start = ((), (), s32[]{:S(2)}) async-start(), calls=%async_computation.4 | async-start | bytes 4423680 | tf_op jit(solution)/shard_map/reduce_scatter | solution.py:1000
  206.8 18.9 %collective-permute-start.28 = (bf16[128,1536]{1,0:T(8,128)(2,1)}, bf16[128,1536]{1,0:T(8,128)(2,1)S(1)}, u32[]{:S(2)}, u32[]{:S(2)}) collective-permute-start(bf16[128,1536]{1,0:T(8,128)(2,1)} %get-tuple-element.142), channel_id=1, source_target_pairs={{0,2},{1,3},{2,0},{3,1},{4,6},{5,7},{6,4},{7,5},{8,10},{9,11},{10,... | collective-permute-start | bytes 1179656 | tf_op jit(solution)/shard_map/ppermute | solution.py:730
  228.2 20.6 %collective-permute-start.30 = (bf16[128,1664]{1,0:T(8,128)(2,1)S(1)}, bf16[128,1664]{1,0:T(8,128)(2,1)S(1)}, u32[]{:S(2)}, u32[]{:S(2)}) collective-permute-start(bf16[128,1664]{1,0:T(8,128)(2,1)S(1)} %pad_maximum_fusion.4.refs_0_), channel_id=1, source_target_pairs={{0,3},{1,0},{2,1},{3,2},{4,7},{5,4},{6,5},{7,6},{8,11},{9,8},{10,9... | collective-permute-start | bytes 1277960 | tf_op jit(solution)/shard_map/ppermute | solution.py:730
  230.5 18.4 %collective-permute-start.31 = (bf16[128,1664]{1,0:T(8,128)(2,1)S(1)}, bf16[128,1664]{1,0:T(8,128)(2,1)S(1)}, u32[]{:S(2)}, u32[]{:S(2)}) collective-permute-start(bf16[128,1664]{1,0:T(8,128)(2,1)S(1)} %pad_maximum_fusion.4.refs_0_), channel_id=1, source_target_pairs={{0,2},{1,3},{2,0},{3,1},{4,6},{5,7},{6,4},{7,5},{8,10},{9,11},{10,... | collective-permute-start | bytes 1277960 | tf_op jit(solution)/shard_map/ppermute | solution.py:730
  231.0 21.5 %collective-permute-start.32 = (bf16[128,1664]{1,0:T(8,128)(2,1)S(1)}, bf16[128,1664]{1,0:T(8,128)(2,1)S(1)}, u32[]{:S(2)}, u32[]{:S(2)}) collective-permute-start(bf16[128,1664]{1,0:T(8,128)(2,1)S(1)} %pad_maximum_fusion.4.refs_0_), channel_id=1, source_target_pairs={{0,1},{1,2},{2,3},{3,0},{4,5},{5,6},{6,7},{7,4},{8,9},{9,10},{10,1... | collective-permute-start | bytes 1277960 | tf_op jit(solution)/shard_map/ppermute | solution.py:730
  297.1 21.6 %collective-permute-start.35 = (bf16[128,1536]{1,0:T(8,128)(2,1)S(1)}, bf16[128,1536]{1,0:T(8,128)(2,1)S(1)}, u32[]{:S(2)}, u32[]{:S(2)}) collective-permute-start(bf16[128,1536]{1,0:T(8,128)(2,1)S(1)} %get-tuple-element.170), channel_id=1, source_target_pairs={{0,1},{1,2},{2,3},{3,0},{4,5},{5,6},{6,7},{7,4},{8,9},{9,10},{10,1... | collective-permute-start | bytes 1179656 | tf_op jit(solution)/shard_map/ppermute | solution.py:730
  297.2 21.6 %collective-permute-start.36 = (bf16[128,1536]{1,0:T(8,128)(2,1)S(1)}, bf16[128,1536]{1,0:T(8,128)(2,1)S(1)}, u32[]{:S(2)}, u32[]{:S(2)}) collective-permute-start(bf16[128,1536]{1,0:T(8,128)(2,1)S(1)} %get-tuple-element.171), channel_id=1, source_target_pairs={{0,2},{1,3},{2,0},{3,1},{4,6},{5,7},{6,4},{7,5},{8,10},{9,11},{10,... | collective-permute-start | bytes 1179656 | tf_op jit(solution)/shard_map/ppermute | solution.py:730
  299.2 20.5 %collective-permute-start.37 = (bf16[128,1536]{1,0:T(8,128)(2,1)S(1)}, bf16[128,1536]{1,0:T(8,128)(2,1)S(1)}, u32[]{:S(2)}, u32[]{:S(2)}) collective-permute-start(bf16[128,1536]{1,0:T(8,128)(2,1)S(1)} %get-tuple-element.172), channel_id=1, source_target_pairs={{0,3},{1,0},{2,1},{3,2},{4,7},{5,4},{6,5},{7,6},{8,11},{9,8},{10,9... | collective-permute-start | bytes 1179656 | tf_op jit(solution)/shard_map/ppermute | solution.py:730
  300.5 36.0 %collective-permute-start.38 = (bf16[128,1664]{1,0:T(8,128)(2,1)S(1)}, bf16[128,1664]{1,0:T(8,128)(2,1)S(1)}, u32[]{:S(2)}, u32[]{:S(2)}) collective-permute-start(bf16[128,1664]{1,0:T(8,128)(2,1)S(1)} %copy-done.40), channel_id=1, source_target_pairs={{0,1},{1,2},{2,3},{3,0},{4,5},{5,6},{6,7},{7,4},{8,9},{9,10},{10,1... | collective-permute-start | bytes 1277960 | tf_op jit(solution)/shard_map/ppermute | solution.py:730
  301.4 35.1 %collective-permute-start.39 = (bf16[128,1664]{1,0:T(8,128)(2,1)S(1)}, bf16[128,1664]{1,0:T(8,128)(2,1)S(1)}, u32[]{:S(2)}, u32[]{:S(2)}) collective-permute-start(bf16[128,1664]{1,0:T(8,128)(2,1)S(1)} %copy-done.39), channel_id=1, source_target_pairs={{0,2},{1,3},{2,0},{3,1},{4,6},{5,7},{6,4},{7,5},{8,10},{9,11},{10,... | collective-permute-start | bytes 1277960 | tf_op jit(solution)/shard_map/ppermute | solution.py:730
  318.7 18.4 %collective-permute-start.40 = (bf16[128,1664]{1,0:T(8,128)(2,1)S(1)}, bf16[128,1664]{1,0:T(8,128)(2,1)S(1)}, u32[]{:S(2)}, u32[]{:S(2)}) collective-permute-start(bf16[128,1664]{1,0:T(8,128)(2,1)S(1)} %copy-done.38), channel_id=1, source_target_pairs={{0,3},{1,0},{2,1},{3,2},{4,7},{5,4},{6,5},{7,6},{8,11},{9,8},{10,9... | collective-permute-start | bytes 1277960 | tf_op jit(solution)/shard_map/ppermute | solution.py:730
  348.1 69.8 %all-gather.11.cloned.1.call-start = ((), (), s32[]{:S(2)}) async-start(), calls=%async_computation.7 | async-start | bytes 7729152 | tf_op jit(solution)/shard_map/all_gather | solution.py:1031
  364.9 23.1 %collective-permute-start.42 = (bf16[128,1536]{1,0:T(8,128)(2,1)S(1)}, bf16[128,1536]{1,0:T(8,128)(2,1)S(1)}, u32[]{:S(2)}, u32[]{:S(2)}) collective-permute-start(bf16[128,1536]{1,0:T(8,128)(2,1)S(1)} %convert_element_type.333), channel_id=1, source_target_pairs={{0,64},{1,65},{2,66},{3,67},{4,68},{5,69},{6,70},{7,71},{8,72},{9,... | collective-permute-start | bytes 1179656 | tf_op jit(solution)/shard_map/ppermute | solution.py:1015
  372.5 20.5 %collective-permute-start.41 = (bf16[128,1536]{1,0:T(8,128)(2,1)S(1)}, bf16[128,1536]{1,0:T(8,128)(2,1)S(1)}, u32[]{:S(2)}, u32[]{:S(2)}) collective-permute-start(bf16[128,1536]{1,0:T(8,128)(2,1)S(1)} %convert_element_type.332), channel_id=1, source_target_pairs={{64,0},{65,1},{66,2},{67,3},{68,4},{69,5},{70,6},{71,7},{72,8},{73... | collective-permute-start | bytes 1179656 | tf_op jit(solution)/shard_map/ppermute | solution.py:1016
  374.1 18.3 %collective-permute-start.46 = (f32[276,128]{1,0:T(8,128)S(1)}, f32[276,128]{1,0:T(8,128)S(1)}, u32[]{:S(2)}, u32[]{:S(2)}) collective-permute-start(f32[276,128]{1,0:T(8,128)S(1)} %add.453), channel_id=1, source_target_pairs={{0,16},{4,20},{8,24},{12,28},{16,0},{20,4},{24,8},{28,12},{32,48},... | collective-permute-start | bytes 423944 | tf_op jit(solution)/shard_map/ppermute | solution.py:783
  (86 other events, 1048.5 us)
Sparse Core Ops, SparseCore 0:
  34.1 55.9 all-gather.6
  92.5 50.8 all-gather.8
  204.9 75.4 reduce-scatter.2
  287.1 49.3 reduce-scatter.4
  359.1 57.8 all-gather.10

commit v12 on v11

--- a/solution.py
+++ b/solution.py
@@ -778,7 +778,6 @@
 
 
 def sum_small(v):
-    v = v + lax.ppermute(v, DP, dp_pairs(lambda x, z, c: (x, z, 1 - c)))
     v = v + sum(
         lax.ppermute(v, DP, dp_pairs(lambda x, z, c: (x, (z + k) % 4, c))) for k in range(1, 4)
     )
@@ -1007,9 +1006,30 @@
         rows = jnp.concatenate([v[:piece], v[2 * piece :]], axis=0)
         return jnp.transpose(rows.reshape(-1, SLOTS, quarter), (1, 0, 2))
 
+    def to_section(v0, v1):
+        kept = jnp.where(first, v0, v1).astype(F32)
+        return kept + swap_section(jnp.where(first, v1, v0)).astype(F32)
+
+    def small_of(by_pair, back, gain_grad):
+        return jnp.concatenate(
+            [
+                by_pair.reshape(-1, LANES),
+                back["small_bc"].reshape(-1, LANES),
+                back["small_dt"],
+                gain_grad.reshape(-1, LANES),
+                back["gdt"].reshape(-1, LANES),
+            ],
+            axis=0,
+        )
+
+    small0 = small_of(small_gate + small_scan, back0, gain_grad0)
+    small1 = small_of(back1["small"], back1, gain_grad1)
+    small_half = to_section(small0, small1)
+    small_half = small_half + cross_core(small_half)
+
     rows1 = by_row(owned1)
-    owned0, owned1, rows1, gain_grad0, dtokens, result = lax.optimization_barrier(
-        (owned0, owned1, rows1, gain_grad0, dtokens, result)
+    owned0, owned1, rows1, small_half, dtokens = lax.optimization_barrier(
+        (owned0, owned1, rows1, small_half, dtokens)
     )
 
     result_moved = lax.ppermute(result.astype(BF16), "section", [(0, 1)]).astype(F32)
@@ -1017,10 +1037,6 @@
     ends = jnp.where(
         first, jnp.stack([dtokens, dtokens_moved]), jnp.stack([result_moved, result])
     )[None]
-
-    def to_section(v0, v1):
-        kept = jnp.where(first, v0, v1).astype(F32)
-        return kept + swap_section(jnp.where(first, v1, v0)).astype(F32)
 
     got = across(jnp.concatenate([by_row(owned0), rows1], axis=0))
     out_rows = to_section(owned0[piece : 2 * piece], owned1[piece : 2 * piece]).astype(BF16)
@@ -1042,21 +1058,7 @@
         tiled=False,
     )
 
-    def small_of(by_pair, back, gain_grad):
-        return jnp.concatenate(
-            [
-                by_pair.reshape(-1, LANES),
-                back["small_bc"].reshape(-1, LANES),
-                back["small_dt"],
-                gain_grad.reshape(-1, LANES),
-                back["gdt"].reshape(-1, LANES),
-            ],
-            axis=0,
-        )
-
-    small0 = small_of(small_gate + small_scan, back0, gain_grad0)
-    small1 = small_of(back1["small"], back1, gain_grad1)
-    small_sum = sum_small(to_section(small0, small1))
+    small_sum = sum_small(small_half)
     everyone = in_order(gather_slots(small_sum), 1)
     n_pair, n_bc = PAIRS * 8, 2 * 8
     by_pair = everyone[:, :n_pair].reshape(SLOTS, PAIRS, 8, LANES)

time: 443 us -> 459 us (1.036)
  waiting for transfers between devices: 186 us -> 196 us
  starting transfers between devices: 78.6 us -> 84.4 us
    reduce_scatter x1, waiting for transfers between devices: 0.02 us -> 5.51 us  [shards(): lax.psum_scatter(owned0, ('x', 'z'), scatter_dimension=0, tiled=False)]
    ppermute x1, waiting for transfers between devices: 9.16 us -> 3.9 us  [shards(): lax.ppermute(result.astype(BF16), 'section', [(0, 1)]).astype(F32)]
    ppermute x1, starting transfers between devices: 1.47 us -> 6.09 us  [shards(): lax.ppermute(dtokens.astype(BF16), 'section', [(1, 0)]).astype(F32)]
    unnamed x112 -> x110, local copies, waits for them, and re-layouts: 12.6 us -> 12.6 us
  transfers between devices with their start and end apart: 59 -> 59, of which waited for: 32 -> 35; matrix products, arithmetic and copies ran while one was open for 8% -> 8% of each run, Pallas kernels for 9% -> 9%
where the time goes in v12:
time: 459 us; the launch traced here: 451 us
  waiting for transfers between devices  196 us (43%)
  Pallas kernels  94.5 us (21%)
  starting transfers between devices  84.4 us (18%)
  local copies, waits for them, and re-layouts  34.1 us (7%)
  other arithmetic  27.1 us (6%)
  between operations  15.6 us (3%)
    ppermute x36, waiting for transfers between devices, send_shard(): return lax.ppermute(v, 'shard', ring(SLOTS, k)) if k else v  132 us
    pallas_call x6, Pallas kernels, kernel_call(): pl.pallas_call(run, in_specs=[pl.BlockSpec(memory_space=pltpu.VMEM if len...  84.6 us
    ppermute x36, starting transfers between devices, send_shard(): return lax.ppermute(v, 'shard', ring(SLOTS, k)) if k else v  50.5 us
    ppermute x4, waiting for transfers between devices, swap_section(): return lax.ppermute(v, 'section', [(0, 1), (1, 0)])  19.9 us
    unnamed x110, local copies, waits for them, and re-layouts  12.6 us
    pallas_call x1, Pallas kernels, assemble(): pl.pallas_call(body, grid=(9,), in_specs=[pl.BlockSpec((16, 48, quarter),...  9.95 us
    ppermute x4, starting transfers between devices, send_across(): return lax.ppermute(v, ('section', 'shard'), pairs)  9.45 us
  transfers between devices with their start and end apart: 59, of which 35 were waited for; matrix products, arithmetic and copies ran while one was open for 8% of the time, Pallas kernels for 9%

profile of v12, /device:TPU:4, one launch (start us, length us, event | category | flops | bytes accessed | tf_op | source)
XLA Modules:
  0.0 451.5 jit_solution(13174548284926304625)
XLA Ops:
  13.0 5.7 %collective-permute-start.4 = (bf16[112,384]{1,0:T(8,128)(2,1)S(1)}, bf16[112,384]{1,0:T(8,128)(2,1)S(1)}, u32[]{:S(2)}, u32[]{:S(2)}) collective-permute-start(bf16[112,384]{1,0:T(8,128)(2,1)S(1)} %get-tuple-element.260), channel_id=1, source_target_pairs={{0,66},{1,67},{2,64},{3,65},{64,2},{65,3},{66,0},{67,1},{4,70},{5,... | collective-permute-start | bytes 258056 | tf_op jit(solution)/shard_map/weights/ppermute | solution.py:739
  67.1 7.7 %collective-permute-done.17 = bf16[4,187,128]{2,1,0:T(8,128)(2,1)S(1)} collective-permute-done((bf16[4,187,128]{2,1,0:T(8,128)(2,1)S(1)}, bf16[4,187,128]{2,1,0:T(8,128)(2,1)S(1)}, u32[]{:S(2)}, u32[]{:S(2)}) %collective-permute-start.17) | collective-permute-done | bytes 191520 | tf_op jit(solution)/shard_map/small_weights/ppermute | solution.py:747
  84.3 5.9 %all-gather.7.cloned.1.call-done = bf16[2560,1536]{1,0:T(8,128)(2,1)} async-done(((bf16[160,1536]{1,0:T(8,128)(2,1)}), bf16[2560,1536]{1,0:T(8,128)(2,1)}) %all-gather.7.cloned.1.call-update) | async-done | bytes 7864336 | tf_op jit(solution)/shard_map/weights/all_gather | solution.py:867
  90.7 14.3 %layer_forward.2 = (bf16[128,1664]{1,0:T(8,128)(2,1)}, bf16[128,1664]{1,0:T(8,128)(2,1)}, bf16[128,1664]{1,0:T(8,128)(2,1)}, bf16[128,1664]{1,0:T(8,128)(2,1)}, ...) custom-call(bf16[128,1536]{1,0:T(8,128)(2,1)} %copy-done.14, ...), custom_call_target="tpu_custom_call" | custom-call | flops 19800000512 | bytes 1048576 | tf_op jit(solution)/shard_map/layer_forward/pallas_call | solution.py:156
  110.8 7.7 %collective-permute-done.18 = bf16[128,1664]{1,0:T(8,128)(2,1)S(1)} collective-permute-done((bf16[128,1664]{1,0:T(8,128)(2,1)}, bf16[128,1664]{1,0:T(8,128)(2,1)S(1)}, u32[]{:S(2)}, u32[]{:S(2)}) %collective-permute-start.18) | collective-permute-done | bytes 426016 | tf_op jit(solution)/shard_map/ppermute | solution.py:730
  118.5 10.1 %collective-permute-done.19 = bf16[128,1664]{1,0:T(8,128)(2,1)S(1)} collective-permute-done((bf16[128,1664]{1,0:T(8,128)(2,1)}, bf16[128,1664]{1,0:T(8,128)(2,1)S(1)}, u32[]{:S(2)}, u32[]{:S(2)}) %collective-permute-start.19) | collective-permute-done | bytes 426016 | tf_op jit(solution)/shard_map/ppermute | solution.py:730
  134.6 15.0 %collective-permute-done.21.refs_1_ = bf16[128,1536]{1,0:T(8,128)(2,1)S(1)} collective-permute-done((bf16[128,1536]{1,0:T(8,128)(2,1)S(1)}, bf16[128,1536]{1,0:T(8,128)(2,1)S(1)}, u32[]{:S(2)}, u32[]{:S(2)}) %collective-permute-start.21) | collective-permute-done | bytes 393248 | tf_op jit(solution)/shard_map/ppermute | solution.py:730
  154.1 14.9 %layer_forward.3 = (bf16[128,1664]{1,0:T(8,128)(2,1)}, bf16[128,1664]{1,0:T(8,128)(2,1)}, bf16[128,1664]{1,0:T(8,128)(2,1)}, bf16[128,1664]{1,0:T(8,128)(2,1)}, ...) custom-call(bf16[128,1536]{1,0:T(8,128)(2,1)} %copy-done.17, ...), custom_call_target="tpu_custom_call" | custom-call | flops 19800000512 | bytes 1048576 | tf_op jit(solution)/shard_map/layer_forward/pallas_call | solution.py:156
  175.8 28.9 %backward_1.1 = (bf16[512,768]{1,0:T(8,128)(2,1)}, bf16[512,768]{1,0:T(8,128)(2,1)}, f32[6,8,128]{2,1,0:T(8,128)}, bf16[512,768]{1,0:T(8,128)(2,1)}, bf16[512,38...) custom-call(bf16[128,1536]{1,0:T(8,128)(2,1)} %copy-done.24, ...), custom_call_target="tpu_custom_call" | custom-call | flops 30799998976 | bytes 1048576 | tf_op jit(solution)/shard_map/backward_1/pallas_call | solution.py:156
  209.9 7.8 %collective-permute-done.27 = bf16[128,1536]{1,0:T(8,128)(2,1)S(1)} collective-permute-done((bf16[128,1536]{1,0:T(8,128)(2,1)}, bf16[128,1536]{1,0:T(8,128)(2,1)S(1)}, u32[]{:S(2)}, u32[]{:S(2)}) %collective-permute-start.27) | collective-permute-done | bytes 393248 | tf_op jit(solution)/shard_map/ppermute | solution.py:730
  217.7 8.1 %collective-permute-done.28 = bf16[128,1536]{1,0:T(8,128)(2,1)S(1)} collective-permute-done((bf16[128,1536]{1,0:T(8,128)(2,1)}, bf16[128,1536]{1,0:T(8,128)(2,1)S(1)}, u32[]{:S(2)}, u32[]{:S(2)}) %collective-permute-start.28) | collective-permute-done | bytes 393248 | tf_op jit(solution)/shard_map/ppermute | solution.py:730
  231.1 17.3 %collective-permute-done.30.refs_1_ = bf16[128,1664]{1,0:T(8,128)(2,1)S(1)} collective-permute-done((bf16[128,1664]{1,0:T(8,128)(2,1)S(1)}, bf16[128,1664]{1,0:T(8,128)(2,1)S(1)}, u32[]{:S(2)}, u32[]{:S(2)}) %collective-permute-start.30) | collective-permute-done | bytes 426016 | tf_op jit(solution)/shard_map/ppermute | solution.py:730
  256.9 10.6 %backward_0_gate.1 = (bf16[512,768]{1,0:T(8,128)(2,1)}, bf16[512,768]{1,0:T(8,128)(2,1)S(1)}, f32[512,768]{1,0:T(8,128)S(1)}, f32[6,8,128]{2,1,0:T(8,128)S(1)}, ...) custom-call(bf16[128,1664]{1,0:T(8,128)(2,1)S(1)} %pad_maximum_fusion.4.refs_0_, ...), custom_call_target="tpu_custom_call" | custom-call | flops 15399999488 | bytes 1048576 | tf_op jit(solution)/shard_map/backward_0_gate/pallas_call | solution.py:156
  267.7 11.1 %backward_0_scan.1 = (f32[6,8,128]{2,1,0:T(8,128)S(1)}, bf16[512,768]{1,0:T(8,128)(2,1)S(1)}, bf16[512,384]{1,0:T(8,128)(2,1)S(1)}, f32[2,8,128]{2,1,0:T(8,128)S...) custom-call(f32[2,512,768]{2,1,0:T(8,128)S(1)} %copy-done.6, ...), custom_call_target="tpu_custom_call" | custom-call | flops 22000001024 | bytes 1048576 | tf_op jit(solution)/shard_map/backward_0_scan/pallas_call | solution.py:156
  303.0 15.2 %collective-permute-done.35 = bf16[128,1536]{1,0:T(8,128)(2,1)S(1)} collective-permute-done((bf16[128,1536]{1,0:T(8,128)(2,1)S(1)}, bf16[128,1536]{1,0:T(8,128)(2,1)S(1)}, u32[]{:S(2)}, u32[]{:S(2)}) %collective-permute-start.35) | collective-permute-done | bytes 393248 | tf_op jit(solution)/shard_map/ppermute | solution.py:730
  322.3 9.9 %collective-permute-done.38 = f32[276,128]{1,0:T(8,128)S(1)} collective-permute-done((f32[276,128]{1,0:T(8,128)S(1)}, f32[276,128]{1,0:T(8,128)S(1)}, u32[]{:S(2)}, u32[]{:S(2)}) %collective-permute-start.38) | collective-permute-done | bytes 141344 | tf_op jit(solution)/shard_map/ppermute | solution.py:747
  343.4 7.2 %all-to-all-start = ((bf16[8,112,384]{2,1,0:T(8,128)(2,1)}), bf16[8,112,384]{2,1,0:T(8,128)(2,1)S(1)}, u32[]{:S(2)}, u32[]{:S(2)}) async-start(bf16[8,112,384]{2,1,0:T(8,128)(2,1)} %pad_maximum_fusion.1), calls=%async_computation.2 | async-start | bytes 1376256 | tf_op jit(solution)/shard_map/all_to_all | solution.py:743
  351.8 8.9 %all-to-all-done = bf16[8,112,384]{2,1,0:T(8,128)(2,1)S(1)} async-done(((bf16[8,112,384]{2,1,0:T(8,128)(2,1)}), bf16[8,112,384]{2,1,0:T(8,128)(2,1)S(1)}, u32[]{:S(2)}, u32[]{:S(2)}) %all-to-all-start) | async-done | bytes 688160 | tf_op jit(solution)/shard_map/all_to_all | solution.py:743
  365.5 10.0 %collective-permute-done.41 = bf16[128,1664]{1,0:T(8,128)(2,1)S(1)} collective-permute-done((bf16[128,1664]{1,0:T(8,128)(2,1)}, bf16[128,1664]{1,0:T(8,128)(2,1)S(1)}, u32[]{:S(2)}, u32[]{:S(2)}) %collective-permute-start.41) | collective-permute-done | bytes 426016 | tf_op jit(solution)/shard_map/ppermute | solution.py:730
  375.5 8.4 %collective-permute-done.42 = bf16[128,1664]{1,0:T(8,128)(2,1)S(1)} collective-permute-done((bf16[128,1664]{1,0:T(8,128)(2,1)}, bf16[128,1664]{1,0:T(8,128)(2,1)S(1)}, u32[]{:S(2)}, u32[]{:S(2)}) %collective-permute-start.42) | collective-permute-done | bytes 426016 | tf_op jit(solution)/shard_map/ppermute | solution.py:730
  389.3 6.1 %collective-permute-start.40 = (bf16[128,1536]{1,0:T(8,128)(2,1)S(1)}, bf16[128,1536]{1,0:T(8,128)(2,1)S(1)}, u32[]{:S(2)}, u32[]{:S(2)}) collective-permute-start(bf16[128,1536]{1,0:T(8,128)(2,1)S(1)} %convert_element_type.328), channel_id=1, source_target_pairs={{64,0},{65,1},{66,2},{67,3},{68,4},{69,5},{70,6},{71,7},{72,8},{73... | collective-permute-start | bytes 1179656 | tf_op jit(solution)/shard_map/ppermute | solution.py:1036
  395.4 5.6 %collective-permute-done.46 = f32[276,128]{1,0:T(8,128)S(1)} collective-permute-done((f32[276,128]{1,0:T(8,128)S(1)}, f32[276,128]{1,0:T(8,128)S(1)}, u32[]{:S(2)}, u32[]{:S(2)}) %collective-permute-start.46) | collective-permute-done | bytes 141344 | tf_op jit(solution)/shard_map/ppermute | solution.py:782
  408.4 7.4 %collective-permute-done.48 = f32[276,128]{1,0:T(8,128)S(1)} collective-permute-done((f32[276,128]{1,0:T(8,128)S(1)}, f32[276,128]{1,0:T(8,128)S(1)}, u32[]{:S(2)}, u32[]{:S(2)}) %collective-permute-start.48) | collective-permute-done | bytes 141344 | tf_op jit(solution)/shard_map/ppermute | solution.py:784
  434.5 10.0 %assemble.1 = (f32[6448,384]{1,0:T(8,128)}, f32[768,1536]{1,0:T(8,128)}) custom-call(bf16[16,592,384]{2,1,0:T(8,128)(2,1)} %bitcast.181, bf16[16,592,384]{2,1,0:T(8,128)(2,1)} %bitcast.182, bf16[16,592,384]{2,1,0:T(8,128)(2,1)} %bitcast.183, f32[48,384]{1,0:T(8,128)} %reshape.502.dt), custom_call_target="tpu_custom_call" | custom-call | tf_op jit(solution)/shard_map/assemble/pallas_call | solution.py:700
  (388 shorter events, 182.0 us)
Async XLA Ops:
  7.2 83.0 %all-gather.7.cloned.1.call-start = ((), (), s32[]{:S(2)}) async-start(), calls=%async_computation.5 | async-start | bytes 8355840 | tf_op jit(solution)/shard_map/weights/all_gather | solution.py:867
  34.0 119.3 %all-gather.9.cloned.1.call-start = ((), (), s32[]{:S(2)}) async-start(), calls=%async_computation.6 | async-start | bytes 8355840 | tf_op jit(solution)/shard_map/all_gather | solution.py:925
  64.8 19.5 %collective-permute-start.11 = (bf16[128,1536]{1,0:T(8,128)(2,1)S(1)}, bf16[128,1536]{1,0:T(8,128)(2,1)S(1)}, u32[]{:S(2)}, u32[]{:S(2)}) collective-permute-start(bf16[128,1536]{1,0:T(8,128)(2,1)S(1)} %fusion.6.refs_4_.refs_0_), channel_id=1, source_target_pairs={{0,3},{1,0},{2,1},{3,2},{4,7},{5,4},{6,5},{7,6},{8,11},{9,8},{10,9... | collective-permute-start | bytes 1179656 | tf_op jit(solution)/shard_map/ppermute | solution.py:730
  64.9 19.4 %collective-permute-start.12 = (bf16[128,1536]{1,0:T(8,128)(2,1)S(1)}, bf16[128,1536]{1,0:T(8,128)(2,1)S(1)}, u32[]{:S(2)}, u32[]{:S(2)}) collective-permute-start(bf16[128,1536]{1,0:T(8,128)(2,1)S(1)} %fusion.6.refs_4_.refs_0_), channel_id=1, source_target_pairs={{0,2},{1,3},{2,0},{3,1},{4,6},{5,7},{6,4},{7,5},{8,10},{9,11},{10,... | collective-permute-start | bytes 1179656 | tf_op jit(solution)/shard_map/ppermute | solution.py:730
  66.3 18.0 %collective-permute-start.13 = (bf16[128,1536]{1,0:T(8,128)(2,1)S(1)}, bf16[128,1536]{1,0:T(8,128)(2,1)S(1)}, u32[]{:S(2)}, u32[]{:S(2)}) collective-permute-start(bf16[128,1536]{1,0:T(8,128)(2,1)S(1)} %fusion.6.refs_4_.refs_0_), channel_id=1, source_target_pairs={{0,1},{1,2},{2,3},{3,0},{4,5},{5,6},{6,7},{7,4},{8,9},{9,10},{10,1... | collective-permute-start | bytes 1179656 | tf_op jit(solution)/shard_map/ppermute | solution.py:730
  90.2 192.2 %reduce-scatter.3.cloned.1.call-start = ((), (), s32[]{:S(2)}) async-start(), calls=%async_computation.3 | async-start | bytes 8355840 | tf_op jit(solution)/shard_map/reduce_scatter | solution.py:970
  106.6 22.0 %collective-permute-start.19 = (bf16[128,1664]{1,0:T(8,128)(2,1)}, bf16[128,1664]{1,0:T(8,128)(2,1)S(1)}, u32[]{:S(2)}, u32[]{:S(2)}) collective-permute-start(bf16[128,1664]{1,0:T(8,128)(2,1)} %get-tuple-element.122), channel_id=1, source_target_pairs={{0,2},{1,3},{2,0},{3,1},{4,6},{5,7},{6,4},{7,5},{8,10},{9,11},{10,... | collective-permute-start | bytes 1277960 | tf_op jit(solution)/shard_map/ppermute | solution.py:730
  109.3 19.3 %collective-permute-start.20 = (bf16[128,1664]{1,0:T(8,128)(2,1)}, bf16[128,1664]{1,0:T(8,128)(2,1)S(1)}, u32[]{:S(2)}, u32[]{:S(2)}) collective-permute-start(bf16[128,1664]{1,0:T(8,128)(2,1)} %get-tuple-element.123), channel_id=1, source_target_pairs={{0,3},{1,0},{2,1},{3,2},{4,7},{5,4},{6,5},{7,6},{8,11},{9,8},{10,9... | collective-permute-start | bytes 1277960 | tf_op jit(solution)/shard_map/ppermute | solution.py:730
  130.3 19.3 %collective-permute-start.21 = (bf16[128,1536]{1,0:T(8,128)(2,1)S(1)}, bf16[128,1536]{1,0:T(8,128)(2,1)S(1)}, u32[]{:S(2)}, u32[]{:S(2)}) collective-permute-start(bf16[128,1536]{1,0:T(8,128)(2,1)S(1)} %get-tuple-element.206.refs_0_), channel_id=1, source_target_pairs={{0,3},{1,0},{2,1},{3,2},{4,7},{5,4},{6,5},{7,6},{8,11},{9,8},{10,9... | collective-permute-start | bytes 1179656 | tf_op jit(solution)/shard_map/ppermute | solution.py:730
  133.7 19.5 %collective-permute-start.23 = (bf16[128,1536]{1,0:T(8,128)(2,1)S(1)}, bf16[128,1536]{1,0:T(8,128)(2,1)S(1)}, u32[]{:S(2)}, u32[]{:S(2)}) collective-permute-start(bf16[128,1536]{1,0:T(8,128)(2,1)S(1)} %get-tuple-element.206.refs_0_), channel_id=1, source_target_pairs={{0,1},{1,2},{2,3},{3,0},{4,5},{5,6},{6,7},{7,4},{8,9},{9,10},{10,1... | collective-permute-start | bytes 1179656 | tf_op jit(solution)/shard_map/ppermute | solution.py:730
  204.8 134.7 %reduce-scatter.5.cloned.1.call-start = ((), (), s32[]{:S(2)}) async-start(), calls=%async_computation.4 | async-start | bytes 4423680 | tf_op jit(solution)/shard_map/reduce_scatter | solution.py:999
  206.8 18.9 %collective-permute-start.28 = (bf16[128,1536]{1,0:T(8,128)(2,1)}, bf16[128,1536]{1,0:T(8,128)(2,1)S(1)}, u32[]{:S(2)}, u32[]{:S(2)}) collective-permute-start(bf16[128,1536]{1,0:T(8,128)(2,1)} %get-tuple-element.141), channel_id=1, source_target_pairs={{0,2},{1,3},{2,0},{3,1},{4,6},{5,7},{6,4},{7,5},{8,10},{9,11},{10,... | collective-permute-start | bytes 1179656 | tf_op jit(solution)/shard_map/ppermute | solution.py:730
  227.8 20.6 %collective-permute-start.30 = (bf16[128,1664]{1,0:T(8,128)(2,1)S(1)}, bf16[128,1664]{1,0:T(8,128)(2,1)S(1)}, u32[]{:S(2)}, u32[]{:S(2)}) collective-permute-start(bf16[128,1664]{1,0:T(8,128)(2,1)S(1)} %pad_maximum_fusion.4.refs_0_), channel_id=1, source_target_pairs={{0,3},{1,0},{2,1},{3,2},{4,7},{5,4},{6,5},{7,6},{8,11},{9,8},{10,9... | collective-permute-start | bytes 1277960 | tf_op jit(solution)/shard_map/ppermute | solution.py:730
  230.0 18.4 %collective-permute-start.31 = (bf16[128,1664]{1,0:T(8,128)(2,1)S(1)}, bf16[128,1664]{1,0:T(8,128)(2,1)S(1)}, u32[]{:S(2)}, u32[]{:S(2)}) collective-permute-start(bf16[128,1664]{1,0:T(8,128)(2,1)S(1)} %pad_maximum_fusion.4.refs_0_), channel_id=1, source_target_pairs={{0,2},{1,3},{2,0},{3,1},{4,6},{5,7},{6,4},{7,5},{8,10},{9,11},{10,... | collective-permute-start | bytes 1277960 | tf_op jit(solution)/shard_map/ppermute | solution.py:730
  230.5 21.5 %collective-permute-start.32 = (bf16[128,1664]{1,0:T(8,128)(2,1)S(1)}, bf16[128,1664]{1,0:T(8,128)(2,1)S(1)}, u32[]{:S(2)}, u32[]{:S(2)}) collective-permute-start(bf16[128,1664]{1,0:T(8,128)(2,1)S(1)} %pad_maximum_fusion.4.refs_0_), channel_id=1, source_target_pairs={{0,1},{1,2},{2,3},{3,0},{4,5},{5,6},{6,7},{7,4},{8,9},{9,10},{10,1... | collective-permute-start | bytes 1277960 | tf_op jit(solution)/shard_map/ppermute | solution.py:730
  297.0 21.1 %collective-permute-start.35 = (bf16[128,1536]{1,0:T(8,128)(2,1)S(1)}, bf16[128,1536]{1,0:T(8,128)(2,1)S(1)}, u32[]{:S(2)}, u32[]{:S(2)}) collective-permute-start(bf16[128,1536]{1,0:T(8,128)(2,1)S(1)} %get-tuple-element.173), channel_id=1, source_target_pairs={{0,1},{1,2},{2,3},{3,0},{4,5},{5,6},{6,7},{7,4},{8,9},{9,10},{10,1... | collective-permute-start | bytes 1179656 | tf_op jit(solution)/shard_map/ppermute | solution.py:730
  297.1 21.0 %collective-permute-start.36 = (bf16[128,1536]{1,0:T(8,128)(2,1)S(1)}, bf16[128,1536]{1,0:T(8,128)(2,1)S(1)}, u32[]{:S(2)}, u32[]{:S(2)}) collective-permute-start(bf16[128,1536]{1,0:T(8,128)(2,1)S(1)} %get-tuple-element.174), channel_id=1, source_target_pairs={{0,2},{1,3},{2,0},{3,1},{4,6},{5,7},{6,4},{7,5},{8,10},{9,11},{10,... | collective-permute-start | bytes 1179656 | tf_op jit(solution)/shard_map/ppermute | solution.py:730
  299.2 19.6 %collective-permute-start.37 = (bf16[128,1536]{1,0:T(8,128)(2,1)S(1)}, bf16[128,1536]{1,0:T(8,128)(2,1)S(1)}, u32[]{:S(2)}, u32[]{:S(2)}) collective-permute-start(bf16[128,1536]{1,0:T(8,128)(2,1)S(1)} %get-tuple-element.175), channel_id=1, source_target_pairs={{0,3},{1,0},{2,1},{3,2},{4,7},{5,4},{6,5},{7,6},{8,11},{9,8},{10,9... | collective-permute-start | bytes 1179656 | tf_op jit(solution)/shard_map/ppermute | solution.py:730
  343.4 17.4 %all-to-all-start = ((bf16[8,112,384]{2,1,0:T(8,128)(2,1)}), bf16[8,112,384]{2,1,0:T(8,128)(2,1)S(1)}, u32[]{:S(2)}, u32[]{:S(2)}) async-start(bf16[8,112,384]{2,1,0:T(8,128)(2,1)} %pad_maximum_fusion.1), calls=%async_computation.2 | async-start | bytes 1376256 | tf_op jit(solution)/shard_map/all_to_all | solution.py:743
  350.6 83.9 %all-gather.11.cloned.1.call-start = ((), (), s32[]{:S(2)}) async-start(), calls=%async_computation.7 | async-start | bytes 7729152 | tf_op jit(solution)/shard_map/all_gather | solution.py:1047
  362.7 21.1 %collective-permute-start.42 = (bf16[128,1664]{1,0:T(8,128)(2,1)}, bf16[128,1664]{1,0:T(8,128)(2,1)S(1)}, u32[]{:S(2)}, u32[]{:S(2)}) collective-permute-start(bf16[128,1664]{1,0:T(8,128)(2,1)} %get-tuple-element.184), channel_id=1, source_target_pairs={{0,2},{1,3},{2,0},{3,1},{4,6},{5,7},{6,4},{7,5},{8,10},{9,11},{10,... | collective-permute-start | bytes 1277960 | tf_op jit(solution)/shard_map/ppermute | solution.py:730
  364.8 19.6 %collective-permute-start.43 = (bf16[128,1664]{1,0:T(8,128)(2,1)S(1)}, bf16[128,1664]{1,0:T(8,128)(2,1)S(1)}, u32[]{:S(2)}, u32[]{:S(2)}) collective-permute-start(bf16[128,1664]{1,0:T(8,128)(2,1)S(1)} %copy-done.39), channel_id=1, source_target_pairs={{0,3},{1,0},{2,1},{3,2},{4,7},{5,4},{6,5},{7,6},{8,11},{9,8},{10,9... | collective-permute-start | bytes 1277960 | tf_op jit(solution)/shard_map/ppermute | solution.py:730
  384.7 23.7 %collective-permute-start.44 = (bf16[128,1536]{1,0:T(8,128)(2,1)S(1)}, bf16[128,1536]{1,0:T(8,128)(2,1)S(1)}, u32[]{:S(2)}, u32[]{:S(2)}) collective-permute-start(bf16[128,1536]{1,0:T(8,128)(2,1)S(1)} %get-tuple-element.198), channel_id=1, source_target_pairs={{0,64},{1,65},{2,66},{3,67},{4,68},{5,69},{6,70},{7,71},{8,72},{9,... | collective-permute-start | bytes 1179656 | tf_op jit(solution)/shard_map/ppermute | solution.py:1035
  389.3 31.2 %collective-permute-start.40 = (bf16[128,1536]{1,0:T(8,128)(2,1)S(1)}, bf16[128,1536]{1,0:T(8,128)(2,1)S(1)}, u32[]{:S(2)}, u32[]{:S(2)}) collective-permute-start(bf16[128,1536]{1,0:T(8,128)(2,1)S(1)} %convert_element_type.328), channel_id=1, source_target_pairs={{64,0},{65,1},{66,2},{67,3},{68,4},{69,5},{70,6},{71,7},{72,8},{73... | collective-permute-start | bytes 1179656 | tf_op jit(solution)/shard_map/ppermute | solution.py:1036
  (85 other events, 1058.2 us)
Sparse Core Ops, SparseCore 0:
  34.2 55.9 all-gather.6
  92.5 50.8 all-gather.8
  204.9 75.5 reduce-scatter.2
  287.0 52.4 reduce-scatter.4
  361.9 54.2 all-gather.10

commit v13 on v11

--- a/solution.py
+++ b/solution.py
@@ -20,7 +20,7 @@
 WIDE = HALF * LANES
 VMEM_LIMIT = 34 * 1024 * 1024
 VMEM_MOST = 60 * 1024 * 1024
-VMEM_BACK = 56 * 1024 * 1024
+VMEM_BACK = 40 * 1024 * 1024
 DP = ("x", "z", "core")
 
 

time: 443 us -> 448 us (1.011)
    unnamed x112 -> x132, local copies, waits for them, and re-layouts: 12.6 us -> 19.3 us
  transfers between devices with their start and end apart: 59 -> 59, of which waited for: 32 -> 33; matrix products, arithmetic and copies ran while one was open for 8% -> 8% of each run, Pallas kernels for 9% -> 9%
where the time goes in v13:
time: 448 us; the launch traced here: 440 us
  waiting for transfers between devices  186 us (42%)
  Pallas kernels  92.1 us (21%)
  starting transfers between devices  80.4 us (18%)
  local copies, waits for them, and re-layouts  38.3 us (9%)
  other arithmetic  26.8 us (6%)
  between operations  15.8 us (4%)
    ppermute x36, waiting for transfers between devices, send_shard(): return lax.ppermute(v, 'shard', ring(SLOTS, k)) if k else v  130 us
    pallas_call x6, Pallas kernels, kernel_call(): pl.pallas_call(run, in_specs=[pl.BlockSpec(memory_space=pltpu.VMEM if len...  82.2 us
    ppermute x36, starting transfers between devices, send_shard(): return lax.ppermute(v, 'shard', ring(SLOTS, k)) if k else v  47.8 us
    unnamed x132, local copies, waits for them, and re-layouts  19.3 us
    ppermute x4, waiting for transfers between devices, swap_section(): return lax.ppermute(v, 'section', [(0, 1), (1, 0)])  14.4 us
    pallas_call x1, Pallas kernels, assemble(): pl.pallas_call(body, grid=(9,), in_specs=[pl.BlockSpec((16, 48, quarter),...  9.94 us
    ppermute x4, starting transfers between devices, send_across(): return lax.ppermute(v, ('section', 'shard'), pairs)  9.45 us
    all_to_all x1, waiting for transfers between devices, across(): return lax.all_to_all(v, ('section', 'shard'), 0, 0)  9.05 us
  transfers between devices with their start and end apart: 59, of which 33 were waited for; matrix products, arithmetic and copies ran while one was open for 8% of the time, Pallas kernels for 9%

profile of v13, /device:TPU:4, one launch (start us, length us, event | category | flops | bytes accessed | tf_op | source)
XLA Modules:
  0.0 439.9 jit_solution(2856119582644569082)
XLA Ops:
  13.0 5.7 %collective-permute-start.4 = (bf16[112,384]{1,0:T(8,128)(2,1)S(1)}, bf16[112,384]{1,0:T(8,128)(2,1)S(1)}, u32[]{:S(2)}, u32[]{:S(2)}) collective-permute-start(bf16[112,384]{1,0:T(8,128)(2,1)S(1)} %get-tuple-element.260), channel_id=1, source_target_pairs={{0,66},{1,67},{2,64},{3,65},{64,2},{65,3},{66,0},{67,1},{4,70},{5,... | collective-permute-start | bytes 258056 | tf_op jit(solution)/shard_map/weights/ppermute | solution.py:739
  41.2 5.3 %collective-permute-done.10.refs_3_ = bf16[128,1536]{1,0:T(8,128)(2,1)S(1)} collective-permute-done((bf16[128,1536]{1,0:T(8,128)(2,1)S(1)}, bf16[128,1536]{1,0:T(8,128)(2,1)S(1)}, u32[]{:S(2)}, u32[]{:S(2)}) %collective-permute-start.10) | collective-permute-done | bytes 393248 | tf_op jit(solution)/shard_map/weights/ppermute | solution.py:730
  46.6 5.0 %collective-permute-done.8.refs_1_ = bf16[128,1536]{1,0:T(8,128)(2,1)S(1)} collective-permute-done((bf16[128,1536]{1,0:T(8,128)(2,1)S(1)}, bf16[128,1536]{1,0:T(8,128)(2,1)S(1)}, u32[]{:S(2)}, u32[]{:S(2)}) %collective-permute-start.8) | collective-permute-done | bytes 393248 | tf_op jit(solution)/shard_map/weights/ppermute | solution.py:730
  67.1 7.7 %collective-permute-done.17 = bf16[4,187,128]{2,1,0:T(8,128)(2,1)S(1)} collective-permute-done((bf16[4,187,128]{2,1,0:T(8,128)(2,1)S(1)}, bf16[4,187,128]{2,1,0:T(8,128)(2,1)S(1)}, u32[]{:S(2)}, u32[]{:S(2)}) %collective-permute-start.17) | collective-permute-done | bytes 191520 | tf_op jit(solution)/shard_map/small_weights/ppermute | solution.py:747
  84.3 5.9 %all-gather.7.cloned.1.call-done = bf16[2560,1536]{1,0:T(8,128)(2,1)} async-done(((bf16[160,1536]{1,0:T(8,128)(2,1)}), bf16[2560,1536]{1,0:T(8,128)(2,1)}) %all-gather.7.cloned.1.call-update) | async-done | bytes 7864336 | tf_op jit(solution)/shard_map/weights/all_gather | solution.py:868
  90.7 14.3 %layer_forward.2 = (bf16[128,1664]{1,0:T(8,128)(2,1)}, bf16[128,1664]{1,0:T(8,128)(2,1)}, bf16[128,1664]{1,0:T(8,128)(2,1)}, bf16[128,1664]{1,0:T(8,128)(2,1)}, ...) custom-call(bf16[128,1536]{1,0:T(8,128)(2,1)} %copy-done.32, ...), custom_call_target="tpu_custom_call" | custom-call | flops 19800000512 | bytes 1048576 | tf_op jit(solution)/shard_map/layer_forward/pallas_call | solution.py:156
  110.8 7.7 %collective-permute-done.18 = bf16[128,1664]{1,0:T(8,128)(2,1)S(1)} collective-permute-done((bf16[128,1664]{1,0:T(8,128)(2,1)}, bf16[128,1664]{1,0:T(8,128)(2,1)S(1)}, u32[]{:S(2)}, u32[]{:S(2)}) %collective-permute-start.18) | collective-permute-done | bytes 426016 | tf_op jit(solution)/shard_map/ppermute | solution.py:730
  118.5 10.1 %collective-permute-done.19 = bf16[128,1664]{1,0:T(8,128)(2,1)S(1)} collective-permute-done((bf16[128,1664]{1,0:T(8,128)(2,1)}, bf16[128,1664]{1,0:T(8,128)(2,1)S(1)}, u32[]{:S(2)}, u32[]{:S(2)}) %collective-permute-start.19) | collective-permute-done | bytes 426016 | tf_op jit(solution)/shard_map/ppermute | solution.py:730
  135.4 15.0 %collective-permute-done.21.refs_1_ = bf16[128,1536]{1,0:T(8,128)(2,1)S(1)} collective-permute-done((bf16[128,1536]{1,0:T(8,128)(2,1)S(1)}, bf16[128,1536]{1,0:T(8,128)(2,1)S(1)}, u32[]{:S(2)}, u32[]{:S(2)}) %collective-permute-start.21) | collective-permute-done | bytes 393248 | tf_op jit(solution)/shard_map/ppermute | solution.py:730
  154.9 15.0 %layer_forward.3 = (bf16[128,1664]{1,0:T(8,128)(2,1)}, bf16[128,1664]{1,0:T(8,128)(2,1)}, bf16[128,1664]{1,0:T(8,128)(2,1)}, bf16[128,1664]{1,0:T(8,128)(2,1)}, ...) custom-call(bf16[128,1536]{1,0:T(8,128)(2,1)} %copy-done.35, ...), custom_call_target="tpu_custom_call" | custom-call | flops 19800000512 | bytes 1048576 | tf_op jit(solution)/shard_map/layer_forward/pallas_call | solution.py:156
  182.0 26.8 %backward_1.1 = (bf16[512,768]{1,0:T(8,128)(2,1)}, bf16[512,768]{1,0:T(8,128)(2,1)}, f32[6,8,128]{2,1,0:T(8,128)S(1)}, bf16[512,768]{1,0:T(8,128)(2,1)}, bf16[51...) custom-call(bf16[128,1536]{1,0:T(8,128)(2,1)S(1)} %copy-done.3, ...), custom_call_target="tpu_custom_call" | custom-call | flops 30799998976 | bytes 1048576 | tf_op jit(solution)/shard_map/backward_1/pallas_call | solution.py:156
  213.7 7.9 %collective-permute-done.27 = bf16[128,1536]{1,0:T(8,128)(2,1)} collective-permute-done((bf16[128,1536]{1,0:T(8,128)(2,1)S(1)}, bf16[128,1536]{1,0:T(8,128)(2,1)}, u32[]{:S(2)}, u32[]{:S(2)}) %collective-permute-start.27) | collective-permute-done | bytes 393248 | tf_op jit(solution)/shard_map/ppermute | solution.py:730
  221.6 7.9 %collective-permute-done.28 = bf16[128,1536]{1,0:T(8,128)(2,1)} collective-permute-done((bf16[128,1536]{1,0:T(8,128)(2,1)S(1)}, bf16[128,1536]{1,0:T(8,128)(2,1)}, u32[]{:S(2)}, u32[]{:S(2)}) %collective-permute-start.28) | collective-permute-done | bytes 393248 | tf_op jit(solution)/shard_map/ppermute | solution.py:730
  237.3 17.5 %collective-permute-done.30.refs_1_ = bf16[128,1664]{1,0:T(8,128)(2,1)S(1)} collective-permute-done((bf16[128,1664]{1,0:T(8,128)(2,1)S(1)}, bf16[128,1664]{1,0:T(8,128)(2,1)S(1)}, u32[]{:S(2)}, u32[]{:S(2)}) %collective-permute-start.30) | collective-permute-done | bytes 426016 | tf_op jit(solution)/shard_map/ppermute | solution.py:730
  263.3 10.7 %backward_0_gate.1 = (bf16[512,768]{1,0:T(8,128)(2,1)}, bf16[512,768]{1,0:T(8,128)(2,1)S(1)}, f32[512,768]{1,0:T(8,128)S(1)}, f32[6,8,128]{2,1,0:T(8,128)S(1)}, ...) custom-call(bf16[128,1664]{1,0:T(8,128)(2,1)S(1)} %pad_maximum_fusion.4.refs_0_, ...), custom_call_target="tpu_custom_call" | custom-call | flops 15399999488 | bytes 1048576 | tf_op jit(solution)/shard_map/backward_0_gate/pallas_call | solution.py:156
  274.2 10.8 %backward_0_scan.1 = (f32[6,8,128]{2,1,0:T(8,128)S(1)}, bf16[512,768]{1,0:T(8,128)(2,1)S(1)}, bf16[512,384]{1,0:T(8,128)(2,1)S(1)}, f32[2,8,128]{2,1,0:T(8,128)S...) custom-call(f32[2,512,768]{2,1,0:T(8,128)S(1)} %copy-done.18, ...), custom_call_target="tpu_custom_call" | custom-call | flops 22000001024 | bytes 1048576 | tf_op jit(solution)/shard_map/backward_0_scan/pallas_call | solution.py:156
  309.9 15.0 %collective-permute-done.35 = bf16[128,1536]{1,0:T(8,128)(2,1)S(1)} collective-permute-done((bf16[128,1536]{1,0:T(8,128)(2,1)S(1)}, bf16[128,1536]{1,0:T(8,128)(2,1)S(1)}, u32[]{:S(2)}, u32[]{:S(2)}) %collective-permute-start.35) | collective-permute-done | bytes 393248 | tf_op jit(solution)/shard_map/ppermute | solution.py:730
  326.7 15.8 %collective-permute-done.38 = bf16[128,1664]{1,0:T(8,128)(2,1)S(1)} collective-permute-done((bf16[128,1664]{1,0:T(8,128)(2,1)S(1)}, bf16[128,1664]{1,0:T(8,128)(2,1)S(1)}, u32[]{:S(2)}, u32[]{:S(2)}) %collective-permute-start.38) | collective-permute-done | bytes 426016 | tf_op jit(solution)/shard_map/ppermute | solution.py:730
  347.6 6.6 %all-to-all-start = ((bf16[8,112,384]{2,1,0:T(8,128)(2,1)}), bf16[8,112,384]{2,1,0:T(8,128)(2,1)S(1)}, u32[]{:S(2)}, u32[]{:S(2)}) async-start(bf16[8,112,384]{2,1,0:T(8,128)(2,1)} %pad_maximum_fusion.1), calls=%async_computation.2 | async-start | bytes 1376256 | tf_op jit(solution)/shard_map/all_to_all | solution.py:743
  355.2 9.0 %all-to-all-done = bf16[8,112,384]{2,1,0:T(8,128)(2,1)S(1)} async-done(((bf16[8,112,384]{2,1,0:T(8,128)(2,1)}), bf16[8,112,384]{2,1,0:T(8,128)(2,1)S(1)}, u32[]{:S(2)}, u32[]{:S(2)}) %all-to-all-start) | async-done | bytes 688160 | tf_op jit(solution)/shard_map/all_to_all | solution.py:743
  381.8 7.9 %collective-permute-done.42 = bf16[128,1536]{1,0:T(8,128)(2,1)S(1)} collective-permute-done((bf16[128,1536]{1,0:T(8,128)(2,1)S(1)}, bf16[128,1536]{1,0:T(8,128)(2,1)S(1)}, u32[]{:S(2)}, u32[]{:S(2)}) %collective-permute-start.42) | collective-permute-done | bytes 393248 | tf_op jit(solution)/shard_map/ppermute | solution.py:1015
  389.9 5.3 %collective-permute-done.46 = f32[276,128]{1,0:T(8,128)S(1)} collective-permute-done((f32[276,128]{1,0:T(8,128)S(1)}, f32[276,128]{1,0:T(8,128)S(1)}, u32[]{:S(2)}, u32[]{:S(2)}) %collective-permute-start.46) | collective-permute-done | bytes 141344 | tf_op jit(solution)/shard_map/ppermute | solution.py:783
  396.5 8.0 %collective-permute-done.48 = f32[276,128]{1,0:T(8,128)S(1)} collective-permute-done((f32[276,128]{1,0:T(8,128)S(1)}, f32[276,128]{1,0:T(8,128)S(1)}, u32[]{:S(2)}, u32[]{:S(2)}) %collective-permute-start.48) | collective-permute-done | bytes 141344 | tf_op jit(solution)/shard_map/ppermute | solution.py:785
  423.0 9.9 %assemble.1 = (f32[6448,384]{1,0:T(8,128)}, f32[768,1536]{1,0:T(8,128)}) custom-call(bf16[16,592,384]{2,1,0:T(8,128)(2,1)} %bitcast.183, bf16[16,592,384]{2,1,0:T(8,128)(2,1)} %bitcast.184, bf16[16,592,384]{2,1,0:T(8,128)(2,1)} %bitcast.185, f32[48,384]{1,0:T(8,128)} %reshape.502.dt), custom_call_target="tpu_custom_call" | custom-call | tf_op jit(solution)/shard_map/assemble/pallas_call | solution.py:700
  (411 shorter events, 173.3 us)
Async XLA Ops:
  7.2 83.0 %all-gather.7.cloned.1.call-start = ((), (), s32[]{:S(2)}) async-start(), calls=%async_computation.5 | async-start | bytes 8355840 | tf_op jit(solution)/shard_map/weights/all_gather | solution.py:868
  34.0 120.0 %all-gather.9.cloned.1.call-start = ((), (), s32[]{:S(2)}) async-start(), calls=%async_computation.6 | async-start | bytes 8355840 | tf_op jit(solution)/shard_map/all_gather | solution.py:926
  64.8 19.5 %collective-permute-start.11 = (bf16[128,1536]{1,0:T(8,128)(2,1)S(1)}, bf16[128,1536]{1,0:T(8,128)(2,1)S(1)}, u32[]{:S(2)}, u32[]{:S(2)}) collective-permute-start(bf16[128,1536]{1,0:T(8,128)(2,1)S(1)} %fusion.6.refs_4_.refs_0_), channel_id=1, source_target_pairs={{0,3},{1,0},{2,1},{3,2},{4,7},{5,4},{6,5},{7,6},{8,11},{9,8},{10,9... | collective-permute-start | bytes 1179656 | tf_op jit(solution)/shard_map/ppermute | solution.py:730
  64.9 19.4 %collective-permute-start.12 = (bf16[128,1536]{1,0:T(8,128)(2,1)S(1)}, bf16[128,1536]{1,0:T(8,128)(2,1)S(1)}, u32[]{:S(2)}, u32[]{:S(2)}) collective-permute-start(bf16[128,1536]{1,0:T(8,128)(2,1)S(1)} %fusion.6.refs_4_.refs_0_), channel_id=1, source_target_pairs={{0,2},{1,3},{2,0},{3,1},{4,6},{5,7},{6,4},{7,5},{8,10},{9,11},{10,... | collective-permute-start | bytes 1179656 | tf_op jit(solution)/shard_map/ppermute | solution.py:730
  66.3 18.0 %collective-permute-start.13 = (bf16[128,1536]{1,0:T(8,128)(2,1)S(1)}, bf16[128,1536]{1,0:T(8,128)(2,1)S(1)}, u32[]{:S(2)}, u32[]{:S(2)}) collective-permute-start(bf16[128,1536]{1,0:T(8,128)(2,1)S(1)} %fusion.6.refs_4_.refs_0_), channel_id=1, source_target_pairs={{0,1},{1,2},{2,3},{3,0},{4,5},{5,6},{6,7},{7,4},{8,9},{9,10},{10,1... | collective-permute-start | bytes 1179656 | tf_op jit(solution)/shard_map/ppermute | solution.py:730
  90.2 198.4 %reduce-scatter.3.cloned.1.call-start = ((), (), s32[]{:S(2)}) async-start(), calls=%async_computation.3 | async-start | bytes 8355840 | tf_op jit(solution)/shard_map/reduce_scatter | solution.py:971
  106.6 22.0 %collective-permute-start.19 = (bf16[128,1664]{1,0:T(8,128)(2,1)}, bf16[128,1664]{1,0:T(8,128)(2,1)S(1)}, u32[]{:S(2)}, u32[]{:S(2)}) collective-permute-start(bf16[128,1664]{1,0:T(8,128)(2,1)} %get-tuple-element.123), channel_id=1, source_target_pairs={{0,2},{1,3},{2,0},{3,1},{4,6},{5,7},{6,4},{7,5},{8,10},{9,11},{10,... | collective-permute-start | bytes 1277960 | tf_op jit(solution)/shard_map/ppermute | solution.py:730
  109.3 19.3 %collective-permute-start.20 = (bf16[128,1664]{1,0:T(8,128)(2,1)}, bf16[128,1664]{1,0:T(8,128)(2,1)S(1)}, u32[]{:S(2)}, u32[]{:S(2)}) collective-permute-start(bf16[128,1664]{1,0:T(8,128)(2,1)} %get-tuple-element.124), channel_id=1, source_target_pairs={{0,3},{1,0},{2,1},{3,2},{4,7},{5,4},{6,5},{7,6},{8,11},{9,8},{10,9... | collective-permute-start | bytes 1277960 | tf_op jit(solution)/shard_map/ppermute | solution.py:730
  131.1 19.3 %collective-permute-start.21 = (bf16[128,1536]{1,0:T(8,128)(2,1)S(1)}, bf16[128,1536]{1,0:T(8,128)(2,1)S(1)}, u32[]{:S(2)}, u32[]{:S(2)}) collective-permute-start(bf16[128,1536]{1,0:T(8,128)(2,1)S(1)} %get-tuple-element.206.refs_0_), channel_id=1, source_target_pairs={{0,3},{1,0},{2,1},{3,2},{4,7},{5,4},{6,5},{7,6},{8,11},{9,8},{10,9... | collective-permute-start | bytes 1179656 | tf_op jit(solution)/shard_map/ppermute | solution.py:730
  134.5 19.5 %collective-permute-start.23 = (bf16[128,1536]{1,0:T(8,128)(2,1)S(1)}, bf16[128,1536]{1,0:T(8,128)(2,1)S(1)}, u32[]{:S(2)}, u32[]{:S(2)}) collective-permute-start(bf16[128,1536]{1,0:T(8,128)(2,1)S(1)} %get-tuple-element.206.refs_0_), channel_id=1, source_target_pairs={{0,1},{1,2},{2,3},{3,0},{4,5},{5,6},{6,7},{7,4},{8,9},{9,10},{10,1... | collective-permute-start | bytes 1179656 | tf_op jit(solution)/shard_map/ppermute | solution.py:730
  208.8 134.9 %reduce-scatter.5.cloned.1.call-start = ((), (), s32[]{:S(2)}) async-start(), calls=%async_computation.4 | async-start | bytes 4423680 | tf_op jit(solution)/shard_map/reduce_scatter | solution.py:1000
  210.7 18.8 %collective-permute-start.28 = (bf16[128,1536]{1,0:T(8,128)(2,1)S(1)}, bf16[128,1536]{1,0:T(8,128)(2,1)}, u32[]{:S(2)}, u32[]{:S(2)}) collective-permute-start(bf16[128,1536]{1,0:T(8,128)(2,1)S(1)} %get-tuple-element.142), channel_id=1, source_target_pairs={{0,2},{1,3},{2,0},{3,1},{4,6},{5,7},{6,4},{7,5},{8,10},{9,11},{10,... | collective-permute-start | bytes 1179656 | tf_op jit(solution)/shard_map/ppermute | solution.py:730
  234.1 20.7 %collective-permute-start.30 = (bf16[128,1664]{1,0:T(8,128)(2,1)S(1)}, bf16[128,1664]{1,0:T(8,128)(2,1)S(1)}, u32[]{:S(2)}, u32[]{:S(2)}) collective-permute-start(bf16[128,1664]{1,0:T(8,128)(2,1)S(1)} %pad_maximum_fusion.4.refs_0_), channel_id=1, source_target_pairs={{0,3},{1,0},{2,1},{3,2},{4,7},{5,4},{6,5},{7,6},{8,11},{9,8},{10,9... | collective-permute-start | bytes 1277960 | tf_op jit(solution)/shard_map/ppermute | solution.py:730
  236.3 18.4 %collective-permute-start.31 = (bf16[128,1664]{1,0:T(8,128)(2,1)S(1)}, bf16[128,1664]{1,0:T(8,128)(2,1)S(1)}, u32[]{:S(2)}, u32[]{:S(2)}) collective-permute-start(bf16[128,1664]{1,0:T(8,128)(2,1)S(1)} %pad_maximum_fusion.4.refs_0_), channel_id=1, source_target_pairs={{0,2},{1,3},{2,0},{3,1},{4,6},{5,7},{6,4},{7,5},{8,10},{9,11},{10,... | collective-permute-start | bytes 1277960 | tf_op jit(solution)/shard_map/ppermute | solution.py:730
  236.9 21.5 %collective-permute-start.32 = (bf16[128,1664]{1,0:T(8,128)(2,1)S(1)}, bf16[128,1664]{1,0:T(8,128)(2,1)S(1)}, u32[]{:S(2)}, u32[]{:S(2)}) collective-permute-start(bf16[128,1664]{1,0:T(8,128)(2,1)S(1)} %pad_maximum_fusion.4.refs_0_), channel_id=1, source_target_pairs={{0,1},{1,2},{2,3},{3,0},{4,5},{5,6},{6,7},{7,4},{8,9},{9,10},{10,1... | collective-permute-start | bytes 1277960 | tf_op jit(solution)/shard_map/ppermute | solution.py:730
  303.2 21.7 %collective-permute-start.35 = (bf16[128,1536]{1,0:T(8,128)(2,1)S(1)}, bf16[128,1536]{1,0:T(8,128)(2,1)S(1)}, u32[]{:S(2)}, u32[]{:S(2)}) collective-permute-start(bf16[128,1536]{1,0:T(8,128)(2,1)S(1)} %get-tuple-element.170), channel_id=1, source_target_pairs={{0,1},{1,2},{2,3},{3,0},{4,5},{5,6},{6,7},{7,4},{8,9},{9,10},{10,1... | collective-permute-start | bytes 1179656 | tf_op jit(solution)/shard_map/ppermute | solution.py:730
  303.3 21.6 %collective-permute-start.36 = (bf16[128,1536]{1,0:T(8,128)(2,1)S(1)}, bf16[128,1536]{1,0:T(8,128)(2,1)S(1)}, u32[]{:S(2)}, u32[]{:S(2)}) collective-permute-start(bf16[128,1536]{1,0:T(8,128)(2,1)S(1)} %get-tuple-element.171), channel_id=1, source_target_pairs={{0,2},{1,3},{2,0},{3,1},{4,6},{5,7},{6,4},{7,5},{8,10},{9,11},{10,... | collective-permute-start | bytes 1179656 | tf_op jit(solution)/shard_map/ppermute | solution.py:730
  305.4 20.4 %collective-permute-start.37 = (bf16[128,1536]{1,0:T(8,128)(2,1)S(1)}, bf16[128,1536]{1,0:T(8,128)(2,1)S(1)}, u32[]{:S(2)}, u32[]{:S(2)}) collective-permute-start(bf16[128,1536]{1,0:T(8,128)(2,1)S(1)} %get-tuple-element.172), channel_id=1, source_target_pairs={{0,3},{1,0},{2,1},{3,2},{4,7},{5,4},{6,5},{7,6},{8,11},{9,8},{10,9... | collective-permute-start | bytes 1179656 | tf_op jit(solution)/shard_map/ppermute | solution.py:730
  306.5 36.0 %collective-permute-start.38 = (bf16[128,1664]{1,0:T(8,128)(2,1)S(1)}, bf16[128,1664]{1,0:T(8,128)(2,1)S(1)}, u32[]{:S(2)}, u32[]{:S(2)}) collective-permute-start(bf16[128,1664]{1,0:T(8,128)(2,1)S(1)} %copy-done.53), channel_id=1, source_target_pairs={{0,1},{1,2},{2,3},{3,0},{4,5},{5,6},{6,7},{7,4},{8,9},{9,10},{10,1... | collective-permute-start | bytes 1277960 | tf_op jit(solution)/shard_map/ppermute | solution.py:730
  307.5 35.0 %collective-permute-start.39 = (bf16[128,1664]{1,0:T(8,128)(2,1)S(1)}, bf16[128,1664]{1,0:T(8,128)(2,1)S(1)}, u32[]{:S(2)}, u32[]{:S(2)}) collective-permute-start(bf16[128,1664]{1,0:T(8,128)(2,1)S(1)} %copy-done.52), channel_id=1, source_target_pairs={{0,2},{1,3},{2,0},{3,1},{4,6},{5,7},{6,4},{7,5},{8,10},{9,11},{10,... | collective-permute-start | bytes 1277960 | tf_op jit(solution)/shard_map/ppermute | solution.py:730
  324.9 18.4 %collective-permute-start.40 = (bf16[128,1664]{1,0:T(8,128)(2,1)S(1)}, bf16[128,1664]{1,0:T(8,128)(2,1)S(1)}, u32[]{:S(2)}, u32[]{:S(2)}) collective-permute-start(bf16[128,1664]{1,0:T(8,128)(2,1)S(1)} %copy-done.51), channel_id=1, source_target_pairs={{0,3},{1,0},{2,1},{3,2},{4,7},{5,4},{6,5},{7,6},{8,11},{9,8},{10,9... | collective-permute-start | bytes 1277960 | tf_op jit(solution)/shard_map/ppermute | solution.py:730
  354.2 68.8 %all-gather.11.cloned.1.call-start = ((), (), s32[]{:S(2)}) async-start(), calls=%async_computation.7 | async-start | bytes 7729152 | tf_op jit(solution)/shard_map/all_gather | solution.py:1031
  368.4 21.4 %collective-permute-start.42 = (bf16[128,1536]{1,0:T(8,128)(2,1)S(1)}, bf16[128,1536]{1,0:T(8,128)(2,1)S(1)}, u32[]{:S(2)}, u32[]{:S(2)}) collective-permute-start(bf16[128,1536]{1,0:T(8,128)(2,1)S(1)} %convert_element_type.333), channel_id=1, source_target_pairs={{0,64},{1,65},{2,66},{3,67},{4,68},{5,69},{6,70},{7,71},{8,72},{9,... | collective-permute-start | bytes 1179656 | tf_op jit(solution)/shard_map/ppermute | solution.py:1015
  374.3 22.1 %collective-permute-start.41 = (bf16[128,1536]{1,0:T(8,128)(2,1)S(1)}, bf16[128,1536]{1,0:T(8,128)(2,1)S(1)}, u32[]{:S(2)}, u32[]{:S(2)}) collective-permute-start(bf16[128,1536]{1,0:T(8,128)(2,1)S(1)} %convert_element_type.332), channel_id=1, source_target_pairs={{64,0},{65,1},{66,2},{67,3},{68,4},{69,5},{70,6},{71,7},{72,8},{73... | collective-permute-start | bytes 1179656 | tf_op jit(solution)/shard_map/ppermute | solution.py:1016
  (96 other events, 1217.7 us)
Sparse Core Ops, SparseCore 0:
  34.2 55.9 all-gather.6
  92.5 50.8 all-gather.8
  208.9 75.4 reduce-scatter.2
  293.2 49.3 reduce-scatter.4
  365.4 57.5 all-gather.10
